TPU v7x, 32 devices: a whole 2x2x4 slice. The times are simulated.
32 devices in a mesh: dp: 4 (over z), blk: 8 (over y, x, core).
Axes of the slice: x: 2, y: 2, z: 4, core: 2. Of those that a mesh axis runs over, the one named last changes fastest.
Arguments:
- tokens: bfloat16 [8, 2048, 1024], P('dp', 'blk'), may hold values from -6 to 6
- doc_lengths: int32 [8, 8], P('dp'), may hold values from 1 to 1793, 2048 in all within a row
- g_attn: float32 [1024], replicated, may hold values from 0.5 to 1.5
- w_query: bfloat16 [1024, 1024], replicated, may hold values from -0.1875 to 0.1875
- w_key: bfloat16 [1024, 512], replicated, may hold values from -0.1875 to 0.1875
- w_value: bfloat16 [1024, 512], replicated, may hold values from -0.1875 to 0.1875
- q_gain: float32 [64], replicated, may hold values from 0.1 to 1.9
- k_gain: float32 [64], replicated, may hold values from 0.1 to 1.9
- w_out: bfloat16 [1024, 1024], replicated, may hold values from -1 to 1
- g_ffn: float32 [1024], replicated, may hold values from 0.5 to 1.5
- w_gate: bfloat16 [1024, 4608], replicated, may hold values from -0.1875 to 0.1875
- w_up: bfloat16 [1024, 4608], replicated, may hold values from -0.1875 to 0.1875
- w_down: bfloat16 [4608, 1024], replicated, may hold values from -0.09375 to 0.09375
- cotangent: bfloat16 [8, 2048, 1024], P('dp', 'blk'), may hold values from -6 to 6
Outputs:
- output: bfloat16 [8, 2048, 1024], P('dp', 'blk')
- input_grad: bfloat16 [8, 2048, 1024], P('dp', 'blk')
- grad_g_attn: float32 [1024], replicated
- grad_w_query: float32 [1024, 1024], P(('dp', 'blk'))
- grad_w_key: float32 [1024, 512], P(('dp', 'blk'))
- grad_w_value: float32 [1024, 512], P(('dp', 'blk'))
- grad_q_gain: float32 [64], replicated
- grad_k_gain: float32 [64], replicated
- grad_w_out: float32 [1024, 1024], P(('dp', 'blk'))
- grad_g_ffn: float32 [1024], replicated
- grad_w_gate: float32 [1024, 4608], P(('dp', 'blk'))
- grad_w_up: float32 [1024, 4608], P(('dp', 'blk'))
- grad_w_down: float32 [4608, 1024], P(('dp', 'blk'))
Inputs may be any that keep to these rules, and one draw needn't show every extreme that they name: `doc_lengths`: in each sequence the lengths sum to 2048, and one document has exactly 1793 tokens.
All inputs are finite; a program needn't handle non-finite values.
Results may differ from a plain program's by a relative error of at most 0.02.
Values may be sent and summed in bfloat16 or wider, within the bound.
A program may use at most 384 MiB of HBM per device.

v0:
```python
import jax
import jax.numpy as jnp
from jax import lax
from jax.sharding import PartitionSpec as P

HEADS = 16
KV_HEADS = 8
HEAD_DIM = 64


EPSILON = 1e-05
ROPE_BASE = 1000000.0
NEGATIVE = -1e30


def norm_rows(values, norm_gain):
    row_scale = lax.rsqrt(jnp.mean(values * values, axis=-1, keepdims=True) + EPSILON)
    normal = values * row_scale
    return (normal * norm_gain, normal, row_scale)


def norm_back(normal, row_scale, norm_gain, grad_out):
    pushed = grad_out * norm_gain
    inner = jnp.mean(pushed * normal, axis=-1, keepdims=True)
    grad_in = row_scale * (pushed - normal * inner)
    leading = tuple(range(grad_out.ndim - 1))
    return (grad_in, jnp.sum(grad_out * normal, axis=leading))


def doc_layout(lengths, places):
    ends = jnp.cumsum(lengths, axis=1)
    past = places[None, :, None] >= ends[:, None, :]
    docs = jnp.sum(past.astype(jnp.int32), axis=2)
    before = jnp.sum(jnp.where(past, lengths[:, None, :], 0), axis=2)
    return (docs, places[None, :] - before)


def rope_angles(positions):
    half = HEAD_DIM // 2
    freqs = ROPE_BASE ** (-jnp.arange(half, dtype=jnp.float32) / half)
    angles = positions.astype(jnp.float32)[..., None] * freqs
    return (jnp.cos(angles), jnp.sin(angles))


def rotate(values, cosine, sine):
    half = values.shape[-1] // 2
    first_half = values[..., :half]
    second_half = values[..., half:]
    cos_col = cosine[:, :, None, :]
    sin_col = sine[:, :, None, :]
    return jnp.concatenate(
        [
            first_half * cos_col - second_half * sin_col,
            second_half * cos_col + first_half * sin_col,
        ],
        axis=-1,
    )


def local(
    tokens,
    doc_lengths,
    g_attn,
    w_query,
    w_key,
    w_value,
    q_gain,
    k_gain,
    w_out,
    g_ffn,
    w_gate,
    w_up,
    w_down,
    cotangent,
):
    row_count, tok_count, width = tokens.shape
    grouping = HEADS // KV_HEADS
    flat_rows = row_count * tok_count
    kv_width = KV_HEADS * HEAD_DIM
    softmax_scale = HEAD_DIM ** (-0.5)
    places = lax.axis_index("blk") * tok_count + jnp.arange(tok_count, dtype=jnp.int32)
    query_docs, query_pos = doc_layout(doc_lengths, places)
    cosine, sine = rope_angles(query_pos)
    inputs = tokens.reshape(flat_rows, width).astype(jnp.float32)
    normed, normal_in, scale_in = norm_rows(inputs, g_attn)
    hidden_in = normed.astype(jnp.bfloat16)
    query_proj = jnp.dot(hidden_in, w_query, preferred_element_type=jnp.float32).reshape(
        row_count, tok_count, HEADS, HEAD_DIM
    )
    key_proj = jnp.dot(hidden_in, w_key, preferred_element_type=jnp.float32).reshape(
        row_count, tok_count, KV_HEADS, HEAD_DIM
    )
    value_b = (
        jnp.dot(hidden_in, w_value, preferred_element_type=jnp.float32)
        .astype(jnp.bfloat16)
        .reshape(row_count, tok_count, kv_width)
    )
    query_norm, query_normal, query_scale = norm_rows(query_proj, q_gain)
    key_norm, key_normal, key_scale = norm_rows(key_proj, k_gain)
    query_b = (
        rotate(query_norm, cosine, sine)
        .astype(jnp.bfloat16)
        .reshape(row_count, tok_count, KV_HEADS, grouping, HEAD_DIM)
    )
    key_b = (
        rotate(key_norm, cosine, sine).astype(jnp.bfloat16).reshape(row_count, tok_count, kv_width)
    )

    def piece_mask(size):
        key_places = jnp.arange(size, dtype=jnp.int32)
        key_docs, unused = doc_layout(doc_lengths, key_places)
        return (key_places[None, None, :] <= places[None, :, None]) & (
            key_docs[:, None, :] == query_docs[:, :, None]
        )

    def piece_scores(key_piece, allowed):
        key_heads = key_piece.reshape(row_count, key_piece.shape[1], KV_HEADS, HEAD_DIM)
        raw_scores = (
            jnp.einsum("rqkgd,rpkd->rkgqp", query_b, key_heads, preferred_element_type=jnp.float32)
            * softmax_scale
        )
        return (jnp.where(allowed[:, None, None], raw_scores, -jnp.inf), key_heads)

    stat_shape = (row_count, KV_HEADS, grouping, tok_count)
    key_piece = lax.all_gather(key_b, "blk", axis=1, tiled=True)
    value_piece = lax.all_gather(value_b, "blk", axis=1, tiled=True)
    allowed = piece_mask(key_piece.shape[1])
    running_max = jnp.full(stat_shape, NEGATIVE, jnp.float32)
    scores, key_heads = piece_scores(key_piece, allowed)
    new_max = jnp.maximum(running_max, jnp.max(scores, axis=-1))
    weights = jnp.exp(scores - new_max[..., None])
    value_heads = value_piece.reshape(row_count, value_piece.shape[1], KV_HEADS, HEAD_DIM)
    added = jnp.einsum(
        "rkgqp,rpkd->rkgqd",
        weights.astype(jnp.bfloat16),
        value_heads,
        preferred_element_type=jnp.float32,
    )
    running_sum = jnp.sum(weights, axis=-1)
    attended = added / running_sum[..., None]
    log_total = new_max + jnp.log(running_sum)
    attended_b = (
        jnp.transpose(attended, (0, 3, 1, 2, 4))
        .reshape(flat_rows, HEADS * HEAD_DIM)
        .astype(jnp.bfloat16)
    )
    middle = inputs + jnp.dot(attended_b, w_out, preferred_element_type=jnp.float32)
    normed_ffn, normal_ffn, scale_ffn = norm_rows(middle, g_ffn)
    hidden_ffn = normed_ffn.astype(jnp.bfloat16)
    gate = jnp.dot(hidden_ffn, w_gate, preferred_element_type=jnp.float32)
    up_proj = jnp.dot(hidden_ffn, w_up, preferred_element_type=jnp.float32)
    sigmoid_gate = jax.nn.sigmoid(gate)
    silu_gate = gate * sigmoid_gate
    hidden = (silu_gate * up_proj).astype(jnp.bfloat16)
    result = middle + jnp.dot(hidden, w_down, preferred_element_type=jnp.float32)
    output = result.astype(jnp.bfloat16).reshape(row_count, tok_count, width)
    grad_out = cotangent.reshape(flat_rows, width)
    grad_w_down = jnp.einsum("tf,td->fd", hidden, grad_out, preferred_element_type=jnp.float32)
    grad_hidden = jnp.einsum("td,fd->tf", grad_out, w_down, preferred_element_type=jnp.float32)
    grad_gate = (grad_hidden * up_proj * sigmoid_gate * (1.0 + gate * (1.0 - sigmoid_gate))).astype(
        jnp.bfloat16
    )
    grad_up = (grad_hidden * silu_gate).astype(jnp.bfloat16)
    grad_w_gate = jnp.einsum("td,tf->df", hidden_ffn, grad_gate, preferred_element_type=jnp.float32)
    grad_w_up = jnp.einsum("td,tf->df", hidden_ffn, grad_up, preferred_element_type=jnp.float32)
    grad_h2 = jnp.einsum(
        "tf,df->td", grad_gate, w_gate, preferred_element_type=jnp.float32
    ) + jnp.einsum("tf,df->td", grad_up, w_up, preferred_element_type=jnp.float32)
    grad_mid, grad_ffn_gain = norm_back(normal_ffn, scale_ffn, g_ffn, grad_h2)
    grad_mid = grad_out.astype(jnp.float32) + grad_mid
    grad_attn = grad_mid.astype(jnp.bfloat16)
    grad_w_out = jnp.einsum("tc,td->cd", attended_b, grad_attn, preferred_element_type=jnp.float32)
    grad_attended = jnp.einsum(
        "td,cd->tc", grad_attn, w_out, preferred_element_type=jnp.float32
    ).astype(jnp.bfloat16)
    grad_heads = grad_attended.reshape(row_count, tok_count, KV_HEADS, grouping, HEAD_DIM)
    deltas = jnp.einsum("rqkgd,rkgqd->rkgq", grad_heads.astype(jnp.float32), attended)
    key_piece = lax.all_gather(key_b, "blk", axis=1, tiled=True)
    value_piece = lax.all_gather(value_b, "blk", axis=1, tiled=True)
    size = key_piece.shape[1]
    allowed = piece_mask(size)
    scores, key_heads = piece_scores(key_piece, allowed)
    probs = jnp.exp(scores - log_total[..., None])
    value_heads = value_piece.reshape(row_count, size, KV_HEADS, HEAD_DIM)
    value_piece_grad = jnp.einsum(
        "rkgqp,rqkgd->rpkd",
        probs.astype(jnp.bfloat16),
        grad_heads,
        preferred_element_type=jnp.float32,
    )
    grad_probs = jnp.einsum(
        "rqkgd,rpkd->rkgqp", grad_heads, value_heads, preferred_element_type=jnp.float32
    )
    grad_scores = (probs * (grad_probs - deltas[..., None])).astype(jnp.bfloat16)
    grad_query = jnp.einsum(
        "rkgqp,rpkd->rkgqd", grad_scores, key_heads, preferred_element_type=jnp.float32
    )
    key_piece_grad = jnp.einsum(
        "rkgqp,rqkgd->rpkd", grad_scores, query_b, preferred_element_type=jnp.float32
    )
    grad_keys = key_piece_grad.reshape(row_count, size, kv_width)
    grad_values = value_piece_grad.reshape(row_count, size, kv_width)
    grad_query, grad_keys, grad_values = (grad_query, grad_keys, grad_values)
    key_grad_mine, value_grad_mine = (
        lax.psum_scatter(
            grad_keys.astype(jnp.bfloat16), "blk", scatter_dimension=1, tiled=True
        ).astype(jnp.float32),
        lax.psum_scatter(
            grad_values.astype(jnp.bfloat16), "blk", scatter_dimension=1, tiled=True
        ).astype(jnp.float32),
    )
    grad_q_rot = (jnp.transpose(grad_query, (0, 3, 1, 2, 4)) * softmax_scale).reshape(
        row_count, tok_count, HEADS, HEAD_DIM
    )
    grad_k_rot = (key_grad_mine * softmax_scale).reshape(row_count, tok_count, KV_HEADS, HEAD_DIM)
    grad_q_proj, grad_query_gain = norm_back(
        query_normal, query_scale, q_gain, rotate(grad_q_rot, cosine, -sine)
    )
    grad_k_proj, grad_key_gain = norm_back(
        key_normal, key_scale, k_gain, rotate(grad_k_rot, cosine, -sine)
    )
    grad_q_b = grad_q_proj.astype(jnp.bfloat16).reshape(flat_rows, HEADS * HEAD_DIM)
    grad_k_b = grad_k_proj.astype(jnp.bfloat16).reshape(flat_rows, kv_width)
    grad_v_b = value_grad_mine.astype(jnp.bfloat16).reshape(flat_rows, kv_width)
    grad_w_query = jnp.einsum("td,tc->dc", hidden_in, grad_q_b, preferred_element_type=jnp.float32)
    grad_w_key = jnp.einsum("td,tc->dc", hidden_in, grad_k_b, preferred_element_type=jnp.float32)
    grad_w_value = jnp.einsum("td,tc->dc", hidden_in, grad_v_b, preferred_element_type=jnp.float32)
    grad_h1 = jnp.einsum("tc,dc->td", grad_q_b, w_query, preferred_element_type=jnp.float32)
    grad_h1 = grad_h1 + jnp.einsum("tc,dc->td", grad_k_b, w_key, preferred_element_type=jnp.float32)
    grad_h1 = grad_h1 + jnp.einsum(
        "tc,dc->td", grad_v_b, w_value, preferred_element_type=jnp.float32
    )
    grad_base, grad_attn_gain = norm_back(normal_in, scale_in, g_attn, grad_h1)
    input_grad = (grad_mid + grad_base).astype(jnp.bfloat16).reshape(row_count, tok_count, width)
    gain_attn, gain_query, gain_key, gain_ffn = lax.psum(
        (grad_attn_gain, grad_query_gain, grad_key_gain, grad_ffn_gain), ("dp", "blk")
    )
    locals_all = (
        grad_w_query,
        grad_w_key,
        grad_w_value,
        grad_w_out,
        grad_w_gate,
        grad_w_up,
        grad_w_down,
    )
    shared = (
        lax.psum_scatter(locals_all[0], ("dp", "blk"), scatter_dimension=0, tiled=True),
        lax.psum_scatter(locals_all[1], ("dp", "blk"), scatter_dimension=0, tiled=True),
        lax.psum_scatter(locals_all[2], ("dp", "blk"), scatter_dimension=0, tiled=True),
        lax.psum_scatter(locals_all[3], ("dp", "blk"), scatter_dimension=0, tiled=True),
        lax.psum_scatter(locals_all[4], ("dp", "blk"), scatter_dimension=0, tiled=True),
        lax.psum_scatter(locals_all[5], ("dp", "blk"), scatter_dimension=0, tiled=True),
        lax.psum_scatter(locals_all[6], ("dp", "blk"), scatter_dimension=0, tiled=True),
    )
    return (
        output,
        input_grad,
        gain_attn,
        shared[0],
        shared[1],
        shared[2],
        gain_query,
        gain_key,
        shared[3],
        gain_ffn,
        shared[4],
        shared[5],
        shared[6],
    )


def solution(mesh):
    return jax.shard_map(
        local,
        mesh=mesh,
        in_specs=(
            P("dp", "blk", None),
            P("dp", None),
            P(),
            P(),
            P(),
            P(),
            P(),
            P(),
            P(),
            P(),
            P(),
            P(),
            P(),
            P("dp", "blk", None),
        ),
        out_specs=(
            P("dp", "blk", None),
            P("dp", "blk", None),
            P(),
            P(("dp", "blk"), None),
            P(("dp", "blk"), None),
            P(("dp", "blk"), None),
            P(),
            P(),
            P(("dp", "blk"), None),
            P(),
            P(("dp", "blk"), None),
            P(("dp", "blk"), None),
            P(("dp", "blk"), None),
        ),
        check_vma=False,
    )
```

profile of v0, /device:TPU:0, one launch (start us, length us, event | category | flops | bytes accessed | tf_op | source)
XLA Modules:
  0.0 1564.7 jit_solution(11452451289347398913)
XLA Ops:
  34.6 23.7 %all-gather.3.cloned.1.call-done = bf16[2,2048,512]{1,2,0:T(8,128)(2,1)} async-done(((bf16[2,256,512]{1,2,0:T(8,128)(2,1)}), bf16[2,2048,512]{1,2,0:T(8,128)(2,1)}) %all-gather.3.cloned.1.call-update) | async-done | bytes 4194320 | tf_op jit(solution)/shard_map/all_gather | solution.py:125
  58.3 27.0 %fusion.44 = (f32[2,8,2,256]{3,2,1,0:T(2,128)S(1)}, f32[2,8,2,256,2048]{3,4,2,1,0:T(8,128)}) fusion(bf16[2,2048,8,64,1]{1,3,4,2,0:T(8,128)(2,1)} %bitcast.166, bf16[2,256,8,2,32]{1,4,3,2,0:T(8,128)(2,1)} %bitcast.176, bf16[2,256,8,2,32]{1,4,3,2,0:T(8,128)(2,1)} %bitcast.174, pred[2,256,2048]{1,2,0:T(8,128)(4,1)} %compare_and_fusion), kind=kOutput, calls=%fused_computation.113 | convolution fusion | flops 2199904256 | bytes 73433088 | tf_op jit(solution)/shard_map/rqkgd,rpkd->rkgqp/dot_general | solution.py:119
  85.3 21.3 %fusion.2 = f32[2,8,2,256]{3,2,1,0:T(2,128)S(1)} fusion(f32[2,8,2,256,2048]{3,4,2,1,0:T(8,128)} %get-tuple-element.48, f32[2,8,2,256]{3,2,1,0:T(2,128)S(1)} %broadcast_maximum_fusion), kind=kLoop, calls=%fused_computation.6 | loop fusion | flops 33546240 | bytes 67174400 | tf_op jit(solution)/shard_map/reduce_sum | solution.py:139
  113.0 26.3 %fusion.14 = (bf16[2,256,8,2,64]{1,4,3,2,0:T(8,128)(2,1)}, f32[2,8,2,256,64]{3,4,2,1,0:T(8,128)}) fusion(f32[2,256,8,2]{1,3,2,0:T(2,128)S(1)} %bitcast.193, bf16[2,2048,8,64,1]{1,3,4,2,0:T(8,128)(2,1)} %bitcast.163, f32[2,8,2,256,2048]{3,4,2,1,0:T(8,128)} %get-tuple-element.48, f32[2,8,2,256]{3,2,1,0:T(2,128)S(1)} %broadcast_maximum_fusion), kind=kOutput, calls=%fused_computation.23 | convolution fusion | flops 2182086656 | bytes 74514432 | tf_op jit(solution)/shard_map/rkgqp,rpkd->rkgqd/dot_general | solution.py:133
  144.9 12.1 fusion.45
  164.6 20.2 %multiply_convert_fusion = (bf16[512,4608]{1,0:T(8,128)(2,1)}, bf16[512,4608]{1,0:T(8,128)(2,1)}, bf16[512,4608]{1,0:T(8,128)(2,1)}) fusion(f32[512,4608]{1,0:T(8,128)} %fusion.45, f32[512,4608]{1,0:T(8,128)} %fusion.46, bf16[512,1024]{1,0:T(8,128)(2,1)S(1)} %bitcast.190, bf16[4608,1024]{1,0:T(8,128)(2,1)} %param.26), kind=kOutput, calls=%fused_computation.13 | convolution fusion | flops 4867227648 | bytes 43515904 | tf_op jit(solution)/shard_map/td,fd->tf/dot_general | solution.py:159
  184.8 9.2 fusion.47
  210.6 35.2 %fusion.1 = bf16[2,8,2,256,2048]{3,4,2,1,0:T(8,128)(2,1)} fusion(f32[2,8,2,256,2048]{3,4,2,1,0:T(8,128)} %get-tuple-element.48, bf16[2,2048,8,64,1]{1,3,4,2,0:T(8,128)(2,1)S(1)} %bitcast.164, f32[2,8,2,256]{3,2,1,0:T(2,128)S(1)} %multiply_reduce_fusion, f32[2,8,2,256]{3,2,1,0:T(2,128)S(1)} %log_add_fusion, bf16[2,256,8,2,64]{1,0,4,3,2:T(2,128)(2,1)S(1)} %reshape.273), kind=kOutput, calls=%fused_computation.2 | convolution fusion | flops 2214592512 | bytes 105971712 | tf_op jit(solution)/shard_map/rqkgd,rpkd->rkgqp/dot_general | solution.py:191
  245.8 17.3 %bitcast_convert_fusion.1 = bf16[2,8,64,2048]{3,2,1,0:T(8,128)(2,1)} fusion(bf16[2,8,2,256,2048]{3,4,2,1,0:T(8,128)(2,1)} %fusion.1, bf16[2,256,8,2,32]{1,4,3,2,0:T(8,128)(2,1)S(1)} %bitcast.177, bf16[2,256,8,2,32]{1,4,3,2,0:T(8,128)(2,1)S(1)} %bitcast.175), kind=kOutput, calls=%fused_computation.19 | convolution fusion | flops 2151677952 | bytes 38797312 | tf_op jit(solution)/shard_map/rkgqp,rqkgd->rpkd/dot_general | solution.py:198
  263.2 28.1 %bitcast_convert_fusion = bf16[2,8,64,2048]{3,2,1,0:T(8,128)(2,1)} fusion(f32[2,8,2,256,2048]{3,4,2,1,0:T(8,128)} %get-tuple-element.48, f32[2,8,2,256]{3,2,1,0:T(2,128)S(1)} %log_add_fusion, bf16[2,256,8,2,64]{1,0,4,3,2:T(2,128)(2,1)S(1)} %reshape.273), kind=kOutput, calls=%fused_computation.18 | convolution fusion | flops 2183135232 | bytes 72384512 | tf_op jit(solution)/shard_map/rkgqp,rqkgd->rpkd/dot_general | solution.py:185
  302.9 19.4 %convolution_multiply_fusion = f32[2,8,2,256,64]{3,4,2,1,0:T(8,128)} fusion(bf16[2,2048,8,64,1]{1,3,4,2,0:T(8,128)(2,1)} %bitcast.167, bf16[2,8,2,256,2048]{3,4,2,1,0:T(8,128)(2,1)} %fusion.1), kind=kOutput, calls=%fused_computation.57 | convolution fusion | flops 2148007936 | bytes 39845888 | tf_op jit(solution)/shard_map/rkgqp,rpkd->rkgqd/dot_general | solution.py:195
  336.3 33.2 %reduce-scatter.12.cloned.1.call-done = bf16[2,256,512]{2,1,0:T(8,128)(2,1)} async-done(((bf16[2,2048,512]{2,1,0:T(8,128)(2,1)}), bf16[2,256,512]{2,1,0:T(8,128)(2,1)}) %reduce-scatter.12.cloned.1.call-update) | async-done | bytes 524304 | tf_op jit(solution)/shard_map/reduce_scatter | solution.py:208
  372.9 11.5 fusion.53
  384.5 11.6 fusion.52
  397.3 11.4 fusion.54
  411.9 9.9 add_convert_fusion
  425.9 39.9 %all-reduce = (f32[1024]{0:T(1024)}, f32[64]{0:T(128)}, f32[64]{0:T(128)}, f32[1024]{0:T(1024)}) all-reduce(f32[1024]{0:T(1024)S(1)} %get-tuple-element.17, f32[64]{0:T(128)S(1)} %get-tuple-element.13, f32[64]{0:T(128)S(1)} %get-tuple-element.19, f32[1024]{0:T(1024)S(1)} %copy-done.50), channel_id=1, replica_groups=mesh['dp'=4,'blk'=8] {'dp','blk'}, use_global_device_ids=true, to_apply=%region_17.18 | all-reduce | flops 2176 | bytes 17408 | tf_op jit(solution)/shard_map/psum | solution.py:235
  469.7 43.8 %reduce-scatter.20.cloned.1.call-done = f32[32,1024]{1,0:T(8,128)} async-done(((f32[1024,1024]{1,0:T(8,128)}), f32[32,1024]{1,0:T(8,128)}) %reduce-scatter.20.cloned.1.call-update) | async-done | bytes 131088 | tf_op jit(solution)/shard_map/reduce_scatter | solution.py:251
  513.5 139.3 %reduce-scatter.14.cloned.1.call-done = f32[32,1024]{1,0:T(8,128)} async-done(((f32[1024,1024]{1,0:T(8,128)}), f32[32,1024]{1,0:T(8,128)}) %reduce-scatter.14.cloned.1.call-update) | async-done | bytes 131088 | tf_op jit(solution)/shard_map/reduce_scatter | solution.py:248
  652.8 135.1 %reduce-scatter.16.cloned.1.call-done = f32[32,512]{1,0:T(8,128)} async-done(((f32[1024,512]{1,0:T(8,128)}), f32[32,512]{1,0:T(8,128)}) %reduce-scatter.16.cloned.1.call-update) | async-done | bytes 65552 | tf_op jit(solution)/shard_map/reduce_scatter | solution.py:249
  787.9 135.1 %reduce-scatter.18.cloned.1.call-done = f32[32,512]{1,0:T(8,128)} async-done(((f32[1024,512]{1,0:T(8,128)}), f32[32,512]{1,0:T(8,128)}) %reduce-scatter.18.cloned.1.call-update) | async-done | bytes 65552 | tf_op jit(solution)/shard_map/reduce_scatter | solution.py:250
  923.0 209.6 %reduce-scatter.24.cloned.1.call-done = f32[32,4608]{1,0:T(8,128)} async-done(((f32[1024,4608]{1,0:T(8,128)}), f32[32,4608]{1,0:T(8,128)}) %reduce-scatter.24.cloned.1.call-update) | async-done | bytes 589840 | tf_op jit(solution)/shard_map/reduce_scatter | solution.py:253
  1132.7 212.5 %reduce-scatter.22.cloned.1.call-done = f32[32,4608]{1,0:T(8,128)} async-done(((f32[1024,4608]{1,0:T(8,128)}), f32[32,4608]{1,0:T(8,128)}) %reduce-scatter.22.cloned.1.call-update) | async-done | bytes 589840 | tf_op jit(solution)/shard_map/reduce_scatter | solution.py:252
  1345.1 212.6 %reduce-scatter.26.cloned.1.call-done = f32[144,1024]{1,0:T(8,128)} async-done(((f32[4608,1024]{1,0:T(8,128)}), f32[144,1024]{1,0:T(8,128)}) %reduce-scatter.26.cloned.1.call-update) | async-done | bytes 589840 | tf_op jit(solution)/shard_map/reduce_scatter | solution.py:254
  (199 shorter events, 104.3 us)
Async XLA Ops:
  7.2 134.7 %copy-start = (bf16[1024,1024]{1,0:T(8,128)(2,1)S(1)}, bf16[1024,1024]{1,0:T(8,128)(2,1)}, u32[]{:S(2)}) copy-start(bf16[1024,1024]{1,0:T(8,128)(2,1)} %param.22) | copy-start | bytes 6291460
  7.2 51.0 %all-gather.3.cloned.1.call-start = ((), (), s32[]{:S(2)}) async-start(), calls=%async_computation.9 | async-start | bytes 4718592 | tf_op jit(solution)/shard_map/all_gather | solution.py:125
  15.5 14.7 copy-start.28
  18.0 88.8 %all-gather.5.cloned.1.call-start = ((), (), s32[]{:S(2)}) async-start(), calls=%async_computation.10 | async-start | bytes 4718592 | tf_op jit(solution)/shard_map/all_gather | solution.py:126
  20.8 310.5 %reduce-scatter.10.cloned.1.call-start = ((), (), s32[]{:S(2)}) async-start(), calls=%async_computation.11 | async-start | bytes 4718592 | tf_op jit(solution)/shard_map/reduce_scatter | solution.py:205
  141.9 15.1 slice-start
  144.9 12.1 copy-start.17
  144.9 12.1 slice-start.1
  144.9 12.1 slice-start.2
  210.6 35.2 %copy-start.20 = (bf16[2,256,16,32]{1,3,2,0:T(8,128)(2,1)S(1)}, bf16[2,256,16,32]{1,3,2,0:T(8,128)(2,1)}, u32[]{:S(2)}) copy-start(bf16[2,256,16,32]{1,3,2,0:T(8,128)(2,1)} %get-tuple-element.32) | copy-start | bytes 1572868
  210.6 35.2 %copy-start.21 = (bf16[2,256,16,32]{1,3,2,0:T(8,128)(2,1)S(1)}, bf16[2,256,16,32]{1,3,2,0:T(8,128)(2,1)}, u32[]{:S(2)}) copy-start(bf16[2,256,16,32]{1,3,2,0:T(8,128)(2,1)} %get-tuple-element.33) | copy-start | bytes 1572868
  263.1 106.4 %reduce-scatter.12.cloned.1.call-start = ((), (), s32[]{:S(2)}) async-start(), calls=%async_computation.12 | async-start | bytes 4718592 | tf_op jit(solution)/shard_map/reduce_scatter | solution.py:208
  297.5 216.0 %reduce-scatter.20.cloned.1.call-start = ((), (), s32[]{:S(2)}) async-start(), calls=%async_computation.16 | async-start | bytes 4325376 | tf_op jit(solution)/shard_map/reduce_scatter | solution.py:251
  302.6 19.7 %copy-start.29 = (f32[2,256,32]{1,2,0:T(8,128)S(1)}, f32[2,256,32]{1,2,0:T(8,128)}, u32[]{:S(2)}) copy-start(f32[2,256,32]{1,2,0:T(8,128)} %copy-done.28) | copy-start | bytes 196612
  302.6 19.7 %copy-start.35 = (f32[2,256,32]{1,2,0:T(8,128)S(1)}, f32[2,256,32]{1,2,0:T(8,128)}, u32[]{:S(2)}) copy-start(f32[2,256,32]{1,2,0:T(8,128)} %get-tuple-element.38) | copy-start | bytes 196612
  302.6 350.2 %reduce-scatter.14.cloned.1.call-start = ((), (), s32[]{:S(2)}) async-start(), calls=%async_computation.13 | async-start | bytes 4325376 | tf_op jit(solution)/shard_map/reduce_scatter | solution.py:248
  331.2 456.6 %reduce-scatter.16.cloned.1.call-start = ((), (), s32[]{:S(2)}) async-start(), calls=%async_computation.14 | async-start | bytes 2162688 | tf_op jit(solution)/shard_map/reduce_scatter | solution.py:249
  336.2 36.7 %copy-start.18 = (bf16[512,1024]{1,0:T(8,128)(2,1)S(1)}, bf16[512,1024]{1,0:T(8,128)(2,1)}, u32[]{:S(2)}) copy-start(bf16[512,1024]{1,0:T(8,128)(2,1)} %copy-done.17) | copy-start | bytes 3145732
  336.2 586.8 %reduce-scatter.18.cloned.1.call-start = ((), (), s32[]{:S(2)}) async-start(), calls=%async_computation.15 | async-start | bytes 2162688 | tf_op jit(solution)/shard_map/reduce_scatter | solution.py:250
  372.6 760.0 %reduce-scatter.24.cloned.1.call-start = ((), (), s32[]{:S(2)}) async-start(), calls=%async_computation.18 | async-start | bytes 19464192 | tf_op jit(solution)/shard_map/reduce_scatter | solution.py:253
  384.4 960.7 %reduce-scatter.22.cloned.1.call-start = ((), (), s32[]{:S(2)}) async-start(), calls=%async_computation.17 | async-start | bytes 19464192 | tf_op jit(solution)/shard_map/reduce_scatter | solution.py:252
  396.1 1161.6 %reduce-scatter.26.cloned.1.call-start = ((), (), s32[]{:S(2)}) async-start(), calls=%async_computation.19 | async-start | bytes 19464192 | tf_op jit(solution)/shard_map/reduce_scatter | solution.py:254
  411.9 10.0 copy-start.23
  465.8 1092.0 %copy-start.1 = (bf16[1024,1024]{1,0:T(8,128)(2,1)S(1)}, bf16[1024,1024]{1,0:T(8,128)(2,1)}, u32[]{:S(2)}) copy-start(bf16[1024,1024]{1,0:T(8,128)(2,1)} %param.22) | copy-start | bytes 6291460
  (41 other events, 112.1 us)
Sparse Core Ops, SparseCore 0:
  18.1 40.1 all-gather.2
  60.2 36.7 all-gather.4
  263.2 51.3 reduce-scatter.9
  318.2 51.2 reduce-scatter.11
  372.2 141.2 reduce-scatter.19
  516.2 136.5 reduce-scatter.13
  655.6 132.1 reduce-scatter.15
  790.8 132.1 reduce-scatter.17
  930.0 202.6 reduce-scatter.23
  1139.5 205.5 reduce-scatter.21
  1352.1 205.5 reduce-scatter.25
where the time goes:
time: 1570 us; the launch traced here: 1560 us
  waiting for transfers between devices  1150 us (73%)
  matrix products  283 us (18%)
  other arithmetic  44.5 us (3%)
  blocking collectives  39.9 us (3%)
  local copies, waits for them, and re-layouts  36.2 us (2%)
    reduce_scatter x1, waiting for transfers between devices, local(): lax.psum_scatter(locals_all[6], ('dp', 'blk'), scatter_dimension=0, tiled...  213 us
    reduce_scatter x1, waiting for transfers between devices, local(): lax.psum_scatter(locals_all[4], ('dp', 'blk'), scatter_dimension=0, tiled...  212 us
    reduce_scatter x1, waiting for transfers between devices, local(): lax.psum_scatter(locals_all[5], ('dp', 'blk'), scatter_dimension=0, tiled...  210 us
    reduce_scatter x1, waiting for transfers between devices, local(): lax.psum_scatter(locals_all[0], ('dp', 'blk'), scatter_dimension=0, tiled...  139 us
    reduce_scatter x1, waiting for transfers between devices, local(): lax.psum_scatter(locals_all[2], ('dp', 'blk'), scatter_dimension=0, tiled...  135 us
    reduce_scatter x1, waiting for transfers between devices, local(): lax.psum_scatter(locals_all[1], ('dp', 'blk'), scatter_dimension=0, tiled...  135 us
    reduce_scatter x1, waiting for transfers between devices, local(): lax.psum_scatter(locals_all[3], ('dp', 'blk'), scatter_dimension=0, tiled...  43.8 us
    psum x1, blocking collectives, local(): lax.psum((grad_attn_gain, grad_query_gain, grad_key_gain, grad_ffn_gain),...  39.9 us
  transfers between devices with their start and end apart: 11, of which 9 were waited for; matrix products, arithmetic and copies ran while one was open for 12% of the time, Pallas kernels for 0%

commit v1 on v0

--- a/solution.py
+++ b/solution.py
@@ -1,6 +1,11 @@
+import functools
+import math
+
 import jax
 import jax.numpy as jnp
 from jax import lax
+from jax.experimental import pallas as pl
+from jax.experimental.pallas import tpu as pltpu
 from jax.sharding import PartitionSpec as P
 
 HEADS = 16
@@ -270,9 +275,1017 @@
     )
 
 
+BF16 = jnp.bfloat16
+F32 = jnp.float32
+LANES = 128
+FF_TILE = 256
+FFN_CALLS = 3
+VMEM_BYTES = 56 * 1024 * 1024
+LOG2_E = math.log2(math.e)
+QUERY_SCALE = HEAD_DIM ** (-0.5) * LOG2_E
+MASKED = -1e30
+
+
+def nn_dot(left, right):
+    return lax.dot_general(left, right, (((1,), (0,)), ((), ())), preferred_element_type=F32)
+
+
+def nt_dot(left, right):
+    return lax.dot_general(left, right, (((1,), (1,)), ((), ())), preferred_element_type=F32)
+
+
+def tn_dot(left, right):
+    return lax.dot_general(left, right, (((0,), (0,)), ((), ())), preferred_element_type=F32)
+
+
+def kernel_params(**more):
+    return pltpu.CompilerParams(vmem_limit_bytes=VMEM_BYTES, **more)
+
+
+def whole_block(shape):
+    return pl.BlockSpec(shape, lambda *ids: (0,) * len(shape))
+
+
+def swap_blocks_kernel(send_ref, out_ref, send_sem, recv_sem, own_sem):
+    count = send_ref.shape[0]
+    mine = lax.axis_index("blk")
+    group = lax.axis_index("dp")
+    barrier = pltpu.get_barrier_semaphore()
+    for step in range(1, count):
+        pl.semaphore_signal(
+            barrier,
+            inc=1,
+            device_id=(group, lax.rem(mine + step, count)),
+            device_id_type=pl.DeviceIdType.MESH,
+        )
+    pl.semaphore_wait(barrier, count - 1)
+    copies = []
+    for step in range(1, count):
+        target = lax.rem(mine + step, count)
+        copy = pltpu.make_async_remote_copy(
+            src_ref=send_ref.at[target],
+            dst_ref=out_ref.at[mine],
+            send_sem=send_sem.at[step],
+            recv_sem=recv_sem.at[step],
+            device_id=(group, target),
+            device_id_type=pl.DeviceIdType.MESH,
+        )
+        copy.start()
+        copies.append(copy)
+    own = pltpu.make_async_copy(send_ref.at[mine], out_ref.at[mine], own_sem)
+    own.start()
+    own.wait()
+    for copy in copies:
+        copy.wait()
+
+
+def swap_blocks(blocks, collective_id):
+    count = blocks.shape[0]
+    return pl.pallas_call(
+        swap_blocks_kernel,
+        name=f"swap_blocks_{collective_id}",
+        out_shape=jax.ShapeDtypeStruct(blocks.shape, blocks.dtype),
+        in_specs=[pl.BlockSpec(memory_space=pl.ANY)],
+        out_specs=pl.BlockSpec(memory_space=pl.ANY),
+        scratch_shapes=[
+            pltpu.SemaphoreType.DMA((count,)),
+            pltpu.SemaphoreType.DMA((count,)),
+            pltpu.SemaphoreType.DMA,
+        ],
+        compiler_params=kernel_params(collective_id=collective_id, has_side_effects=True),
+    )(blocks)
+
+
+def head_means(values):
+    rows = lax.broadcasted_iota(jnp.int32, (LANES, LANES), 0) // HEAD_DIM
+    cols = lax.broadcasted_iota(jnp.int32, (LANES, LANES), 1) // HEAD_DIM
+    spread = jnp.where(rows == cols, 1.0 / HEAD_DIM, 0.0).astype(BF16)
+    high = values.astype(BF16)
+    low = (values - high.astype(F32)).astype(BF16)
+    return nn_dot(high, spread) + nn_dot(low, spread)
+
+
+def half_partner(values):
+    lane = lax.broadcasted_iota(jnp.int32, values.shape, 1)
+    half = HEAD_DIM // 2
+    ahead = pltpu.roll(values, LANES - half, 1)
+    behind = pltpu.roll(values, half, 1)
+    return jnp.where(lane % HEAD_DIM < half, ahead, behind)
+
+
+def project_kernel(
+    tokens_ref,
+    gain_ref,
+    wq_ref,
+    wk_ref,
+    wv_ref,
+    q_gain_ref,
+    k_gain_ref,
+    cos_ref,
+    sin_ref,
+    hidden_ref,
+    proj_ref,
+    send_ref,
+):
+    rows = tokens_ref.shape[0]
+
+    @pl.when(pl.program_id(0) == 0)
+    def _():
+        inputs = tokens_ref[...].astype(F32)
+        scale = lax.rsqrt(jnp.mean(inputs * inputs, axis=-1, keepdims=True) + EPSILON)
+        hidden_ref[...] = (inputs * scale * gain_ref[...]).astype(BF16)
+
+    hidden = hidden_ref[...]
+    half = rows // 2
+
+    def put(block, lane):
+        send_ref[0, :, lane : lane + LANES] = block[:half]
+        send_ref[1, :, lane : lane + LANES] = block[half:]
+
+    queries = nn_dot(hidden, wq_ref[...])
+    keys = nn_dot(hidden, wk_ref[...])
+    values = nn_dot(hidden, wv_ref[...])
+    q_width = queries.shape[1]
+    blocks = [(queries[:, at : at + LANES], at, q_gain_ref, QUERY_SCALE) for at in range(0, q_width, LANES)]
+    blocks.append((keys, q_width, k_gain_ref, 1.0))
+    for block, lane, head_gain, factor in blocks:
+        proj_ref[0, :, lane : lane + LANES] = block
+        scale = lax.rsqrt(head_means(block * block) + EPSILON)
+        normed = block * scale * head_gain[...]
+        turned = normed * cos_ref[...] + half_partner(normed) * sin_ref[...]
+        put((turned * factor).astype(BF16), lane)
+    put(values.astype(BF16), q_width + LANES)
+
+
+def project(tokens, gain, wq, wk, wv, q_gain, k_gain, cosine, sine):
+    rows, width = tokens.shape
+    chips = wk.shape[1] // LANES
+    q_width = wq.shape[1] // chips
+    block_width = q_width + 2 * LANES
+    return pl.pallas_call(
+        project_kernel,
+        name="project",
+        grid=(chips,),
+        in_specs=[
+            whole_block((rows, width)),
+            whole_block((1, width)),
+            pl.BlockSpec((width, q_width), lambda p: (0, p)),
+            pl.BlockSpec((width, LANES), lambda p: (0, p)),
+            pl.BlockSpec((width, LANES), lambda p: (0, p)),
+            whole_block((1, LANES)),
+            whole_block((1, LANES)),
+            whole_block((rows, LANES)),
+            whole_block((rows, LANES)),
+        ],
+        out_specs=[
+            whole_block((rows, width)),
+            pl.BlockSpec((1, rows, q_width + LANES), lambda p: (p, 0, 0)),
+            pl.BlockSpec((2, rows // 2, block_width), lambda p: (p, 0, 0)),
+        ],
+        out_shape=[
+            jax.ShapeDtypeStruct((rows, width), BF16),
+            jax.ShapeDtypeStruct((chips, rows, q_width + LANES), F32),
+            jax.ShapeDtypeStruct((2 * chips, rows // 2, block_width), BF16),
+        ],
+        compiler_params=kernel_params(),
+    )(tokens, gain, wq, wk, wv, q_gain, k_gain, cosine, sine)
+
+
+def low_lanes(shape):
+    return lax.broadcasted_iota(jnp.int32, shape, 1) < HEAD_DIM
+
+
+def doubled(pair, group):
+    turned = pltpu.roll(pair.astype(F32), HEAD_DIM, 1).astype(BF16)
+    low = low_lanes(pair.shape)
+    return jnp.where(low, pair, turned) if group == 0 else jnp.where(low, turned, pair)
+
+
+def stacked_heads(pair):
+    low = low_lanes(pair.shape)
+    none = jnp.zeros_like(pair)
+    return jnp.concatenate([jnp.where(low, pair, none), jnp.where(low, none, pair)], axis=0)
+
+
+def in_three(column):
+    lane = lax.broadcasted_iota(jnp.int32, (column.shape[0], LANES), 1)
+    wide = jnp.broadcast_to(column, (column.shape[0], LANES))
+    first = wide.astype(BF16).astype(F32)
+    second = (wide - first).astype(BF16).astype(F32)
+    third = wide - first - second
+    return jnp.where(
+        lane == 0, first, jnp.where(lane == 1, second, jnp.where(lane == 2, third, 0.0))
+    ).astype(BF16)
+
+
+def minus_three(rows):
+    lane = lax.broadcasted_iota(jnp.int32, (rows, LANES), 1)
+    return jnp.where(lane < 3, -1.0, 0.0).astype(BF16)
+
+
+def attend_kernel(groups, block, qkv_ref, starts_ref, out_ref, logs_ref, keys, values, total):
+    size = qkv_ref.shape[0]
+    q_width = groups * LANES
+    here = pl.program_id(0)
+
+    @pl.when(here == 0)
+    def _():
+        for g in range(groups):
+            keys[g] = doubled(qkv_ref[:, q_width : q_width + LANES], g)
+            values[g, :, :LANES] = doubled(qkv_ref[:, q_width + LANES : q_width + 2 * LANES], g)
+            values[g, :, LANES:] = jnp.ones((size, LANES), BF16)
+
+    at = pl.multiple_of(here * block, block)
+    starts = jnp.concatenate([starts_ref[pl.ds(at, block), :]] * 2, axis=0)
+    queries = [
+        stacked_heads(qkv_ref[pl.ds(at, block), g * LANES : (g + 1) * LANES]) for g in range(groups)
+    ]
+    column = lax.broadcasted_iota(jnp.int32, (2 * block, block), 1)
+    row = lax.broadcasted_iota(jnp.int32, (2 * block, block), 0) % block
+
+    def step(j, diagonal):
+        key_at = pl.multiple_of(j * block, block)
+        allowed = column >= starts - key_at
+        if diagonal:
+            allowed = allowed & (column <= row)
+        for g in range(groups):
+            scores = nt_dot(queries[g], keys[g, pl.ds(key_at, block), :])
+            weights = jnp.exp2(jnp.where(allowed, scores, MASKED)).astype(BF16)
+            part = nn_dot(weights, values[g, pl.ds(key_at, block), :])
+            if diagonal:
+                total[g] = part
+            else:
+                total[g] += part
+
+    step(here, True)
+
+    def body(j, carry):
+        step(j, False)
+        return carry
+
+    lax.fori_loop(0, here, body, 0)
+    for g in range(groups):
+        sums = total[g, :, LANES:]
+        mean = total[g, :, :LANES] / sums
+        low = low_lanes((block, LANES))
+        out_ref[0, :, g * LANES : (g + 1) * LANES] = jnp.where(low, mean[:block], mean[block:]).astype(BF16)
+        logs_ref[g] = in_three(jnp.log2(sums[:, :1]))
+
+
+def attend(qkv, starts, block):
+    size, width = qkv.shape
+    groups = (width - 2 * LANES) // LANES
+    blocks = size // block
+    return pl.pallas_call(
+        functools.partial(attend_kernel, groups, block),
+        name="attend",
+        grid=(blocks,),
+        in_specs=[whole_block((size, width)), whole_block((size, 1))],
+        out_specs=[
+            pl.BlockSpec((1, block, groups * LANES), lambda i: (i, 0, 0)),
+            pl.BlockSpec((groups, 2 * block, LANES), lambda i: (0, i, 0)),
+        ],
+        out_shape=[
+            jax.ShapeDtypeStruct((blocks, block, groups * LANES), BF16),
+            jax.ShapeDtypeStruct((groups, 2 * size, LANES), BF16),
+        ],
+        scratch_shapes=[
+            pltpu.VMEM((groups, size, LANES), BF16),
+            pltpu.VMEM((groups, size, 2 * LANES), BF16),
+            pltpu.VMEM((groups, 2 * block, 2 * LANES), F32),
+        ],
+        compiler_params=kernel_params(),
+    )(qkv, starts)
+
+
+def attend_back_kernel(
+    groups,
+    block,
+    qkv_ref,
+    logs_ref,
+    out_ref,
+    grad_ref,
+    starts_ref,
+    result_ref,
+    queries,
+    keys,
+    values,
+    grads,
+    query_grad,
+    pair_grad,
+):
+    size = qkv_ref.shape[0]
+    blocks = size // block
+    q_width = groups * LANES
+    here = pl.program_id(0)
+
+    @pl.when(here == 0)
+    def _():
+        query_grad[...] = jnp.zeros_like(query_grad)
+        for g in range(groups):
+            lanes = slice(g * LANES, (g + 1) * LANES)
+            keys[g, :, :LANES] = doubled(qkv_ref[:, q_width : q_width + LANES], g)
+            keys[g, :, LANES:] = minus_three(size)
+            values[g, :, :LANES] = doubled(qkv_ref[:, q_width + LANES : q_width + 2 * LANES], g)
+            values[g, :, LANES:] = minus_three(size)
+
+            def fill(i, carry):
+                at = pl.multiple_of(i * block, block)
+                to = pl.multiple_of(i * 2 * block, 2 * block)
+                queries[g, pl.ds(to, 2 * block), :LANES] = stacked_heads(qkv_ref[pl.ds(at, block), lanes])
+                queries[g, pl.ds(to, 2 * block), LANES:] = logs_ref[g, pl.ds(to, 2 * block), :]
+                grad = stacked_heads(grad_ref[pl.ds(at, block), lanes])
+                mean = stacked_heads(out_ref[pl.ds(at, block), lanes])
+                delta = jnp.sum(grad.astype(F32) * mean.astype(F32), axis=1, keepdims=True)
+                grads[g, pl.ds(to, 2 * block), :LANES] = grad
+                grads[g, pl.ds(to, 2 * block), LANES:] = in_three(delta)
+                return carry
+
+            lax.fori_loop(0, blocks, fill, 0)
+
+    key_at = pl.multiple_of(here * block, block)
+    key_rows = pl.ds(key_at, block)
+    row = lax.broadcasted_iota(jnp.int32, (block, 2 * block), 0)
+    column = lax.broadcasted_iota(jnp.int32, (block, 2 * block), 1) % block
+
+    def step(i, diagonal):
+        at = pl.multiple_of(i * 2 * block, 2 * block)
+        stack = pl.ds(at, 2 * block)
+        allowed = row >= starts_ref[:, stack] - key_at
+        if diagonal:
+            allowed = allowed & (row <= column)
+        for g in range(groups):
+            query = queries[g, stack, :]
+            grad = grads[g, stack, :]
+            key = keys[g, key_rows, :]
+            scores = nt_dot(key, query)
+            probs = jnp.exp2(jnp.where(allowed, scores, MASKED))
+            pushed = (probs * nt_dot(values[g, key_rows, :], grad)).astype(BF16)
+            value_part = nn_dot(probs.astype(BF16), grad[:, :LANES])
+            key_part = nn_dot(pushed, query[:, :LANES])
+            if diagonal:
+                pair_grad[g, :, LANES:] = value_part
+                pair_grad[g, :, :LANES] = key_part
+            else:
+                pair_grad[g, :, LANES:] += value_part
+                pair_grad[g, :, :LANES] += key_part
+            query_grad[g, stack, :] += tn_dot(pushed, key[:, :LANES])
+
+    step(here, True)
+
+    def body(i, carry):
+        step(i, False)
+        return carry
+
+    lax.fori_loop(here + 1, blocks, body, 0)
+    low = low_lanes((block, LANES))
+    for part in range(2):
+        sums = []
+        for g in range(groups):
+            both = pair_grad[g, :, part * LANES : (part + 1) * LANES]
+            sums.append(both + pltpu.roll(both, HEAD_DIM, 1))
+        joined = jnp.where(low, sums[0], sums[1])
+        if part == 0:
+            joined = joined * (1.0 / LOG2_E)
+        lane = q_width + part * LANES
+        result_ref[key_rows, lane : lane + LANES] = joined.astype(BF16)
+
+    @pl.when(here == blocks - 1)
+    def _():
+        for g in range(groups):
+
+            def finish(i, carry):
+                at = pl.multiple_of(i * block, block)
+                to = pl.multiple_of(i * 2 * block, 2 * block)
+                first = query_grad[g, pl.ds(to, block), :]
+                second = query_grad[g, pl.ds(to + block, block), :]
+                joined = jnp.where(low, first, second) * HEAD_DIM ** (-0.5)
+                result_ref[pl.ds(at, block), g * LANES : (g + 1) * LANES] = joined.astype(BF16)
+                return carry
+
+            lax.fori_loop(0, blocks, finish, 0)
+
+
+def attend_back(qkv, logs, out, grad, starts, block):
+    size, width = qkv.shape
+    groups = (width - 2 * LANES) // LANES
+    return pl.pallas_call(
+        functools.partial(attend_back_kernel, groups, block),
+        name="attend_back",
+        grid=(size // block,),
+        in_specs=[
+            whole_block(qkv.shape),
+            whole_block(logs.shape),
+            whole_block(out.shape),
+            whole_block(grad.shape),
+            whole_block(starts.shape),
+        ],
+        out_specs=whole_block(qkv.shape),
+        out_shape=jax.ShapeDtypeStruct(qkv.shape, BF16),
+        scratch_shapes=[
+            pltpu.VMEM((groups, 2 * size, 2 * LANES), BF16),
+            pltpu.VMEM((groups, size, 2 * LANES), BF16),
+            pltpu.VMEM((groups, size, 2 * LANES), BF16),
+            pltpu.VMEM((groups, 2 * size, 2 * LANES), BF16),
+            pltpu.VMEM((groups, 2 * size, LANES), F32),
+            pltpu.VMEM((groups, block, 2 * LANES), F32),
+        ],
+        compiler_params=kernel_params(),
+    )(qkv, logs, out, grad, starts)
+
+
+def middle_kernel(tokens_ref, heads_ref, w_out_ref, gain_ref, middle_ref, hidden_ref):
+    half = heads_ref.shape[1]
+    width = heads_ref.shape[2]
+    total = tokens_ref[...].astype(F32)
+    for p in range(heads_ref.shape[0] // 2):
+        block = jnp.concatenate([heads_ref[2 * p], heads_ref[2 * p + 1]], axis=0)
+        total = total + nn_dot(block, w_out_ref[p * width : (p + 1) * width, :])
+    middle_ref[...] = total
+    scale = lax.rsqrt(jnp.mean(total * total, axis=-1, keepdims=True) + EPSILON)
+    hidden_ref[...] = (total * scale * gain_ref[...]).astype(BF16)
+
+
+def middle_layer(tokens, heads, w_out, gain):
+    return pl.pallas_call(
+        middle_kernel,
+        name="middle",
+        out_shape=[
+            jax.ShapeDtypeStruct(tokens.shape, F32),
+            jax.ShapeDtypeStruct(tokens.shape, BF16),
+        ],
+        compiler_params=kernel_params(),
+    )(tokens, heads, w_out, gain)
+
+
+def ffn_kernel(
+    first,
+    last,
+    core_ref,
+    hidden_ref,
+    flipped_ref,
+    grad_ref,
+    w_gate_ref,
+    w_up_ref,
+    w_down_ref,
+    *refs,
+):
+    if first:
+        sums_in, refs = None, refs
+    else:
+        sums_in, refs = refs[:2], refs[2:]
+    g_gate_ref, g_up_ref, g_down_ref = refs[:3]
+    if last:
+        finals, refs = refs[3:7], refs[7:]
+    else:
+        finals, refs = refs[3:5], refs[5:]
+    out_sum, back_sum, acts, gate_grads, up_grads = refs
+    step = pl.program_id(0)
+    count = pl.num_programs(0)
+    rows = hidden_ref.shape[0]
+    chunk = min(256, rows)
+
+    @pl.when(step == 0)
+    def _():
+        if first:
+            out_sum[...] = jnp.zeros_like(out_sum)
+            back_sum[...] = jnp.zeros_like(back_sum)
+        else:
+            out_sum[...] = sums_in[0][...]
+            back_sum[...] = sums_in[1][...]
+
+    def forward(m, carry):
+        part = pl.ds(pl.multiple_of(m * chunk, chunk), chunk)
+        hidden = hidden_ref[part, :]
+        gate = nn_dot(hidden, w_gate_ref[...])
+        up = nn_dot(hidden, w_up_ref[...])
+        pushed = nt_dot(grad_ref[part, :], w_down_ref[...])
+        opened = jax.nn.sigmoid(gate)
+        silu = gate * opened
+        act = (silu * up).astype(BF16)
+        gate_grad = (pushed * up * opened * (1.0 + gate * (1.0 - opened))).astype(BF16)
+        up_grad = (pushed * silu).astype(BF16)
+        acts[part, :] = act
+        gate_grads[part, :] = gate_grad
+        up_grads[part, :] = up_grad
+        out_sum[part, :] += nn_dot(act, w_down_ref[...])
+        back_sum[part, :] += nt_dot(gate_grad, w_gate_ref[...]) + nt_dot(up_grad, w_up_ref[...])
+        return carry
+
+    lax.fori_loop(0, rows // chunk, forward, 0)
+    width = flipped_ref.shape[0]
+
+    def weights(m, carry):
+        part = pl.ds(pl.multiple_of(m * chunk, chunk), chunk)
+        flipped = flipped_ref[part, :]
+        g_gate_ref[part, :] = nn_dot(flipped, gate_grads[...]).astype(BF16)
+        g_up_ref[part, :] = nn_dot(flipped, up_grads[...]).astype(BF16)
+        return carry
+
+    lax.fori_loop(0, width // chunk, weights, 0)
+    g_down_ref[...] = tn_dot(acts[...], grad_ref[...]).astype(BF16)
+
+    @pl.when(step == count - 1)
+    def _():
+        if last:
+            half = rows // 2
+            finals[0][...] = out_sum[:half, :]
+            finals[1][...] = out_sum[half:, :].astype(BF16)
+            finals[2][...] = back_sum[:half, :]
+            finals[3][...] = back_sum[half:, :].astype(BF16)
+        else:
+            finals[0][...] = out_sum[...]
+            finals[1][...] = back_sum[...]
+
+
+def ffn_part(core, hidden, flipped, grad, w_gate, w_up, w_down, sums, begin, tiles, last):
+    rows, width = hidden.shape
+    per_core = w_gate.shape[1] // 2 // FF_TILE
+    first = sums is None
+
+    def keep(shape):
+        return pl.BlockSpec(shape, lambda f, c: (0,) * len(shape), pipeline_mode=pl.Buffered(1))
+
+    in_specs = [
+        keep((rows, width)),
+        keep((width, rows)),
+        keep((rows, width)),
+        pl.BlockSpec((width, FF_TILE), lambda f, c: (0, c[0] * per_core + begin + f)),
+        pl.BlockSpec((width, FF_TILE), lambda f, c: (0, c[0] * per_core + begin + f)),
+        pl.BlockSpec((FF_TILE, width), lambda f, c: (c[0] * per_core + begin + f, 0)),
+    ]
+    args = [hidden, flipped, grad, w_gate, w_up, w_down]
+    if not first:
+        in_specs += [keep((rows, width))] * 2
+        args += list(sums)
+    out_specs = [
+        pl.BlockSpec((width, FF_TILE), lambda f, c: (0, f)),
+        pl.BlockSpec((width, FF_TILE), lambda f, c: (0, f)),
+        pl.BlockSpec((FF_TILE, width), lambda f, c: (f, 0)),
+    ]
+    out_shape = [
+        jax.ShapeDtypeStruct((width, tiles * FF_TILE), BF16),
+        jax.ShapeDtypeStruct((width, tiles * FF_TILE), BF16),
+        jax.ShapeDtypeStruct((tiles * FF_TILE, width), BF16),
+    ]
+    if last:
+        half = (rows // 2, width)
+        out_specs += [keep(half)] * 4
+        out_shape += [jax.ShapeDtypeStruct(half, kind) for kind in (F32, BF16, F32, BF16)]
+    else:
+        out_specs += [keep((rows, width))] * 2
+        out_shape += [jax.ShapeDtypeStruct((rows, width), F32)] * 2
+    flops = 18 * rows * width * FF_TILE * tiles
+    return pl.pallas_call(
+        functools.partial(ffn_kernel, first, last),
+        name=f"ffn_{begin}",
+        grid_spec=pltpu.PrefetchScalarGridSpec(
+            num_scalar_prefetch=1,
+            grid=(tiles,),
+            in_specs=in_specs,
+            out_specs=out_specs,
+            scratch_shapes=[
+                pltpu.VMEM((rows, width), F32),
+                pltpu.VMEM((rows, width), F32),
+                pltpu.VMEM((rows, FF_TILE), BF16),
+                pltpu.VMEM((rows, FF_TILE), BF16),
+                pltpu.VMEM((rows, FF_TILE), BF16),
+            ],
+        ),
+        out_shape=out_shape,
+        compiler_params=kernel_params(),
+        cost_estimate=pl.CostEstimate(
+            flops=flops, bytes_accessed=12 * width * FF_TILE * tiles, transcendentals=0
+        ),
+    )(core, *args)
+
+
+def turn_kernel(
+    middle_ref,
+    out_own_ref,
+    out_got_ref,
+    back_own_ref,
+    back_got_ref,
+    grad_ref,
+    gain_ref,
+    heads_ref,
+    w_out_ref,
+    output_ref,
+    mid_ref,
+    gain_grad_ref,
+    w_grad_ref,
+    send_ref,
+    low_grad,
+):
+    @pl.when(pl.program_id(0) == 0)
+    def _():
+        middle = middle_ref[...]
+        result = middle + (out_own_ref[...] + out_got_ref[...].astype(F32))
+        output_ref[...] = result.astype(BF16)
+        scale = lax.rsqrt(jnp.mean(middle * middle, axis=-1, keepdims=True) + EPSILON)
+        normal = middle * scale
+        back = back_own_ref[...] + back_got_ref[...].astype(F32)
+        gain_grad_ref[...] = jnp.sum(back * normal, axis=0, keepdims=True)
+        pushed = back * gain_ref[...]
+        inner = jnp.mean(pushed * normal, axis=-1, keepdims=True)
+        mid = grad_ref[...].astype(F32) + scale * (pushed - normal * inner)
+        mid_ref[...] = mid
+        low_grad[...] = mid.astype(BF16)
+
+    half = heads_ref.shape[1]
+    heads = jnp.concatenate([heads_ref[0], heads_ref[1]], axis=0)
+    grad = low_grad[...]
+    w_grad_ref[...] = tn_dot(heads, grad).astype(BF16)
+    send = nt_dot(grad, w_out_ref[...]).astype(BF16)
+    send_ref[0] = send[:half]
+    send_ref[1] = send[half:]
+
+
+def turn(middle, out_own, out_got, back_own, back_got, grad, gain, heads, w_out):
+    rows, width = middle.shape
+    count, half, lanes = heads.shape
+    chips = count // 2
+    return pl.pallas_call(
+        turn_kernel,
+        name="turn",
+        grid=(chips,),
+        in_specs=[whole_block((rows, width))] * 6
+        + [
+            whole_block((1, width)),
+            pl.BlockSpec((2, half, lanes), lambda p: (p, 0, 0)),
+            pl.BlockSpec((lanes, width), lambda p: (p, 0)),
+        ],
+        out_specs=[
+            whole_block((rows, width)),
+            whole_block((rows, width)),
+            whole_block((1, width)),
+            pl.BlockSpec((lanes, width), lambda p: (p, 0)),
+            pl.BlockSpec((2, half, lanes), lambda p: (p, 0, 0)),
+        ],
+        out_shape=[
+            jax.ShapeDtypeStruct((rows, width), BF16),
+            jax.ShapeDtypeStruct((rows, width), F32),
+            jax.ShapeDtypeStruct((1, width), F32),
+            jax.ShapeDtypeStruct((chips * lanes, width), BF16),
+            jax.ShapeDtypeStruct(heads.shape, BF16),
+        ],
+        scratch_shapes=[pltpu.VMEM((rows, width), BF16)],
+        compiler_params=kernel_params(),
+    )(middle, out_own, out_got, back_own, back_got, grad, gain, heads, w_out)
+
+
+def project_back_kernel(
+    got_ref,
+    proj_ref,
+    hidden_ref,
+    tokens_ref,
+    mid_ref,
+    gain_ref,
+    wq_ref,
+    wk_ref,
+    wv_ref,
+    q_gain_ref,
+    k_gain_ref,
+    cos_ref,
+    sin_ref,
+    input_ref,
+    gain_grad_ref,
+    q_gain_grad_ref,
+    k_gain_grad_ref,
+    gq_ref,
+    gk_ref,
+    gv_ref,
+    total,
+):
+    step = pl.program_id(0)
+
+    @pl.when(step == 0)
+    def _():
+        total[...] = jnp.zeros_like(total)
+        q_gain_grad_ref[...] = jnp.zeros_like(q_gain_grad_ref)
+        k_gain_grad_ref[...] = jnp.zeros_like(k_gain_grad_ref)
+
+    q_width = wq_ref.shape[1]
+    hidden = hidden_ref[...]
+
+    def back(lane, head_gain, gain_out):
+        got = jnp.concatenate(
+            [got_ref[0, :, lane : lane + LANES], got_ref[1, :, lane : lane + LANES]], axis=0
+        ).astype(F32)
+        turned = got * cos_ref[...] - half_partner(got) * sin_ref[...]
+        block = proj_ref[0, :, lane : lane + LANES]
+        scale = lax.rsqrt(head_means(block * block) + EPSILON)
+        normal = block * scale
+        gain_out[...] += jnp.sum(turned * normal, axis=0, keepdims=True)
+        pushed = turned * head_gain[...]
+        inner = head_means(pushed * normal)
+        return (scale * (pushed - normal * inner)).astype(BF16)
+
+    query = jnp.concatenate(
+        [back(at, q_gain_ref, q_gain_grad_ref) for at in range(0, q_width, LANES)], axis=1
+    )
+    key = back(q_width, k_gain_ref, k_gain_grad_ref)
+    lane = q_width + LANES
+    value = jnp.concatenate(
+        [got_ref[0, :, lane : lane + LANES], got_ref[1, :, lane : lane + LANES]], axis=0
+    )
+    gq_ref[...] = tn_dot(hidden, query).astype(BF16)
+    gk_ref[...] = tn_dot(hidden, key).astype(BF16)
+    gv_ref[...] = tn_dot(hidden, value).astype(BF16)
+    total[...] += (
+        nt_dot(query, wq_ref[...]) + nt_dot(key, wk_ref[...]) + nt_dot(value, wv_ref[...])
+    )
+
+    @pl.when(step == pl.num_programs(0) - 1)
+    def _():
+        inputs = tokens_ref[...].astype(F32)
+        scale = lax.rsqrt(jnp.mean(inputs * inputs, axis=-1, keepdims=True) + EPSILON)
+        normal = inputs * scale
+        grad = total[...]
+        gain_grad_ref[...] = jnp.sum(grad * normal, axis=0, keepdims=True)
+        pushed = grad * gain_ref[...]
+        inner = jnp.mean(pushed * normal, axis=-1, keepdims=True)
+        input_ref[...] = (mid_ref[...] + scale * (pushed - normal * inner)).astype(BF16)
+
+
+def project_back(got, proj, hidden, tokens, mid, gain, wq, wk, wv, q_gain, k_gain, cosine, sine):
+    rows, width = tokens.shape
+    count, half, lanes = got.shape
+    chips = count // 2
+    q_width = wq.shape[1] // chips
+    return pl.pallas_call(
+        project_back_kernel,
+        name="project_back",
+        grid=(chips,),
+        in_specs=[
+            pl.BlockSpec((2, half, lanes), lambda p: (p, 0, 0)),
+            pl.BlockSpec((1, rows, q_width + LANES), lambda p: (p, 0, 0)),
+            whole_block((rows, width)),
+            whole_block((rows, width)),
+            whole_block((rows, width)),
+            whole_block((1, width)),
+            pl.BlockSpec((width, q_width), lambda p: (0, p)),
+            pl.BlockSpec((width, LANES), lambda p: (0, p)),
+            pl.BlockSpec((width, LANES), lambda p: (0, p)),
+            whole_block((1, LANES)),
+            whole_block((1, LANES)),
+            whole_block((rows, LANES)),
+            whole_block((rows, LANES)),
+        ],
+        out_specs=[
+            whole_block((rows, width)),
+            whole_block((1, width)),
+            whole_block((1, LANES)),
+            whole_block((1, LANES)),
+            pl.BlockSpec((width, q_width), lambda p: (0, p)),
+            pl.BlockSpec((width, LANES), lambda p: (0, p)),
+            pl.BlockSpec((width, LANES), lambda p: (0, p)),
+        ],
+        out_shape=[
+            jax.ShapeDtypeStruct((rows, width), BF16),
+            jax.ShapeDtypeStruct((1, width), F32),
+            jax.ShapeDtypeStruct((1, LANES), F32),
+            jax.ShapeDtypeStruct((1, LANES), F32),
+            jax.ShapeDtypeStruct(wq.shape, BF16),
+            jax.ShapeDtypeStruct(wk.shape, BF16),
+            jax.ShapeDtypeStruct(wv.shape, BF16),
+        ],
+        scratch_shapes=[pltpu.VMEM((rows, width), F32)],
+        compiler_params=kernel_params(),
+    )(got, proj, hidden, tokens, mid, gain, wq, wk, wv, q_gain, k_gain, cosine, sine)
+
+
+def flip_pairs(count, bit):
+    return [(i, i ^ bit) for i in range(count)]
+
+
+def sum_pair(parts, axis, count, bit, dim):
+    mine = (lax.axis_index(axis) // bit) % 2
+    send = lax.dynamic_index_in_dim(parts, 1 - mine, dim, keepdims=False)
+    own = lax.dynamic_index_in_dim(parts, mine, dim, keepdims=False)
+    return own + lax.ppermute(send, axis, flip_pairs(count, bit))
+
+
+def sum_line(parts, axis, count):
+    mine = lax.axis_index(axis)
+    total = lax.dynamic_index_in_dim(parts, mine, 0, keepdims=False)
+    for way in (1, -1):
+        got = None
+        for step in range(1, count):
+            target = jnp.clip(mine + way * (count - step), 0, count - 1)
+            send = lax.dynamic_index_in_dim(parts, target, 0, keepdims=False)
+            if got is not None:
+                send = send + got
+            if way == 1:
+                pairs = [(i, i + 1) for i in range(step)]
+            else:
+                pairs = [(count - 1 - i, count - 2 - i) for i in range(step)]
+            got = lax.ppermute(send, axis, pairs)
+        total = total + got
+    return total
+
+
+def sum_chips(parts, order, dp_count, blk_count):
+    bits = []
+    bit = blk_count // 2
+    while bit > 1:
+        bits.append(bit)
+        bit //= 2
+    left = ["z"] + bits
+    for stage in order:
+        dim = left.index(stage)
+        left.pop(dim)
+        if stage == "z":
+            parts = sum_line(jnp.moveaxis(parts, dim, 0) if dim else parts, "dp", dp_count)
+        else:
+            parts = sum_pair(parts, "blk", blk_count, stage, dim)
+    return parts
+
+
+def swap_core(block, blk_count):
+    return lax.ppermute(block, "blk", flip_pairs(blk_count, 1))
+
+
+def fast_local(
+    dp_count,
+    blk_count,
+    tokens,
+    doc_lengths,
+    g_attn,
+    w_query,
+    w_key,
+    w_value,
+    q_gain,
+    k_gain,
+    w_out,
+    g_ffn,
+    w_gate,
+    w_up,
+    w_down,
+    cotangent,
+):
+    row_count, tok_count, width = tokens.shape
+    rows = row_count * tok_count
+    chips = blk_count // 2
+    size = tok_count * blk_count
+    index = lax.axis_index("blk")
+    core = index % 2
+    bits = []
+    bit = blk_count // 2
+    while bit > 1:
+        bits.append(bit)
+        bit //= 2
+    chip_dims = (dp_count,) + (2,) * len(bits)
+    all_chips = dp_count * chips
+    places = index * tok_count + jnp.arange(tok_count, dtype=jnp.int32)
+    unused, positions = doc_layout(doc_lengths, places)
+    cosine, sine = rope_angles(positions)
+    cosine = jnp.tile(cosine.reshape(rows, -1), (1, 4))
+    sine = sine.reshape(rows, -1)
+    sine = jnp.concatenate([-sine, sine, -sine, sine], axis=1)
+    q_gain2 = jnp.tile(q_gain, 2)[None]
+    k_gain2 = jnp.tile(k_gain, 2)[None]
+    all_places = jnp.arange(size, dtype=jnp.int32)
+    row_lengths = lax.dynamic_slice_in_dim(doc_lengths, core, 1, axis=0)
+    unused, all_positions = doc_layout(row_lengths, all_places)
+    starts = all_places - all_positions[0]
+    starts_two = jnp.broadcast_to(
+        starts.reshape(blk_count, 1, tok_count), (blk_count, 2, tok_count)
+    ).reshape(1, 2 * size)
+    flat = tokens.reshape(rows, width)
+    grad_own = cotangent.reshape(rows, width)
+    grad_both = jnp.concatenate([grad_own, swap_core(grad_own, blk_count)], axis=0)
+
+    hidden_in, proj, send = project(
+        flat, g_attn[None], w_query, w_key, w_value, q_gain2, k_gain2, cosine, sine
+    )
+    qkv = swap_blocks(send, 0).reshape(size, -1)
+    attended, logs = attend(qkv, starts[:, None], tok_count)
+    heads = swap_blocks(attended, 1)
+    middle, hidden_own = middle_layer(flat, heads, w_out, g_ffn[None])
+    hidden = jnp.concatenate([hidden_own, swap_core(hidden_own, blk_count)], axis=0)
+    flipped = hidden.T
+    core_arg = core.reshape(1)
+    tiles = w_gate.shape[1] // 2 // FF_TILE
+    sums = None
+    gate_sums, up_sums, down_parts = [], [], []
+    each = tiles // FFN_CALLS
+    forward_order = bits + ["z"]
+    other_order = bits[::-1] + ["z"]
+    for call in range(FFN_CALLS):
+        last = call == FFN_CALLS - 1
+        made = ffn_part(
+            core_arg, hidden, flipped, grad_both, w_gate, w_up, w_down, sums, call * each, each, last
+        )
+        gate_parts, up_parts, down_part = made[:3]
+        sums = made[3:]
+        down_parts.append(down_part)
+        gate_sums.append(
+            sum_chips(gate_parts.reshape(chip_dims + (-1, each * FF_TILE)), forward_order, dp_count, blk_count)
+        )
+        up_sums.append(
+            sum_chips(up_parts.reshape(chip_dims + (-1, each * FF_TILE)), other_order, dp_count, blk_count)
+        )
+    out_own, out_send, back_own, back_send = sums
+    back_got = swap_core(back_send, blk_count)
+    out_got = swap_core(out_send, blk_count)
+    output, mid, ffn_gain_grad, w_out_parts, send = turn(
+        middle, out_own, out_got, back_own, back_got, grad_own, g_ffn[None], heads, w_out
+    )
+    half_width = width // 2
+    down_half = jnp.concatenate(down_parts, axis=0)
+    down_own = lax.dynamic_slice_in_dim(down_half, core * half_width, half_width, axis=1)
+    down_got = swap_core(
+        lax.dynamic_slice_in_dim(down_half, (1 - core) * half_width, half_width, axis=1), blk_count
+    )
+    down_low = jnp.where(core == 0, down_own, down_got)
+    down_high = jnp.where(core == 0, down_got, down_own)
+    down_all = jnp.concatenate([down_low, down_high], axis=0).reshape(
+        chip_dims + (-1, half_width)
+    )
+    quarter = half_width // 2
+    down_sums = [
+        sum_chips(down_all[..., :quarter], ["z"] + bits, dp_count, blk_count),
+        sum_chips(down_all[..., quarter:], ["z"] + bits[::-1], dp_count, blk_count),
+    ]
+    grad_heads = swap_blocks(send, 2).reshape(size, -1)
+    back = attend_back(qkv, logs, attended.reshape(size, -1), grad_heads, starts_two, tok_count)
+    got = swap_blocks(back.reshape(blk_count, tok_count, -1), 3)
+    input_grad, attn_gain_grad, query_gain_grad, key_gain_grad, gq, gk, gv = project_back(
+        got,
+        proj,
+        hidden_in,
+        flat,
+        mid,
+        g_attn[None],
+        w_query,
+        w_key,
+        w_value,
+        q_gain2,
+        k_gain2,
+        cosine,
+        sine,
+    )
+
+    def sum_all(parts, order):
+        parts = parts.reshape(chip_dims + (2, -1, parts.shape[-1]))
+        parts = sum_pair(parts, "blk", blk_count, 1, len(chip_dims))
+        return sum_chips(parts, order, dp_count, blk_count).astype(F32)
+
+    grad_w_out = sum_all(w_out_parts, forward_order)
+    grad_w_query = sum_all(gq, forward_order)
+    both = sum_all(jnp.concatenate([gk, gv], axis=1), other_order)
+    grad_w_key, grad_w_value = jnp.split(both, 2, axis=1)
+
+    def join(block, dim):
+        count = block.shape[0] // 2
+        own = lax.dynamic_slice_in_dim(block, core * count, count, axis=0)
+        got = swap_core(
+            lax.dynamic_slice_in_dim(block, (1 - core) * count, count, axis=0), blk_count
+        )
+        low = jnp.where(core == 0, own, got)
+        high = jnp.where(core == 0, got, own)
+        return jnp.concatenate([low, high], axis=1).astype(F32)
+
+    grad_w_gate = join(jnp.concatenate(gate_sums, axis=1), 1)
+    grad_w_up = join(jnp.concatenate(up_sums, axis=1), 1)
+    grad_w_down = join(jnp.concatenate(down_sums, axis=1), 1)
+    fold = lambda both: both[0, :HEAD_DIM] + both[0, HEAD_DIM:]
+    gain_attn, gain_query, gain_key, gain_ffn = lax.psum(
+        (attn_gain_grad[0], fold(query_gain_grad), fold(key_gain_grad), ffn_gain_grad[0]),
+        ("dp", "blk"),
+    )
+    return (
+        output.reshape(tokens.shape),
+        input_grad.reshape(tokens.shape),
+        gain_attn,
+        grad_w_query,
+        grad_w_key,
+        grad_w_value,
+        gain_query,
+        gain_key,
+        grad_w_out,
+        gain_ffn,
+        grad_w_gate,
+        grad_w_up,
+        grad_w_down,
+    )
+
+
+def fits(mesh):
+    blk_count = mesh.shape["blk"]
+    chips = blk_count // 2
+    power = blk_count & (blk_count - 1) == 0
+    return power and blk_count > 2 and (KV_HEADS * HEAD_DIM) == chips * LANES
+
+
 def solution(mesh):
+    if fits(mesh):
+        body = functools.partial(fast_local, mesh.shape["dp"], mesh.shape["blk"])
+    else:
+        body = local
     return jax.shard_map(
-        local,
+        body,
         mesh=mesh,
         in_specs=(
             P("dp", "blk", None),

time: 1570 us -> 760 us (0.48)
  waiting for transfers between devices: 1150 us -> 106 us
  Pallas kernels: 0 us -> 286 us
  matrix products: 283 us -> 0 us
  starting transfers between devices: 1.13 us -> 253 us
  other arithmetic: 44.5 us -> 27.9 us
    reduce_scatter x9 -> x0, waiting for transfers between devices: 1120 us -> none  [the longest x1 213 us: local(): lax.psum_scatter(locals_all[6], ('dp', 'blk'), scatter_dimension=0, tiled...]
    pallas_call x0 -> x13, Pallas kernels: none -> 286 us  [the longest x3 91.7 us: ffn_part(): pl.pallas_call(functools.partial(ffn_kernel, first, last), name=f'ffn_{be...]
    dot_general x27 -> x0, matrix products: 283 us -> none  [the longest x1 35.2 us: local(): jnp.einsum('rqkgd,rpkd->rkgqp', grad_heads, value_heads, preferred_elemen...]
    ppermute x0 -> x99, starting transfers between devices: none -> 253 us  [the longest x66 224 us: sum_line(): got = lax.ppermute(send, axis, pairs)]
    ppermute x0 -> x99, waiting for transfers between devices: none -> 106 us  [the longest x25 53.3 us: sum_pair(): return own + lax.ppermute(send, axis, flip_pairs(count, bit))]
    all_gather x2 -> x0, waiting for transfers between devices: 23.7 us -> none  [the longest x1 23.7 us: local(): key_piece = lax.all_gather(key_b, 'blk', axis=1, tiled=True)]
    reduce_sum x6 -> x2, other arithmetic: 24.4 us -> 0.85 us  [doc_layout(): before = jnp.sum(jnp.where(past, lengths[:, None, :], 0), axis=2)]
  transfers between devices with their start and end apart: 11 -> 99, of which waited for: 9 -> 42; matrix products, arithmetic and copies ran while one was open for 12% -> 5% of each run, Pallas kernels for 0% -> 23%
where the time goes in v1:
time: 760 us; the launch traced here: 750 us
  Pallas kernels  286 us (38%)
  starting transfers between devices  253 us (33%)
  waiting for transfers between devices  106 us (14%)
  blocking collectives  40.8 us (5%)
  local copies, waits for them, and re-layouts  32.1 us (4%)
  other arithmetic  27.9 us (4%)
    ppermute x66, starting transfers between devices, sum_line(): got = lax.ppermute(send, axis, pairs)  224 us
    pallas_call x3, Pallas kernels, ffn_part(): pl.pallas_call(functools.partial(ffn_kernel, first, last), name=f'ffn_{be...  91.7 us
    pallas_call x4, Pallas kernels, swap_blocks(): pl.pallas_call(swap_blocks_kernel, name=f'swap_blocks_{collective_id}', o...  81.9 us
    ppermute x25, waiting for transfers between devices, sum_pair(): return own + lax.ppermute(send, axis, flip_pairs(count, bit))  53.3 us
    ppermute x66, waiting for transfers between devices, sum_line(): got = lax.ppermute(send, axis, pairs)  48.3 us
    pallas_call x1, Pallas kernels, attend_back(): pl.pallas_call(functools.partial(attend_back_kernel, groups, block), name...  46.7 us
    psum x1, blocking collectives, fast_local(): lax.psum((attn_gain_grad[0], fold(query_gain_grad), fold(key_gain_grad),...  40.8 us
    ppermute x25, starting transfers between devices, sum_pair(): return own + lax.ppermute(send, axis, flip_pairs(count, bit))  27 us
  transfers between devices with their start and end apart: 99, of which 42 were waited for; matrix products, arithmetic and copies ran while one was open for 5% of the time, Pallas kernels for 23%

profile of v1, /device:TPU:0, one launch (start us, length us, event | category | flops | bytes accessed | tf_op | source)
XLA Modules:
  0.0 749.8 jit_solution(1804952624377150085)
XLA Ops:
  10.9 8.6 %project.1 = (bf16[512,1024]{1,0:T(8,128)(2,1)}, f32[4,512,384]{2,1,0:T(8,128)}, bf16[8,256,512]{2,1,0:T(8,128)(2,1)}) custom-call(bf16[512,1024]{1,0:T(8,128)(2,1)} %bitcast.325, f32[1,1024]{1,0:T(1,128)} %bitcast.358, bf16[1024,1024]{1,0:T(8,128)(2,1)} %wq_ref.3, bf16[1024,512]{1,0:T(8,128)(2,1)} %wk_ref.3, bf16[1024,512]{1,0:T(8,128)(2,1)} %wv_ref.3, ...), custom_call_target="tpu_custom_call" | custom-call | tf_op jit(solution)/shard_map/project/pallas_call | solution.py:425
  19.5 27.4 %swap_blocks_0.1 = bf16[8,256,512]{2,1,0:T(8,128)(2,1)} custom-call(bf16[8,256,512]{2,1,0:T(8,128)(2,1)} %get-tuple-element.49.send_ref), custom_call_target="tpu_custom_call" | custom-call | tf_op jit(solution)/shard_map/swap_blocks_0/pallas_call | solution.py:344
  46.9 25.4 %attend.1 = (bf16[8,256,256]{2,1,0:T(8,128)(2,1)}, bf16[2,4096,128]{2,1,0:T(8,128)(2,1)}) custom-call(bf16[2048,512]{1,0:T(8,128)(2,1)} %bitcast.323, s32[2048,1]{1,0:T(8,128)} %subtract_subtract_fusion.starts_ref), custom_call_target="tpu_custom_call" | custom-call | tf_op jit(solution)/shard_map/attend/pallas_call | solution.py:539
  72.2 15.1 %swap_blocks_1.1.heads_ref = bf16[8,256,256]{2,1,0:T(8,128)(2,1)} custom-call(bf16[8,256,256]{2,1,0:T(8,128)(2,1)} %get-tuple-element.50.send_ref), custom_call_target="tpu_custom_call" | custom-call | tf_op jit(solution)/shard_map/swap_blocks_1/pallas_call | solution.py:344
  87.3 5.3 middle.1
  106.3 29.0 %ffn_0.1 = (bf16[1024,768]{1,0:T(8,128)(2,1)}, bf16[1024,768]{1,0:T(8,128)(2,1)}, bf16[768,1024]{1,0:T(8,128)(2,1)}, f32[1024,1024]{1,0:T(8,128)}, f32[1024,1024]{1,0:T(8,128)}) custom-call(s32[1]{0:T(128)} %bitcast.9.core_ref, bf16[1024,1024]{1,0:T(8,128)(2,1)} %copy.70.hidden_ref, bf16[1024,1024]{1,0:T(8,128)(2,1)} %get-tuple-element.107.flipped_ref, ...), custom_call_target="tpu_custom_call" | custom-call | flops 14495514624 | bytes 9437184 | tf_op jit(solution)/shard_map/ffn_0/pallas_call | solution.py:839
  142.6 31.8 %ffn_3.1 = (bf16[1024,768]{1,0:T(8,128)(2,1)}, bf16[1024,768]{1,0:T(8,128)(2,1)}, bf16[768,1024]{1,0:T(8,128)(2,1)}, f32[1024,1024]{1,0:T(8,128)}, f32[1024,1024]{1,0:T(8,128)}) custom-call(s32[1]{0:T(128)} %bitcast.9.core_ref, bf16[1024,1024]{1,0:T(8,128)(2,1)} %copy.70.hidden_ref, bf16[1024,1024]{1,0:T(8,128)(2,1)} %get-tuple-element.107.flipped_ref, ...), custom_call_target="tpu_custom_call" | custom-call | flops 14495514624 | bytes 9437184 | tf_op jit(solution)/shard_map/ffn_3/pallas_call | solution.py:839
  174.5 30.9 %ffn_6.1 = (bf16[1024,768]{1,0:T(8,128)(2,1)}, bf16[1024,768]{1,0:T(8,128)(2,1)}, bf16[768,1024]{1,0:T(8,128)(2,1)}, f32[512,1024]{1,0:T(8,128)}, bf16[512,1024]...) custom-call(s32[1]{0:T(128)} %bitcast.9.core_ref, bf16[1024,1024]{1,0:T(8,128)(2,1)} %copy.70.hidden_ref, ...), custom_call_target="tpu_custom_call" | custom-call | flops 14495514624 | bytes 9437184 | tf_op jit(solution)/shard_map/ffn_6/pallas_call | solution.py:839
  215.1 12.4 %collective-permute-done.64 = bf16[4,2,64,768]{3,2,1,0:T(8,128)(2,1)S(1)} collective-permute-done((bf16[4,2,64,768]{3,2,1,0:T(8,128)(2,1)S(1)}, bf16[4,2,64,768]{3,2,1,0:T(8,128)(2,1)S(1)}, u32[]{:S(2)}, u32[]{:S(2)}) %collective-permute-start.64) | collective-permute-done | bytes 786464 | tf_op jit(solution)/shard_map/ppermute | solution.py:1066
  231.7 11.4 %collective-permute-done.72 = bf16[4,2,64,768]{3,2,1,0:T(8,128)(2,1)S(1)} collective-permute-done((bf16[4,2,64,768]{3,2,1,0:T(8,128)(2,1)S(1)}, bf16[4,2,64,768]{3,2,1,0:T(8,128)(2,1)S(1)}, u32[]{:S(2)}, u32[]{:S(2)}) %collective-permute-start.72) | collective-permute-done | bytes 786464 | tf_op jit(solution)/shard_map/ppermute | solution.py:1066
  249.4 10.1 %turn.1 = (bf16[512,1024]{1,0:T(8,128)(2,1)}, f32[512,1024]{1,0:T(8,128)}, f32[1,1024]{1,0:T(1,128)}, bf16[1024,1024]{1,0:T(8,128)(2,1)}, bf16[8,256,256]{2,1,0:T(8,128)(2,1)}) custom-call(f32[512,1024]{1,0:T(8,128)} %get-tuple-element.51.middle_ref, f32[512,1024]{1,0:T(8,128)} %get-tuple-element.57.out_own_ref, bf16[512,1024]{1,0:T(8,128)(2,1)} %copy-done.24, ...), custom_call_target="tpu_custom_call" | custom-call | tf_op jit(solution)/shard_map/turn/pallas_call | solution.py:908
  259.5 13.2 %swap_blocks_2.1 = bf16[8,256,256]{2,1,0:T(8,128)(2,1)} custom-call(bf16[8,256,256]{2,1,0:T(8,128)(2,1)} %get-tuple-element.63.send_ref), custom_call_target="tpu_custom_call" | custom-call | tf_op jit(solution)/shard_map/swap_blocks_2/pallas_call | solution.py:344
  272.7 46.7 %attend_back.1 = bf16[2048,512]{1,0:T(8,128)(2,1)} custom-call(bf16[2048,512]{1,0:T(8,128)(2,1)} %bitcast.324, bf16[2,4096,128]{2,1,0:T(8,128)(2,1)} %get-tuple-element.62.logs_ref, bf16[2048,256]{1,0:T(8,128)(2,1)} %bitcast.335, bf16[2048,256]{1,0:T(8,128)(2,1)} %bitcast.336, s32[1,4096]{1,0:T(1,128)} %reshape.257.starts_ref), custom_call_target="tpu_custom_call" | custom-call | tf_op jit(solution)/shard_map/attend_back/pallas_call | solution.py:672
  319.4 26.3 %swap_blocks_3.1.got_ref = bf16[8,256,512]{2,1,0:T(8,128)(2,1)} custom-call(bf16[8,256,512]{2,1,0:T(8,128)(2,1)} %bitcast.331), custom_call_target="tpu_custom_call" | custom-call | tf_op jit(solution)/shard_map/swap_blocks_3/pallas_call | solution.py:344
  345.7 16.7 %project_back.1 = (bf16[512,1024]{1,0:T(8,128)(2,1)}, f32[1,1024]{1,0:T(1,128)}, f32[1,128]{1,0:T(1,128)}, f32[1,128]{1,0:T(1,128)}, bf16[1024,1024]{1,0:T(8,128...) custom-call(bf16[8,256,512]{2,1,0:T(8,128)(2,1)} %swap_blocks_3.1.got_ref, ...), custom_call_target="tpu_custom_call" | custom-call | tf_op jit(solution)/shard_map/project_back/pallas_call | solution.py:1016
  369.8 40.8 %all-reduce = (f32[1024]{0:T(1024)}, f32[64]{0:T(128)}, f32[64]{0:T(128)}, f32[1024]{0:T(1024)}) all-reduce(f32[1024]{0:T(1024)S(1)} %bitcast.364, f32[64]{0:T(128)S(1)} %get-tuple-element.159, f32[64]{0:T(128)S(1)} %get-tuple-element.158, f32[1024]{0:T(1024)S(1)} %bitcast.363), channel_id=1, replica_groups=mesh['dp'=4,'blk'=8] {'dp','blk'}, use_global_device_ids=true, to_apply=%region_4.5 | all-reduce | flops 2176 | bytes 17408 | tf_op jit(solution)/shard_map/psum | solution.py:1254
  507.0 41.3 %collective-permute-start.68 = (bf16[64,768]{1,0:T(8,128)(2,1)S(1)}, bf16[64,768]{1,0:T(8,128)(2,1)S(1)}, u32[]{:S(2)}, u32[]{:S(2)}) collective-permute-start(bf16[64,768]{1,0:T(8,128)(2,1)S(1)} %get-tuple-element.119), channel_id=1, source_target_pairs={{0,8},{8,16},{16,24},{1,9},{9,17},{17,25},{2,10},{10,18},{18,26},{... | collective-permute-start | bytes 294920 | tf_op jit(solution)/shard_map/ppermute | solution.py:1083
  606.8 5.2 collective-permute-done.23
  613.5 6.0 collective-permute-done.15
  621.0 5.2 collective-permute-done.24
  661.3 13.3 %collective-permute-start.9 = (bf16[32,1024]{1,0:T(8,128)(2,1)S(1)}, bf16[32,1024]{1,0:T(8,128)(2,1)S(1)}, u32[]{:S(2)}, u32[]{:S(2)}) collective-permute-start(bf16[32,1024]{1,0:T(8,128)(2,1)S(1)} %get-tuple-element.147), channel_id=1, source_target_pairs={{0,8},{8,16},{16,24},{1,9},{9,17},{17,25},{2,10},{10,18},{18,26},{... | collective-permute-start | bytes 196616 | tf_op jit(solution)/shard_map/ppermute | solution.py:1083
  678.1 8.6 %collective-permute-start.27 = (bf16[32,1024]{1,0:T(8,128)(2,1)S(1)}, bf16[32,1024]{1,0:T(8,128)(2,1)S(1)}, u32[]{:S(2)}, u32[]{:S(2)}) collective-permute-start(bf16[32,1024]{1,0:T(8,128)(2,1)S(1)} %get-tuple-element.139), channel_id=1, source_target_pairs={{0,8},{8,16},{16,24},{1,9},{9,17},{17,25},{2,10},{10,18},{18,26},{... | collective-permute-start | bytes 196616 | tf_op jit(solution)/shard_map/ppermute | solution.py:1083
  696.3 12.5 %collective-permute-start.92 = (bf16[2,2,288,256]{3,2,1,0:T(8,128)(2,1)S(1)}, bf16[2,2,288,256]{3,2,1,0:T(8,128)(2,1)S(1)}, u32[]{:S(2)}, u32[]{:S(2)}) collective-permute-start(bf16[2,2,288,256]{3,2,1,0:T(8,128)(2,1)S(1)} %get-tuple-element.93), channel_id=1, source_target_pairs={{0,8},{8,16},{16,24},{1,9},{9,17},{17,25},{2,10},{10,18},{18,26},{... | collective-permute-start | bytes 1769480 | tf_op jit(solution)/shard_map/ppermute | solution.py:1083
  710.1 12.8 %collective-permute-start.84 = (bf16[2,2,288,256]{3,2,1,0:T(8,128)(2,1)S(1)}, bf16[2,2,288,256]{3,2,1,0:T(8,128)(2,1)S(1)}, u32[]{:S(2)}, u32[]{:S(2)}) collective-permute-start(bf16[2,2,288,256]{3,2,1,0:T(8,128)(2,1)S(1)} %get-tuple-element.97), channel_id=1, source_target_pairs={{0,8},{8,16},{16,24},{1,9},{9,17},{17,25},{2,10},{10,18},{18,26},{... | collective-permute-start | bytes 1769480 | tf_op jit(solution)/shard_map/ppermute | solution.py:1083
  (418 shorter events, 290.8 us)
Async XLA Ops:
  137.6 76.0 %collective-permute-start.56 = (bf16[4,2,64,768]{3,2,1,0:T(8,128)(2,1)}, bf16[4,2,64,768]{3,2,1,0:T(8,128)(2,1)S(1)}, u32[]{:S(2)}, u32[]{:S(2)}) collective-permute-start(bf16[4,2,64,768]{3,2,1,0:T(8,128)(2,1)} %dynamic-slice_bitcast_fusion.2), channel_id=1, source_target_pairs={{0,2},{1,3},{2,0},{3,1},{4,6},{5,7},{6,4},{7,5},{8,10},{9,11},{10,... | collective-permute-start | bytes 2359304 | tf_op jit(solution)/shard_map/ppermute | solution.py:1066
  141.1 86.6 %collective-permute-start.31 = (bf16[4,2,64,768]{3,2,1,0:T(8,128)(2,1)}, bf16[4,2,64,768]{3,2,1,0:T(8,128)(2,1)S(1)}, u32[]{:S(2)}, u32[]{:S(2)}) collective-permute-start(bf16[4,2,64,768]{3,2,1,0:T(8,128)(2,1)} %dynamic-slice_bitcast_fusion.5), channel_id=1, source_target_pairs={{0,4},{1,5},{2,6},{3,7},{4,0},{5,1},{6,2},{7,3},{8,12},{9,13},{10,... | collective-permute-start | bytes 2359304 | tf_op jit(solution)/shard_map/ppermute | solution.py:1066
  208.3 34.8 %collective-permute-start.72 = (bf16[4,2,64,768]{3,2,1,0:T(8,128)(2,1)S(1)}, bf16[4,2,64,768]{3,2,1,0:T(8,128)(2,1)S(1)}, u32[]{:S(2)}, u32[]{:S(2)}) collective-permute-start(bf16[4,2,64,768]{3,2,1,0:T(8,128)(2,1)S(1)} %dynamic-slice_bitcast_fusion), channel_id=1, source_target_pairs={{0,2},{1,3},{2,0},{3,1},{4,6},{5,7},{6,4},{7,5},{8,10},{9,11},{10,... | collective-permute-start | bytes 2359304 | tf_op jit(solution)/shard_map/ppermute | solution.py:1066
  213.5 31.1 %collective-permute-start.47 = (bf16[4,2,64,768]{3,2,1,0:T(8,128)(2,1)S(1)}, bf16[4,2,64,768]{3,2,1,0:T(8,128)(2,1)S(1)}, u32[]{:S(2)}, u32[]{:S(2)}) collective-permute-start(bf16[4,2,64,768]{3,2,1,0:T(8,128)(2,1)S(1)} %dynamic-slice_bitcast_fusion.3), channel_id=1, source_target_pairs={{0,4},{1,5},{2,6},{3,7},{4,0},{5,1},{6,2},{7,3},{8,12},{9,13},{10,... | collective-permute-start | bytes 2359304 | tf_op jit(solution)/shard_map/ppermute | solution.py:1066
  228.4 362.2 %collective-permute-start.81 = (bf16[2304,512]{1,0:T(8,128)(2,1)}, bf16[2304,512]{1,0:T(8,128)(2,1)}, u32[]{:S(2)}, u32[]{:S(2)}) collective-permute-start(bf16[2304,512]{1,0:T(8,128)(2,1)} %constant_dynamic-slice_fusion), channel_id=1, source_target_pairs={{0,1},{1,0},{2,3},{3,2},{4,5},{5,4},{6,7},{7,6},{8,9},{9,8},{10,11... | collective-permute-start | bytes 7077896 | tf_op jit(solution)/shard_map/ppermute | solution.py:1106
  243.1 167.4 %collective-permute-start.57 = (bf16[4,64,768]{2,1,0:T(8,128)(2,1)}, bf16[4,64,768]{2,1,0:T(8,128)(2,1)}, u32[]{:S(2)}, u32[]{:S(2)}) collective-permute-start(bf16[4,64,768]{2,1,0:T(8,128)(2,1)} %dynamic-slice_bitcast_fusion.15), channel_id=1, source_target_pairs={{0,4},{1,5},{2,6},{3,7},{4,0},{5,1},{6,2},{7,3},{8,12},{9,13},{10,... | collective-permute-start | bytes 1179656 | tf_op jit(solution)/shard_map/ppermute | solution.py:1066
  244.8 169.7 %collective-permute-start.32 = (bf16[4,64,768]{2,1,0:T(8,128)(2,1)}, bf16[4,64,768]{2,1,0:T(8,128)(2,1)}, u32[]{:S(2)}, u32[]{:S(2)}) collective-permute-start(bf16[4,64,768]{2,1,0:T(8,128)(2,1)} %dynamic-slice_bitcast_fusion.18), channel_id=1, source_target_pairs={{0,2},{1,3},{2,0},{3,1},{4,6},{5,7},{6,4},{7,5},{8,10},{9,11},{10,... | collective-permute-start | bytes 1179656 | tf_op jit(solution)/shard_map/ppermute | solution.py:1066
  246.5 170.0 %collective-permute-start.65 = (bf16[4,64,768]{2,1,0:T(8,128)(2,1)}, bf16[4,64,768]{2,1,0:T(8,128)(2,1)}, u32[]{:S(2)}, u32[]{:S(2)}) collective-permute-start(bf16[4,64,768]{2,1,0:T(8,128)(2,1)} %dynamic-slice_bitcast_fusion.14), channel_id=1, source_target_pairs={{0,4},{1,5},{2,6},{3,7},{4,0},{5,1},{6,2},{7,3},{8,12},{9,13},{10,... | collective-permute-start | bytes 1179656 | tf_op jit(solution)/shard_map/ppermute | solution.py:1066
  247.9 169.8 %collective-permute-start.40 = (bf16[4,64,768]{2,1,0:T(8,128)(2,1)}, bf16[4,64,768]{2,1,0:T(8,128)(2,1)}, u32[]{:S(2)}, u32[]{:S(2)}) collective-permute-start(bf16[4,64,768]{2,1,0:T(8,128)(2,1)} %dynamic-slice_bitcast_fusion.17), channel_id=1, source_target_pairs={{0,2},{1,3},{2,0},{3,1},{4,6},{5,7},{6,4},{7,5},{8,10},{9,11},{10,... | collective-permute-start | bytes 1179656 | tf_op jit(solution)/shard_map/ppermute | solution.py:1066
  416.5 170.1 %collective-permute-start.4 = (bf16[4,2,2,32,1024]{4,3,2,0,1:T(8,128)(2,1)}, bf16[4,2,2,32,1024]{4,3,2,0,1:T(8,128)(2,1)S(1)}, u32[]{:S(2)}, u32[]{:S(2)}) collective-permute-start(bf16[4,2,2,32,1024]{4,3,2,0,1:T(8,128)(2,1)} %bitcast.354), channel_id=1, source_target_pairs={{0,1},{1,0},{2,3},{3,2},{4,5},{5,4},{6,7},{7,6},{8,9},{9,8},{10,11... | collective-permute-start | bytes 3145736 | tf_op jit(solution)/shard_map/ppermute | solution.py:1066
  417.8 169.7 %collective-permute-start.13 = (bf16[4,2,2,32,1024]{4,3,1,0,2:T(8,128)(2,1)S(1)}, bf16[4,2,2,32,1024]{4,3,1,0,2:T(8,128)(2,1)S(1)}, u32[]{:S(2)}, u32[]{:S(2)}) collective-permute-start(bf16[4,2,2,32,1024]{4,3,1,0,2:T(8,128)(2,1)S(1)} %bitcast.353), channel_id=1, source_target_pairs={{0,1},{1,0},{2,3},{3,2},{4,5},{5,4},{6,7},{7,6},{8,9},{9,8},{10,11... | collective-permute-start | bytes 3145736 | tf_op jit(solution)/shard_map/ppermute | solution.py:1066
  425.0 40.1 %collective-permute-start.61 = (bf16[64,768]{1,0:T(8,128)(2,1)S(1)}, bf16[64,768]{1,0:T(8,128)(2,1)S(1)}, u32[]{:S(2)}, u32[]{:S(2)}) collective-permute-start(bf16[64,768]{1,0:T(8,128)(2,1)S(1)} %get-tuple-element.118), channel_id=1, source_target_pairs={{24,16},{25,17},{26,18},{27,19},{28,20},{29,21},{30,22},{31,23}} | collective-permute-start | bytes 294920 | tf_op jit(solution)/shard_map/ppermute | solution.py:1083
  505.7 43.9 %collective-permute-start.63 = (bf16[64,768]{1,0:T(8,128)(2,1)S(1)}, bf16[64,768]{1,0:T(8,128)(2,1)S(1)}, u32[]{:S(2)}, u32[]{:S(2)}) collective-permute-start(bf16[64,768]{1,0:T(8,128)(2,1)S(1)} %bitcast_add_fusion.46), channel_id=1, source_target_pairs={{24,16},{16,8},{8,0},{25,17},{17,9},{9,1},{26,18},{18,10},{10,2},{... | collective-permute-start | bytes 294920 | tf_op jit(solution)/shard_map/ppermute | solution.py:1083
  507.0 43.9 %collective-permute-start.68 = (bf16[64,768]{1,0:T(8,128)(2,1)S(1)}, bf16[64,768]{1,0:T(8,128)(2,1)S(1)}, u32[]{:S(2)}, u32[]{:S(2)}) collective-permute-start(bf16[64,768]{1,0:T(8,128)(2,1)S(1)} %get-tuple-element.119), channel_id=1, source_target_pairs={{0,8},{8,16},{16,24},{1,9},{9,17},{17,25},{2,10},{10,18},{18,26},{... | collective-permute-start | bytes 294920 | tf_op jit(solution)/shard_map/ppermute | solution.py:1083
  594.5 35.4 %collective-permute-start.90 = (bf16[2,2,288,256]{3,2,1,0:T(8,128)(2,1)S(1)}, bf16[2,2,288,256]{3,2,1,0:T(8,128)(2,1)S(1)}, u32[]{:S(2)}, u32[]{:S(2)}) collective-permute-start(bf16[2,2,288,256]{3,2,1,0:T(8,128)(2,1)S(1)} %get-tuple-element.95), channel_id=1, source_target_pairs={{0,8},{1,9},{2,10},{3,11},{4,12},{5,13},{6,14},{7,15}} | collective-permute-start | bytes 1769480 | tf_op jit(solution)/shard_map/ppermute | solution.py:1083
  598.2 76.4 %collective-permute-start.93 = (bf16[2,2,288,256]{3,2,1,0:T(8,128)(2,1)S(1)}, bf16[2,2,288,256]{3,2,1,0:T(8,128)(2,1)S(1)}, u32[]{:S(2)}, u32[]{:S(2)}) collective-permute-start(bf16[2,2,288,256]{3,2,1,0:T(8,128)(2,1)S(1)} %get-tuple-element.96), channel_id=1, source_target_pairs={{24,16},{25,17},{26,18},{27,19},{28,20},{29,21},{30,22},{31,23}} | collective-permute-start | bytes 1769480 | tf_op jit(solution)/shard_map/ppermute | solution.py:1083
  601.6 29.0 %collective-permute-start.82 = (bf16[2,2,288,256]{3,2,1,0:T(8,128)(2,1)S(1)}, bf16[2,2,288,256]{3,2,1,0:T(8,128)(2,1)S(1)}, u32[]{:S(2)}, u32[]{:S(2)}) collective-permute-start(bf16[2,2,288,256]{3,2,1,0:T(8,128)(2,1)S(1)} %get-tuple-element.99), channel_id=1, source_target_pairs={{0,8},{1,9},{2,10},{3,11},{4,12},{5,13},{6,14},{7,15}} | collective-permute-start | bytes 1769480 | tf_op jit(solution)/shard_map/ppermute | solution.py:1083
  612.8 65.3 %collective-permute-start.85 = (bf16[2,2,288,256]{3,2,1,0:T(8,128)(2,1)S(1)}, bf16[2,2,288,256]{3,2,1,0:T(8,128)(2,1)S(1)}, u32[]{:S(2)}, u32[]{:S(2)}) collective-permute-start(bf16[2,2,288,256]{3,2,1,0:T(8,128)(2,1)S(1)} %get-tuple-element.100), channel_id=1, source_target_pairs={{24,16},{25,17},{26,18},{27,19},{28,20},{29,21},{30,22},{31,23}} | collective-permute-start | bytes 1769480 | tf_op jit(solution)/shard_map/ppermute | solution.py:1083
  653.4 23.2 %collective-permute-start.91 = (bf16[2,2,288,256]{3,2,1,0:T(8,128)(2,1)S(1)}, bf16[2,2,288,256]{3,2,1,0:T(8,128)(2,1)S(1)}, u32[]{:S(2)}, u32[]{:S(2)}) collective-permute-start(bf16[2,2,288,256]{3,2,1,0:T(8,128)(2,1)S(1)} %bitcast_add_fusion.11), channel_id=1, source_target_pairs={{0,8},{8,16},{1,9},{9,17},{2,10},{10,18},{3,11},{11,19},{4,12},{12... | collective-permute-start | bytes 1769480 | tf_op jit(solution)/shard_map/ppermute | solution.py:1083
  657.8 28.9 %collective-permute-start.83 = (bf16[2,2,288,256]{3,2,1,0:T(8,128)(2,1)S(1)}, bf16[2,2,288,256]{3,2,1,0:T(8,128)(2,1)S(1)}, u32[]{:S(2)}, u32[]{:S(2)}) collective-permute-start(bf16[2,2,288,256]{3,2,1,0:T(8,128)(2,1)S(1)} %bitcast_add_fusion.16), channel_id=1, source_target_pairs={{0,8},{8,16},{1,9},{9,17},{2,10},{10,18},{3,11},{11,19},{4,12},{12... | collective-permute-start | bytes 1769480 | tf_op jit(solution)/shard_map/ppermute | solution.py:1083
  661.3 26.9 %collective-permute-start.9 = (bf16[32,1024]{1,0:T(8,128)(2,1)S(1)}, bf16[32,1024]{1,0:T(8,128)(2,1)S(1)}, u32[]{:S(2)}, u32[]{:S(2)}) collective-permute-start(bf16[32,1024]{1,0:T(8,128)(2,1)S(1)} %get-tuple-element.147), channel_id=1, source_target_pairs={{0,8},{8,16},{16,24},{1,9},{9,17},{17,25},{2,10},{10,18},{18,26},{... | collective-permute-start | bytes 196616 | tf_op jit(solution)/shard_map/ppermute | solution.py:1083
  678.1 44.9 %collective-permute-start.27 = (bf16[32,1024]{1,0:T(8,128)(2,1)S(1)}, bf16[32,1024]{1,0:T(8,128)(2,1)S(1)}, u32[]{:S(2)}, u32[]{:S(2)}) collective-permute-start(bf16[32,1024]{1,0:T(8,128)(2,1)S(1)} %get-tuple-element.139), channel_id=1, source_target_pairs={{0,8},{8,16},{16,24},{1,9},{9,17},{17,25},{2,10},{10,18},{18,26},{... | collective-permute-start | bytes 196616 | tf_op jit(solution)/shard_map/ppermute | solution.py:1083
  694.9 29.4 %collective-permute-start.30 = (bf16[32,1024]{1,0:T(8,128)(2,1)S(1)}, bf16[32,1024]{1,0:T(8,128)(2,1)S(1)}, u32[]{:S(2)}, u32[]{:S(2)}) collective-permute-start(bf16[32,1024]{1,0:T(8,128)(2,1)S(1)} %bitcast_add_fusion.66), channel_id=1, source_target_pairs={{24,16},{16,8},{8,0},{25,17},{17,9},{9,1},{26,18},{18,10},{10,2},{... | collective-permute-start | bytes 196616 | tf_op jit(solution)/shard_map/ppermute | solution.py:1083
  696.3 28.7 %collective-permute-start.92 = (bf16[2,2,288,256]{3,2,1,0:T(8,128)(2,1)S(1)}, bf16[2,2,288,256]{3,2,1,0:T(8,128)(2,1)S(1)}, u32[]{:S(2)}, u32[]{:S(2)}) collective-permute-start(bf16[2,2,288,256]{3,2,1,0:T(8,128)(2,1)S(1)} %get-tuple-element.93), channel_id=1, source_target_pairs={{0,8},{8,16},{16,24},{1,9},{9,17},{17,25},{2,10},{10,18},{18,26},{... | collective-permute-start | bytes 1769480 | tf_op jit(solution)/shard_map/ppermute | solution.py:1083
  (111 other events, 939.8 us)

commit v2 on v1

--- a/solution.py
+++ b/solution.py
@@ -279,7 +279,6 @@
 F32 = jnp.float32
 LANES = 128
 FF_TILE = 256
-FFN_CALLS = 3
 VMEM_BYTES = 56 * 1024 * 1024
 LOG2_E = math.log2(math.e)
 QUERY_SCALE = HEAD_DIM ** (-0.5) * LOG2_E
@@ -558,142 +557,6 @@
     )(qkv, starts)
 
 
-def attend_back_kernel(
-    groups,
-    block,
-    qkv_ref,
-    logs_ref,
-    out_ref,
-    grad_ref,
-    starts_ref,
-    result_ref,
-    queries,
-    keys,
-    values,
-    grads,
-    query_grad,
-    pair_grad,
-):
-    size = qkv_ref.shape[0]
-    blocks = size // block
-    q_width = groups * LANES
-    here = pl.program_id(0)
-
-    @pl.when(here == 0)
-    def _():
-        query_grad[...] = jnp.zeros_like(query_grad)
-        for g in range(groups):
-            lanes = slice(g * LANES, (g + 1) * LANES)
-            keys[g, :, :LANES] = doubled(qkv_ref[:, q_width : q_width + LANES], g)
-            keys[g, :, LANES:] = minus_three(size)
-            values[g, :, :LANES] = doubled(qkv_ref[:, q_width + LANES : q_width + 2 * LANES], g)
-            values[g, :, LANES:] = minus_three(size)
-
-            def fill(i, carry):
-                at = pl.multiple_of(i * block, block)
-                to = pl.multiple_of(i * 2 * block, 2 * block)
-                queries[g, pl.ds(to, 2 * block), :LANES] = stacked_heads(qkv_ref[pl.ds(at, block), lanes])
-                queries[g, pl.ds(to, 2 * block), LANES:] = logs_ref[g, pl.ds(to, 2 * block), :]
-                grad = stacked_heads(grad_ref[pl.ds(at, block), lanes])
-                mean = stacked_heads(out_ref[pl.ds(at, block), lanes])
-                delta = jnp.sum(grad.astype(F32) * mean.astype(F32), axis=1, keepdims=True)
-                grads[g, pl.ds(to, 2 * block), :LANES] = grad
-                grads[g, pl.ds(to, 2 * block), LANES:] = in_three(delta)
-                return carry
-
-            lax.fori_loop(0, blocks, fill, 0)
-
-    key_at = pl.multiple_of(here * block, block)
-    key_rows = pl.ds(key_at, block)
-    row = lax.broadcasted_iota(jnp.int32, (block, 2 * block), 0)
-    column = lax.broadcasted_iota(jnp.int32, (block, 2 * block), 1) % block
-
-    def step(i, diagonal):
-        at = pl.multiple_of(i * 2 * block, 2 * block)
-        stack = pl.ds(at, 2 * block)
-        allowed = row >= starts_ref[:, stack] - key_at
-        if diagonal:
-            allowed = allowed & (row <= column)
-        for g in range(groups):
-            query = queries[g, stack, :]
-            grad = grads[g, stack, :]
-            key = keys[g, key_rows, :]
-            scores = nt_dot(key, query)
-            probs = jnp.exp2(jnp.where(allowed, scores, MASKED))
-            pushed = (probs * nt_dot(values[g, key_rows, :], grad)).astype(BF16)
-            value_part = nn_dot(probs.astype(BF16), grad[:, :LANES])
-            key_part = nn_dot(pushed, query[:, :LANES])
-            if diagonal:
-                pair_grad[g, :, LANES:] = value_part
-                pair_grad[g, :, :LANES] = key_part
-            else:
-                pair_grad[g, :, LANES:] += value_part
-                pair_grad[g, :, :LANES] += key_part
-            query_grad[g, stack, :] += tn_dot(pushed, key[:, :LANES])
-
-    step(here, True)
-
-    def body(i, carry):
-        step(i, False)
-        return carry
-
-    lax.fori_loop(here + 1, blocks, body, 0)
-    low = low_lanes((block, LANES))
-    for part in range(2):
-        sums = []
-        for g in range(groups):
-            both = pair_grad[g, :, part * LANES : (part + 1) * LANES]
-            sums.append(both + pltpu.roll(both, HEAD_DIM, 1))
-        joined = jnp.where(low, sums[0], sums[1])
-        if part == 0:
-            joined = joined * (1.0 / LOG2_E)
-        lane = q_width + part * LANES
-        result_ref[key_rows, lane : lane + LANES] = joined.astype(BF16)
-
-    @pl.when(here == blocks - 1)
-    def _():
-        for g in range(groups):
-
-            def finish(i, carry):
-                at = pl.multiple_of(i * block, block)
-                to = pl.multiple_of(i * 2 * block, 2 * block)
-                first = query_grad[g, pl.ds(to, block), :]
-                second = query_grad[g, pl.ds(to + block, block), :]
-                joined = jnp.where(low, first, second) * HEAD_DIM ** (-0.5)
-                result_ref[pl.ds(at, block), g * LANES : (g + 1) * LANES] = joined.astype(BF16)
-                return carry
-
-            lax.fori_loop(0, blocks, finish, 0)
-
-
-def attend_back(qkv, logs, out, grad, starts, block):
-    size, width = qkv.shape
-    groups = (width - 2 * LANES) // LANES
-    return pl.pallas_call(
-        functools.partial(attend_back_kernel, groups, block),
-        name="attend_back",
-        grid=(size // block,),
-        in_specs=[
-            whole_block(qkv.shape),
-            whole_block(logs.shape),
-            whole_block(out.shape),
-            whole_block(grad.shape),
-            whole_block(starts.shape),
-        ],
-        out_specs=whole_block(qkv.shape),
-        out_shape=jax.ShapeDtypeStruct(qkv.shape, BF16),
-        scratch_shapes=[
-            pltpu.VMEM((groups, 2 * size, 2 * LANES), BF16),
-            pltpu.VMEM((groups, size, 2 * LANES), BF16),
-            pltpu.VMEM((groups, size, 2 * LANES), BF16),
-            pltpu.VMEM((groups, 2 * size, 2 * LANES), BF16),
-            pltpu.VMEM((groups, 2 * size, LANES), F32),
-            pltpu.VMEM((groups, block, 2 * LANES), F32),
-        ],
-        compiler_params=kernel_params(),
-    )(qkv, logs, out, grad, starts)
-
-
 def middle_kernel(tokens_ref, heads_ref, w_out_ref, gain_ref, middle_ref, hidden_ref):
     half = heads_ref.shape[1]
     width = heads_ref.shape[2]
@@ -719,43 +582,33 @@
 
 
 def ffn_kernel(
-    first,
-    last,
     core_ref,
     hidden_ref,
-    flipped_ref,
     grad_ref,
     w_gate_ref,
     w_up_ref,
     w_down_ref,
-    *refs,
+    gate_grad_ref,
+    up_grad_ref,
+    acts_ref,
+    out_own_ref,
+    out_send_ref,
+    back_own_ref,
+    back_send_ref,
+    out_sum,
+    back_sum,
 ):
-    if first:
-        sums_in, refs = None, refs
-    else:
-        sums_in, refs = refs[:2], refs[2:]
-    g_gate_ref, g_up_ref, g_down_ref = refs[:3]
-    if last:
-        finals, refs = refs[3:7], refs[7:]
-    else:
-        finals, refs = refs[3:5], refs[5:]
-    out_sum, back_sum, acts, gate_grads, up_grads = refs
     step = pl.program_id(0)
-    count = pl.num_programs(0)
     rows = hidden_ref.shape[0]
     chunk = min(256, rows)
 
     @pl.when(step == 0)
     def _():
-        if first:
-            out_sum[...] = jnp.zeros_like(out_sum)
-            back_sum[...] = jnp.zeros_like(back_sum)
-        else:
-            out_sum[...] = sums_in[0][...]
-            back_sum[...] = sums_in[1][...]
-
-    def forward(m, carry):
-        part = pl.ds(pl.multiple_of(m * chunk, chunk), chunk)
+        out_sum[...] = jnp.zeros_like(out_sum)
+        back_sum[...] = jnp.zeros_like(back_sum)
+
+    for m in range(rows // chunk):
+        part = slice(m * chunk, (m + 1) * chunk)
         hidden = hidden_ref[part, :]
         gate = nn_dot(hidden, w_gate_ref[...])
         up = nn_dot(hidden, w_up_ref[...])
@@ -765,99 +618,58 @@
         act = (silu * up).astype(BF16)
         gate_grad = (pushed * up * opened * (1.0 + gate * (1.0 - opened))).astype(BF16)
         up_grad = (pushed * silu).astype(BF16)
-        acts[part, :] = act
-        gate_grads[part, :] = gate_grad
-        up_grads[part, :] = up_grad
+        acts_ref[:, part] = act.T
+        gate_grad_ref[part, :] = gate_grad
+        up_grad_ref[part, :] = up_grad
         out_sum[part, :] += nn_dot(act, w_down_ref[...])
         back_sum[part, :] += nt_dot(gate_grad, w_gate_ref[...]) + nt_dot(up_grad, w_up_ref[...])
-        return carry
-
-    lax.fori_loop(0, rows // chunk, forward, 0)
-    width = flipped_ref.shape[0]
-
-    def weights(m, carry):
-        part = pl.ds(pl.multiple_of(m * chunk, chunk), chunk)
-        flipped = flipped_ref[part, :]
-        g_gate_ref[part, :] = nn_dot(flipped, gate_grads[...]).astype(BF16)
-        g_up_ref[part, :] = nn_dot(flipped, up_grads[...]).astype(BF16)
-        return carry
-
-    lax.fori_loop(0, width // chunk, weights, 0)
-    g_down_ref[...] = tn_dot(acts[...], grad_ref[...]).astype(BF16)
-
-    @pl.when(step == count - 1)
+
+    @pl.when(step == pl.num_programs(0) - 1)
     def _():
-        if last:
-            half = rows // 2
-            finals[0][...] = out_sum[:half, :]
-            finals[1][...] = out_sum[half:, :].astype(BF16)
-            finals[2][...] = back_sum[:half, :]
-            finals[3][...] = back_sum[half:, :].astype(BF16)
-        else:
-            finals[0][...] = out_sum[...]
-            finals[1][...] = back_sum[...]
-
-
-def ffn_part(core, hidden, flipped, grad, w_gate, w_up, w_down, sums, begin, tiles, last):
+        half = rows // 2
+        out_own_ref[...] = out_sum[:half, :]
+        out_send_ref[...] = out_sum[half:, :].astype(BF16)
+        back_own_ref[...] = back_sum[:half, :]
+        back_send_ref[...] = back_sum[half:, :].astype(BF16)
+
+
+def feed_forward(core, hidden, grad, w_gate, w_up, w_down):
     rows, width = hidden.shape
-    per_core = w_gate.shape[1] // 2 // FF_TILE
-    first = sums is None
+    tiles = w_gate.shape[1] // 2 // FF_TILE
+    half = (rows // 2, width)
 
     def keep(shape):
         return pl.BlockSpec(shape, lambda f, c: (0,) * len(shape), pipeline_mode=pl.Buffered(1))
 
-    in_specs = [
-        keep((rows, width)),
-        keep((width, rows)),
-        keep((rows, width)),
-        pl.BlockSpec((width, FF_TILE), lambda f, c: (0, c[0] * per_core + begin + f)),
-        pl.BlockSpec((width, FF_TILE), lambda f, c: (0, c[0] * per_core + begin + f)),
-        pl.BlockSpec((FF_TILE, width), lambda f, c: (c[0] * per_core + begin + f, 0)),
-    ]
-    args = [hidden, flipped, grad, w_gate, w_up, w_down]
-    if not first:
-        in_specs += [keep((rows, width))] * 2
-        args += list(sums)
-    out_specs = [
-        pl.BlockSpec((width, FF_TILE), lambda f, c: (0, f)),
-        pl.BlockSpec((width, FF_TILE), lambda f, c: (0, f)),
-        pl.BlockSpec((FF_TILE, width), lambda f, c: (f, 0)),
-    ]
-    out_shape = [
-        jax.ShapeDtypeStruct((width, tiles * FF_TILE), BF16),
-        jax.ShapeDtypeStruct((width, tiles * FF_TILE), BF16),
-        jax.ShapeDtypeStruct((tiles * FF_TILE, width), BF16),
-    ]
-    if last:
-        half = (rows // 2, width)
-        out_specs += [keep(half)] * 4
-        out_shape += [jax.ShapeDtypeStruct(half, kind) for kind in (F32, BF16, F32, BF16)]
-    else:
-        out_specs += [keep((rows, width))] * 2
-        out_shape += [jax.ShapeDtypeStruct((rows, width), F32)] * 2
-    flops = 18 * rows * width * FF_TILE * tiles
     return pl.pallas_call(
-        functools.partial(ffn_kernel, first, last),
-        name=f"ffn_{begin}",
+        ffn_kernel,
+        name="feed_forward",
         grid_spec=pltpu.PrefetchScalarGridSpec(
             num_scalar_prefetch=1,
             grid=(tiles,),
-            in_specs=in_specs,
-            out_specs=out_specs,
-            scratch_shapes=[
-                pltpu.VMEM((rows, width), F32),
-                pltpu.VMEM((rows, width), F32),
-                pltpu.VMEM((rows, FF_TILE), BF16),
-                pltpu.VMEM((rows, FF_TILE), BF16),
-                pltpu.VMEM((rows, FF_TILE), BF16),
+            in_specs=[
+                keep((rows, width)),
+                keep((rows, width)),
+                pl.BlockSpec((width, FF_TILE), lambda f, c: (0, c[0] * tiles + f)),
+                pl.BlockSpec((width, FF_TILE), lambda f, c: (0, c[0] * tiles + f)),
+                pl.BlockSpec((FF_TILE, width), lambda f, c: (c[0] * tiles + f, 0)),
             ],
+            out_specs=[
+                pl.BlockSpec((rows, FF_TILE), lambda f, c: (0, f)),
+                pl.BlockSpec((rows, FF_TILE), lambda f, c: (0, f)),
+                pl.BlockSpec((FF_TILE, rows), lambda f, c: (f, 0)),
+            ]
+            + [keep(half)] * 4,
+            scratch_shapes=[pltpu.VMEM((rows, width), F32), pltpu.VMEM((rows, width), F32)],
         ),
-        out_shape=out_shape,
+        out_shape=[
+            jax.ShapeDtypeStruct((rows, tiles * FF_TILE), BF16),
+            jax.ShapeDtypeStruct((rows, tiles * FF_TILE), BF16),
+            jax.ShapeDtypeStruct((tiles * FF_TILE, rows), BF16),
+        ]
+        + [jax.ShapeDtypeStruct(half, kind) for kind in (F32, BF16, F32, BF16)],
         compiler_params=kernel_params(),
-        cost_estimate=pl.CostEstimate(
-            flops=flops, bytes_accessed=12 * width * FF_TILE * tiles, transcendentals=0
-        ),
-    )(core, *args)
+    )(core, hidden, grad, w_gate, w_up, w_down)
 
 
 def turn_kernel(
@@ -1053,6 +865,463 @@
         scratch_shapes=[pltpu.VMEM((rows, width), F32)],
         compiler_params=kernel_params(),
     )(got, proj, hidden, tokens, mid, gain, wq, wk, wv, q_gain, k_gain, cosine, sine)
+
+
+def pair_of(bit):
+    index = lax.axis_index("blk")
+    mine = lax.rem(index // bit, 2)
+    return mine, (lax.axis_index("dp"), index + bit * (1 - 2 * mine))
+
+
+class Stream:
+    def __init__(self, path, dims, block, line, kind=BF16):
+        self.path, self.block, self.line, self.kind = path, block, line, kind
+        self.dims = [tuple(dims)]
+        left = list(dims)
+        names = [name for name, unused in dims]
+        for stage in path:
+            if isinstance(stage, tuple):
+                if stage[1] == line - 1:
+                    at = [n for n, unused in left].index("z")
+                    left = left[:at] + left[at + 1 :]
+            else:
+                at = [n for n, unused in left].index(stage)
+                left = left[:at] + left[at + 1 :]
+            self.dims.append(tuple(left))
+        assert not left and "z" in names
+
+    def is_hop(self, k):
+        return isinstance(self.path[k], tuple)
+
+    def starts_work(self, k):
+        return k == 0 or not self.is_hop(k) or self.path[k][1] == 1
+
+    def shape(self, dims):
+        return tuple(count for unused, count in dims) + self.block
+
+    def slots(self, k):
+        return self.line if self.is_hop(k) else 2
+
+    def scratch(self):
+        shapes = []
+        for k in range(len(self.path)):
+            if self.starts_work(k):
+                shapes.append(pltpu.VMEM((self.slots(k),) + self.shape(self.dims[k]), self.kind))
+            if self.is_hop(k):
+                rest = tuple(d for d in self.dims[k] if d[0] != "z")
+                shapes.append(pltpu.VMEM((2, 2) + self.shape(rest), self.kind))
+                shapes += [pltpu.SemaphoreType.DMA((2, 2))] * 2
+            else:
+                shapes.append(pltpu.VMEM((2,) + self.shape(self.dims[k + 1]), self.kind))
+                shapes += [pltpu.SemaphoreType.DMA((2,))] * 2
+        return shapes
+
+    def bind(self, refs, units, finish, first_z=None):
+        refs = list(refs)
+        self.units, self.finish = units, finish
+        self.first_z = 0 if first_z is None else first_z
+        self.work, self.got, self.sent_sem, self.got_sem = [], [], [], []
+        for k in range(len(self.path)):
+            self.work.append(refs.pop(0) if self.starts_work(k) else self.work[-1])
+            self.got.append(refs.pop(0))
+            self.sent_sem.append(refs.pop(0))
+            self.got_sem.append(refs.pop(0))
+        self.source = self.work[0]
+
+    def z_count(self, k):
+        return dict(self.dims[k])["z"]
+
+    def keeps(self, z, k):
+        return (z >= self.first_z) & (z < self.first_z + self.z_count(k))
+
+    def keeper(self, k):
+        if "z" in [name for name, unused in self.dims[k]] or dict(self.dims[0])["z"] == self.line:
+            return None
+        z = lax.axis_index("dp")
+        return (z >= self.first_z) & (z < self.first_z + dict(self.dims[0])["z"])
+
+    def pair_copy(self, k, u):
+        bit = self.path[k]
+        mine, partner = pair_of(bit)
+        at = [name for name, unused in self.dims[k]].index(bit)
+        whole = (slice(None),) * at
+        slot = lax.rem(u, 2)
+        copy = pltpu.make_async_remote_copy(
+            src_ref=self.work[k].at[(lax.rem(u, self.slots(k)),) + whole + (1 - mine,)],
+            dst_ref=self.got[k].at[slot],
+            send_sem=self.sent_sem[k].at[slot],
+            recv_sem=self.got_sem[k].at[slot],
+            device_id=partner,
+            device_id_type=pl.DeviceIdType.MESH,
+        )
+        return copy, whole + (mine,)
+
+    def hop_copy(self, k, u, way, block):
+        z, index = lax.axis_index("dp"), lax.axis_index("blk")
+        slot = lax.rem(u, 2)
+        side = (1 - way) // 2
+        return pltpu.make_async_remote_copy(
+            src_ref=self.work[k].at[lax.rem(u, self.slots(k)), block],
+            dst_ref=self.got[k].at[slot, side],
+            send_sem=self.sent_sem[k].at[slot, side],
+            recv_sem=self.got_sem[k].at[slot, side],
+            device_id=(z + way, index),
+            device_id_type=pl.DeviceIdType.MESH,
+        )
+
+    def hop_ends(self, k, way):
+        z = lax.axis_index("dp")
+        reach = way * (self.line - self.path[k][1])
+        goes, comes = z + reach, z - way + reach
+        sends = self.keeps(goes, k)
+        takes = self.keeps(comes, k) & (z - way >= 0) & (z - way < self.line)
+        return goes - self.first_z, sends, comes - self.first_z, takes
+
+    def send(self, k, step):
+        u = step - k - 1
+        due = (u >= 0) & (u < self.units)
+        if not self.is_hop(k):
+            keeper = self.keeper(k)
+
+            @pl.when(due if keeper is None else due & keeper)
+            def _():
+                self.pair_copy(k, u)[0].start()
+
+            return
+        for way in (1, -1):
+            block, sends, unused, unused = self.hop_ends(k, way)
+
+            @pl.when(due & sends)
+            def _():
+                self.hop_copy(k, u, way, block).start()
+
+    def take(self, k, step):
+        u = step - k - 2
+        due = (u >= 0) & (u < self.units)
+        keeper = self.keeper(k + 1)
+        last = k == len(self.path) - 1
+
+        def pass_on(value):
+            if last:
+                self.finish(u, value)
+            else:
+                self.work[k + 1][lax.rem(u, self.slots(k + 1))] = value
+
+        if not self.is_hop(k):
+            keeper = self.keeper(k)
+
+            @pl.when(due if keeper is None else due & keeper)
+            def _():
+                copy, mine = self.pair_copy(k, u)
+                copy.wait()
+                own = self.work[k][(lax.rem(u, self.slots(k)),) + mine]
+                pass_on(own + self.got[k][lax.rem(u, 2)])
+
+            return
+        slot = lax.rem(u, self.slots(k))
+        for way in (1, -1):
+            out_block, sends, in_block, takes = self.hop_ends(k, way)
+
+            @pl.when(due & sends)
+            def _():
+                self.hop_copy(k, u, way, out_block).wait_send()
+
+            @pl.when(due & takes)
+            def _():
+                self.hop_copy(k, u, way, in_block).wait_recv()
+                self.work[k][slot, in_block] += self.got[k][lax.rem(u, 2), (1 - way) // 2]
+
+        if self.path[k][1] == self.line - 1:
+            own = lax.axis_index("dp") - self.first_z
+
+            @pl.when(due if keeper is None else due & keeper)
+            def _():
+                pass_on(self.work[k][slot, own])
+
+
+def hops(line):
+    return [("z", t) for t in range(1, line)]
+
+
+def greet(bits, line):
+    barrier = pltpu.get_barrier_semaphore()
+    z, index = lax.axis_index("dp"), lax.axis_index("blk")
+    for bit in bits:
+        pl.semaphore_signal(barrier, inc=1, device_id=pair_of(bit)[1], device_id_type=pl.DeviceIdType.MESH)
+    for way in (1, -1):
+
+        @pl.when((z + way >= 0) & (z + way < line))
+        def _():
+            pl.semaphore_signal(
+                barrier, inc=1, device_id=(z + way, index), device_id_type=pl.DeviceIdType.MESH
+            )
+
+    beside = jnp.minimum(z, 1) + jnp.minimum(line - 1 - z, 1)
+    pl.semaphore_wait(barrier, len(bits) + beside)
+
+
+def step_streams(streams, step, steps, line, ready):
+    longest = max(len(stream.path) for stream in streams)
+    z, index = lax.axis_index("dp"), lax.axis_index("blk")
+    for k in range(longest):
+        for stream in streams:
+            if k < len(stream.path):
+                stream.take(k, step)
+    for way in (1, -1):
+        there = (z + way >= 0) & (z + way < line)
+
+        @pl.when(there & (step < steps - 1))
+        def _():
+            pl.semaphore_signal(
+                ready.at[(1 - way) // 2],
+                inc=1,
+                device_id=(z + way, index),
+                device_id_type=pl.DeviceIdType.MESH,
+            )
+
+        @pl.when(there & (step > 0))
+        def _():
+            pl.semaphore_wait(ready.at[(1 + way) // 2], 1)
+
+    for k in range(longest):
+        for stream in streams:
+            if k < len(stream.path):
+                stream.send(k, step)
+
+
+def back_kernel(
+    groups,
+    block,
+    line,
+    bits,
+    streams,
+    units,
+    qkv_ref,
+    logs_ref,
+    out_ref,
+    grad_ref,
+    starts_ref,
+    flipped_ref,
+    dy_ref,
+    gate_grad_ref,
+    up_grad_ref,
+    acts_ref,
+    result_ref,
+    gate_out_ref,
+    up_out_ref,
+    down_out_ref,
+    queries,
+    keys,
+    values,
+    grads,
+    query_grad,
+    pair_grad,
+    ready,
+    *refs,
+):
+    size = qkv_ref.shape[0]
+    blocks = size // block
+    q_width = groups * LANES
+    n = pl.program_id(0)
+    core = lax.rem(lax.axis_index("blk"), 2)
+    gate_stream, up_stream, down_stream = streams
+
+    def finish_gate(u, value):
+        gate_out_ref[:, pl.ds(pl.multiple_of(u * FF_TILE, FF_TILE), FF_TILE)] = value
+
+    def finish_up(u, value):
+        up_out_ref[:, pl.ds(pl.multiple_of(u * FF_TILE, FF_TILE), FF_TILE)] = value
+
+    def finish_down(u, value):
+        rows = value.shape[0]
+        down_out_ref[pl.ds(pl.multiple_of(u * rows, rows), rows), :] = value
+
+    at = 0
+    for stream, finish, first_z in (
+        (gate_stream, finish_gate, None),
+        (up_stream, finish_up, None),
+        (down_stream, finish_down, core * (line // 2)),
+    ):
+        count = len(stream.scratch())
+        stream.bind(refs[at : at + count], units, finish, first_z)
+        at += count
+
+    @pl.when(n == 0)
+    def _():
+        greet(bits, line)
+        down_out_ref[...] = jnp.zeros_like(down_out_ref)
+        query_grad[...] = jnp.zeros_like(query_grad)
+        pair_grad[...] = jnp.zeros_like(pair_grad)
+        for g in range(groups):
+            lanes = slice(g * LANES, (g + 1) * LANES)
+            keys[g, :, :LANES] = doubled(qkv_ref[:, q_width : q_width + LANES], g)
+            keys[g, :, LANES:] = minus_three(size)
+            values[g, :, :LANES] = doubled(qkv_ref[:, q_width + LANES : q_width + 2 * LANES], g)
+            values[g, :, LANES:] = minus_three(size)
+
+            def fill(i, carry):
+                at = pl.multiple_of(i * block, block)
+                to = pl.multiple_of(i * 2 * block, 2 * block)
+                queries[g, pl.ds(to, 2 * block), :LANES] = stacked_heads(qkv_ref[pl.ds(at, block), lanes])
+                queries[g, pl.ds(to, 2 * block), LANES:] = logs_ref[g, pl.ds(to, 2 * block), :]
+                grad = stacked_heads(grad_ref[pl.ds(at, block), lanes])
+                mean = stacked_heads(out_ref[pl.ds(at, block), lanes])
+                delta = jnp.sum(grad.astype(F32) * mean.astype(F32), axis=1, keepdims=True)
+                grads[g, pl.ds(to, 2 * block), :LANES] = grad
+                grads[g, pl.ds(to, 2 * block), LANES:] = in_three(delta)
+                return carry
+
+            lax.fori_loop(0, blocks, fill, 0)
+
+    step_streams(streams, n, pl.num_programs(0), line, ready)
+
+    @pl.when(n < units)
+    def _():
+        chunk = 256
+        width = flipped_ref.shape[0]
+        gate_shape = gate_stream.shape(gate_stream.dims[0])
+        down_shape = down_stream.shape(down_stream.dims[0])
+        slot = lax.rem(n, 2)
+        each = chunk * gate_shape[0] // width
+
+        def weights(m, carry):
+            flipped = flipped_ref[pl.ds(pl.multiple_of(m * chunk, chunk), chunk), :]
+            part = pl.ds(m * each, each)
+            piece = (each,) + gate_shape[1:]
+            gate_stream.source[slot, part] = nn_dot(flipped, gate_grad_ref[...]).astype(BF16).reshape(piece)
+            up_stream.source[slot, part] = nn_dot(flipped, up_grad_ref[...]).astype(BF16).reshape(piece)
+            return carry
+
+        lax.fori_loop(0, width // chunk, weights, 0)
+        acts = acts_ref[...].reshape(-1, acts_ref.shape[-1])
+        made = nn_dot(acts, dy_ref[...]).astype(BF16)
+        down_stream.source[lax.rem(n, down_stream.slots(0))] = made.reshape(down_shape)
+
+    row = lax.broadcasted_iota(jnp.int32, (block, 2 * block), 0)
+    column = lax.broadcasted_iota(jnp.int32, (block, 2 * block), 1) % block
+
+    @pl.when(n < blocks + 1)
+    def _():
+        def pair(m, carry):
+            late = (n + m) // blocks
+            j = m + late * (blocks - 1 - 2 * m)
+            i = (1 - late) * (m + n) + late * (n - 1)
+            key_at = pl.multiple_of(j * block, block)
+            at = pl.multiple_of(i * 2 * block, 2 * block)
+            key_rows = pl.ds(key_at, block)
+            stack = pl.ds(at, 2 * block)
+            allowed = (row >= starts_ref[:, stack] - key_at) & (row - column <= (i - j) * block)
+            for g in range(groups):
+                query = queries[g, stack, :]
+                grad = grads[g, stack, :]
+                key = keys[g, key_rows, :]
+                scores = nt_dot(key, query)
+                probs = jnp.exp2(jnp.where(allowed, scores, MASKED))
+                pushed = (probs * nt_dot(values[g, key_rows, :], grad)).astype(BF16)
+                pair_grad[g, key_rows, LANES:] += nn_dot(probs.astype(BF16), grad[:, :LANES])
+                pair_grad[g, key_rows, :LANES] += nn_dot(pushed, query[:, :LANES])
+                query_grad[g, stack, :] += tn_dot(pushed, key[:, :LANES])
+            return carry
+
+        lax.fori_loop(0, blocks // 2, pair, 0)
+
+    @pl.when(n == blocks + 1)
+    def _():
+        low = low_lanes((block, LANES))
+
+        def finish(i, carry):
+            at = pl.multiple_of(i * block, block)
+            to = pl.multiple_of(i * 2 * block, 2 * block)
+            here = pl.ds(at, block)
+            for g in range(groups):
+                first = query_grad[g, pl.ds(to, block), :]
+                second = query_grad[g, pl.ds(to + block, block), :]
+                joined = jnp.where(low, first, second) * HEAD_DIM ** (-0.5)
+                result_ref[here, g * LANES : (g + 1) * LANES] = joined.astype(BF16)
+            for part in range(2):
+                sums = []
+                for g in range(groups):
+                    both = pair_grad[g, here, part * LANES : (part + 1) * LANES]
+                    sums.append(both + pltpu.roll(both, HEAD_DIM, 1))
+                joined = jnp.where(low, sums[0], sums[1])
+                if part == 0:
+                    joined = joined * (1.0 / LOG2_E)
+                lane = q_width + part * LANES
+                result_ref[here, lane : lane + LANES] = joined.astype(BF16)
+            return carry
+
+        lax.fori_loop(0, blocks, finish, 0)
+
+
+def back(line, bits, qkv, logs, out, grad, starts, block, flipped, dy, gate_grad, up_grad, acts):
+    size, width = qkv.shape
+    groups = (width - 2 * LANES) // LANES
+    units = gate_grad.shape[1] // FF_TILE
+    model, rows = flipped.shape
+    chips = line * 2 ** len(bits)
+    sides = [(bit, 2) for bit in bits]
+    gate_block = (model // chips, FF_TILE)
+    down_rows = acts.shape[0] // (chips // 2)
+    down_block = (down_rows // units, model)
+    whole = [("z", line)] + sides
+    half = [("z", line // 2)] + sides
+    streams = [
+        Stream(bits[::-1] + hops(line), whole, gate_block, line),
+        Stream(bits + hops(line), whole, gate_block, line),
+        Stream(hops(line) + bits, half, down_block, line),
+    ]
+    longest = max(len(stream.path) for stream in streams)
+    steps = units + longest + 1
+
+    def keep(shape):
+        return pl.BlockSpec(shape, lambda n: (0,) * len(shape), pipeline_mode=pl.Buffered(1))
+
+    tile = lambda n: (0, jnp.minimum(n, units - 1))
+    acts = acts.reshape(chips // 2, down_rows, rows)
+    scratch = [
+        pltpu.VMEM((groups, 2 * size, 2 * LANES), BF16),
+        pltpu.VMEM((groups, size, 2 * LANES), BF16),
+        pltpu.VMEM((groups, size, 2 * LANES), BF16),
+        pltpu.VMEM((groups, 2 * size, 2 * LANES), BF16),
+        pltpu.VMEM((groups, 2 * size, LANES), F32),
+        pltpu.VMEM((groups, size, 2 * LANES), F32),
+        pltpu.SemaphoreType.REGULAR((2,)),
+    ]
+    for stream in streams:
+        scratch += stream.scratch()
+    return pl.pallas_call(
+        functools.partial(back_kernel, groups, block, line, bits, streams, units),
+        name="back",
+        grid=(steps,),
+        in_specs=[
+            keep(qkv.shape),
+            keep(logs.shape),
+            keep(out.shape),
+            keep(grad.shape),
+            keep(starts.shape),
+            keep(flipped.shape),
+            keep(dy.shape),
+            pl.BlockSpec((rows, FF_TILE), tile),
+            pl.BlockSpec((rows, FF_TILE), tile),
+            pl.BlockSpec(
+                (chips // 2, down_block[0], rows), lambda n: (0, jnp.minimum(n, units - 1), 0)
+            ),
+        ],
+        out_specs=[
+            keep(qkv.shape),
+            keep((gate_block[0], units * FF_TILE)),
+            keep((gate_block[0], units * FF_TILE)),
+            keep((down_rows, model)),
+        ],
+        out_shape=[
+            jax.ShapeDtypeStruct(qkv.shape, BF16),
+            jax.ShapeDtypeStruct((gate_block[0], units * FF_TILE), BF16),
+            jax.ShapeDtypeStruct((gate_block[0], units * FF_TILE), BF16),
+            jax.ShapeDtypeStruct((down_rows, model), BF16),
+        ],
+        scratch_shapes=scratch,
+        compiler_params=kernel_params(collective_id=4, has_side_effects=True),
+    )(qkv, logs, out, grad, starts, flipped, dy, gate_grad, up_grad, acts)
 
 
 def flip_pairs(count, bit):
@@ -1166,51 +1435,33 @@
     hidden = jnp.concatenate([hidden_own, swap_core(hidden_own, blk_count)], axis=0)
     flipped = hidden.T
     core_arg = core.reshape(1)
-    tiles = w_gate.shape[1] // 2 // FF_TILE
-    sums = None
-    gate_sums, up_sums, down_parts = [], [], []
-    each = tiles // FFN_CALLS
-    forward_order = bits + ["z"]
-    other_order = bits[::-1] + ["z"]
-    for call in range(FFN_CALLS):
-        last = call == FFN_CALLS - 1
-        made = ffn_part(
-            core_arg, hidden, flipped, grad_both, w_gate, w_up, w_down, sums, call * each, each, last
-        )
-        gate_parts, up_parts, down_part = made[:3]
-        sums = made[3:]
-        down_parts.append(down_part)
-        gate_sums.append(
-            sum_chips(gate_parts.reshape(chip_dims + (-1, each * FF_TILE)), forward_order, dp_count, blk_count)
-        )
-        up_sums.append(
-            sum_chips(up_parts.reshape(chip_dims + (-1, each * FF_TILE)), other_order, dp_count, blk_count)
-        )
-    out_own, out_send, back_own, back_send = sums
+    gate_grad, up_grad, acts, out_own, out_send, back_own, back_send = feed_forward(
+        core_arg, hidden, grad_both, w_gate, w_up, w_down
+    )
     back_got = swap_core(back_send, blk_count)
     out_got = swap_core(out_send, blk_count)
     output, mid, ffn_gain_grad, w_out_parts, send = turn(
         middle, out_own, out_got, back_own, back_got, grad_own, g_ffn[None], heads, w_out
     )
-    half_width = width // 2
-    down_half = jnp.concatenate(down_parts, axis=0)
-    down_own = lax.dynamic_slice_in_dim(down_half, core * half_width, half_width, axis=1)
-    down_got = swap_core(
-        lax.dynamic_slice_in_dim(down_half, (1 - core) * half_width, half_width, axis=1), blk_count
-    )
-    down_low = jnp.where(core == 0, down_own, down_got)
-    down_high = jnp.where(core == 0, down_got, down_own)
-    down_all = jnp.concatenate([down_low, down_high], axis=0).reshape(
-        chip_dims + (-1, half_width)
-    )
-    quarter = half_width // 2
-    down_sums = [
-        sum_chips(down_all[..., :quarter], ["z"] + bits, dp_count, blk_count),
-        sum_chips(down_all[..., quarter:], ["z"] + bits[::-1], dp_count, blk_count),
-    ]
     grad_heads = swap_blocks(send, 2).reshape(size, -1)
-    back = attend_back(qkv, logs, attended.reshape(size, -1), grad_heads, starts_two, tok_count)
-    got = swap_blocks(back.reshape(blk_count, tok_count, -1), 3)
+    qkv_grad, gate_sum, up_sum, down_sum = back(
+        dp_count,
+        bits,
+        qkv,
+        logs,
+        attended.reshape(size, -1),
+        grad_heads,
+        starts_two,
+        tok_count,
+        flipped,
+        grad_both,
+        gate_grad,
+        up_grad,
+        acts,
+    )
+    forward_order = bits + ["z"]
+    other_order = bits[::-1] + ["z"]
+    got = swap_blocks(qkv_grad.reshape(blk_count, tok_count, -1), 3)
     input_grad, attn_gain_grad, query_gain_grad, key_gain_grad, gq, gk, gv = project_back(
         got,
         proj,
@@ -1247,9 +1498,15 @@
         high = jnp.where(core == 0, got, own)
         return jnp.concatenate([low, high], axis=1).astype(F32)
 
-    grad_w_gate = join(jnp.concatenate(gate_sums, axis=1), 1)
-    grad_w_up = join(jnp.concatenate(up_sums, axis=1), 1)
-    grad_w_down = join(jnp.concatenate(down_sums, axis=1), 1)
+    grad_w_gate = join(gate_sum, 1)
+    grad_w_up = join(up_sum, 1)
+    down_rows = down_sum.shape[0] // 2
+    down_own = lax.dynamic_slice_in_dim(down_sum, core * down_rows, down_rows, axis=0)
+    down_got = swap_core(
+        lax.dynamic_slice_in_dim(down_sum, (1 - core) * down_rows, down_rows, axis=0), blk_count
+    )
+    holder = lax.axis_index("dp") // (dp_count // 2)
+    grad_w_down = jnp.where(holder == core, down_own, down_got).astype(F32)
     fold = lambda both: both[0, :HEAD_DIM] + both[0, HEAD_DIM:]
     gain_attn, gain_query, gain_key, gain_ffn = lax.psum(
         (attn_gain_grad[0], fold(query_gain_grad), fold(key_gain_grad), ffn_gain_grad[0]),

time: 760 us -> 509 us (0.67); the launches traced: 750 us -> 508 us
  starting transfers between devices: 253 us -> 48.3 us
  waiting for transfers between devices: 106 us -> 29.2 us
  Pallas kernels: 286 us -> 349 us
  local copies, waits for them, and re-layouts: 32.1 us -> 20 us
    ppermute x66 -> x18, starting transfers between devices: 224 us -> 36.6 us  [sum_line(): got = lax.ppermute(send, axis, pairs)]
    pallas_call x4 -> x2, Pallas kernels: 138 us -> 201 us  [the longest x1 159 us: back(): pl.pallas_call(functools.partial(back_kernel, groups, block, line, bits,...]
    ppermute x66 -> x18, waiting for transfers between devices: 48.3 us -> 5.43 us  [sum_line(): got = lax.ppermute(send, axis, pairs)]
    ppermute x25 -> x9, waiting for transfers between devices: 53.3 us -> 17.7 us  [sum_pair(): return own + lax.ppermute(send, axis, flip_pairs(count, bit))]
    ppermute x25 -> x9, starting transfers between devices: 27 us -> 9.62 us  [sum_pair(): return own + lax.ppermute(send, axis, flip_pairs(count, bit))]
    squeeze x22 -> x6, local copies, waits for them, and re-layouts: 10.1 us -> 0.22 us  [sum_pair(): send = lax.dynamic_index_in_dim(parts, 1 - mine, dim, keepdims=False)]
  transfers between devices with their start and end apart: 99 -> 34, of which waited for: 42 -> 9; matrix products, arithmetic and copies ran while one was open for 5% -> 5% of each run, Pallas kernels for 23% -> 8%
where the time goes in v2:
time: 509 us; the launch traced here: 508 us
  Pallas kernels  349 us (69%)
  starting transfers between devices  48.3 us (9%)
  blocking collectives  39.4 us (8%)
  waiting for transfers between devices  29.2 us (6%)
  other arithmetic  20.6 us (4%)
  local copies, waits for them, and re-layouts  20 us (4%)
    pallas_call x1, Pallas kernels, back(): pl.pallas_call(functools.partial(back_kernel, groups, block, line, bits,...  159 us
    pallas_call x4, Pallas kernels, swap_blocks(): pl.pallas_call(swap_blocks_kernel, name=f'swap_blocks_{collective_id}', o...  82.1 us
    pallas_call x1, Pallas kernels, feed_forward(): pl.pallas_call(ffn_kernel, name='feed_forward', grid_spec=pltpu.PrefetchS...  41.8 us
    psum x1, blocking collectives, fast_local(): lax.psum((attn_gain_grad[0], fold(query_gain_grad), fold(key_gain_grad),...  39.4 us
    ppermute x18, starting transfers between devices, sum_line(): got = lax.ppermute(send, axis, pairs)  36.6 us
    pallas_call x1, Pallas kernels, attend(): pl.pallas_call(functools.partial(attend_kernel, groups, block), name='att...  25.4 us
    ppermute x9, waiting for transfers between devices, sum_pair(): return own + lax.ppermute(send, axis, flip_pairs(count, bit))  17.7 us
    pallas_call x1, Pallas kernels, project_back(): pl.pallas_call(project_back_kernel, name='project_back', grid=(chips,), i...  16.7 us
  transfers between devices with their start and end apart: 34, of which 9 were waited for; matrix products, arithmetic and copies ran while one was open for 5% of the time, Pallas kernels for 8%

profile of v2, /device:TPU:0, one launch (start us, length us, event | category | flops | bytes accessed | tf_op | source)
XLA Modules:
  0.0 507.7 jit_solution(5587558438121732492)
XLA Ops:
  9.0 8.5 %project.1 = (bf16[512,1024]{1,0:T(8,128)(2,1)}, f32[4,512,384]{2,1,0:T(8,128)}, bf16[8,256,512]{2,1,0:T(8,128)(2,1)}) custom-call(bf16[512,1024]{1,0:T(8,128)(2,1)} %bitcast.126, f32[1,1024]{1,0:T(1,128)} %bitcast.144, bf16[1024,1024]{1,0:T(8,128)(2,1)} %wq_ref.3, bf16[1024,512]{1,0:T(8,128)(2,1)} %wk_ref.3, bf16[1024,512]{1,0:T(8,128)(2,1)} %wv_ref.3, ...), custom_call_target="tpu_custom_call" | custom-call | tf_op jit(solution)/shard_map/project/pallas_call | solution.py:424
  17.5 27.4 %swap_blocks_0.1 = bf16[8,256,512]{2,1,0:T(8,128)(2,1)} custom-call(bf16[8,256,512]{2,1,0:T(8,128)(2,1)} %get-tuple-element.43.send_ref), custom_call_target="tpu_custom_call" | custom-call | tf_op jit(solution)/shard_map/swap_blocks_0/pallas_call | solution.py:343
  44.9 25.4 %attend.1 = (bf16[8,256,256]{2,1,0:T(8,128)(2,1)}, bf16[2,4096,128]{2,1,0:T(8,128)(2,1)}) custom-call(bf16[2048,512]{1,0:T(8,128)(2,1)} %bitcast.124, s32[2048,1]{1,0:T(8,128)} %subtract_subtract_fusion.starts_ref), custom_call_target="tpu_custom_call" | custom-call | tf_op jit(solution)/shard_map/attend/pallas_call | solution.py:538
  70.3 15.0 %swap_blocks_1.1.heads_ref = bf16[8,256,256]{2,1,0:T(8,128)(2,1)} custom-call(bf16[8,256,256]{2,1,0:T(8,128)(2,1)} %get-tuple-element.44.send_ref), custom_call_target="tpu_custom_call" | custom-call | tf_op jit(solution)/shard_map/swap_blocks_1/pallas_call | solution.py:343
  85.3 5.3 %middle.1 = (f32[512,1024]{1,0:T(8,128)}, bf16[512,1024]{1,0:T(8,128)(2,1)}) custom-call(bf16[512,1024]{1,0:T(8,128)(2,1)} %bitcast.127, bf16[8,256,256]{2,1,0:T(8,128)(2,1)} %swap_blocks_1.1.heads_ref, bf16[1024,1024]{1,0:T(8,128)(2,1)} %w_out_ref.3, f32[1,1024]{1,0:T(1,128)} %bitcast.142), custom_call_target="tpu_custom_call" | custom-call | tf_op jit(solution)/shard_map/middle/pallas_call | solution.py:573
  93.2 2.8 collective-permute-done
  96.0 3.1 fusion.7
  101.7 2.8 pad_maximum_fusion.1.grad_ref.dy_ref
  104.5 41.8 %feed_forward.1 = (bf16[1024,2304]{1,0:T(8,128)(2,1)}, bf16[1024,2304]{1,0:T(8,128)(2,1)}, bf16[2304,1024]{1,0:T(8,128)(2,1)}, f32[512,1024]{1,0:T(8,128)}, bf16...) custom-call(s32[1]{0:T(128)} %bitcast.9.core_ref, bf16[1024,1024]{1,0:T(8,128)(2,1)} %copy.62.hidden_ref, ...), custom_call_target="tpu_custom_call" | custom-call | tf_op jit(solution)/shard_map/feed_forward/pallas_call | solution.py:644
  151.8 10.1 %turn.1 = (bf16[512,1024]{1,0:T(8,128)(2,1)}, f32[512,1024]{1,0:T(8,128)}, f32[1,1024]{1,0:T(1,128)}, bf16[1024,1024]{1,0:T(8,128)(2,1)}, bf16[8,256,256]{2,1,0:T(8,128)(2,1)}) custom-call(f32[512,1024]{1,0:T(8,128)} %get-tuple-element.45.middle_ref, f32[512,1024]{1,0:T(8,128)} %get-tuple-element.47.out_own_ref, bf16[512,1024]{1,0:T(8,128)(2,1)} %copy-done.4, ...), custom_call_target="tpu_custom_call" | custom-call | tf_op jit(solution)/shard_map/turn/pallas_call | solution.py:720
  161.9 14.6 %swap_blocks_2.1 = bf16[8,256,256]{2,1,0:T(8,128)(2,1)} custom-call(bf16[8,256,256]{2,1,0:T(8,128)(2,1)} %get-tuple-element.53.send_ref), custom_call_target="tpu_custom_call" | custom-call | tf_op jit(solution)/shard_map/swap_blocks_2/pallas_call | solution.py:343
  176.4 159.0 %back.1 = (bf16[2048,512]{1,0:T(8,128)(2,1)}, bf16[64,2304]{1,0:T(8,128)(2,1)}, bf16[64,2304]{1,0:T(8,128)(2,1)}, bf16[288,1024]{1,0:T(8,128)(2,1)}) custom-call(bf16[2048,512]{1,0:T(8,128)(2,1)} %bitcast.125, bf16[2,4096,128]{2,1,0:T(8,128)(2,1)} %get-tuple-element.52.logs_ref, bf16[2048,256]{1,0:T(8,128)(2,1)} %bitcast.134, bf16[2048,256]{1,0:T(8,128)(2,1)} %bitcast.135, ...), custom_call_target="tpu_custom_call" | custom-call | tf_op jit(solution)/shard_map/back/pallas_call | solution.py:1292
  340.8 25.1 %swap_blocks_3.1.got_ref = bf16[8,256,512]{2,1,0:T(8,128)(2,1)} custom-call(bf16[8,256,512]{2,1,0:T(8,128)(2,1)} %bitcast.138), custom_call_target="tpu_custom_call" | custom-call | tf_op jit(solution)/shard_map/swap_blocks_3/pallas_call | solution.py:343
  365.9 16.7 %project_back.1 = (bf16[512,1024]{1,0:T(8,128)(2,1)}, f32[1,1024]{1,0:T(1,128)}, f32[1,128]{1,0:T(1,128)}, f32[1,128]{1,0:T(1,128)}, bf16[1024,1024]{1,0:T(8,128...) custom-call(bf16[8,256,512]{2,1,0:T(8,128)(2,1)} %swap_blocks_3.1.got_ref, ...), custom_call_target="tpu_custom_call" | custom-call | tf_op jit(solution)/shard_map/project_back/pallas_call | solution.py:828
  390.1 39.4 %all-reduce = (f32[1024]{0:T(1024)}, f32[64]{0:T(128)}, f32[64]{0:T(128)}, f32[1024]{0:T(1024)}) all-reduce(f32[1024]{0:T(1024)S(1)} %bitcast.150, f32[64]{0:T(128)S(1)} %get-tuple-element.111, f32[64]{0:T(128)S(1)} %get-tuple-element.110, f32[1024]{0:T(1024)S(1)} %bitcast.149), channel_id=1, replica_groups=mesh['dp'=4,'blk'=8] {'dp','blk'}, use_global_device_ids=true, to_apply=%region_4.5 | all-reduce | flops 2176 | bytes 17408 | tf_op jit(solution)/shard_map/psum | solution.py:1511
  434.8 2.6 collective-permute-start.23
  440.8 8.8 %collective-permute-done.23 = bf16[4,2,32,1024]{3,2,1,0:T(8,128)(2,1)S(1)} collective-permute-done((bf16[4,2,32,1024]{3,2,1,0:T(8,128)(2,1)S(1)}, bf16[4,2,32,1024]{3,2,1,0:T(8,128)(2,1)S(1)}, u32[]{:S(2)}, u32[]{:S(2)}) %collective-permute-start.23) | collective-permute-done | bytes 524320 | tf_op jit(solution)/shard_map/ppermute | solution.py:1335
  453.7 7.1 %collective-permute-done.5 = bf16[4,2,32,1024]{3,2,1,0:T(8,128)(2,1)S(1)} collective-permute-done((bf16[4,2,32,1024]{3,2,1,0:T(8,128)(2,1)S(1)}, bf16[4,2,32,1024]{3,2,1,0:T(8,128)(2,1)S(1)}, u32[]{:S(2)}, u32[]{:S(2)}) %collective-permute-start.5) | collective-permute-done | bytes 524320 | tf_op jit(solution)/shard_map/ppermute | solution.py:1335
  463.0 3.2 collective-permute-start.25
  467.0 2.7 collective-permute-start.16
  476.4 2.8 collective-permute-start.17
  485.1 5.2 %collective-permute-start.18 = (bf16[32,1024]{1,0:T(8,128)(2,1)S(1)}, bf16[32,1024]{1,0:T(8,128)(2,1)S(1)}, u32[]{:S(2)}, u32[]{:S(2)}) collective-permute-start(bf16[32,1024]{1,0:T(8,128)(2,1)S(1)} %get-tuple-element.93), channel_id=1, source_target_pairs={{0,8},{8,16},{16,24},{1,9},{9,17},{17,25},{2,10},{10,18},{18,26},{... | collective-permute-start | bytes 196616 | tf_op jit(solution)/shard_map/ppermute | solution.py:1352
  491.1 5.2 %collective-permute-start.9 = (bf16[32,1024]{1,0:T(8,128)(2,1)S(1)}, bf16[32,1024]{1,0:T(8,128)(2,1)S(1)}, u32[]{:S(2)}, u32[]{:S(2)}) collective-permute-start(bf16[32,1024]{1,0:T(8,128)(2,1)S(1)} %get-tuple-element.97), channel_id=1, source_target_pairs={{0,8},{8,16},{16,24},{1,9},{9,17},{17,25},{2,10},{10,18},{18,26},{... | collective-permute-start | bytes 196616 | tf_op jit(solution)/shard_map/ppermute | solution.py:1352
  500.2 3.0 collective-permute-done.30
  (160 shorter events, 68.8 us)
Async XLA Ops:
  93.1 8.5 %collective-permute-start.1 = (bf16[512,1024]{1,0:T(8,128)(2,1)S(1)}, bf16[512,1024]{1,0:T(8,128)(2,1)}, u32[]{:S(2)}, u32[]{:S(2)}) collective-permute-start(bf16[512,1024]{1,0:T(8,128)(2,1)S(1)} %bitcast.132), channel_id=1, source_target_pairs={{0,1},{1,0},{2,3},{3,2},{4,5},{5,4},{6,7},{7,6},{8,9},{9,8},{10,11... | collective-permute-start | bytes 3145736 | tf_op jit(solution)/shard_map/ppermute | solution.py:1375
  337.2 95.4 %collective-permute-start.33 = (bf16[144,1024]{1,0:T(8,128)(2,1)}, bf16[144,1024]{1,0:T(8,128)(2,1)}, u32[]{:S(2)}, u32[]{:S(2)}) collective-permute-start(bf16[144,1024]{1,0:T(8,128)(2,1)} %constant_dynamic-slice_fusion), channel_id=1, source_target_pairs={{0,1},{1,0},{2,3},{3,2},{4,5},{5,4},{6,7},{7,6},{8,9},{9,8},{10,11... | collective-permute-start | bytes 884744 | tf_op jit(solution)/shard_map/ppermute | solution.py:1375
  338.7 90.7 %collective-permute-start.31 = (bf16[32,2304]{1,0:T(8,128)(2,1)}, bf16[32,2304]{1,0:T(8,128)(2,1)}, u32[]{:S(2)}, u32[]{:S(2)}) collective-permute-start(bf16[32,2304]{1,0:T(8,128)(2,1)} %constant_dynamic-slice_fusion.2), channel_id=1, source_target_pairs={{0,1},{1,0},{2,3},{3,2},{4,5},{5,4},{6,7},{7,6},{8,9},{9,8},{10,11... | collective-permute-start | bytes 442376 | tf_op jit(solution)/shard_map/ppermute | solution.py:1375
  340.8 88.8 %collective-permute-start.32 = (bf16[32,2304]{1,0:T(8,128)(2,1)}, bf16[32,2304]{1,0:T(8,128)(2,1)}, u32[]{:S(2)}, u32[]{:S(2)}) collective-permute-start(bf16[32,2304]{1,0:T(8,128)(2,1)} %constant_dynamic-slice_fusion.1), channel_id=1, source_target_pairs={{0,1},{1,0},{2,3},{3,2},{4,5},{5,4},{6,7},{7,6},{8,9},{9,8},{10,11... | collective-permute-start | bytes 442376 | tf_op jit(solution)/shard_map/ppermute | solution.py:1375
  386.6 46.8 %collective-permute-start.22 = (bf16[4,2,2,32,1024]{4,3,2,0,1:T(8,128)(2,1)}, bf16[4,2,2,32,1024]{4,3,2,0,1:T(8,128)(2,1)}, u32[]{:S(2)}, u32[]{:S(2)}) collective-permute-start(bf16[4,2,2,32,1024]{4,3,2,0,1:T(8,128)(2,1)} %bitcast.121), channel_id=1, source_target_pairs={{0,1},{1,0},{2,3},{3,2},{4,5},{5,4},{6,7},{7,6},{8,9},{9,8},{10,11... | collective-permute-start | bytes 3145736 | tf_op jit(solution)/shard_map/ppermute | solution.py:1335
  388.7 48.8 %collective-permute-start.13 = (bf16[4,2,2,32,1024]{4,3,1,0,2:T(8,128)(2,1)}, bf16[4,2,2,32,1024]{4,3,1,0,2:T(8,128)(2,1)}, u32[]{:S(2)}, u32[]{:S(2)}) collective-permute-start(bf16[4,2,2,32,1024]{4,3,1,0,2:T(8,128)(2,1)} %bitcast.122), channel_id=1, source_target_pairs={{0,1},{1,0},{2,3},{3,2},{4,5},{5,4},{6,7},{7,6},{8,9},{9,8},{10,11... | collective-permute-start | bytes 3145736 | tf_op jit(solution)/shard_map/ppermute | solution.py:1335
  429.5 10.7 %collective-permute-start.4 = (bf16[4,2,2,32,1024]{4,3,2,0,1:T(8,128)(2,1)}, bf16[4,2,2,32,1024]{4,3,2,0,1:T(8,128)(2,1)S(1)}, u32[]{:S(2)}, u32[]{:S(2)}) collective-permute-start(bf16[4,2,2,32,1024]{4,3,2,0,1:T(8,128)(2,1)} %bitcast.140), channel_id=1, source_target_pairs={{0,1},{1,0},{2,3},{3,2},{4,5},{5,4},{6,7},{7,6},{8,9},{9,8},{10,11... | collective-permute-start | bytes 3145736 | tf_op jit(solution)/shard_map/ppermute | solution.py:1335
  434.8 14.8 %collective-permute-start.23 = (bf16[4,2,32,1024]{3,2,1,0:T(8,128)(2,1)S(1)}, bf16[4,2,32,1024]{3,2,1,0:T(8,128)(2,1)S(1)}, u32[]{:S(2)}, u32[]{:S(2)}) collective-permute-start(bf16[4,2,32,1024]{3,2,1,0:T(8,128)(2,1)S(1)} %dynamic-slice_bitcast_fusion), channel_id=1, source_target_pairs={{0,4},{1,5},{2,6},{3,7},{4,0},{5,1},{6,2},{7,3},{8,12},{9,13},{10,... | collective-permute-start | bytes 1572872 | tf_op jit(solution)/shard_map/ppermute | solution.py:1335
  438.8 14.7 %collective-permute-start.14 = (bf16[4,2,32,1024]{3,2,1,0:T(8,128)(2,1)S(1)}, bf16[4,2,32,1024]{3,2,1,0:T(8,128)(2,1)S(1)}, u32[]{:S(2)}, u32[]{:S(2)}) collective-permute-start(bf16[4,2,32,1024]{3,2,1,0:T(8,128)(2,1)S(1)} %dynamic-slice_bitcast_fusion.1), channel_id=1, source_target_pairs={{0,2},{1,3},{2,0},{3,1},{4,6},{5,7},{6,4},{7,5},{8,10},{9,11},{10,... | collective-permute-start | bytes 1572872 | tf_op jit(solution)/shard_map/ppermute | solution.py:1335
  440.3 20.5 %collective-permute-start.5 = (bf16[4,2,32,1024]{3,2,1,0:T(8,128)(2,1)S(1)}, bf16[4,2,32,1024]{3,2,1,0:T(8,128)(2,1)S(1)}, u32[]{:S(2)}, u32[]{:S(2)}) collective-permute-start(bf16[4,2,32,1024]{3,2,1,0:T(8,128)(2,1)S(1)} %dynamic-slice_bitcast_fusion.2), channel_id=1, source_target_pairs={{0,4},{1,5},{2,6},{3,7},{4,0},{5,1},{6,2},{7,3},{8,12},{9,13},{10,... | collective-permute-start | bytes 1572872 | tf_op jit(solution)/shard_map/ppermute | solution.py:1335
  449.7 13.3 %collective-permute-start.24 = (bf16[4,32,1024]{2,1,0:T(8,128)(2,1)S(1)}, bf16[4,32,1024]{2,1,0:T(8,128)(2,1)S(1)}, u32[]{:S(2)}, u32[]{:S(2)}) collective-permute-start(bf16[4,32,1024]{2,1,0:T(8,128)(2,1)S(1)} %dynamic-slice_bitcast_fusion.3), channel_id=1, source_target_pairs={{0,2},{1,3},{2,0},{3,1},{4,6},{5,7},{6,4},{7,5},{8,10},{9,11},{10,... | collective-permute-start | bytes 786440 | tf_op jit(solution)/shard_map/ppermute | solution.py:1335
  453.7 13.2 %collective-permute-start.15 = (bf16[4,32,1024]{2,1,0:T(8,128)(2,1)S(1)}, bf16[4,32,1024]{2,1,0:T(8,128)(2,1)S(1)}, u32[]{:S(2)}, u32[]{:S(2)}) collective-permute-start(bf16[4,32,1024]{2,1,0:T(8,128)(2,1)S(1)} %dynamic-slice_bitcast_fusion.4), channel_id=1, source_target_pairs={{0,4},{1,5},{2,6},{3,7},{4,0},{5,1},{6,2},{7,3},{8,12},{9,13},{10,... | collective-permute-start | bytes 786440 | tf_op jit(solution)/shard_map/ppermute | solution.py:1335
  460.9 9.4 %collective-permute-start.6 = (bf16[4,32,1024]{2,1,0:T(8,128)(2,1)S(1)}, bf16[4,32,1024]{2,1,0:T(8,128)(2,1)S(1)}, u32[]{:S(2)}, u32[]{:S(2)}) collective-permute-start(bf16[4,32,1024]{2,1,0:T(8,128)(2,1)S(1)} %dynamic-slice_bitcast_fusion.5), channel_id=1, source_target_pairs={{0,2},{1,3},{2,0},{3,1},{4,6},{5,7},{6,4},{7,5},{8,10},{9,11},{10,... | collective-permute-start | bytes 786440 | tf_op jit(solution)/shard_map/ppermute | solution.py:1335
  463.0 10.0 %collective-permute-start.25 = (bf16[32,1024]{1,0:T(8,128)(2,1)S(1)}, bf16[32,1024]{1,0:T(8,128)(2,1)S(1)}, u32[]{:S(2)}, u32[]{:S(2)}) collective-permute-start(bf16[32,1024]{1,0:T(8,128)(2,1)S(1)} %get-tuple-element.91), channel_id=1, source_target_pairs={{0,8},{1,9},{2,10},{3,11},{4,12},{5,13},{6,14},{7,15}} | collective-permute-start | bytes 196616 | tf_op jit(solution)/shard_map/ppermute | solution.py:1352
  466.2 13.0 %collective-permute-start.28 = (bf16[32,1024]{1,0:T(8,128)(2,1)S(1)}, bf16[32,1024]{1,0:T(8,128)(2,1)S(1)}, u32[]{:S(2)}, u32[]{:S(2)}) collective-permute-start(bf16[32,1024]{1,0:T(8,128)(2,1)S(1)} %get-tuple-element.92), channel_id=1, source_target_pairs={{24,16},{25,17},{26,18},{27,19},{28,20},{29,21},{30,22},{31,23}} | collective-permute-start | bytes 196616 | tf_op jit(solution)/shard_map/ppermute | solution.py:1352
  469.7 12.2 %collective-permute-start.19 = (bf16[32,1024]{1,0:T(8,128)(2,1)S(1)}, bf16[32,1024]{1,0:T(8,128)(2,1)S(1)}, u32[]{:S(2)}, u32[]{:S(2)}) collective-permute-start(bf16[32,1024]{1,0:T(8,128)(2,1)S(1)} %get-tuple-element.96), channel_id=1, source_target_pairs={{24,16},{25,17},{26,18},{27,19},{28,20},{29,21},{30,22},{31,23}} | collective-permute-start | bytes 196616 | tf_op jit(solution)/shard_map/ppermute | solution.py:1352
  473.0 12.1 %collective-permute-start.10 = (bf16[32,1024]{1,0:T(8,128)(2,1)S(1)}, bf16[32,1024]{1,0:T(8,128)(2,1)S(1)}, u32[]{:S(2)}, u32[]{:S(2)}) collective-permute-start(bf16[32,1024]{1,0:T(8,128)(2,1)S(1)} %get-tuple-element.100), channel_id=1, source_target_pairs={{24,16},{25,17},{26,18},{27,19},{28,20},{29,21},{30,22},{31,23}} | collective-permute-start | bytes 196616 | tf_op jit(solution)/shard_map/ppermute | solution.py:1352
  479.2 11.1 %collective-permute-start.8 = (bf16[32,1024]{1,0:T(8,128)(2,1)S(1)}, bf16[32,1024]{1,0:T(8,128)(2,1)S(1)}, u32[]{:S(2)}, u32[]{:S(2)}) collective-permute-start(bf16[32,1024]{1,0:T(8,128)(2,1)S(1)} %bitcast_add_fusion.21), channel_id=1, source_target_pairs={{0,8},{8,16},{1,9},{9,17},{2,10},{10,18},{3,11},{11,19},{4,12},{12... | collective-permute-start | bytes 196616 | tf_op jit(solution)/shard_map/ppermute | solution.py:1352
  481.2 9.9 %collective-permute-start.29 = (bf16[32,1024]{1,0:T(8,128)(2,1)S(1)}, bf16[32,1024]{1,0:T(8,128)(2,1)S(1)}, u32[]{:S(2)}, u32[]{:S(2)}) collective-permute-start(bf16[32,1024]{1,0:T(8,128)(2,1)S(1)} %get-tuple-element.90), channel_id=1, source_target_pairs={{24,16},{16,8},{25,17},{17,9},{26,18},{18,10},{27,19},{19,11},{28,... | collective-permute-start | bytes 196616 | tf_op jit(solution)/shard_map/ppermute | solution.py:1352
  481.9 17.1 %collective-permute-start.27 = (bf16[32,1024]{1,0:T(8,128)(2,1)S(1)}, bf16[32,1024]{1,0:T(8,128)(2,1)S(1)}, u32[]{:S(2)}, u32[]{:S(2)}) collective-permute-start(bf16[32,1024]{1,0:T(8,128)(2,1)S(1)} %get-tuple-element.89), channel_id=1, source_target_pairs={{0,8},{8,16},{16,24},{1,9},{9,17},{17,25},{2,10},{10,18},{18,26},{... | collective-permute-start | bytes 196616 | tf_op jit(solution)/shard_map/ppermute | solution.py:1352
  484.5 11.8 %collective-permute-start.20 = (bf16[32,1024]{1,0:T(8,128)(2,1)S(1)}, bf16[32,1024]{1,0:T(8,128)(2,1)S(1)}, u32[]{:S(2)}, u32[]{:S(2)}) collective-permute-start(bf16[32,1024]{1,0:T(8,128)(2,1)S(1)} %get-tuple-element.94), channel_id=1, source_target_pairs={{24,16},{16,8},{25,17},{17,9},{26,18},{18,10},{27,19},{19,11},{28,... | collective-permute-start | bytes 196616 | tf_op jit(solution)/shard_map/ppermute | solution.py:1352
  485.1 18.7 %collective-permute-start.18 = (bf16[32,1024]{1,0:T(8,128)(2,1)S(1)}, bf16[32,1024]{1,0:T(8,128)(2,1)S(1)}, u32[]{:S(2)}, u32[]{:S(2)}) collective-permute-start(bf16[32,1024]{1,0:T(8,128)(2,1)S(1)} %get-tuple-element.93), channel_id=1, source_target_pairs={{0,8},{8,16},{16,24},{1,9},{9,17},{17,25},{2,10},{10,18},{18,26},{... | collective-permute-start | bytes 196616 | tf_op jit(solution)/shard_map/ppermute | solution.py:1352
  491.1 14.7 %collective-permute-start.9 = (bf16[32,1024]{1,0:T(8,128)(2,1)S(1)}, bf16[32,1024]{1,0:T(8,128)(2,1)S(1)}, u32[]{:S(2)}, u32[]{:S(2)}) collective-permute-start(bf16[32,1024]{1,0:T(8,128)(2,1)S(1)} %get-tuple-element.97), channel_id=1, source_target_pairs={{0,8},{8,16},{16,24},{1,9},{9,17},{17,25},{2,10},{10,18},{18,26},{... | collective-permute-start | bytes 196616 | tf_op jit(solution)/shard_map/ppermute | solution.py:1352
  498.9 8.0 %collective-permute-start.12 = (bf16[32,1024]{1,0:T(8,128)(2,1)S(1)}, bf16[32,1024]{1,0:T(8,128)(2,1)S(1)}, u32[]{:S(2)}, u32[]{:S(2)}) collective-permute-start(bf16[32,1024]{1,0:T(8,128)(2,1)S(1)} %bitcast_add_fusion.20), channel_id=1, source_target_pairs={{24,16},{16,8},{8,0},{25,17},{17,9},{9,1},{26,18},{18,10},{10,2},{... | collective-permute-start | bytes 196616 | tf_op jit(solution)/shard_map/ppermute | solution.py:1352
  (25 other events, 131.4 us)

commit v3 on v2

--- a/solution.py
+++ b/solution.py
@@ -744,127 +744,6 @@
         scratch_shapes=[pltpu.VMEM((rows, width), BF16)],
         compiler_params=kernel_params(),
     )(middle, out_own, out_got, back_own, back_got, grad, gain, heads, w_out)
-
-
-def project_back_kernel(
-    got_ref,
-    proj_ref,
-    hidden_ref,
-    tokens_ref,
-    mid_ref,
-    gain_ref,
-    wq_ref,
-    wk_ref,
-    wv_ref,
-    q_gain_ref,
-    k_gain_ref,
-    cos_ref,
-    sin_ref,
-    input_ref,
-    gain_grad_ref,
-    q_gain_grad_ref,
-    k_gain_grad_ref,
-    gq_ref,
-    gk_ref,
-    gv_ref,
-    total,
-):
-    step = pl.program_id(0)
-
-    @pl.when(step == 0)
-    def _():
-        total[...] = jnp.zeros_like(total)
-        q_gain_grad_ref[...] = jnp.zeros_like(q_gain_grad_ref)
-        k_gain_grad_ref[...] = jnp.zeros_like(k_gain_grad_ref)
-
-    q_width = wq_ref.shape[1]
-    hidden = hidden_ref[...]
-
-    def back(lane, head_gain, gain_out):
-        got = jnp.concatenate(
-            [got_ref[0, :, lane : lane + LANES], got_ref[1, :, lane : lane + LANES]], axis=0
-        ).astype(F32)
-        turned = got * cos_ref[...] - half_partner(got) * sin_ref[...]
-        block = proj_ref[0, :, lane : lane + LANES]
-        scale = lax.rsqrt(head_means(block * block) + EPSILON)
-        normal = block * scale
-        gain_out[...] += jnp.sum(turned * normal, axis=0, keepdims=True)
-        pushed = turned * head_gain[...]
-        inner = head_means(pushed * normal)
-        return (scale * (pushed - normal * inner)).astype(BF16)
-
-    query = jnp.concatenate(
-        [back(at, q_gain_ref, q_gain_grad_ref) for at in range(0, q_width, LANES)], axis=1
-    )
-    key = back(q_width, k_gain_ref, k_gain_grad_ref)
-    lane = q_width + LANES
-    value = jnp.concatenate(
-        [got_ref[0, :, lane : lane + LANES], got_ref[1, :, lane : lane + LANES]], axis=0
-    )
-    gq_ref[...] = tn_dot(hidden, query).astype(BF16)
-    gk_ref[...] = tn_dot(hidden, key).astype(BF16)
-    gv_ref[...] = tn_dot(hidden, value).astype(BF16)
-    total[...] += (
-        nt_dot(query, wq_ref[...]) + nt_dot(key, wk_ref[...]) + nt_dot(value, wv_ref[...])
-    )
-
-    @pl.when(step == pl.num_programs(0) - 1)
-    def _():
-        inputs = tokens_ref[...].astype(F32)
-        scale = lax.rsqrt(jnp.mean(inputs * inputs, axis=-1, keepdims=True) + EPSILON)
-        normal = inputs * scale
-        grad = total[...]
-        gain_grad_ref[...] = jnp.sum(grad * normal, axis=0, keepdims=True)
-        pushed = grad * gain_ref[...]
-        inner = jnp.mean(pushed * normal, axis=-1, keepdims=True)
-        input_ref[...] = (mid_ref[...] + scale * (pushed - normal * inner)).astype(BF16)
-
-
-def project_back(got, proj, hidden, tokens, mid, gain, wq, wk, wv, q_gain, k_gain, cosine, sine):
-    rows, width = tokens.shape
-    count, half, lanes = got.shape
-    chips = count // 2
-    q_width = wq.shape[1] // chips
-    return pl.pallas_call(
-        project_back_kernel,
-        name="project_back",
-        grid=(chips,),
-        in_specs=[
-            pl.BlockSpec((2, half, lanes), lambda p: (p, 0, 0)),
-            pl.BlockSpec((1, rows, q_width + LANES), lambda p: (p, 0, 0)),
-            whole_block((rows, width)),
-            whole_block((rows, width)),
-            whole_block((rows, width)),
-            whole_block((1, width)),
-            pl.BlockSpec((width, q_width), lambda p: (0, p)),
-            pl.BlockSpec((width, LANES), lambda p: (0, p)),
-            pl.BlockSpec((width, LANES), lambda p: (0, p)),
-            whole_block((1, LANES)),
-            whole_block((1, LANES)),
-            whole_block((rows, LANES)),
-            whole_block((rows, LANES)),
-        ],
-        out_specs=[
-            whole_block((rows, width)),
-            whole_block((1, width)),
-            whole_block((1, LANES)),
-            whole_block((1, LANES)),
-            pl.BlockSpec((width, q_width), lambda p: (0, p)),
-            pl.BlockSpec((width, LANES), lambda p: (0, p)),
-            pl.BlockSpec((width, LANES), lambda p: (0, p)),
-        ],
-        out_shape=[
-            jax.ShapeDtypeStruct((rows, width), BF16),
-            jax.ShapeDtypeStruct((1, width), F32),
-            jax.ShapeDtypeStruct((1, LANES), F32),
-            jax.ShapeDtypeStruct((1, LANES), F32),
-            jax.ShapeDtypeStruct(wq.shape, BF16),
-            jax.ShapeDtypeStruct(wk.shape, BF16),
-            jax.ShapeDtypeStruct(wv.shape, BF16),
-        ],
-        scratch_shapes=[pltpu.VMEM((rows, width), F32)],
-        compiler_params=kernel_params(),
-    )(got, proj, hidden, tokens, mid, gain, wq, wk, wv, q_gain, k_gain, cosine, sine)
 
 
 def pair_of(bit):
@@ -1324,51 +1203,358 @@
     )(qkv, logs, out, grad, starts, flipped, dy, gate_grad, up_grad, acts)
 
 
+def sum_gains(rounds, n, first, gains, gains_got, sent_sem, got_sem):
+    for r, partner in enumerate(rounds):
+
+        def copy():
+            return pltpu.make_async_remote_copy(
+                src_ref=gains.at[r],
+                dst_ref=gains_got.at[r],
+                send_sem=sent_sem.at[r],
+                recv_sem=got_sem.at[r],
+                device_id=partner,
+                device_id_type=pl.DeviceIdType.MESH,
+            )
+
+        @pl.when(n == first + r + 1)
+        def _():
+            copy().wait()
+            gains[r + 1] = gains[r] + gains_got[r]
+
+    for r, partner in enumerate(rounds):
+
+        @pl.when(n == first + r)
+        def _():
+            pltpu.make_async_remote_copy(
+                src_ref=gains.at[r],
+                dst_ref=gains_got.at[r],
+                send_sem=sent_sem.at[r],
+                recv_sem=got_sem.at[r],
+                device_id=partner,
+                device_id_type=pl.DeviceIdType.MESH,
+            ).start()
+
+
+def finish_kernel(
+    line,
+    bits,
+    streams,
+    units,
+    got_ref,
+    proj_ref,
+    hidden_ref,
+    tokens_ref,
+    mid_ref,
+    gain_ref,
+    wq_ref,
+    wk_ref,
+    wv_ref,
+    q_gain_ref,
+    k_gain_ref,
+    cos_ref,
+    sin_ref,
+    w_out_parts_ref,
+    ffn_gain_ref,
+    gate_ref,
+    up_ref,
+    down_ref,
+    input_ref,
+    gains_ref,
+    gq_ref,
+    gk_ref,
+    gv_ref,
+    go_ref,
+    gate_out_ref,
+    up_out_ref,
+    down_out_ref,
+    total,
+    gains,
+    gains_got,
+    gains_sent_sem,
+    gains_got_sem,
+    half_got,
+    down_got,
+    half_sent_sem,
+    half_got_sem,
+    ready,
+    *refs,
+):
+    n = pl.program_id(0)
+    z, index = lax.axis_index("dp"), lax.axis_index("blk")
+    core, sibling = pair_of(1)
+    steps = pl.num_programs(0)
+    qkv_stream, out_stream = streams
+    q_width = wq_ref.shape[1]
+
+    def finish_qkv(u, value):
+        gq_ref[:, pl.ds(pl.multiple_of(u * q_width, q_width), q_width)] = value[:, :q_width]
+        here = pl.ds(pl.multiple_of(u * LANES, LANES), LANES)
+        gk_ref[:, here] = value[:, q_width : q_width + LANES]
+        gv_ref[:, here] = value[:, q_width + LANES :]
+
+    def finish_out(u, value):
+        go_ref[:, pl.ds(pl.multiple_of(u * q_width, q_width), q_width)] = value
+
+    at = 0
+    for stream, finish in ((qkv_stream, finish_qkv), (out_stream, finish_out)):
+        count = len(stream.scratch())
+        stream.bind(refs[at : at + count], units, finish)
+        at += count
+
+    rounds = [pair_of(bit)[1] for bit in (1,) + tuple(bits)]
+    reach = 1
+    while reach < line:
+        rounds.append((z + reach * (1 - 2 * lax.rem(z // reach, 2)), index))
+        reach *= 2
+
+    rows = gate_ref.shape[0] // 2
+    columns = gate_ref.shape[1]
+    down_rows = down_ref.shape[0] // 2
+    give = pl.ds(pl.multiple_of((1 - core) * rows, rows), rows)
+    keep = pl.ds(pl.multiple_of(core * rows, rows), rows)
+    down_give = pl.ds(pl.multiple_of((1 - core) * down_rows, down_rows), down_rows)
+    down_keep = pl.ds(pl.multiple_of(core * down_rows, down_rows), down_rows)
+
+    def half_copies():
+        sources = (gate_ref.at[give, :], up_ref.at[give, :], down_ref.at[down_give, :])
+        targets = (half_got.at[0], half_got.at[1], down_got)
+        return [
+            pltpu.make_async_remote_copy(
+                src_ref=source,
+                dst_ref=target,
+                send_sem=half_sent_sem.at[i],
+                recv_sem=half_got_sem.at[i],
+                device_id=sibling,
+                device_id_type=pl.DeviceIdType.MESH,
+            )
+            for i, (source, target) in enumerate(zip(sources, targets))
+        ]
+
+    @pl.when(n == 0)
+    def _():
+        barrier = pltpu.get_barrier_semaphore()
+        for peer in rounds:
+            pl.semaphore_signal(barrier, inc=1, device_id=peer, device_id_type=pl.DeviceIdType.MESH)
+        for way in (1, -1):
+
+            @pl.when((z + way >= 0) & (z + way < line))
+            def _():
+                pl.semaphore_signal(
+                    barrier, inc=1, device_id=(z + way, index), device_id_type=pl.DeviceIdType.MESH
+                )
+
+        beside = jnp.minimum(z, 1) + jnp.minimum(line - 1 - z, 1)
+        pl.semaphore_wait(barrier, len(rounds) + beside)
+        for copy in half_copies():
+            copy.start()
+        total[...] = jnp.zeros_like(total)
+        gains[0] = jnp.zeros_like(gains[0])
+
+    @pl.when(n == units)
+    def _():
+        for copy in half_copies():
+            copy.wait()
+        own = pl.ds(pl.multiple_of(core * columns, LANES), columns)
+        other = pl.ds(pl.multiple_of((1 - core) * columns, LANES), columns)
+        gate_out_ref[:, own] = gate_ref[keep, :]
+        gate_out_ref[:, other] = half_got[0]
+        up_out_ref[:, own] = up_ref[keep, :]
+        up_out_ref[:, other] = half_got[1]
+        holder = z // (line // 2)
+
+        @pl.when(holder == core)
+        def _():
+            down_out_ref[...] = down_ref[down_keep, :]
+
+        @pl.when(holder != core)
+        def _():
+            down_out_ref[...] = down_got[...]
+
+    step_streams(streams, n, steps, line, ready)
+    sum_gains(rounds, n, units, gains, gains_got, gains_sent_sem, gains_got_sem)
+
+    @pl.when(n == steps - 1)
+    def _():
+        gains_ref[...] = gains[len(rounds)]
+
+    @pl.when(n < units)
+    def _():
+        hidden = hidden_ref[...]
+
+        def back(lane, head_gain, place):
+            got = jnp.concatenate(
+                [got_ref[0, :, lane : lane + LANES], got_ref[1, :, lane : lane + LANES]], axis=0
+            ).astype(F32)
+            turned = got * cos_ref[...] - half_partner(got) * sin_ref[...]
+            block = proj_ref[0, :, lane : lane + LANES]
+            scale = lax.rsqrt(head_means(block * block) + EPSILON)
+            normal = block * scale
+            gains[0, place : place + 1, :] += jnp.sum(turned * normal, axis=0, keepdims=True)
+            pushed = turned * head_gain[...]
+            inner = head_means(pushed * normal)
+            return (scale * (pushed - normal * inner)).astype(BF16)
+
+        width = tokens_ref.shape[1]
+        lines = width // LANES
+        query = jnp.concatenate(
+            [back(at, q_gain_ref, 2 * lines) for at in range(0, q_width, LANES)], axis=1
+        )
+        key = back(q_width, k_gain_ref, 2 * lines + 1)
+        lane = q_width + LANES
+        value = jnp.concatenate(
+            [got_ref[0, :, lane : lane + LANES], got_ref[1, :, lane : lane + LANES]], axis=0
+        )
+        slot = lax.rem(n, 2)
+        shape = qkv_stream.shape(qkv_stream.dims[0])
+        whole = (slot,) + (slice(None),) * (len(shape) - 1)
+        both = jnp.concatenate([query, key, value], axis=1)
+        made = tn_dot(hidden, both).astype(BF16)
+        qkv_stream.source[whole] = made.reshape(shape)
+        out_stream.source[slot] = w_out_parts_ref[...].reshape(out_stream.shape(out_stream.dims[0]))
+        total[...] += (
+            nt_dot(query, wq_ref[...]) + nt_dot(key, wk_ref[...]) + nt_dot(value, wv_ref[...])
+        )
+
+        @pl.when(n == units - 1)
+        def _():
+            inputs = tokens_ref[...].astype(F32)
+            scale = lax.rsqrt(jnp.mean(inputs * inputs, axis=-1, keepdims=True) + EPSILON)
+            normal = inputs * scale
+            grad = total[...]
+            gain_grad = jnp.sum(grad * normal, axis=0, keepdims=True)
+            for i in range(lines):
+                here = slice(i * LANES, (i + 1) * LANES)
+                gains[0, i : i + 1, :] = gain_grad[:, here]
+                gains[0, lines + i : lines + i + 1, :] = ffn_gain_ref[:, here]
+            pushed = grad * gain_ref[...]
+            inner = jnp.mean(pushed * normal, axis=-1, keepdims=True)
+            input_ref[...] = (mid_ref[...] + scale * (pushed - normal * inner)).astype(BF16)
+
+
+def finish(
+    line,
+    bits,
+    got,
+    proj,
+    hidden,
+    tokens,
+    mid,
+    gain,
+    wq,
+    wk,
+    wv,
+    q_gain,
+    k_gain,
+    cosine,
+    sine,
+    w_out_parts,
+    ffn_gain,
+    gate_sum,
+    up_sum,
+    down_sum,
+):
+    rows, width = tokens.shape
+    count, half, lanes = got.shape
+    units = count // 2
+    q_width = wq.shape[1] // units
+    chips = line * 2 ** len(bits)
+    sides = [(bit, 2) for bit in bits]
+    dims = [("z", line)] + sides + [(1, 2)]
+    mine = width // chips // 2
+    streams = [
+        Stream([1] + bits[::-1] + hops(line), dims, (mine, lanes), line),
+        Stream([1] + bits + hops(line), dims, (mine, q_width), line),
+    ]
+    rounds = 1 + len(bits) + (line - 1).bit_length()
+    steps = units + max(len(stream.path) for stream in streams) + 1
+    gain_rows = -(-(2 * width // LANES + 2) // 8) * 8
+    half_rows = gate_sum.shape[0] // 2
+    down_rows = down_sum.shape[0] // 2
+    columns = gate_sum.shape[1]
+
+    def keep(shape):
+        return pl.BlockSpec(shape, lambda n: (0,) * len(shape), pipeline_mode=pl.Buffered(1))
+
+    def at(n):
+        return jnp.minimum(n, units - 1)
+
+    scratch = [
+        pltpu.VMEM((rows, width), F32),
+        pltpu.VMEM((rounds + 1, gain_rows, LANES), F32),
+        pltpu.VMEM((rounds, gain_rows, LANES), F32),
+        pltpu.SemaphoreType.DMA((rounds,)),
+        pltpu.SemaphoreType.DMA((rounds,)),
+        pltpu.VMEM((2, half_rows, columns), BF16),
+        pltpu.VMEM((down_rows, down_sum.shape[1]), BF16),
+        pltpu.SemaphoreType.DMA((3,)),
+        pltpu.SemaphoreType.DMA((3,)),
+        pltpu.SemaphoreType.REGULAR((2,)),
+    ]
+    for stream in streams:
+        scratch += stream.scratch()
+    outs = [
+        ((rows, width), BF16),
+        ((gain_rows, LANES), F32),
+        ((mine, wq.shape[1]), BF16),
+        ((mine, wk.shape[1]), BF16),
+        ((mine, wv.shape[1]), BF16),
+        ((mine, width), BF16),
+        ((half_rows, 2 * columns), BF16),
+        ((half_rows, 2 * columns), BF16),
+        ((down_rows, down_sum.shape[1]), BF16),
+    ]
+    return pl.pallas_call(
+        functools.partial(finish_kernel, line, bits, streams, units),
+        name="finish",
+        grid=(steps,),
+        in_specs=[
+            pl.BlockSpec((2, half, lanes), lambda n: (at(n), 0, 0)),
+            pl.BlockSpec((1, rows, q_width + LANES), lambda n: (at(n), 0, 0)),
+            keep((rows, width)),
+            keep((rows, width)),
+            keep((rows, width)),
+            keep((1, width)),
+            pl.BlockSpec((width, q_width), lambda n: (0, at(n))),
+            pl.BlockSpec((width, LANES), lambda n: (0, at(n))),
+            pl.BlockSpec((width, LANES), lambda n: (0, at(n))),
+            keep((1, LANES)),
+            keep((1, LANES)),
+            keep((rows, LANES)),
+            keep((rows, LANES)),
+            pl.BlockSpec((width, q_width), lambda n: (0, at(n))),
+            keep((1, width)),
+            keep(gate_sum.shape),
+            keep(up_sum.shape),
+            keep(down_sum.shape),
+        ],
+        out_specs=[keep(shape) for shape, unused in outs],
+        out_shape=[jax.ShapeDtypeStruct(shape, kind) for shape, kind in outs],
+        scratch_shapes=scratch,
+        compiler_params=kernel_params(collective_id=5, has_side_effects=True),
+    )(
+        got,
+        proj,
+        hidden,
+        tokens,
+        mid,
+        gain,
+        wq,
+        wk,
+        wv,
+        q_gain,
+        k_gain,
+        cosine,
+        sine,
+        w_out_parts,
+        ffn_gain,
+        gate_sum,
+        up_sum,
+        down_sum,
+    )
+
+
 def flip_pairs(count, bit):
     return [(i, i ^ bit) for i in range(count)]
-
-
-def sum_pair(parts, axis, count, bit, dim):
-    mine = (lax.axis_index(axis) // bit) % 2
-    send = lax.dynamic_index_in_dim(parts, 1 - mine, dim, keepdims=False)
-    own = lax.dynamic_index_in_dim(parts, mine, dim, keepdims=False)
-    return own + lax.ppermute(send, axis, flip_pairs(count, bit))
-
-
-def sum_line(parts, axis, count):
-    mine = lax.axis_index(axis)
-    total = lax.dynamic_index_in_dim(parts, mine, 0, keepdims=False)
-    for way in (1, -1):
-        got = None
-        for step in range(1, count):
-            target = jnp.clip(mine + way * (count - step), 0, count - 1)
-            send = lax.dynamic_index_in_dim(parts, target, 0, keepdims=False)
-            if got is not None:
-                send = send + got
-            if way == 1:
-                pairs = [(i, i + 1) for i in range(step)]
-            else:
-                pairs = [(count - 1 - i, count - 2 - i) for i in range(step)]
-            got = lax.ppermute(send, axis, pairs)
-        total = total + got
-    return total
-
-
-def sum_chips(parts, order, dp_count, blk_count):
-    bits = []
-    bit = blk_count // 2
-    while bit > 1:
-        bits.append(bit)
-        bit //= 2
-    left = ["z"] + bits
-    for stage in order:
-        dim = left.index(stage)
-        left.pop(dim)
-        if stage == "z":
-            parts = sum_line(jnp.moveaxis(parts, dim, 0) if dim else parts, "dp", dp_count)
-        else:
-            parts = sum_pair(parts, "blk", blk_count, stage, dim)
-    return parts
 
 
 def swap_core(block, blk_count):
@@ -1459,10 +1645,10 @@
         up_grad,
         acts,
     )
-    forward_order = bits + ["z"]
-    other_order = bits[::-1] + ["z"]
     got = swap_blocks(qkv_grad.reshape(blk_count, tok_count, -1), 3)
-    input_grad, attn_gain_grad, query_gain_grad, key_gain_grad, gq, gk, gv = project_back(
+    input_grad, gains, *sums = finish(
+        dp_count,
+        bits,
         got,
         proj,
         hidden_in,
@@ -1476,42 +1662,20 @@
         k_gain2,
         cosine,
         sine,
-    )
-
-    def sum_all(parts, order):
-        parts = parts.reshape(chip_dims + (2, -1, parts.shape[-1]))
-        parts = sum_pair(parts, "blk", blk_count, 1, len(chip_dims))
-        return sum_chips(parts, order, dp_count, blk_count).astype(F32)
-
-    grad_w_out = sum_all(w_out_parts, forward_order)
-    grad_w_query = sum_all(gq, forward_order)
-    both = sum_all(jnp.concatenate([gk, gv], axis=1), other_order)
-    grad_w_key, grad_w_value = jnp.split(both, 2, axis=1)
-
-    def join(block, dim):
-        count = block.shape[0] // 2
-        own = lax.dynamic_slice_in_dim(block, core * count, count, axis=0)
-        got = swap_core(
-            lax.dynamic_slice_in_dim(block, (1 - core) * count, count, axis=0), blk_count
-        )
-        low = jnp.where(core == 0, own, got)
-        high = jnp.where(core == 0, got, own)
-        return jnp.concatenate([low, high], axis=1).astype(F32)
-
-    grad_w_gate = join(gate_sum, 1)
-    grad_w_up = join(up_sum, 1)
-    down_rows = down_sum.shape[0] // 2
-    down_own = lax.dynamic_slice_in_dim(down_sum, core * down_rows, down_rows, axis=0)
-    down_got = swap_core(
-        lax.dynamic_slice_in_dim(down_sum, (1 - core) * down_rows, down_rows, axis=0), blk_count
-    )
-    holder = lax.axis_index("dp") // (dp_count // 2)
-    grad_w_down = jnp.where(holder == core, down_own, down_got).astype(F32)
-    fold = lambda both: both[0, :HEAD_DIM] + both[0, HEAD_DIM:]
-    gain_attn, gain_query, gain_key, gain_ffn = lax.psum(
-        (attn_gain_grad[0], fold(query_gain_grad), fold(key_gain_grad), ffn_gain_grad[0]),
-        ("dp", "blk"),
-    )
+        w_out_parts,
+        ffn_gain_grad,
+        gate_sum,
+        up_sum,
+        down_sum,
+    )
+    grad_w_query, grad_w_key, grad_w_value, grad_w_out, grad_w_gate, grad_w_up, grad_w_down = [
+        part.astype(F32) for part in sums
+    ]
+    lines = width // LANES
+    gain_attn = gains[:lines].reshape(width)
+    gain_ffn = gains[lines : 2 * lines].reshape(width)
+    gain_query = gains[2 * lines, :HEAD_DIM] + gains[2 * lines, HEAD_DIM:]
+    gain_key = gains[2 * lines + 1, :HEAD_DIM] + gains[2 * lines + 1, HEAD_DIM:]
     return (
         output.reshape(tokens.shape),
         input_grad.reshape(tokens.shape),

time: 509 us -> 437 us (0.86)
  Pallas kernels: 349 us -> 397 us
  starting transfers between devices: 48.3 us -> 1.61 us
  blocking collectives: 39.4 us -> 0 us
  waiting for transfers between devices: 29.2 us -> 6.02 us
  local copies, waits for them, and re-layouts: 20 us -> 12.1 us
    pallas_call x1, Pallas kernels: 16.7 us -> 64.5 us  [finish(): pl.pallas_call(functools.partial(finish_kernel, line, bits, streams, unit...]
    ppermute x27 -> x0, starting transfers between devices: 46.2 us -> none  [the longest x18 36.6 us: sum_line(): got = lax.ppermute(send, axis, pairs)]
    psum x1 -> x0, blocking collectives: 39.4 us -> none  [fast_local(): lax.psum((attn_gain_grad[0], fold(query_gain_grad), fold(key_gain_grad),...]
    ppermute x27 -> x0, waiting for transfers between devices: 23.2 us -> none  [the longest x9 17.7 us: sum_pair(): return own + lax.ppermute(send, axis, flip_pairs(count, bit))]
    dynamic_slice x8 -> x0, local copies, waits for them, and re-layouts: 8.91 us -> none  [the longest x3 3.22 us: sum_pair(): send = lax.dynamic_index_in_dim(parts, 1 - mine, dim, keepdims=False)]
  transfers between devices with their start and end apart: 34 -> 4, of which waited for: 9 -> 3; matrix products, arithmetic and copies ran while one was open for 5% -> 1% of each run, Pallas kernels for 8% -> 0%
where the time goes in v3:
time: 437 us
  Pallas kernels  397 us (91%)
  other arithmetic  19.6 us (4%)
  local copies, waits for them, and re-layouts  12.1 us (3%)
  waiting for transfers between devices  6.02 us (1%)
    pallas_call x1, Pallas kernels, back(): pl.pallas_call(functools.partial(back_kernel, groups, block, line, bits,...  159 us
    pallas_call x4, Pallas kernels, swap_blocks(): pl.pallas_call(swap_blocks_kernel, name=f'swap_blocks_{collective_id}', o...  82 us
    pallas_call x1, Pallas kernels, finish(): pl.pallas_call(functools.partial(finish_kernel, line, bits, streams, unit...  64.5 us
    pallas_call x1, Pallas kernels, feed_forward(): pl.pallas_call(ffn_kernel, name='feed_forward', grid_spec=pltpu.PrefetchS...  41.8 us
    pallas_call x1, Pallas kernels, attend(): pl.pallas_call(functools.partial(attend_kernel, groups, block), name='att...  25.4 us
    pallas_call x1, Pallas kernels, turn(): pl.pallas_call(turn_kernel, name='turn', grid=(chips,), in_specs=[whole_b...  10 us
  transfers between devices with their start and end apart: 4, of which 3 were waited for; matrix products, arithmetic and copies ran while one was open for 1% of the time, Pallas kernels for 0%

profile of v3, /device:TPU:0, one launch (start us, length us, event | category | flops | bytes accessed | tf_op | source)
XLA Modules:
  0.0 436.8 jit_solution(1842285532022742765)
XLA Ops:
  3.6 1.1 subtract_subtract_fusion.starts_ref
  9.0 8.5 %project.1 = (bf16[512,1024]{1,0:T(8,128)(2,1)}, f32[4,512,384]{2,1,0:T(8,128)}, bf16[8,256,512]{2,1,0:T(8,128)(2,1)}) custom-call(bf16[512,1024]{1,0:T(8,128)(2,1)} %bitcast.32, f32[1,1024]{1,0:T(1,128)} %bitcast.47, bf16[1024,1024]{1,0:T(8,128)(2,1)} %wq_ref.3, bf16[1024,512]{1,0:T(8,128)(2,1)} %wk_ref.3, bf16[1024,512]{1,0:T(8,128)(2,1)} %wv_ref.3, ...), custom_call_target="tpu_custom_call" | custom-call | tf_op jit(solution)/shard_map/project/pallas_call | solution.py:424
  17.5 27.4 %swap_blocks_0.1 = bf16[8,256,512]{2,1,0:T(8,128)(2,1)} custom-call(bf16[8,256,512]{2,1,0:T(8,128)(2,1)} %get-tuple-element.45.send_ref), custom_call_target="tpu_custom_call" | custom-call | tf_op jit(solution)/shard_map/swap_blocks_0/pallas_call | solution.py:343
  44.9 25.4 %attend.1 = (bf16[8,256,256]{2,1,0:T(8,128)(2,1)}, bf16[2,4096,128]{2,1,0:T(8,128)(2,1)}) custom-call(bf16[2048,512]{1,0:T(8,128)(2,1)} %bitcast.30, s32[2048,1]{1,0:T(8,128)} %subtract_subtract_fusion.starts_ref), custom_call_target="tpu_custom_call" | custom-call | tf_op jit(solution)/shard_map/attend/pallas_call | solution.py:538
  70.3 15.1 %swap_blocks_1.1.heads_ref = bf16[8,256,256]{2,1,0:T(8,128)(2,1)} custom-call(bf16[8,256,256]{2,1,0:T(8,128)(2,1)} %get-tuple-element.46.send_ref), custom_call_target="tpu_custom_call" | custom-call | tf_op jit(solution)/shard_map/swap_blocks_1/pallas_call | solution.py:343
  85.4 5.3 %middle.1 = (f32[512,1024]{1,0:T(8,128)}, bf16[512,1024]{1,0:T(8,128)(2,1)}) custom-call(bf16[512,1024]{1,0:T(8,128)(2,1)} %bitcast.33, bf16[8,256,256]{2,1,0:T(8,128)(2,1)} %swap_blocks_1.1.heads_ref, bf16[1024,1024]{1,0:T(8,128)(2,1)} %w_out_ref.3, f32[1,1024]{1,0:T(1,128)} %bitcast.45), custom_call_target="tpu_custom_call" | custom-call | tf_op jit(solution)/shard_map/middle/pallas_call | solution.py:573
  90.6 1.6 copy.49
  93.3 2.8 collective-permute-done
  96.1 3.1 fusion.1
  99.2 2.6 copy.50.hidden_ref
  101.7 2.8 pad_maximum_fusion.1.grad_ref.dy_ref
  104.5 41.8 %feed_forward.1 = (bf16[1024,2304]{1,0:T(8,128)(2,1)}, bf16[1024,2304]{1,0:T(8,128)(2,1)}, bf16[2304,1024]{1,0:T(8,128)(2,1)}, f32[512,1024]{1,0:T(8,128)}, bf16...) custom-call(s32[1]{0:T(128)} %bitcast.9.core_ref, bf16[1024,1024]{1,0:T(8,128)(2,1)} %copy.50.hidden_ref, ...), custom_call_target="tpu_custom_call" | custom-call | tf_op jit(solution)/shard_map/feed_forward/pallas_call | solution.py:644
  147.6 1.7 collective-permute-done.2.out_got_ref
  149.3 1.5 collective-permute-done.3.back_got_ref
  151.7 10.0 %turn.1 = (bf16[512,1024]{1,0:T(8,128)(2,1)}, f32[512,1024]{1,0:T(8,128)}, f32[1,1024]{1,0:T(1,128)}, bf16[1024,1024]{1,0:T(8,128)(2,1)}, bf16[8,256,256]{2,1,0:T(8,128)(2,1)}) custom-call(f32[512,1024]{1,0:T(8,128)} %get-tuple-element.47.middle_ref, f32[512,1024]{1,0:T(8,128)} %get-tuple-element.49.out_own_ref, bf16[512,1024]{1,0:T(8,128)(2,1)} %copy-done.2, ...), custom_call_target="tpu_custom_call" | custom-call | tf_op jit(solution)/shard_map/turn/pallas_call | solution.py:720
  161.8 14.6 %swap_blocks_2.1 = bf16[8,256,256]{2,1,0:T(8,128)(2,1)} custom-call(bf16[8,256,256]{2,1,0:T(8,128)(2,1)} %get-tuple-element.55.send_ref), custom_call_target="tpu_custom_call" | custom-call | tf_op jit(solution)/shard_map/swap_blocks_2/pallas_call | solution.py:343
  176.4 159.0 %back.1 = (bf16[2048,512]{1,0:T(8,128)(2,1)}, bf16[64,2304]{1,0:T(8,128)(2,1)}, bf16[64,2304]{1,0:T(8,128)(2,1)}, bf16[288,1024]{1,0:T(8,128)(2,1)}) custom-call(bf16[2048,512]{1,0:T(8,128)(2,1)} %bitcast.31, bf16[2,4096,128]{2,1,0:T(8,128)(2,1)} %get-tuple-element.54.logs_ref, bf16[2048,256]{1,0:T(8,128)(2,1)} %bitcast.39, bf16[2048,256]{1,0:T(8,128)(2,1)} %bitcast.40, ...), custom_call_target="tpu_custom_call" | custom-call | tf_op jit(solution)/shard_map/back/pallas_call | solution.py:1171
  335.4 25.0 %swap_blocks_3.1.got_ref = bf16[8,256,512]{2,1,0:T(8,128)(2,1)} custom-call(bf16[8,256,512]{2,1,0:T(8,128)(2,1)} %bitcast.41), custom_call_target="tpu_custom_call" | custom-call | tf_op jit(solution)/shard_map/swap_blocks_3/pallas_call | solution.py:343
  360.4 64.5 %finish.1 = (bf16[512,1024]{1,0:T(8,128)(2,1)}, f32[24,128]{1,0:T(8,128)}, bf16[32,1024]{1,0:T(8,128)(2,1)}, bf16[32,512]{1,0:T(8,128)(2,1)}, bf16[32,512]{1,0:T...) custom-call(bf16[8,256,512]{2,1,0:T(8,128)(2,1)} %swap_blocks_3.1.go, ...), custom_call_target="tpu_custom_call" | custom-call | tf_op jit(solution)/shard_map/finish/pallas_call | solution.py:1506
  424.9 1.4 slice_bitcast_fusion
  426.3 1.4 add_bitcast_fusion
  427.7 1.8 convert_element_type.33
  429.6 1.8 convert_element_type.34
  431.4 1.8 convert_element_type.35
  (58 shorter events, 14.0 us)
Async XLA Ops:
  0.6 4.1 copy-start.9
  3.6 3.2 copy-start.10
  3.6 3.8 copy-start.11
  90.6 2.6 copy-start
  92.2 1.1 copy-start.1
  92.2 3.8 collective-permute-start
  93.2 8.6 %collective-permute-start.1 = (bf16[512,1024]{1,0:T(8,128)(2,1)S(1)}, bf16[512,1024]{1,0:T(8,128)(2,1)}, u32[]{:S(2)}, u32[]{:S(2)}) collective-permute-start(bf16[512,1024]{1,0:T(8,128)(2,1)S(1)} %bitcast.37), channel_id=1, source_target_pairs={{0,1},{1,0},{2,3},{3,2},{4,5},{5,4},{6,7},{7,6},{8,9},{9,8},{10,11... | collective-permute-start | bytes 3145736 | tf_op jit(solution)/shard_map/ppermute | solution.py:1561
  146.3 2.9 collective-permute-start.2
  146.8 4.0 collective-permute-start.3
  149.3 1.5 copy-start.2
  150.8 1.0 copy-start.3
  424.9 8.3 %copy-start.6 = (bf16[32,1024]{1,0:T(8,128)(2,1)S(1)}, bf16[32,1024]{1,0:T(8,128)(2,1)}, u32[]{:S(2)}) copy-start(bf16[32,1024]{1,0:T(8,128)(2,1)} %get-tuple-element.70) | copy-start | bytes 196612
  424.9 9.0 %copy-start.5 = (bf16[32,1024]{1,0:T(8,128)(2,1)S(1)}, bf16[32,1024]{1,0:T(8,128)(2,1)}, u32[]{:S(2)}) copy-start(bf16[32,1024]{1,0:T(8,128)(2,1)} %get-tuple-element.73) | copy-start | bytes 196612
  424.9 9.6 %copy-start.8 = (bf16[32,512]{1,0:T(8,128)(2,1)S(1)}, bf16[32,512]{1,0:T(8,128)(2,1)}, u32[]{:S(2)}) copy-start(bf16[32,512]{1,0:T(8,128)(2,1)} %get-tuple-element.71) | copy-start | bytes 98308
  424.9 10.3 %copy-start.7 = (bf16[32,512]{1,0:T(8,128)(2,1)S(1)}, bf16[32,512]{1,0:T(8,128)(2,1)}, u32[]{:S(2)}) copy-start(bf16[32,512]{1,0:T(8,128)(2,1)} %get-tuple-element.72) | copy-start | bytes 98308
  424.9 10.9 %copy-start.4 = (bf16[512,1024]{1,0:T(8,128)(2,1)S(1)}, bf16[512,1024]{1,0:T(8,128)(2,1)}, u32[]{:S(2)}) copy-start(bf16[512,1024]{1,0:T(8,128)(2,1)} %get-tuple-element.68) | copy-start | bytes 3145732

commit v4 on v3

--- a/solution.py
+++ b/solution.py
@@ -557,195 +557,6 @@
     )(qkv, starts)
 
 
-def middle_kernel(tokens_ref, heads_ref, w_out_ref, gain_ref, middle_ref, hidden_ref):
-    half = heads_ref.shape[1]
-    width = heads_ref.shape[2]
-    total = tokens_ref[...].astype(F32)
-    for p in range(heads_ref.shape[0] // 2):
-        block = jnp.concatenate([heads_ref[2 * p], heads_ref[2 * p + 1]], axis=0)
-        total = total + nn_dot(block, w_out_ref[p * width : (p + 1) * width, :])
-    middle_ref[...] = total
-    scale = lax.rsqrt(jnp.mean(total * total, axis=-1, keepdims=True) + EPSILON)
-    hidden_ref[...] = (total * scale * gain_ref[...]).astype(BF16)
-
-
-def middle_layer(tokens, heads, w_out, gain):
-    return pl.pallas_call(
-        middle_kernel,
-        name="middle",
-        out_shape=[
-            jax.ShapeDtypeStruct(tokens.shape, F32),
-            jax.ShapeDtypeStruct(tokens.shape, BF16),
-        ],
-        compiler_params=kernel_params(),
-    )(tokens, heads, w_out, gain)
-
-
-def ffn_kernel(
-    core_ref,
-    hidden_ref,
-    grad_ref,
-    w_gate_ref,
-    w_up_ref,
-    w_down_ref,
-    gate_grad_ref,
-    up_grad_ref,
-    acts_ref,
-    out_own_ref,
-    out_send_ref,
-    back_own_ref,
-    back_send_ref,
-    out_sum,
-    back_sum,
-):
-    step = pl.program_id(0)
-    rows = hidden_ref.shape[0]
-    chunk = min(256, rows)
-
-    @pl.when(step == 0)
-    def _():
-        out_sum[...] = jnp.zeros_like(out_sum)
-        back_sum[...] = jnp.zeros_like(back_sum)
-
-    for m in range(rows // chunk):
-        part = slice(m * chunk, (m + 1) * chunk)
-        hidden = hidden_ref[part, :]
-        gate = nn_dot(hidden, w_gate_ref[...])
-        up = nn_dot(hidden, w_up_ref[...])
-        pushed = nt_dot(grad_ref[part, :], w_down_ref[...])
-        opened = jax.nn.sigmoid(gate)
-        silu = gate * opened
-        act = (silu * up).astype(BF16)
-        gate_grad = (pushed * up * opened * (1.0 + gate * (1.0 - opened))).astype(BF16)
-        up_grad = (pushed * silu).astype(BF16)
-        acts_ref[:, part] = act.T
-        gate_grad_ref[part, :] = gate_grad
-        up_grad_ref[part, :] = up_grad
-        out_sum[part, :] += nn_dot(act, w_down_ref[...])
-        back_sum[part, :] += nt_dot(gate_grad, w_gate_ref[...]) + nt_dot(up_grad, w_up_ref[...])
-
-    @pl.when(step == pl.num_programs(0) - 1)
-    def _():
-        half = rows // 2
-        out_own_ref[...] = out_sum[:half, :]
-        out_send_ref[...] = out_sum[half:, :].astype(BF16)
-        back_own_ref[...] = back_sum[:half, :]
-        back_send_ref[...] = back_sum[half:, :].astype(BF16)
-
-
-def feed_forward(core, hidden, grad, w_gate, w_up, w_down):
-    rows, width = hidden.shape
-    tiles = w_gate.shape[1] // 2 // FF_TILE
-    half = (rows // 2, width)
-
-    def keep(shape):
-        return pl.BlockSpec(shape, lambda f, c: (0,) * len(shape), pipeline_mode=pl.Buffered(1))
-
-    return pl.pallas_call(
-        ffn_kernel,
-        name="feed_forward",
-        grid_spec=pltpu.PrefetchScalarGridSpec(
-            num_scalar_prefetch=1,
-            grid=(tiles,),
-            in_specs=[
-                keep((rows, width)),
-                keep((rows, width)),
-                pl.BlockSpec((width, FF_TILE), lambda f, c: (0, c[0] * tiles + f)),
-                pl.BlockSpec((width, FF_TILE), lambda f, c: (0, c[0] * tiles + f)),
-                pl.BlockSpec((FF_TILE, width), lambda f, c: (c[0] * tiles + f, 0)),
-            ],
-            out_specs=[
-                pl.BlockSpec((rows, FF_TILE), lambda f, c: (0, f)),
-                pl.BlockSpec((rows, FF_TILE), lambda f, c: (0, f)),
-                pl.BlockSpec((FF_TILE, rows), lambda f, c: (f, 0)),
-            ]
-            + [keep(half)] * 4,
-            scratch_shapes=[pltpu.VMEM((rows, width), F32), pltpu.VMEM((rows, width), F32)],
-        ),
-        out_shape=[
-            jax.ShapeDtypeStruct((rows, tiles * FF_TILE), BF16),
-            jax.ShapeDtypeStruct((rows, tiles * FF_TILE), BF16),
-            jax.ShapeDtypeStruct((tiles * FF_TILE, rows), BF16),
-        ]
-        + [jax.ShapeDtypeStruct(half, kind) for kind in (F32, BF16, F32, BF16)],
-        compiler_params=kernel_params(),
-    )(core, hidden, grad, w_gate, w_up, w_down)
-
-
-def turn_kernel(
-    middle_ref,
-    out_own_ref,
-    out_got_ref,
-    back_own_ref,
-    back_got_ref,
-    grad_ref,
-    gain_ref,
-    heads_ref,
-    w_out_ref,
-    output_ref,
-    mid_ref,
-    gain_grad_ref,
-    w_grad_ref,
-    send_ref,
-    low_grad,
-):
-    @pl.when(pl.program_id(0) == 0)
-    def _():
-        middle = middle_ref[...]
-        result = middle + (out_own_ref[...] + out_got_ref[...].astype(F32))
-        output_ref[...] = result.astype(BF16)
-        scale = lax.rsqrt(jnp.mean(middle * middle, axis=-1, keepdims=True) + EPSILON)
-        normal = middle * scale
-        back = back_own_ref[...] + back_got_ref[...].astype(F32)
-        gain_grad_ref[...] = jnp.sum(back * normal, axis=0, keepdims=True)
-        pushed = back * gain_ref[...]
-        inner = jnp.mean(pushed * normal, axis=-1, keepdims=True)
-        mid = grad_ref[...].astype(F32) + scale * (pushed - normal * inner)
-        mid_ref[...] = mid
-        low_grad[...] = mid.astype(BF16)
-
-    half = heads_ref.shape[1]
-    heads = jnp.concatenate([heads_ref[0], heads_ref[1]], axis=0)
-    grad = low_grad[...]
-    w_grad_ref[...] = tn_dot(heads, grad).astype(BF16)
-    send = nt_dot(grad, w_out_ref[...]).astype(BF16)
-    send_ref[0] = send[:half]
-    send_ref[1] = send[half:]
-
-
-def turn(middle, out_own, out_got, back_own, back_got, grad, gain, heads, w_out):
-    rows, width = middle.shape
-    count, half, lanes = heads.shape
-    chips = count // 2
-    return pl.pallas_call(
-        turn_kernel,
-        name="turn",
-        grid=(chips,),
-        in_specs=[whole_block((rows, width))] * 6
-        + [
-            whole_block((1, width)),
-            pl.BlockSpec((2, half, lanes), lambda p: (p, 0, 0)),
-            pl.BlockSpec((lanes, width), lambda p: (p, 0)),
-        ],
-        out_specs=[
-            whole_block((rows, width)),
-            whole_block((rows, width)),
-            whole_block((1, width)),
-            pl.BlockSpec((lanes, width), lambda p: (p, 0)),
-            pl.BlockSpec((2, half, lanes), lambda p: (p, 0, 0)),
-        ],
-        out_shape=[
-            jax.ShapeDtypeStruct((rows, width), BF16),
-            jax.ShapeDtypeStruct((rows, width), F32),
-            jax.ShapeDtypeStruct((1, width), F32),
-            jax.ShapeDtypeStruct((chips * lanes, width), BF16),
-            jax.ShapeDtypeStruct(heads.shape, BF16),
-        ],
-        scratch_shapes=[pltpu.VMEM((rows, width), BF16)],
-        compiler_params=kernel_params(),
-    )(middle, out_own, out_got, back_own, back_got, grad, gain, heads, w_out)
-
-
 def pair_of(bit):
     index = lax.axis_index("blk")
     mine = lax.rem(index // bit, 2)
@@ -949,7 +760,7 @@
     for way in (1, -1):
         there = (z + way >= 0) & (z + way < line)
 
-        @pl.when(there & (step < steps - 1))
+        @pl.when(there & (step >= 0) & (step < steps - 1))
         def _():
             pl.semaphore_signal(
                 ready.at[(1 - way) // 2],
@@ -966,6 +777,327 @@
         for stream in streams:
             if k < len(stream.path):
                 stream.send(k, step)
+
+
+def greet_all(blk_count, line):
+    barrier = pltpu.get_barrier_semaphore()
+    z, index = lax.axis_index("dp"), lax.axis_index("blk")
+    for step in range(1, blk_count):
+        pl.semaphore_signal(
+            barrier,
+            inc=1,
+            device_id=(z, lax.rem(index + step, blk_count)),
+            device_id_type=pl.DeviceIdType.MESH,
+        )
+    for way in (1, -1):
+
+        @pl.when((z + way >= 0) & (z + way < line))
+        def _():
+            pl.semaphore_signal(
+                barrier, inc=1, device_id=(z + way, index), device_id_type=pl.DeviceIdType.MESH
+            )
+
+    beside = jnp.minimum(z, 1) + jnp.minimum(line - 1 - z, 1)
+    pl.semaphore_wait(barrier, blk_count - 1 + beside)
+
+
+def middle_kernel(
+    line,
+    bits,
+    streams,
+    units,
+    tokens_ref,
+    heads_ref,
+    w_out_ref,
+    gain_ref,
+    dy_own_ref,
+    dy_got_ref,
+    w_gate_ref,
+    w_up_ref,
+    w_down_ref,
+    output_ref,
+    mid_ref,
+    gain_grad_ref,
+    w_grad_ref,
+    grad_heads_ref,
+    acts_ref,
+    gate_out_ref,
+    up_out_ref,
+    hidden,
+    flipped,
+    dy,
+    middle,
+    out_sum,
+    back_sum,
+    gate_grads,
+    up_grads,
+    part_send,
+    part_got,
+    low_grad,
+    do_send,
+    do_got,
+    hidden_sem,
+    part_sent_sem,
+    part_got_sem,
+    do_sent_sem,
+    do_got_sem,
+    ready,
+    *refs,
+):
+    n = pl.program_id(0)
+    steps = pl.num_programs(0)
+    z, index = lax.axis_index("dp"), lax.axis_index("blk")
+    sibling = pair_of(1)[1]
+    own_rows, width = tokens_ref.shape
+    rows = 2 * own_rows
+    blk_count, tok_count, head_lanes = heads_ref.shape
+    chips = blk_count // 2
+    chunk = 256
+    gate_stream, up_stream, both_stream = streams
+    gate_rows = gate_stream.block[0]
+    own, other = pl.ds(0, own_rows), pl.ds(own_rows, own_rows)
+
+    def finish_gate(u, value):
+        gate_out_ref[:gate_rows, pl.ds(pl.multiple_of(u * FF_TILE, FF_TILE), FF_TILE)] = value
+
+    def finish_up(u, value):
+        up_out_ref[:gate_rows, pl.ds(pl.multiple_of(u * FF_TILE, FF_TILE), FF_TILE)] = value
+
+    def finish_both(u, value):
+        here = pl.ds(pl.multiple_of(u * FF_TILE, FF_TILE), FF_TILE)
+        gate_out_ref[gate_rows:, here] = value[:, :FF_TILE]
+        up_out_ref[gate_rows:, here] = value[:, FF_TILE:]
+
+    at = 0
+    for stream, finish in zip(streams, (finish_gate, finish_up, finish_both)):
+        count = len(stream.scratch())
+        stream.bind(refs[at : at + count], units, finish)
+        at += count
+
+    def hidden_copy():
+        return pltpu.make_async_remote_copy(
+            src_ref=hidden.at[own],
+            dst_ref=hidden.at[other],
+            send_sem=hidden_sem.at[0],
+            recv_sem=hidden_sem.at[1],
+            device_id=sibling,
+            device_id_type=pl.DeviceIdType.MESH,
+        )
+
+    def part_copy(i):
+        return pltpu.make_async_remote_copy(
+            src_ref=part_send.at[i],
+            dst_ref=part_got.at[i],
+            send_sem=part_sent_sem.at[i],
+            recv_sem=part_got_sem.at[i],
+            device_id=sibling,
+            device_id_type=pl.DeviceIdType.MESH,
+        )
+
+    def do_copy(target, source):
+        return pltpu.make_async_remote_copy(
+            src_ref=do_send.at[target],
+            dst_ref=do_got.at[source],
+            send_sem=do_sent_sem.at[target],
+            recv_sem=do_got_sem.at[source],
+            device_id=(z, target),
+            device_id_type=pl.DeviceIdType.MESH,
+        )
+
+    def flip(start):
+        for r in range(start, start + own_rows, chunk):
+            for c in range(0, width, chunk):
+                flipped[c : c + chunk, r : r + chunk] = hidden[r : r + chunk, c : c + chunk].T
+
+    @pl.when(n == 0)
+    def _():
+        greet_all(blk_count, line)
+        total = tokens_ref[...].astype(F32)
+        for p in range(chips):
+            block = jnp.concatenate([heads_ref[2 * p], heads_ref[2 * p + 1]], axis=0)
+            total = total + nn_dot(block, w_out_ref[p * head_lanes : (p + 1) * head_lanes, :])
+        middle[...] = total
+        scale = lax.rsqrt(jnp.mean(total * total, axis=-1, keepdims=True) + EPSILON)
+        hidden[own] = (total * scale * gain_ref[...]).astype(BF16)
+        hidden_copy().start()
+        dy[own] = dy_own_ref[...]
+        dy[other] = dy_got_ref[...]
+        out_sum[...] = jnp.zeros_like(out_sum)
+        back_sum[...] = jnp.zeros_like(back_sum)
+        flip(0)
+
+    @pl.when(n == 1)
+    def _():
+        hidden_copy().wait()
+        flip(own_rows)
+
+    step_streams(streams, n - 1, steps - 1, line, ready)
+
+    @pl.when((n >= 1) & (n <= units))
+    def _():
+        for m in range(rows // chunk):
+            part = slice(m * chunk, (m + 1) * chunk)
+            gate = nn_dot(hidden[part, :], w_gate_ref[...])
+            up = nn_dot(hidden[part, :], w_up_ref[...])
+            pushed = nt_dot(dy[part, :], w_down_ref[...])
+            opened = jax.nn.sigmoid(gate)
+            silu = gate * opened
+            act = (silu * up).astype(BF16)
+            gate_grad = (pushed * up * opened * (1.0 + gate * (1.0 - opened))).astype(BF16)
+            up_grad = (pushed * silu).astype(BF16)
+            acts_ref[:, part] = act.T
+            gate_grads[part, :] = gate_grad
+            up_grads[part, :] = up_grad
+            out_sum[part, :] += nn_dot(act, w_down_ref[...])
+            back_sum[part, :] += nt_dot(gate_grad, w_gate_ref[...]) + nt_dot(up_grad, w_up_ref[...])
+        u = n - 1
+        slot, long_slot = lax.rem(u, 2), lax.rem(u, both_stream.slots(0))
+        each = width // line
+        shape = gate_stream.shape(gate_stream.dims[0])[1:-2] + (-1, FF_TILE)
+        for m in range(line):
+            part = slice(m * each, (m + 1) * each)
+            gate_part = nn_dot(flipped[part, :], gate_grads[...]).astype(BF16).reshape(shape)
+            up_part = nn_dot(flipped[part, :], up_grads[...]).astype(BF16).reshape(shape)
+            gate_stream.source[slot, m] = gate_part[..., :gate_rows, :]
+            up_stream.source[slot, m] = up_part[..., :gate_rows, :]
+            both_stream.source[long_slot, m, ..., :FF_TILE] = gate_part[..., gate_rows:, :]
+            both_stream.source[long_slot, m, ..., FF_TILE:] = up_part[..., gate_rows:, :]
+
+    @pl.when(n == units)
+    def _():
+        part_send[0] = back_sum[other].astype(BF16)
+        part_copy(0).start()
+        part_send[1] = out_sum[other].astype(BF16)
+        part_copy(1).start()
+
+    @pl.when(n == units + 1)
+    def _():
+        part_copy(0).wait()
+        values = middle[...]
+        scale = lax.rsqrt(jnp.mean(values * values, axis=-1, keepdims=True) + EPSILON)
+        normal = values * scale
+        back = back_sum[own] + part_got[0].astype(F32)
+        gain_grad_ref[...] = jnp.sum(back * normal, axis=0, keepdims=True)
+        pushed = back * gain_ref[...]
+        inner = jnp.mean(pushed * normal, axis=-1, keepdims=True)
+        mid = dy[own].astype(F32) + scale * (pushed - normal * inner)
+        mid_ref[...] = mid
+        low_grad[...] = mid.astype(BF16)
+        part_copy(1).wait()
+        output_ref[...] = (values + (out_sum[own] + part_got[1].astype(F32))).astype(BF16)
+
+    @pl.when((n > units + 1) & (n <= units + 1 + chips))
+    def _():
+        p = n - units - 2
+        grad = low_grad[...]
+        lanes = pl.ds(pl.multiple_of(p * head_lanes, head_lanes), head_lanes)
+        send = nt_dot(grad, w_out_ref[lanes, :]).astype(BF16)
+        for half in range(2):
+            target = 2 * p + half
+            do_send[target] = send[half * tok_count : (half + 1) * tok_count]
+
+            @pl.when(target != index)
+            def _():
+                do_copy(target, index).start()
+
+            @pl.when(target == index)
+            def _():
+                do_got[target] = send[half * tok_count : (half + 1) * tok_count]
+
+        heads = jnp.concatenate([heads_ref[2 * p], heads_ref[2 * p + 1]], axis=0)
+        w_grad_ref[lanes, :] = tn_dot(heads, grad).astype(BF16)
+
+    @pl.when(n == steps - 1)
+    def _():
+        for other_index in range(blk_count):
+
+            @pl.when(other_index != index)
+            def _():
+                do_copy(other_index, other_index).wait()
+
+        grad_heads_ref[...] = do_got[...]
+
+
+def middle_layer(line, bits, tokens, heads, w_out, gain, dy_own, dy_got, w_gate, w_up, w_down):
+    own_rows, width = tokens.shape
+    rows = 2 * own_rows
+    blk_count, tok_count, head_lanes = heads.shape
+    units = w_gate.shape[1] // 2 // FF_TILE
+    chips = line * 2 ** len(bits)
+    each = width // chips
+    late = each // 4
+    dims = [("z", line)] + [(bit, 2) for bit in bits]
+    streams = [
+        Stream(bits[::-1] + hops(line), dims, (each - late, FF_TILE), line),
+        Stream(bits + hops(line), dims, (each - late, FF_TILE), line),
+        Stream(hops(line) + bits, dims, (late, 2 * FF_TILE), line),
+    ]
+    steps = max(units + 2 + max(len(stream.path) for stream in streams), units + 3 + blk_count // 2)
+
+    def keep(shape):
+        return pl.BlockSpec(shape, lambda n: (0,) * len(shape), pipeline_mode=pl.Buffered(1))
+
+    def tile(n):
+        return jnp.clip(n - 1, 0, units - 1)
+
+    def mine(n):
+        return lax.rem(lax.axis_index("blk"), 2) * units + tile(n)
+
+    scratch = [
+        pltpu.VMEM((rows, width), BF16),
+        pltpu.VMEM((width, rows), BF16),
+        pltpu.VMEM((rows, width), BF16),
+        pltpu.VMEM((own_rows, width), F32),
+        pltpu.VMEM((rows, width), F32),
+        pltpu.VMEM((rows, width), F32),
+        pltpu.VMEM((rows, FF_TILE), BF16),
+        pltpu.VMEM((rows, FF_TILE), BF16),
+        pltpu.VMEM((2, own_rows, width), BF16),
+        pltpu.VMEM((2, own_rows, width), BF16),
+        pltpu.VMEM((own_rows, width), BF16),
+        pltpu.VMEM(heads.shape, BF16),
+        pltpu.VMEM(heads.shape, BF16),
+        pltpu.SemaphoreType.DMA((2,)),
+        pltpu.SemaphoreType.DMA((2,)),
+        pltpu.SemaphoreType.DMA((2,)),
+        pltpu.SemaphoreType.DMA((blk_count,)),
+        pltpu.SemaphoreType.DMA((blk_count,)),
+        pltpu.SemaphoreType.REGULAR((2,)),
+    ]
+    for stream in streams:
+        scratch += stream.scratch()
+    outs = [
+        ((own_rows, width), BF16),
+        ((own_rows, width), F32),
+        ((1, width), F32),
+        (w_out.shape, BF16),
+        (heads.shape, BF16),
+        ((units * FF_TILE, rows), BF16),
+        ((each, units * FF_TILE), BF16),
+        ((each, units * FF_TILE), BF16),
+    ]
+    out_specs = [keep(shape) for shape, unused in outs]
+    out_specs[5] = pl.BlockSpec((FF_TILE, rows), lambda n: (tile(n), 0))
+    return pl.pallas_call(
+        functools.partial(middle_kernel, line, bits, streams, units),
+        name="middle",
+        grid=(steps,),
+        in_specs=[
+            keep(tokens.shape),
+            keep(heads.shape),
+            keep(w_out.shape),
+            keep(gain.shape),
+            keep(dy_own.shape),
+            keep(dy_got.shape),
+            pl.BlockSpec((width, FF_TILE), lambda n: (0, mine(n))),
+            pl.BlockSpec((width, FF_TILE), lambda n: (0, mine(n))),
+            pl.BlockSpec((FF_TILE, width), lambda n: (mine(n), 0)),
+        ],
+        out_specs=out_specs,
+        out_shape=[jax.ShapeDtypeStruct(shape, kind) for shape, kind in outs],
+        scratch_shapes=scratch,
+        compiler_params=kernel_params(collective_id=6, has_side_effects=True),
+    )(tokens, heads, w_out, gain, dy_own, dy_got, w_gate, w_up, w_down)
 
 
 def back_kernel(
@@ -980,14 +1112,10 @@
     out_ref,
     grad_ref,
     starts_ref,
-    flipped_ref,
-    dy_ref,
-    gate_grad_ref,
-    up_grad_ref,
+    dy_own_ref,
+    dy_got_ref,
     acts_ref,
     result_ref,
-    gate_out_ref,
-    up_out_ref,
     down_out_ref,
     queries,
     keys,
@@ -1003,26 +1131,20 @@
     q_width = groups * LANES
     n = pl.program_id(0)
     core = lax.rem(lax.axis_index("blk"), 2)
-    gate_stream, up_stream, down_stream = streams
-
-    def finish_gate(u, value):
-        gate_out_ref[:, pl.ds(pl.multiple_of(u * FF_TILE, FF_TILE), FF_TILE)] = value
-
-    def finish_up(u, value):
-        up_out_ref[:, pl.ds(pl.multiple_of(u * FF_TILE, FF_TILE), FF_TILE)] = value
-
-    def finish_down(u, value):
+    half = down_out_ref.shape[1] // 2
+
+    def finish_low(u, value):
         rows = value.shape[0]
-        down_out_ref[pl.ds(pl.multiple_of(u * rows, rows), rows), :] = value
+        down_out_ref[pl.ds(pl.multiple_of(u * rows, rows), rows), :half] = value
+
+    def finish_high(u, value):
+        rows = value.shape[0]
+        down_out_ref[pl.ds(pl.multiple_of(u * rows, rows), rows), half:] = value
 
     at = 0
-    for stream, finish, first_z in (
-        (gate_stream, finish_gate, None),
-        (up_stream, finish_up, None),
-        (down_stream, finish_down, core * (line // 2)),
-    ):
+    for stream, finish in zip(streams, (finish_low, finish_high)):
         count = len(stream.scratch())
-        stream.bind(refs[at : at + count], units, finish, first_z)
+        stream.bind(refs[at : at + count], units, finish, core * (line // 2))
         at += count
 
     @pl.when(n == 0)
@@ -1056,35 +1178,25 @@
 
     @pl.when(n < units)
     def _():
-        chunk = 256
-        width = flipped_ref.shape[0]
-        gate_shape = gate_stream.shape(gate_stream.dims[0])
-        down_shape = down_stream.shape(down_stream.dims[0])
-        slot = lax.rem(n, 2)
-        each = chunk * gate_shape[0] // width
-
-        def weights(m, carry):
-            flipped = flipped_ref[pl.ds(pl.multiple_of(m * chunk, chunk), chunk), :]
-            part = pl.ds(m * each, each)
-            piece = (each,) + gate_shape[1:]
-            gate_stream.source[slot, part] = nn_dot(flipped, gate_grad_ref[...]).astype(BF16).reshape(piece)
-            up_stream.source[slot, part] = nn_dot(flipped, up_grad_ref[...]).astype(BF16).reshape(piece)
-            return carry
-
-        lax.fori_loop(0, width // chunk, weights, 0)
         acts = acts_ref[...].reshape(-1, acts_ref.shape[-1])
-        made = nn_dot(acts, dy_ref[...]).astype(BF16)
-        down_stream.source[lax.rem(n, down_stream.slots(0))] = made.reshape(down_shape)
+        rows = dy_own_ref.shape[0]
+        made = nn_dot(acts[:, :rows], dy_own_ref[...]) + nn_dot(acts[:, rows:], dy_got_ref[...])
+        made = made.astype(BF16)
+        for stream, part in zip(streams, (made[:, :half], made[:, half:])):
+            shape = stream.shape(stream.dims[0])
+            stream.source[lax.rem(n, stream.slots(0))] = part.reshape(shape)
 
     row = lax.broadcasted_iota(jnp.int32, (block, 2 * block), 0)
     column = lax.broadcasted_iota(jnp.int32, (block, 2 * block), 1) % block
 
-    @pl.when(n < blocks + 1)
+    turn = n - (pl.num_programs(0) - blocks - 2)
+
+    @pl.when((turn >= 0) & (turn < blocks + 1))
     def _():
         def pair(m, carry):
-            late = (n + m) // blocks
+            late = (turn + m) // blocks
             j = m + late * (blocks - 1 - 2 * m)
-            i = (1 - late) * (m + n) + late * (n - 1)
+            i = (1 - late) * (m + turn) + late * (turn - 1)
             key_at = pl.multiple_of(j * block, block)
             at = pl.multiple_of(i * 2 * block, 2 * block)
             key_rows = pl.ds(key_at, block)
@@ -1104,7 +1216,7 @@
 
         lax.fori_loop(0, blocks // 2, pair, 0)
 
-    @pl.when(n == blocks + 1)
+    @pl.when(turn == blocks + 1)
     def _():
         low = low_lanes((block, LANES))
 
@@ -1132,30 +1244,26 @@
         lax.fori_loop(0, blocks, finish, 0)
 
 
-def back(line, bits, qkv, logs, out, grad, starts, block, flipped, dy, gate_grad, up_grad, acts):
+def back(line, bits, qkv, logs, out, grad, starts, block, dy_own, dy_got, acts):
     size, width = qkv.shape
     groups = (width - 2 * LANES) // LANES
-    units = gate_grad.shape[1] // FF_TILE
-    model, rows = flipped.shape
+    model = dy_own.shape[1]
+    rows = acts.shape[1]
+    units = acts.shape[0] // FF_TILE
     chips = line * 2 ** len(bits)
-    sides = [(bit, 2) for bit in bits]
-    gate_block = (model // chips, FF_TILE)
     down_rows = acts.shape[0] // (chips // 2)
-    down_block = (down_rows // units, model)
-    whole = [("z", line)] + sides
-    half = [("z", line // 2)] + sides
+    down_block = (down_rows // units, model // 2)
+    dims = [("z", line // 2)] + [(bit, 2) for bit in bits]
     streams = [
-        Stream(bits[::-1] + hops(line), whole, gate_block, line),
-        Stream(bits + hops(line), whole, gate_block, line),
-        Stream(hops(line) + bits, half, down_block, line),
+        Stream(hops(line) + bits[::-1], dims, down_block, line),
+        Stream(bits + hops(line), dims, down_block, line),
     ]
     longest = max(len(stream.path) for stream in streams)
-    steps = units + longest + 1
+    steps = max(units + longest + 1, size // block + 2)
 
     def keep(shape):
         return pl.BlockSpec(shape, lambda n: (0,) * len(shape), pipeline_mode=pl.Buffered(1))
 
-    tile = lambda n: (0, jnp.minimum(n, units - 1))
     acts = acts.reshape(chips // 2, down_rows, rows)
     scratch = [
         pltpu.VMEM((groups, 2 * size, 2 * LANES), BF16),
@@ -1178,29 +1286,20 @@
             keep(out.shape),
             keep(grad.shape),
             keep(starts.shape),
-            keep(flipped.shape),
-            keep(dy.shape),
-            pl.BlockSpec((rows, FF_TILE), tile),
-            pl.BlockSpec((rows, FF_TILE), tile),
+            keep(dy_own.shape),
+            keep(dy_got.shape),
             pl.BlockSpec(
                 (chips // 2, down_block[0], rows), lambda n: (0, jnp.minimum(n, units - 1), 0)
             ),
         ],
-        out_specs=[
-            keep(qkv.shape),
-            keep((gate_block[0], units * FF_TILE)),
-            keep((gate_block[0], units * FF_TILE)),
-            keep((down_rows, model)),
-        ],
+        out_specs=[keep(qkv.shape), keep((down_rows, model))],
         out_shape=[
             jax.ShapeDtypeStruct(qkv.shape, BF16),
-            jax.ShapeDtypeStruct((gate_block[0], units * FF_TILE), BF16),
-            jax.ShapeDtypeStruct((gate_block[0], units * FF_TILE), BF16),
             jax.ShapeDtypeStruct((down_rows, model), BF16),
         ],
         scratch_shapes=scratch,
         compiler_params=kernel_params(collective_id=4, has_side_effects=True),
-    )(qkv, logs, out, grad, starts, flipped, dy, gate_grad, up_grad, acts)
+    )(qkv, logs, out, grad, starts, dy_own, dy_got, acts)
 
 
 def sum_gains(rounds, n, first, gains, gains_got, sent_sem, got_sem):
@@ -1609,7 +1708,7 @@
     ).reshape(1, 2 * size)
     flat = tokens.reshape(rows, width)
     grad_own = cotangent.reshape(rows, width)
-    grad_both = jnp.concatenate([grad_own, swap_core(grad_own, blk_count)], axis=0)
+    grad_got = swap_core(grad_own, blk_count)
 
     hidden_in, proj, send = project(
         flat, g_attn[None], w_query, w_key, w_value, q_gain2, k_gain2, cosine, sine
@@ -1617,32 +1716,30 @@
     qkv = swap_blocks(send, 0).reshape(size, -1)
     attended, logs = attend(qkv, starts[:, None], tok_count)
     heads = swap_blocks(attended, 1)
-    middle, hidden_own = middle_layer(flat, heads, w_out, g_ffn[None])
-    hidden = jnp.concatenate([hidden_own, swap_core(hidden_own, blk_count)], axis=0)
-    flipped = hidden.T
-    core_arg = core.reshape(1)
-    gate_grad, up_grad, acts, out_own, out_send, back_own, back_send = feed_forward(
-        core_arg, hidden, grad_both, w_gate, w_up, w_down
-    )
-    back_got = swap_core(back_send, blk_count)
-    out_got = swap_core(out_send, blk_count)
-    output, mid, ffn_gain_grad, w_out_parts, send = turn(
-        middle, out_own, out_got, back_own, back_got, grad_own, g_ffn[None], heads, w_out
-    )
-    grad_heads = swap_blocks(send, 2).reshape(size, -1)
-    qkv_grad, gate_sum, up_sum, down_sum = back(
+    output, mid, ffn_gain_grad, w_out_parts, grad_heads, acts, gate_sum, up_sum = middle_layer(
+        dp_count,
+        bits,
+        flat,
+        heads,
+        w_out,
+        g_ffn[None],
+        grad_own,
+        grad_got,
+        w_gate,
+        w_up,
+        w_down,
+    )
+    qkv_grad, down_sum = back(
         dp_count,
         bits,
         qkv,
         logs,
         attended.reshape(size, -1),
-        grad_heads,
+        grad_heads.reshape(size, -1),
         starts_two,
         tok_count,
-        flipped,
-        grad_both,
-        gate_grad,
-        up_grad,
+        grad_own,
+        grad_got,
         acts,
     )
     got = swap_blocks(qkv_grad.reshape(blk_count, tok_count, -1), 3)

time: 437 us -> 404 us (0.924)
  Pallas kernels: 397 us -> 375 us
  waiting for transfers between devices: 6.02 us -> 0.01 us
    pallas_call x1, Pallas kernels: 159 us -> 92.1 us  [back(): pl.pallas_call(functools.partial(back_kernel, groups, block, line, bits,...]
    pallas_call x3 -> x1, Pallas kernels: 57.1 us -> 118 us  [middle_layer(): pl.pallas_call(functools.partial(middle_kernel, line, bits, streams, unit...]
    pallas_call x4 -> x3, Pallas kernels: 82 us -> 66.1 us  [swap_blocks(): pl.pallas_call(swap_blocks_kernel, name=f'swap_blocks_{collective_id}', o...]
    ppermute x4 -> x1, waiting for transfers between devices: 6.02 us -> 0.01 us  [swap_core(): return lax.ppermute(block, 'blk', flip_pairs(blk_count, 1))]
  transfers between devices with their start and end apart: 4 -> 1, of which waited for: 3 -> 0; matrix products, arithmetic and copies ran while one was open for 1% -> 3% of each run, Pallas kernels for 0% -> 19%
where the time goes in v4:
time: 404 us; the launch traced here: 403 us
  Pallas kernels  375 us (93%)
  other arithmetic  16.8 us (4%)
  local copies, waits for them, and re-layouts  10 us (2%)
    pallas_call x1, Pallas kernels, middle_layer(): pl.pallas_call(functools.partial(middle_kernel, line, bits, streams, unit...  118 us
    pallas_call x1, Pallas kernels, back(): pl.pallas_call(functools.partial(back_kernel, groups, block, line, bits,...  92.1 us
    pallas_call x3, Pallas kernels, swap_blocks(): pl.pallas_call(swap_blocks_kernel, name=f'swap_blocks_{collective_id}', o...  66.1 us
    pallas_call x1, Pallas kernels, finish(): pl.pallas_call(functools.partial(finish_kernel, line, bits, streams, unit...  64.5 us
    pallas_call x1, Pallas kernels, attend(): pl.pallas_call(functools.partial(attend_kernel, groups, block), name='att...  25.4 us
    convert_element_type x7, other arithmetic, fast_local(): part.astype(F32)  10.4 us
    pallas_call x1, Pallas kernels, project(): pl.pallas_call(project_kernel, name='project', grid=(chips,), in_specs=[w...  8.54 us
  transfers between devices with their start and end apart: 1, of which 0 were waited for; matrix products, arithmetic and copies ran while one was open for 3% of the time, Pallas kernels for 19%

profile of v4, /device:TPU:0, one launch (start us, length us, event | category | flops | bytes accessed | tf_op | source)
XLA Modules:
  0.0 403.0 jit_solution(15578416179568689025)
XLA Ops:
  2.5 0.9 reduce_window_sum.22
  7.6 1.0 fusion
  10.0 1.0 pad_maximum_fusion.sin_ref
  10.9 8.5 %project.1 = (bf16[512,1024]{1,0:T(8,128)(2,1)}, f32[4,512,384]{2,1,0:T(8,128)}, bf16[8,256,512]{2,1,0:T(8,128)(2,1)}) custom-call(bf16[512,1024]{1,0:T(8,128)(2,1)} %bitcast.29, f32[1,1024]{1,0:T(1,128)} %bitcast.43, bf16[1024,1024]{1,0:T(8,128)(2,1)} %wq_ref.3, bf16[1024,512]{1,0:T(8,128)(2,1)} %wk_ref.3, bf16[1024,512]{1,0:T(8,128)(2,1)} %wv_ref.3, ...), custom_call_target="tpu_custom_call" | custom-call | tf_op jit(solution)/shard_map/project/pallas_call | solution.py:424
  19.5 27.0 %swap_blocks_0.1 = bf16[8,256,512]{2,1,0:T(8,128)(2,1)} custom-call(bf16[8,256,512]{2,1,0:T(8,128)(2,1)} %get-tuple-element.37.send_ref), custom_call_target="tpu_custom_call" | custom-call | tf_op jit(solution)/shard_map/swap_blocks_0/pallas_call | solution.py:343
  46.5 1.1 subtract_subtract_fusion.starts_ref
  47.6 25.4 %attend.1 = (bf16[8,256,256]{2,1,0:T(8,128)(2,1)}, bf16[2,4096,128]{2,1,0:T(8,128)(2,1)}) custom-call(bf16[2048,512]{1,0:T(8,128)(2,1)} %bitcast.27, s32[2048,1]{1,0:T(8,128)} %subtract_subtract_fusion.starts_ref), custom_call_target="tpu_custom_call" | custom-call | tf_op jit(solution)/shard_map/attend/pallas_call | solution.py:538
  73.0 15.0 %swap_blocks_1.1.heads_ref = bf16[8,256,256]{2,1,0:T(8,128)(2,1)} custom-call(bf16[8,256,256]{2,1,0:T(8,128)(2,1)} %get-tuple-element.38.send_ref), custom_call_target="tpu_custom_call" | custom-call | tf_op jit(solution)/shard_map/swap_blocks_1/pallas_call | solution.py:343
  88.0 1.0 copy-done
  89.0 118.3 %middle.1 = (bf16[512,1024]{1,0:T(8,128)(2,1)}, f32[512,1024]{1,0:T(8,128)}, f32[1,1024]{1,0:T(1,128)}, bf16[1024,1024]{1,0:T(8,128)(2,1)}, bf16[8,256,256]{2,1,...) custom-call(bf16[512,1024]{1,0:T(8,128)(2,1)} %bitcast.30, ...), custom_call_target="tpu_custom_call" | custom-call | tf_op jit(solution)/shard_map/middle/pallas_call | solution.py:1081
  207.3 92.1 %back.1 = (bf16[2048,512]{1,0:T(8,128)(2,1)}, bf16[288,1024]{1,0:T(8,128)(2,1)}) custom-call(bf16[2048,512]{1,0:T(8,128)(2,1)} %bitcast.28, bf16[2,4096,128]{2,1,0:T(8,128)(2,1)} %get-tuple-element.40.logs_ref, bf16[2048,256]{1,0:T(8,128)(2,1)} %bitcast.36, bf16[2048,256]{1,0:T(8,128)(2,1)} %bitcast.38, s32[1,4096]{1,0:T(1,128)} %reshape.232.starts_ref, ...), custom_call_target="tpu_custom_call" | custom-call | tf_op jit(solution)/shard_map/back/pallas_call | solution.py:1279
  299.4 24.0 %swap_blocks_3.1.got_ref = bf16[8,256,512]{2,1,0:T(8,128)(2,1)} custom-call(bf16[8,256,512]{2,1,0:T(8,128)(2,1)} %bitcast.37), custom_call_target="tpu_custom_call" | custom-call | tf_op jit(solution)/shard_map/swap_blocks_3/pallas_call | solution.py:343
  323.4 64.5 %finish.1 = (bf16[512,1024]{1,0:T(8,128)(2,1)}, f32[24,128]{1,0:T(8,128)}, bf16[32,1024]{1,0:T(8,128)(2,1)}, bf16[32,512]{1,0:T(8,128)(2,1)}, bf16[32,512]{1,0:T...) custom-call(bf16[8,256,512]{2,1,0:T(8,128)(2,1)} %swap_blocks_3.1.go, ...), custom_call_target="tpu_custom_call" | custom-call | tf_op jit(solution)/shard_map/finish/pallas_call | solution.py:1605
  387.9 1.4 add_bitcast_fusion
  389.4 1.3 slice_bitcast_fusion
  390.6 1.4 convert_element_type.30
  392.0 1.4 convert_element_type.31
  393.4 1.5 convert_element_type.29
  394.9 1.5 convert_element_type.32
  396.4 1.8 convert_element_type.33
  398.2 1.9 convert_element_type.34
  400.1 0.9 convert_element_type.35
  401.0 1.0 copy.43
  402.0 1.0 copy.44
  (30 shorter events, 7.4 us)
Async XLA Ops:
  0.6 87.4 %collective-permute-start = (bf16[512,1024]{1,0:T(8,128)(2,1)}, bf16[512,1024]{1,0:T(8,128)(2,1)S(1)}, u32[]{:S(2)}, u32[]{:S(2)}) collective-permute-start(bf16[512,1024]{1,0:T(8,128)(2,1)} %bitcast.33), channel_id=1, source_target_pairs={{0,1},{1,0},{2,3},{3,2},{4,5},{5,4},{6,7},{7,6},{8,9},{9,8},{10,11... | collective-permute-start | bytes 3145736 | tf_op jit(solution)/shard_map/ppermute | solution.py:1660
  88.0 1.0 copy-start
  387.9 12.2 %copy-start.3 = (bf16[144,1024]{1,0:T(8,128)(2,1)S(1)}, bf16[144,1024]{1,0:T(8,128)(2,1)}, u32[]{:S(2)}) copy-start(bf16[144,1024]{1,0:T(8,128)(2,1)} %get-tuple-element.60) | copy-start | bytes 884740
  387.9 13.1 %copy-start.1 = (bf16[512,1024]{1,0:T(8,128)(2,1)S(1)}, bf16[512,1024]{1,0:T(8,128)(2,1)}, u32[]{:S(2)}) copy-start(bf16[512,1024]{1,0:T(8,128)(2,1)} %get-tuple-element.39) | copy-start | bytes 3145732
  398.2 3.8 copy-start.2

commit v5 on v4

--- a/solution.py
+++ b/solution.py
@@ -279,7 +279,10 @@
 F32 = jnp.float32
 LANES = 128
 FF_TILE = 256
-VMEM_BYTES = 56 * 1024 * 1024
+LAG = 2
+LAST_LAG = 1
+ATTEND_PAIRS = 3
+VMEM_BYTES = 60 * 1024 * 1024
 LOG2_E = math.log2(math.e)
 QUERY_SCALE = HEAD_DIM ** (-0.5) * LOG2_E
 MASKED = -1e30
@@ -305,54 +308,32 @@
     return pl.BlockSpec(shape, lambda *ids: (0,) * len(shape))
 
 
-def swap_blocks_kernel(send_ref, out_ref, send_sem, recv_sem, own_sem):
-    count = send_ref.shape[0]
-    mine = lax.axis_index("blk")
-    group = lax.axis_index("dp")
+def greet_blk(count):
     barrier = pltpu.get_barrier_semaphore()
+    z, index = lax.axis_index("dp"), lax.axis_index("blk")
     for step in range(1, count):
         pl.semaphore_signal(
             barrier,
             inc=1,
-            device_id=(group, lax.rem(mine + step, count)),
+            device_id=(z, lax.rem(index + step, count)),
             device_id_type=pl.DeviceIdType.MESH,
         )
     pl.semaphore_wait(barrier, count - 1)
-    copies = []
-    for step in range(1, count):
-        target = lax.rem(mine + step, count)
-        copy = pltpu.make_async_remote_copy(
-            src_ref=send_ref.at[target],
-            dst_ref=out_ref.at[mine],
-            send_sem=send_sem.at[step],
-            recv_sem=recv_sem.at[step],
-            device_id=(group, target),
-            device_id_type=pl.DeviceIdType.MESH,
-        )
-        copy.start()
-        copies.append(copy)
-    own = pltpu.make_async_copy(send_ref.at[mine], out_ref.at[mine], own_sem)
-    own.start()
-    own.wait()
-    for copy in copies:
-        copy.wait()
-
-
-def swap_blocks(blocks, collective_id):
-    count = blocks.shape[0]
-    return pl.pallas_call(
-        swap_blocks_kernel,
-        name=f"swap_blocks_{collective_id}",
-        out_shape=jax.ShapeDtypeStruct(blocks.shape, blocks.dtype),
-        in_specs=[pl.BlockSpec(memory_space=pl.ANY)],
-        out_specs=pl.BlockSpec(memory_space=pl.ANY),
-        scratch_shapes=[
-            pltpu.SemaphoreType.DMA((count,)),
-            pltpu.SemaphoreType.DMA((count,)),
-            pltpu.SemaphoreType.DMA,
-        ],
-        compiler_params=kernel_params(collective_id=collective_id, has_side_effects=True),
-    )(blocks)
+
+
+def blk_copy(send, got, sent_sem, got_sem, target, source):
+    return pltpu.make_async_remote_copy(
+        src_ref=send.at[target],
+        dst_ref=got.at[source],
+        send_sem=sent_sem.at[target],
+        recv_sem=got_sem.at[source],
+        device_id=(lax.axis_index("dp"), target),
+        device_id_type=pl.DeviceIdType.MESH,
+    )
+
+
+def blk_sems(count):
+    return [pltpu.SemaphoreType.DMA((count,)), pltpu.SemaphoreType.DMA((count,))]
 
 
 def head_means(values):
@@ -384,12 +365,21 @@
     sin_ref,
     hidden_ref,
     proj_ref,
-    send_ref,
+    got_ref,
+    send,
+    got,
+    sent_sem,
+    got_sem,
 ):
     rows = tokens_ref.shape[0]
-
-    @pl.when(pl.program_id(0) == 0)
-    def _():
+    n, chips = pl.program_id(0), pl.num_programs(0)
+    count = send.shape[0]
+    index = lax.axis_index("blk")
+    p = lax.rem(index // 2 + 1 + n, chips)
+
+    @pl.when(n == 0)
+    def _():
+        greet_blk(count)
         inputs = tokens_ref[...].astype(F32)
         scale = lax.rsqrt(jnp.mean(inputs * inputs, axis=-1, keepdims=True) + EPSILON)
         hidden_ref[...] = (inputs * scale * gain_ref[...]).astype(BF16)
@@ -398,8 +388,8 @@
     half = rows // 2
 
     def put(block, lane):
-        send_ref[0, :, lane : lane + LANES] = block[:half]
-        send_ref[1, :, lane : lane + LANES] = block[half:]
+        send[2 * p, :, lane : lane + LANES] = block[:half]
+        send[2 * p + 1, :, lane : lane + LANES] = block[half:]
 
     queries = nn_dot(hidden, wq_ref[...])
     keys = nn_dot(hidden, wk_ref[...])
@@ -414,6 +404,23 @@
         turned = normed * cos_ref[...] + half_partner(normed) * sin_ref[...]
         put((turned * factor).astype(BF16), lane)
     put(values.astype(BF16), q_width + LANES)
+    for part in range(2):
+        target = 2 * p + part
+
+        @pl.when(target != index)
+        def _():
+            blk_copy(send, got, sent_sem, got_sem, target, index).start()
+
+        @pl.when(target == index)
+        def _():
+            got[target] = send[target]
+
+    @pl.when(n == chips - 1)
+    def _():
+        for step in range(1, count):
+            other = lax.rem(index + step, count)
+            blk_copy(send, got, sent_sem, got_sem, other, other).wait()
+        got_ref[...] = got[...]
 
 
 def project(tokens, gain, wq, wk, wv, q_gain, k_gain, cosine, sine):
@@ -421,6 +428,11 @@
     chips = wk.shape[1] // LANES
     q_width = wq.shape[1] // chips
     block_width = q_width + 2 * LANES
+    moved = (2 * chips, rows // 2, block_width)
+
+    def at(n):
+        return lax.rem(lax.axis_index("blk") // 2 + 1 + n, chips)
+
     return pl.pallas_call(
         project_kernel,
         name="project",
@@ -428,9 +440,9 @@
         in_specs=[
             whole_block((rows, width)),
             whole_block((1, width)),
-            pl.BlockSpec((width, q_width), lambda p: (0, p)),
-            pl.BlockSpec((width, LANES), lambda p: (0, p)),
-            pl.BlockSpec((width, LANES), lambda p: (0, p)),
+            pl.BlockSpec((width, q_width), lambda n: (0, at(n))),
+            pl.BlockSpec((width, LANES), lambda n: (0, at(n))),
+            pl.BlockSpec((width, LANES), lambda n: (0, at(n))),
             whole_block((1, LANES)),
             whole_block((1, LANES)),
             whole_block((rows, LANES)),
@@ -438,15 +450,16 @@
         ],
         out_specs=[
             whole_block((rows, width)),
-            pl.BlockSpec((1, rows, q_width + LANES), lambda p: (p, 0, 0)),
-            pl.BlockSpec((2, rows // 2, block_width), lambda p: (p, 0, 0)),
+            pl.BlockSpec((1, rows, q_width + LANES), lambda n: (at(n), 0, 0)),
+            whole_block(moved),
         ],
         out_shape=[
             jax.ShapeDtypeStruct((rows, width), BF16),
             jax.ShapeDtypeStruct((chips, rows, q_width + LANES), F32),
-            jax.ShapeDtypeStruct((2 * chips, rows // 2, block_width), BF16),
+            jax.ShapeDtypeStruct(moved, BF16),
         ],
-        compiler_params=kernel_params(),
+        scratch_shapes=[pltpu.VMEM(moved, BF16), pltpu.VMEM(moved, BF16)] + blk_sems(2 * chips),
+        compiler_params=kernel_params(collective_id=0, has_side_effects=True),
     )(tokens, gain, wq, wk, wv, q_gain, k_gain, cosine, sine)
 
 
@@ -482,13 +495,31 @@
     return jnp.where(lane < 3, -1.0, 0.0).astype(BF16)
 
 
-def attend_kernel(groups, block, qkv_ref, starts_ref, out_ref, logs_ref, keys, values, total):
+def attend_kernel(
+    groups,
+    block,
+    qkv_ref,
+    starts_ref,
+    out_ref,
+    logs_ref,
+    heads_ref,
+    keys,
+    values,
+    total,
+    got,
+    sent_sem,
+    got_sem,
+):
     size = qkv_ref.shape[0]
+    blocks = size // block
     q_width = groups * LANES
-    here = pl.program_id(0)
-
-    @pl.when(here == 0)
-    def _():
+    n = pl.program_id(0)
+    index = lax.axis_index("blk")
+    here = lax.rem(index + 1 + n, blocks)
+
+    @pl.when(n == 0)
+    def _():
+        greet_blk(blocks)
         for g in range(groups):
             keys[g] = doubled(qkv_ref[:, q_width : q_width + LANES], g)
             values[g, :, :LANES] = doubled(qkv_ref[:, q_width + LANES : q_width + 2 * LANES], g)
@@ -499,61 +530,79 @@
     queries = [
         stacked_heads(qkv_ref[pl.ds(at, block), g * LANES : (g + 1) * LANES]) for g in range(groups)
     ]
-    column = lax.broadcasted_iota(jnp.int32, (2 * block, block), 1)
-    row = lax.broadcasted_iota(jnp.int32, (2 * block, block), 0) % block
-
-    def step(j, diagonal):
-        key_at = pl.multiple_of(j * block, block)
+
+    def step(key_at, width, diagonal):
+        column = lax.broadcasted_iota(jnp.int32, (2 * block, width), 1)
         allowed = column >= starts - key_at
         if diagonal:
+            row = lax.broadcasted_iota(jnp.int32, (2 * block, width), 0) % block
             allowed = allowed & (column <= row)
         for g in range(groups):
-            scores = nt_dot(queries[g], keys[g, pl.ds(key_at, block), :])
+            scores = nt_dot(queries[g], keys[g, pl.ds(key_at, width), :])
             weights = jnp.exp2(jnp.where(allowed, scores, MASKED)).astype(BF16)
-            part = nn_dot(weights, values[g, pl.ds(key_at, block), :])
+            part = nn_dot(weights, values[g, pl.ds(key_at, width), :])
             if diagonal:
                 total[g] = part
             else:
                 total[g] += part
 
-    step(here, True)
+    step(at, block, True)
+
+    @pl.when(lax.rem(here, 2) == 1)
+    def _():
+        step(pl.multiple_of((here - 1) * block, block), block, False)
 
     def body(j, carry):
-        step(j, False)
+        step(pl.multiple_of(j * 2 * block, 2 * block), 2 * block, False)
         return carry
 
-    lax.fori_loop(0, here, body, 0)
+    lax.fori_loop(0, here // 2, body, 0)
+    low = low_lanes((block, LANES))
+    to = pl.multiple_of(here * 2 * block, 2 * block)
     for g in range(groups):
         sums = total[g, :, LANES:]
         mean = total[g, :, :LANES] / sums
-        low = low_lanes((block, LANES))
-        out_ref[0, :, g * LANES : (g + 1) * LANES] = jnp.where(low, mean[:block], mean[block:]).astype(BF16)
-        logs_ref[g] = in_three(jnp.log2(sums[:, :1]))
+        out_ref[here, :, g * LANES : (g + 1) * LANES] = jnp.where(low, mean[:block], mean[block:]).astype(BF16)
+        logs_ref[g, pl.ds(to, 2 * block), :] = in_three(jnp.log2(sums[:, :1]))
+
+    @pl.when(here != index)
+    def _():
+        blk_copy(out_ref, got, sent_sem, got_sem, here, index).start()
+
+    @pl.when(n == blocks - 1)
+    def _():
+        got[index] = out_ref[index]
+        for step in range(1, blocks):
+            other = lax.rem(index + step, blocks)
+            blk_copy(out_ref, got, sent_sem, got_sem, other, other).wait()
+        heads_ref[...] = got[...]
 
 
 def attend(qkv, starts, block):
     size, width = qkv.shape
     groups = (width - 2 * LANES) // LANES
     blocks = size // block
+    heads = (blocks, block, groups * LANES)
+    logs = (groups, 2 * size, LANES)
+
+    def keep(shape):
+        return pl.BlockSpec(shape, lambda n: (0,) * len(shape), pipeline_mode=pl.Buffered(1))
+
     return pl.pallas_call(
         functools.partial(attend_kernel, groups, block),
         name="attend",
         grid=(blocks,),
-        in_specs=[whole_block((size, width)), whole_block((size, 1))],
-        out_specs=[
-            pl.BlockSpec((1, block, groups * LANES), lambda i: (i, 0, 0)),
-            pl.BlockSpec((groups, 2 * block, LANES), lambda i: (0, i, 0)),
-        ],
-        out_shape=[
-            jax.ShapeDtypeStruct((blocks, block, groups * LANES), BF16),
-            jax.ShapeDtypeStruct((groups, 2 * size, LANES), BF16),
-        ],
+        in_specs=[keep((size, width)), keep((size, 1))],
+        out_specs=[keep(heads), keep(logs), keep(heads)],
+        out_shape=[jax.ShapeDtypeStruct(shape, BF16) for shape in (heads, logs, heads)],
         scratch_shapes=[
             pltpu.VMEM((groups, size, LANES), BF16),
             pltpu.VMEM((groups, size, 2 * LANES), BF16),
             pltpu.VMEM((groups, 2 * block, 2 * LANES), F32),
-        ],
-        compiler_params=kernel_params(),
+            pltpu.VMEM(heads, BF16),
+        ]
+        + blk_sems(blocks),
+        compiler_params=kernel_params(collective_id=1, has_side_effects=True),
     )(qkv, starts)
 
 
@@ -564,8 +613,10 @@
 
 
 class Stream:
-    def __init__(self, path, dims, block, line, kind=BF16):
-        self.path, self.block, self.line, self.kind = path, block, line, kind
+    def __init__(self, path, dims, block, line, lag, units, kind=BF16):
+        self.path, self.block, self.line, self.lag, self.kind = path, block, line, lag, kind
+        self.units = units
+        self.got_slots = min(2 * lag, units)
         self.dims = [tuple(dims)]
         left = list(dims)
         names = [name for name, unused in dims]
@@ -590,7 +641,13 @@
         return tuple(count for unused, count in dims) + self.block
 
     def slots(self, k):
-        return self.line if self.is_hop(k) else 2
+        return min(((self.line - 1) if self.is_hop(k) else 1) * self.lag + 1, self.units)
+
+    def steps(self):
+        return self.units + self.lag * len(self.path) + 1
+
+    def got_slot(self, u):
+        return lax.rem(u, self.got_slots)
 
     def scratch(self):
         shapes = []
@@ -599,16 +656,16 @@
                 shapes.append(pltpu.VMEM((self.slots(k),) + self.shape(self.dims[k]), self.kind))
             if self.is_hop(k):
                 rest = tuple(d for d in self.dims[k] if d[0] != "z")
-                shapes.append(pltpu.VMEM((2, 2) + self.shape(rest), self.kind))
-                shapes += [pltpu.SemaphoreType.DMA((2, 2))] * 2
+                shapes.append(pltpu.VMEM((self.got_slots, 2) + self.shape(rest), self.kind))
+                shapes += [pltpu.SemaphoreType.DMA((self.got_slots, 2))] * 2
             else:
-                shapes.append(pltpu.VMEM((2,) + self.shape(self.dims[k + 1]), self.kind))
-                shapes += [pltpu.SemaphoreType.DMA((2,))] * 2
+                shapes.append(pltpu.VMEM((self.got_slots,) + self.shape(self.dims[k + 1]), self.kind))
+                shapes += [pltpu.SemaphoreType.DMA((self.got_slots,))] * 2
         return shapes
 
-    def bind(self, refs, units, finish, first_z=None):
+    def bind(self, refs, finish, first_z=None, begin=0):
         refs = list(refs)
-        self.units, self.finish = units, finish
+        self.finish, self.begin = finish, begin
         self.first_z = 0 if first_z is None else first_z
         self.work, self.got, self.sent_sem, self.got_sem = [], [], [], []
         for k in range(len(self.path)):
@@ -635,7 +692,7 @@
         mine, partner = pair_of(bit)
         at = [name for name, unused in self.dims[k]].index(bit)
         whole = (slice(None),) * at
-        slot = lax.rem(u, 2)
+        slot = self.got_slot(u)
         copy = pltpu.make_async_remote_copy(
             src_ref=self.work[k].at[(lax.rem(u, self.slots(k)),) + whole + (1 - mine,)],
             dst_ref=self.got[k].at[slot],
@@ -648,7 +705,7 @@
 
     def hop_copy(self, k, u, way, block):
         z, index = lax.axis_index("dp"), lax.axis_index("blk")
-        slot = lax.rem(u, 2)
+        slot = self.got_slot(u)
         side = (1 - way) // 2
         return pltpu.make_async_remote_copy(
             src_ref=self.work[k].at[lax.rem(u, self.slots(k)), block],
@@ -668,7 +725,7 @@
         return goes - self.first_z, sends, comes - self.first_z, takes
 
     def send(self, k, step):
-        u = step - k - 1
+        u = step - self.begin - self.lag * k - 1
         due = (u >= 0) & (u < self.units)
         if not self.is_hop(k):
             keeper = self.keeper(k)
@@ -686,7 +743,7 @@
                 self.hop_copy(k, u, way, block).start()
 
     def take(self, k, step):
-        u = step - k - 2
+        u = step - self.begin - self.lag * (k + 1) - 1
         due = (u >= 0) & (u < self.units)
         keeper = self.keeper(k + 1)
         last = k == len(self.path) - 1
@@ -705,7 +762,7 @@
                 copy, mine = self.pair_copy(k, u)
                 copy.wait()
                 own = self.work[k][(lax.rem(u, self.slots(k)),) + mine]
-                pass_on(own + self.got[k][lax.rem(u, 2)])
+                pass_on(own + self.got[k][self.got_slot(u)])
 
             return
         slot = lax.rem(u, self.slots(k))
@@ -719,7 +776,7 @@
             @pl.when(due & takes)
             def _():
                 self.hop_copy(k, u, way, in_block).wait_recv()
-                self.work[k][slot, in_block] += self.got[k][lax.rem(u, 2), (1 - way) // 2]
+                self.work[k][slot, in_block] += self.got[k][self.got_slot(u), (1 - way) // 2]
 
         if self.path[k][1] == self.line - 1:
             own = lax.axis_index("dp") - self.first_z
@@ -825,8 +882,6 @@
     up_out_ref,
     hidden,
     flipped,
-    dy,
-    middle,
     out_sum,
     back_sum,
     gate_grads,
@@ -871,7 +926,7 @@
     at = 0
     for stream, finish in zip(streams, (finish_gate, finish_up, finish_both)):
         count = len(stream.scratch())
-        stream.bind(refs[at : at + count], units, finish)
+        stream.bind(refs[at : at + count], finish)
         at += count
 
     def hidden_copy():
@@ -916,12 +971,10 @@
         for p in range(chips):
             block = jnp.concatenate([heads_ref[2 * p], heads_ref[2 * p + 1]], axis=0)
             total = total + nn_dot(block, w_out_ref[p * head_lanes : (p + 1) * head_lanes, :])
-        middle[...] = total
+        mid_ref[...] = total
         scale = lax.rsqrt(jnp.mean(total * total, axis=-1, keepdims=True) + EPSILON)
         hidden[own] = (total * scale * gain_ref[...]).astype(BF16)
         hidden_copy().start()
-        dy[own] = dy_own_ref[...]
-        dy[other] = dy_got_ref[...]
         out_sum[...] = jnp.zeros_like(out_sum)
         back_sum[...] = jnp.zeros_like(back_sum)
         flip(0)
@@ -939,7 +992,9 @@
             part = slice(m * chunk, (m + 1) * chunk)
             gate = nn_dot(hidden[part, :], w_gate_ref[...])
             up = nn_dot(hidden[part, :], w_up_ref[...])
-            pushed = nt_dot(dy[part, :], w_down_ref[...])
+            at = m * chunk % own_rows
+            dy_ref = dy_own_ref if m * chunk < own_rows else dy_got_ref
+            pushed = nt_dot(dy_ref[at : at + chunk, :], w_down_ref[...])
             opened = jax.nn.sigmoid(gate)
             silu = gate * opened
             act = (silu * up).astype(BF16)
@@ -951,13 +1006,14 @@
             out_sum[part, :] += nn_dot(act, w_down_ref[...])
             back_sum[part, :] += nt_dot(gate_grad, w_gate_ref[...]) + nt_dot(up_grad, w_up_ref[...])
         u = n - 1
-        slot, long_slot = lax.rem(u, 2), lax.rem(u, both_stream.slots(0))
+        slot, long_slot = lax.rem(u, gate_stream.slots(0)), lax.rem(u, both_stream.slots(0))
         each = width // line
         shape = gate_stream.shape(gate_stream.dims[0])[1:-2] + (-1, FF_TILE)
         for m in range(line):
             part = slice(m * each, (m + 1) * each)
-            gate_part = nn_dot(flipped[part, :], gate_grads[...]).astype(BF16).reshape(shape)
-            up_part = nn_dot(flipped[part, :], up_grads[...]).astype(BF16).reshape(shape)
+            gate_part = nn_dot(flipped[part, :], gate_grads[...]).astype(BF16)
+            up_part = nn_dot(flipped[part, :], up_grads[...]).astype(BF16)
+            gate_part, up_part = gate_part.reshape(shape), up_part.reshape(shape)
             gate_stream.source[slot, m] = gate_part[..., :gate_rows, :]
             up_stream.source[slot, m] = up_part[..., :gate_rows, :]
             both_stream.source[long_slot, m, ..., :FF_TILE] = gate_part[..., gate_rows:, :]
@@ -973,17 +1029,17 @@
     @pl.when(n == units + 1)
     def _():
         part_copy(0).wait()
-        values = middle[...]
+        values = mid_ref[...]
         scale = lax.rsqrt(jnp.mean(values * values, axis=-1, keepdims=True) + EPSILON)
         normal = values * scale
         back = back_sum[own] + part_got[0].astype(F32)
         gain_grad_ref[...] = jnp.sum(back * normal, axis=0, keepdims=True)
         pushed = back * gain_ref[...]
         inner = jnp.mean(pushed * normal, axis=-1, keepdims=True)
-        mid = dy[own].astype(F32) + scale * (pushed - normal * inner)
+        mid = dy_own_ref[...].astype(F32) + scale * (pushed - normal * inner)
+        part_copy(1).wait()
         mid_ref[...] = mid
         low_grad[...] = mid.astype(BF16)
-        part_copy(1).wait()
         output_ref[...] = (values + (out_sum[own] + part_got[1].astype(F32))).astype(BF16)
 
     @pl.when((n > units + 1) & (n <= units + 1 + chips))
@@ -1018,6 +1074,16 @@
         grad_heads_ref[...] = do_got[...]
 
 
+def column_streams(line, bits, each, units):
+    late = each // 4
+    dims = [("z", line)] + [(bit, 2) for bit in bits]
+    return [
+        Stream(bits[::-1] + hops(line), dims, (each - late, FF_TILE), line, LAG, units),
+        Stream(bits + hops(line), dims, (each - late, FF_TILE), line, LAG, units),
+        Stream(hops(line) + bits, dims, (late, 2 * FF_TILE), line, LAG, units),
+    ]
+
+
 def middle_layer(line, bits, tokens, heads, w_out, gain, dy_own, dy_got, w_gate, w_up, w_down):
     own_rows, width = tokens.shape
     rows = 2 * own_rows
@@ -1025,14 +1091,8 @@
     units = w_gate.shape[1] // 2 // FF_TILE
     chips = line * 2 ** len(bits)
     each = width // chips
-    late = each // 4
-    dims = [("z", line)] + [(bit, 2) for bit in bits]
-    streams = [
-        Stream(bits[::-1] + hops(line), dims, (each - late, FF_TILE), line),
-        Stream(bits + hops(line), dims, (each - late, FF_TILE), line),
-        Stream(hops(line) + bits, dims, (late, 2 * FF_TILE), line),
-    ]
-    steps = max(units + 2 + max(len(stream.path) for stream in streams), units + 3 + blk_count // 2)
+    streams = column_streams(line, bits, each, units)
+    steps = max([1 + stream.steps() for stream in streams] + [units + 3 + blk_count // 2])
 
     def keep(shape):
         return pl.BlockSpec(shape, lambda n: (0,) * len(shape), pipeline_mode=pl.Buffered(1))
@@ -1046,8 +1106,6 @@
     scratch = [
         pltpu.VMEM((rows, width), BF16),
         pltpu.VMEM((width, rows), BF16),
-        pltpu.VMEM((rows, width), BF16),
-        pltpu.VMEM((own_rows, width), F32),
         pltpu.VMEM((rows, width), F32),
         pltpu.VMEM((rows, width), F32),
         pltpu.VMEM((rows, FF_TILE), BF16),
@@ -1115,14 +1173,20 @@
     dy_own_ref,
     dy_got_ref,
     acts_ref,
-    result_ref,
+    w_out_parts_ref,
+    moved_ref,
     down_out_ref,
+    w_out_ref,
     queries,
     keys,
     values,
     grads,
     query_grad,
     pair_grad,
+    result,
+    moved,
+    sent_sem,
+    got_sem,
     ready,
     *refs,
 ):
@@ -1130,27 +1194,54 @@
     blocks = size // block
     q_width = groups * LANES
     n = pl.program_id(0)
-    core = lax.rem(lax.axis_index("blk"), 2)
-    half = down_out_ref.shape[1] // 2
-
-    def finish_low(u, value):
-        rows = value.shape[0]
-        down_out_ref[pl.ds(pl.multiple_of(u * rows, rows), rows), :half] = value
-
-    def finish_high(u, value):
-        rows = value.shape[0]
-        down_out_ref[pl.ds(pl.multiple_of(u * rows, rows), rows), half:] = value
+    index = lax.axis_index("blk")
+    core = lax.rem(index, 2)
+
+    def move(target, source):
+        return pltpu.make_async_remote_copy(
+            src_ref=result.at[target],
+            dst_ref=moved.at[source],
+            send_sem=sent_sem.at[target],
+            recv_sem=got_sem.at[source],
+            device_id=(lax.axis_index("dp"), target),
+            device_id_type=pl.DeviceIdType.MESH,
+        )
+
+    low_half = streams[0].block[1]
+    mid_half = low_half + streams[1].block[1]
+
+    def finish_down(lanes):
+        def put(u, value):
+            rows = value.shape[0]
+            down_out_ref[pl.ds(pl.multiple_of(u * rows, rows), rows), lanes] = value
+
+        return put
+
+    def finish_w_out(u, value):
+        w_out_ref[:, pl.ds(pl.multiple_of(u * LANES, LANES), LANES)] = value
 
     at = 0
-    for stream, finish in zip(streams, (finish_low, finish_high)):
-        count = len(stream.scratch())
-        stream.bind(refs[at : at + count], units, finish, core * (line // 2))
-        at += count
+    columns = w_out_ref.shape[1] // LANES
+    first_z = core * (line // 2)
+    for stream, finish, first, begin in (
+        (streams[0], finish_down(slice(0, low_half)), first_z, 0),
+        (streams[1], finish_down(slice(low_half, mid_half)), first_z, 0),
+        (streams[2], finish_down(slice(mid_half, None)), first_z, 0),
+        (streams[3], finish_w_out, None, 0),
+    ):
+        size_of = len(stream.scratch())
+        stream.bind(refs[at : at + size_of], finish, first, begin)
+        at += size_of
 
     @pl.when(n == 0)
     def _():
-        greet(bits, line)
+        greet_all(blocks, line)
         down_out_ref[...] = jnp.zeros_like(down_out_ref)
+
+    step_streams(streams, n, pl.num_programs(0), line, ready)
+
+    @pl.when(n == 1)
+    def _():
         query_grad[...] = jnp.zeros_like(query_grad)
         pair_grad[...] = jnp.zeros_like(pair_grad)
         for g in range(groups):
@@ -1174,26 +1265,36 @@
 
             lax.fori_loop(0, blocks, fill, 0)
 
-    step_streams(streams, n, pl.num_programs(0), line, ready)
-
     @pl.when(n < units)
     def _():
         acts = acts_ref[...].reshape(-1, acts_ref.shape[-1])
         rows = dy_own_ref.shape[0]
         made = nn_dot(acts[:, :rows], dy_own_ref[...]) + nn_dot(acts[:, rows:], dy_got_ref[...])
         made = made.astype(BF16)
-        for stream, part in zip(streams, (made[:, :half], made[:, half:])):
+        parts = (made[:, :low_half], made[:, low_half:mid_half], made[:, mid_half:])
+        for stream, part in zip(streams[:3], parts):
             shape = stream.shape(stream.dims[0])
             stream.source[lax.rem(n, stream.slots(0))] = part.reshape(shape)
 
+    @pl.when(n < columns)
+    def _():
+        stream = streams[3]
+        part = w_out_parts_ref[...].reshape(stream.shape(stream.dims[0]))
+        stream.source[lax.rem(n, stream.slots(0))] = part
+
     row = lax.broadcasted_iota(jnp.int32, (block, 2 * block), 0)
     column = lax.broadcasted_iota(jnp.int32, (block, 2 * block), 1) % block
 
-    turn = n - (pl.num_programs(0) - blocks - 2)
-
-    @pl.when((turn >= 0) & (turn < blocks + 1))
-    def _():
-        def pair(m, carry):
+    pairs = (blocks + 1) * (blocks // 2)
+    each = ATTEND_PAIRS
+    rounds = pairs // each
+
+    @pl.when((n >= 1) & (n <= rounds))
+    def _():
+        def pair(at, carry):
+            place = (n - 1) * each + at
+            turn = place // (blocks // 2)
+            m = lax.rem(place, blocks // 2)
             late = (turn + m) // blocks
             j = m + late * (blocks - 1 - 2 * m)
             i = (1 - late) * (m + turn) + late * (turn - 1)
@@ -1214,9 +1315,9 @@
                 query_grad[g, stack, :] += tn_dot(pushed, key[:, :LANES])
             return carry
 
-        lax.fori_loop(0, blocks // 2, pair, 0)
-
-    @pl.when(turn == blocks + 1)
+        lax.fori_loop(0, each, pair, 0, unroll=True)
+
+    @pl.when(n == rounds + 1)
     def _():
         low = low_lanes((block, LANES))
 
@@ -1228,7 +1329,7 @@
                 first = query_grad[g, pl.ds(to, block), :]
                 second = query_grad[g, pl.ds(to + block, block), :]
                 joined = jnp.where(low, first, second) * HEAD_DIM ** (-0.5)
-                result_ref[here, g * LANES : (g + 1) * LANES] = joined.astype(BF16)
+                result[i, :, g * LANES : (g + 1) * LANES] = joined.astype(BF16)
             for part in range(2):
                 sums = []
                 for g in range(groups):
@@ -1238,13 +1339,23 @@
                 if part == 0:
                     joined = joined * (1.0 / LOG2_E)
                 lane = q_width + part * LANES
-                result_ref[here, lane : lane + LANES] = joined.astype(BF16)
+                result[i, :, lane : lane + LANES] = joined.astype(BF16)
             return carry
 
         lax.fori_loop(0, blocks, finish, 0)
-
-
-def back(line, bits, qkv, logs, out, grad, starts, block, dy_own, dy_got, acts):
+        for step in range(blocks - 1, 0, -1):
+            move(lax.rem(index + step, blocks), index).start()
+        moved[index] = result[index]
+
+    @pl.when(n == pl.num_programs(0) - 1)
+    def _():
+        for step in range(1, blocks):
+            other = lax.rem(index + step, blocks)
+            move(other, other).wait()
+        moved_ref[...] = moved[...]
+
+
+def back(line, bits, qkv, logs, out, grad, starts, block, dy_own, dy_got, acts, w_out_parts):
     size, width = qkv.shape
     groups = (width - 2 * LANES) // LANES
     model = dy_own.shape[1]
@@ -1252,14 +1363,28 @@
     units = acts.shape[0] // FF_TILE
     chips = line * 2 ** len(bits)
     down_rows = acts.shape[0] // (chips // 2)
-    down_block = (down_rows // units, model // 2)
+    down_each = down_rows // units
     dims = [("z", line // 2)] + [(bit, 2) for bit in bits]
+    quarter = model // 4
+    w_rows = w_out_parts.shape[0] // chips // 2
+    columns = w_out_parts.shape[1] // LANES
     streams = [
-        Stream(hops(line) + bits[::-1], dims, down_block, line),
-        Stream(bits + hops(line), dims, down_block, line),
+        Stream(hops(line) + bits[::-1], dims, (down_each, quarter), line, LAG, units),
+        Stream(bits + hops(line), dims, (down_each, quarter * 3 // 2), line, LAG, units),
+        Stream(bits[::-1] + hops(line), dims, (down_each, quarter * 3 // 2), line, LAG, units),
+        Stream(
+            [1] + bits[::-1] + hops(line),
+            [("z", line)] + [(bit, 2) for bit in bits] + [(1, 2)],
+            (w_rows, LANES),
+            line,
+            LAG,
+            columns,
+        ),
     ]
-    longest = max(len(stream.path) for stream in streams)
-    steps = max(units + longest + 1, size // block + 2)
+    steps = max(
+        [stream.steps() for stream in streams]
+        + [(size // block + 1) * (size // block // 2) // ATTEND_PAIRS + 3]
+    )
 
     def keep(shape):
         return pl.BlockSpec(shape, lambda n: (0,) * len(shape), pipeline_mode=pl.Buffered(1))
@@ -1272,10 +1397,20 @@
         pltpu.VMEM((groups, 2 * size, 2 * LANES), BF16),
         pltpu.VMEM((groups, 2 * size, LANES), F32),
         pltpu.VMEM((groups, size, 2 * LANES), F32),
+        pltpu.VMEM((size // block, block, width), BF16),
+        pltpu.VMEM((size // block, block, width), BF16),
+        pltpu.SemaphoreType.DMA((size // block,)),
+        pltpu.SemaphoreType.DMA((size // block,)),
         pltpu.SemaphoreType.REGULAR((2,)),
     ]
     for stream in streams:
         scratch += stream.scratch()
+
+    outs = [
+        (size // block, block, width),
+        (down_rows, model),
+        (w_rows, w_out_parts.shape[1]),
+    ]
     return pl.pallas_call(
         functools.partial(back_kernel, groups, block, line, bits, streams, units),
         name="back",
@@ -1289,17 +1424,15 @@
             keep(dy_own.shape),
             keep(dy_got.shape),
             pl.BlockSpec(
-                (chips // 2, down_block[0], rows), lambda n: (0, jnp.minimum(n, units - 1), 0)
+                (chips // 2, down_each, rows), lambda n: (0, jnp.minimum(n, units - 1), 0)
             ),
+            pl.BlockSpec((w_out_parts.shape[0], LANES), lambda n: (0, jnp.minimum(n, columns - 1))),
         ],
-        out_specs=[keep(qkv.shape), keep((down_rows, model))],
-        out_shape=[
-            jax.ShapeDtypeStruct(qkv.shape, BF16),
-            jax.ShapeDtypeStruct((down_rows, model), BF16),
-        ],
+        out_specs=[keep(shape) for shape in outs],
+        out_shape=[jax.ShapeDtypeStruct(shape, BF16) for shape in outs],
         scratch_shapes=scratch,
         compiler_params=kernel_params(collective_id=4, has_side_effects=True),
-    )(qkv, logs, out, grad, starts, dy_own, dy_got, acts)
+    )(qkv, logs, out, grad, starts, dy_own, dy_got, acts, w_out_parts)
 
 
 def sum_gains(rounds, n, first, gains, gains_got, sent_sem, got_sem):
@@ -1352,7 +1485,6 @@
     k_gain_ref,
     cos_ref,
     sin_ref,
-    w_out_parts_ref,
     ffn_gain_ref,
     gate_ref,
     up_ref,
@@ -1362,7 +1494,6 @@
     gq_ref,
     gk_ref,
     gv_ref,
-    go_ref,
     gate_out_ref,
     up_out_ref,
     down_out_ref,
@@ -1382,22 +1513,21 @@
     z, index = lax.axis_index("dp"), lax.axis_index("blk")
     core, sibling = pair_of(1)
     steps = pl.num_programs(0)
-    qkv_stream, out_stream = streams
+    query_stream, pair_stream = streams
     q_width = wq_ref.shape[1]
 
-    def finish_qkv(u, value):
-        gq_ref[:, pl.ds(pl.multiple_of(u * q_width, q_width), q_width)] = value[:, :q_width]
+    def finish_query(u, value):
+        gq_ref[:, pl.ds(pl.multiple_of(u * q_width, q_width), q_width)] = value
+
+    def finish_pair(u, value):
         here = pl.ds(pl.multiple_of(u * LANES, LANES), LANES)
-        gk_ref[:, here] = value[:, q_width : q_width + LANES]
-        gv_ref[:, here] = value[:, q_width + LANES :]
-
-    def finish_out(u, value):
-        go_ref[:, pl.ds(pl.multiple_of(u * q_width, q_width), q_width)] = value
+        gk_ref[:, here] = value[:, :LANES]
+        gv_ref[:, here] = value[:, LANES:]
 
     at = 0
-    for stream, finish in ((qkv_stream, finish_qkv), (out_stream, finish_out)):
+    for stream, finish in ((query_stream, finish_query), (pair_stream, finish_pair)):
         count = len(stream.scratch())
-        stream.bind(refs[at : at + count], units, finish)
+        stream.bind(refs[at : at + count], finish)
         at += count
 
     rounds = [pair_of(bit)[1] for bit in (1,) + tuple(bits)]
@@ -1503,13 +1633,10 @@
         value = jnp.concatenate(
             [got_ref[0, :, lane : lane + LANES], got_ref[1, :, lane : lane + LANES]], axis=0
         )
-        slot = lax.rem(n, 2)
-        shape = qkv_stream.shape(qkv_stream.dims[0])
-        whole = (slot,) + (slice(None),) * (len(shape) - 1)
-        both = jnp.concatenate([query, key, value], axis=1)
-        made = tn_dot(hidden, both).astype(BF16)
-        qkv_stream.source[whole] = made.reshape(shape)
-        out_stream.source[slot] = w_out_parts_ref[...].reshape(out_stream.shape(out_stream.dims[0]))
+        for stream, part in ((query_stream, query), (pair_stream, jnp.concatenate([key, value], axis=1))):
+            shape = stream.shape(stream.dims[0])
+            stream.source[lax.rem(n, stream.slots(0))] = tn_dot(hidden, part).astype(BF16).reshape(shape)
+
         total[...] += (
             nt_dot(query, wq_ref[...]) + nt_dot(key, wk_ref[...]) + nt_dot(value, wv_ref[...])
         )
@@ -1546,7 +1673,6 @@
     k_gain,
     cosine,
     sine,
-    w_out_parts,
     ffn_gain,
     gate_sum,
     up_sum,
@@ -1561,11 +1687,11 @@
     dims = [("z", line)] + sides + [(1, 2)]
     mine = width // chips // 2
     streams = [
-        Stream([1] + bits[::-1] + hops(line), dims, (mine, lanes), line),
-        Stream([1] + bits + hops(line), dims, (mine, q_width), line),
+        Stream([1] + bits[::-1] + hops(line), dims, (mine, q_width), line, LAST_LAG, units),
+        Stream([1] + bits + hops(line), dims, (mine, 2 * LANES), line, LAST_LAG, units),
     ]
     rounds = 1 + len(bits) + (line - 1).bit_length()
-    steps = units + max(len(stream.path) for stream in streams) + 1
+    steps = max([stream.steps() for stream in streams] + [units + rounds + 2])
     gain_rows = -(-(2 * width // LANES + 2) // 8) * 8
     half_rows = gate_sum.shape[0] // 2
     down_rows = down_sum.shape[0] // 2
@@ -1597,7 +1723,6 @@
         ((mine, wq.shape[1]), BF16),
         ((mine, wk.shape[1]), BF16),
         ((mine, wv.shape[1]), BF16),
-        ((mine, width), BF16),
         ((half_rows, 2 * columns), BF16),
         ((half_rows, 2 * columns), BF16),
         ((down_rows, down_sum.shape[1]), BF16),
@@ -1620,7 +1745,6 @@
             keep((1, LANES)),
             keep((rows, LANES)),
             keep((rows, LANES)),
-            pl.BlockSpec((width, q_width), lambda n: (0, at(n))),
             keep((1, width)),
             keep(gate_sum.shape),
             keep(up_sum.shape),
@@ -1644,12 +1768,26 @@
         k_gain,
         cosine,
         sine,
-        w_out_parts,
         ffn_gain,
         gate_sum,
         up_sum,
         down_sum,
     )
+
+
+def widen_kernel(*refs):
+    count = len(refs) // 2
+    for source, target in zip(refs[:count], refs[count:]):
+        target[...] = source[...].astype(F32)
+
+
+def widen(parts):
+    return pl.pallas_call(
+        widen_kernel,
+        name="widen",
+        out_shape=[jax.ShapeDtypeStruct(part.shape, F32) for part in parts],
+        compiler_params=kernel_params(),
+    )(*parts)
 
 
 def flip_pairs(count, bit):
@@ -1710,12 +1848,11 @@
     grad_own = cotangent.reshape(rows, width)
     grad_got = swap_core(grad_own, blk_count)
 
-    hidden_in, proj, send = project(
+    hidden_in, proj, qkv = project(
         flat, g_attn[None], w_query, w_key, w_value, q_gain2, k_gain2, cosine, sine
     )
-    qkv = swap_blocks(send, 0).reshape(size, -1)
-    attended, logs = attend(qkv, starts[:, None], tok_count)
-    heads = swap_blocks(attended, 1)
+    qkv = qkv.reshape(size, -1)
+    attended, logs, heads = attend(qkv, starts[:, None], tok_count)
     output, mid, ffn_gain_grad, w_out_parts, grad_heads, acts, gate_sum, up_sum = middle_layer(
         dp_count,
         bits,
@@ -1729,7 +1866,7 @@
         w_up,
         w_down,
     )
-    qkv_grad, down_sum = back(
+    got, down_sum, w_out_sum = back(
         dp_count,
         bits,
         qkv,
@@ -1741,8 +1878,8 @@
         grad_own,
         grad_got,
         acts,
-    )
-    got = swap_blocks(qkv_grad.reshape(blk_count, tok_count, -1), 3)
+        w_out_parts,
+    )
     input_grad, gains, *sums = finish(
         dp_count,
         bits,
@@ -1759,15 +1896,13 @@
         k_gain2,
         cosine,
         sine,
-        w_out_parts,
         ffn_gain_grad,
         gate_sum,
         up_sum,
         down_sum,
     )
-    grad_w_query, grad_w_key, grad_w_value, grad_w_out, grad_w_gate, grad_w_up, grad_w_down = [
-        part.astype(F32) for part in sums
-    ]
+    sums = widen(sums + [w_out_sum])
+    grad_w_query, grad_w_key, grad_w_value, grad_w_gate, grad_w_up, grad_w_down, grad_w_out = sums
     lines = width // LANES
     gain_attn = gains[:lines].reshape(width)
     gain_ffn = gains[lines : 2 * lines].reshape(width)

time: 404 us -> 342 us (0.85)
  Pallas kernels: 375 us -> 324 us
  other arithmetic: 16.8 us -> 6.38 us
    pallas_call x3 -> x1, Pallas kernels: 66.1 us -> 2.54 us  [widen(): pl.pallas_call(widen_kernel, name='widen', out_shape=[jax.ShapeDtypeStruc...]
    pallas_call x1, Pallas kernels: 8.54 us -> 32.3 us  [project(): pl.pallas_call(project_kernel, name='project', grid=(chips,), in_specs=[w...]
    pallas_call x1, Pallas kernels: 64.5 us -> 47.8 us  [finish(): pl.pallas_call(functools.partial(finish_kernel, line, bits, streams, unit...]
    convert_element_type x7 -> x0, other arithmetic: 10.4 us -> none  [fast_local(): part.astype(F32)]
    pallas_call x1, Pallas kernels: 92.1 us -> 98.3 us  [back(): pl.pallas_call(functools.partial(back_kernel, groups, block, line, bits,...]
  transfers between devices with their start and end apart: 1 -> 1, of which waited for: 0 -> 0; matrix products, arithmetic and copies ran while one was open for 3% -> 3% of each run, Pallas kernels for 19% -> 18%
where the time goes in v5:
time: 342 us
  Pallas kernels  324 us (95%)
  local copies, waits for them, and re-layouts  10 us (3%)
  other arithmetic  6.38 us (2%)
    pallas_call x1, Pallas kernels, middle_layer(): pl.pallas_call(functools.partial(middle_kernel, line, bits, streams, unit...  115 us
    pallas_call x1, Pallas kernels, back(): pl.pallas_call(functools.partial(back_kernel, groups, block, line, bits,...  98.3 us
    pallas_call x1, Pallas kernels, finish(): pl.pallas_call(functools.partial(finish_kernel, line, bits, streams, unit...  47.8 us
    pallas_call x1, Pallas kernels, project(): pl.pallas_call(project_kernel, name='project', grid=(chips,), in_specs=[w...  32.3 us
    pallas_call x1, Pallas kernels, attend(): pl.pallas_call(functools.partial(attend_kernel, groups, block), name='att...  28.9 us
  transfers between devices with their start and end apart: 1, of which 0 were waited for; matrix products, arithmetic and copies ran while one was open for 3% of the time, Pallas kernels for 18%

profile of v5, /device:TPU:0, one launch (start us, length us, event | category | flops | bytes accessed | tf_op | source)
XLA Modules:
  0.0 342.0 jit_solution(3121031804774546692)
XLA Ops:
  1.2 0.7 fusion.1
  1.8 0.7 constant_dynamic-slice_fusion
  2.5 0.9 reduce_window_sum.22
  3.6 0.7 tile.8
  4.2 0.6 broadcast_in_dim_tile.6.q_gain_ref
  4.8 0.7 tile.9
  5.5 0.6 broadcast_in_dim_tile.7.k_gain_ref
  6.1 0.8 select_reduce_fusion.1
  7.0 0.6 reshape.229.starts_ref
  7.6 1.0 fusion
  8.8 0.8 copy.37.cos_ref
  10.0 1.0 pad_maximum_fusion.sin_ref
  10.9 32.3 %project.1 = (bf16[512,1024]{1,0:T(8,128)(2,1)}, f32[4,512,384]{2,1,0:T(8,128)}, bf16[8,256,512]{2,1,0:T(8,128)(2,1)}) custom-call(bf16[512,1024]{1,0:T(8,128)(2,1)} %bitcast.26, f32[1,1024]{1,0:T(1,128)} %bitcast.41, bf16[1024,1024]{1,0:T(8,128)(2,1)} %wq_ref.3, bf16[1024,512]{1,0:T(8,128)(2,1)} %wk_ref.3, bf16[1024,512]{1,0:T(8,128)(2,1)} %wv_ref.3, ...), custom_call_target="tpu_custom_call" | custom-call | tf_op jit(solution)/shard_map/project/pallas_call | solution.py:436
  43.2 1.1 subtract_subtract_fusion.starts_ref
  44.3 28.9 %attend.1 = (bf16[8,256,256]{2,1,0:T(8,128)(2,1)}, bf16[2,4096,128]{2,1,0:T(8,128)(2,1)}, bf16[8,256,256]{2,1,0:T(8,128)(2,1)}) custom-call(bf16[2048,512]{1,0:T(8,128)(2,1)} %bitcast.29, s32[2048,1]{1,0:T(8,128)} %subtract_subtract_fusion.starts_ref), custom_call_target="tpu_custom_call" | custom-call | tf_op jit(solution)/shard_map/attend/pallas_call | solution.py:591
  73.2 1.0 copy-done
  74.2 114.5 %middle.1 = (bf16[512,1024]{1,0:T(8,128)(2,1)}, f32[512,1024]{1,0:T(8,128)}, f32[1,1024]{1,0:T(1,128)}, bf16[1024,1024]{1,0:T(8,128)(2,1)}, bf16[8,256,256]{2,1,...) custom-call(bf16[512,1024]{1,0:T(8,128)(2,1)} %bitcast.27, ...), custom_call_target="tpu_custom_call" | custom-call | tf_op jit(solution)/shard_map/middle/pallas_call | solution.py:1139
  188.7 98.3 %back.1 = (bf16[8,256,512]{2,1,0:T(8,128)(2,1)}, bf16[288,1024]{1,0:T(8,128)(2,1)}, bf16[32,1024]{1,0:T(8,128)(2,1)}) custom-call(bf16[2048,512]{1,0:T(8,128)(2,1)} %bitcast.30, bf16[2,4096,128]{2,1,0:T(8,128)(2,1)} %get-tuple-element.48.logs_ref, bf16[2048,256]{1,0:T(8,128)(2,1)} %bitcast.35, bf16[2048,256]{1,0:T(8,128)(2,1)} %bitcast.36, ...), custom_call_target="tpu_custom_call" | custom-call | tf_op jit(solution)/shard_map/back/pallas_call | solution.py:1414
  287.0 47.8 %finish.1 = (bf16[512,1024]{1,0:T(8,128)(2,1)}, f32[24,128]{1,0:T(8,128)}, bf16[32,1024]{1,0:T(8,128)(2,1)}, bf16[32,512]{1,0:T(8,128)(2,1)}, bf16[32,512]{1,0:T...) custom-call(bf16[8,256,512]{2,1,0:T(8,128)(2,1)} %get-tuple-element.53.got_ref, ...), custom_call_target="tpu_custom_call" | custom-call | tf_op jit(solution)/shard_map/finish/pallas_call | solution.py:1730
  334.8 1.4 add_bitcast_fusion
  336.3 1.3 slice_bitcast_fusion
  337.5 2.5 widen.1
  340.1 1.0 copy.43
  341.1 1.0 copy.44
  (19 shorter events, 1.3 us)
Async XLA Ops:
  0.6 72.6 %collective-permute-start = (bf16[512,1024]{1,0:T(8,128)(2,1)}, bf16[512,1024]{1,0:T(8,128)(2,1)S(1)}, u32[]{:S(2)}, u32[]{:S(2)}) collective-permute-start(bf16[512,1024]{1,0:T(8,128)(2,1)} %bitcast.32), channel_id=1, source_target_pairs={{0,1},{1,0},{2,3},{3,2},{4,5},{5,4},{6,7},{7,6},{8,9},{9,8},{10,11... | collective-permute-start | bytes 3145736 | tf_op jit(solution)/shard_map/ppermute | solution.py:1798
  73.2 1.0 copy-start
  287.0 53.1 %copy-start.1 = (bf16[512,1024]{1,0:T(8,128)(2,1)S(1)}, bf16[512,1024]{1,0:T(8,128)(2,1)}, u32[]{:S(2)}) copy-start(bf16[512,1024]{1,0:T(8,128)(2,1)} %get-tuple-element.47) | copy-start | bytes 3145732
  334.8 6.2 %copy-start.2 = (bf16[512,1024]{1,0:T(8,128)(2,1)S(1)}, bf16[512,1024]{1,0:T(8,128)(2,1)}, u32[]{:S(2)}) copy-start(bf16[512,1024]{1,0:T(8,128)(2,1)} %get-tuple-element.61) | copy-start | bytes 3145732

commit v6 on v5

--- a/solution.py
+++ b/solution.py
@@ -281,7 +281,7 @@
 FF_TILE = 256
 LAG = 2
 LAST_LAG = 1
-ATTEND_PAIRS = 3
+ATTEND_PAIRS = 6
 VMEM_BYTES = 60 * 1024 * 1024
 LOG2_E = math.log2(math.e)
 QUERY_SCALE = HEAD_DIM ** (-0.5) * LOG2_E
@@ -606,256 +606,110 @@
     )(qkv, starts)
 
 
-def pair_of(bit):
-    index = lax.axis_index("blk")
-    mine = lax.rem(index // bit, 2)
-    return mine, (lax.axis_index("dp"), index + bit * (1 - 2 * mine))
+def pair_of(name):
+    z, index = lax.axis_index("dp"), lax.axis_index("blk")
+    if isinstance(name, tuple):
+        mine = lax.rem(z // name[1], 2)
+        return mine, (z + name[1] * (1 - 2 * mine), index)
+    mine = lax.rem(index // name, 2)
+    return mine, (z, index + name * (1 - 2 * mine))
 
 
 class Stream:
-    def __init__(self, path, dims, block, line, lag, units, kind=BF16):
-        self.path, self.block, self.line, self.lag, self.kind = path, block, line, lag, kind
-        self.units = units
-        self.got_slots = min(2 * lag, units)
-        self.dims = [tuple(dims)]
-        left = list(dims)
-        names = [name for name, unused in dims]
-        for stage in path:
-            if isinstance(stage, tuple):
-                if stage[1] == line - 1:
-                    at = [n for n, unused in left].index("z")
-                    left = left[:at] + left[at + 1 :]
-            else:
-                at = [n for n, unused in left].index(stage)
-                left = left[:at] + left[at + 1 :]
-            self.dims.append(tuple(left))
-        assert not left and "z" in names
-
-    def is_hop(self, k):
-        return isinstance(self.path[k], tuple)
-
-    def starts_work(self, k):
-        return k == 0 or not self.is_hop(k) or self.path[k][1] == 1
-
-    def shape(self, dims):
-        return tuple(count for unused, count in dims) + self.block
-
-    def slots(self, k):
-        return min(((self.line - 1) if self.is_hop(k) else 1) * self.lag + 1, self.units)
+    def __init__(self, path, names, block, lag, units, swap=None):
+        self.path, self.block, self.lag, self.units, self.swap = path, block, lag, units, swap
+        self.slots = min(2 * lag, units)
+        self.names = [tuple(names)]
+        for k, stage in enumerate(path):
+            left = tuple(name for name in self.names[-1] if name != stage)
+            self.names.append((swap,) + left if swap is not None and k == 0 else left)
+        assert not self.names[-1]
+
+    def shape(self, names):
+        return (2,) * len(names) + self.block
 
     def steps(self):
         return self.units + self.lag * len(self.path) + 1
 
-    def got_slot(self, u):
-        return lax.rem(u, self.got_slots)
+    def slot(self, u):
+        return lax.rem(u, self.slots)
 
     def scratch(self):
         shapes = []
-        for k in range(len(self.path)):
-            if self.starts_work(k):
-                shapes.append(pltpu.VMEM((self.slots(k),) + self.shape(self.dims[k]), self.kind))
-            if self.is_hop(k):
-                rest = tuple(d for d in self.dims[k] if d[0] != "z")
-                shapes.append(pltpu.VMEM((self.got_slots, 2) + self.shape(rest), self.kind))
-                shapes += [pltpu.SemaphoreType.DMA((self.got_slots, 2))] * 2
-            else:
-                shapes.append(pltpu.VMEM((self.got_slots,) + self.shape(self.dims[k + 1]), self.kind))
-                shapes += [pltpu.SemaphoreType.DMA((self.got_slots,))] * 2
+        for k, stage in enumerate(self.path):
+            left = tuple(name for name in self.names[k] if name != stage)
+            shapes.append(pltpu.VMEM((self.slots,) + self.shape(self.names[k]), BF16))
+            shapes.append(pltpu.VMEM((self.slots,) + self.shape(left), BF16))
+            shapes += [pltpu.SemaphoreType.DMA((self.slots,))] * 2
         return shapes
 
-    def bind(self, refs, finish, first_z=None, begin=0):
-        refs = list(refs)
+    def bind(self, refs, finish, begin=0):
         self.finish, self.begin = finish, begin
-        self.first_z = 0 if first_z is None else first_z
-        self.work, self.got, self.sent_sem, self.got_sem = [], [], [], []
-        for k in range(len(self.path)):
-            self.work.append(refs.pop(0) if self.starts_work(k) else self.work[-1])
-            self.got.append(refs.pop(0))
-            self.sent_sem.append(refs.pop(0))
-            self.got_sem.append(refs.pop(0))
+        self.work, self.got, self.sent_sem, self.got_sem = refs[::4], refs[1::4], refs[2::4], refs[3::4]
         self.source = self.work[0]
 
-    def z_count(self, k):
-        return dict(self.dims[k])["z"]
-
-    def keeps(self, z, k):
-        return (z >= self.first_z) & (z < self.first_z + self.z_count(k))
-
-    def keeper(self, k):
-        if "z" in [name for name, unused in self.dims[k]] or dict(self.dims[0])["z"] == self.line:
-            return None
-        z = lax.axis_index("dp")
-        return (z >= self.first_z) & (z < self.first_z + dict(self.dims[0])["z"])
-
-    def pair_copy(self, k, u):
-        bit = self.path[k]
-        mine, partner = pair_of(bit)
-        at = [name for name, unused in self.dims[k]].index(bit)
-        whole = (slice(None),) * at
-        slot = self.got_slot(u)
+    def copy(self, k, u):
+        mine, partner = pair_of(self.path[k])
+        whole = (slice(None),) * self.names[k].index(self.path[k])
+        slot = self.slot(u)
         copy = pltpu.make_async_remote_copy(
-            src_ref=self.work[k].at[(lax.rem(u, self.slots(k)),) + whole + (1 - mine,)],
+            src_ref=self.work[k].at[(slot,) + whole + (1 - mine,)],
             dst_ref=self.got[k].at[slot],
             send_sem=self.sent_sem[k].at[slot],
             recv_sem=self.got_sem[k].at[slot],
             device_id=partner,
             device_id_type=pl.DeviceIdType.MESH,
         )
-        return copy, whole + (mine,)
-
-    def hop_copy(self, k, u, way, block):
-        z, index = lax.axis_index("dp"), lax.axis_index("blk")
-        slot = self.got_slot(u)
-        side = (1 - way) // 2
-        return pltpu.make_async_remote_copy(
-            src_ref=self.work[k].at[lax.rem(u, self.slots(k)), block],
-            dst_ref=self.got[k].at[slot, side],
-            send_sem=self.sent_sem[k].at[slot, side],
-            recv_sem=self.got_sem[k].at[slot, side],
-            device_id=(z + way, index),
-            device_id_type=pl.DeviceIdType.MESH,
-        )
-
-    def hop_ends(self, k, way):
-        z = lax.axis_index("dp")
-        reach = way * (self.line - self.path[k][1])
-        goes, comes = z + reach, z - way + reach
-        sends = self.keeps(goes, k)
-        takes = self.keeps(comes, k) & (z - way >= 0) & (z - way < self.line)
-        return goes - self.first_z, sends, comes - self.first_z, takes
+        return copy, (slot,) + whole + (mine,), mine
 
     def send(self, k, step):
         u = step - self.begin - self.lag * k - 1
-        due = (u >= 0) & (u < self.units)
-        if not self.is_hop(k):
-            keeper = self.keeper(k)
-
-            @pl.when(due if keeper is None else due & keeper)
-            def _():
-                self.pair_copy(k, u)[0].start()
-
-            return
-        for way in (1, -1):
-            block, sends, unused, unused = self.hop_ends(k, way)
-
-            @pl.when(due & sends)
-            def _():
-                self.hop_copy(k, u, way, block).start()
+
+        @pl.when((u >= 0) & (u < self.units))
+        def _():
+            self.copy(k, u)[0].start()
 
     def take(self, k, step):
         u = step - self.begin - self.lag * (k + 1) - 1
-        due = (u >= 0) & (u < self.units)
-        keeper = self.keeper(k + 1)
-        last = k == len(self.path) - 1
-
-        def pass_on(value):
-            if last:
-                self.finish(u, value)
+
+        @pl.when((u >= 0) & (u < self.units))
+        def _():
+            copy, own, mine = self.copy(k, u)
+            copy.wait()
+            slot = self.slot(u)
+            if self.swap is not None and k == 0:
+                self.work[1][slot, mine] = self.work[0][own]
+                self.work[1][slot, 1 - mine] = self.got[0][slot]
+            elif k == len(self.path) - 1:
+                self.finish(u, self.work[k][own] + self.got[k][slot])
             else:
-                self.work[k + 1][lax.rem(u, self.slots(k + 1))] = value
-
-        if not self.is_hop(k):
-            keeper = self.keeper(k)
-
-            @pl.when(due if keeper is None else due & keeper)
-            def _():
-                copy, mine = self.pair_copy(k, u)
-                copy.wait()
-                own = self.work[k][(lax.rem(u, self.slots(k)),) + mine]
-                pass_on(own + self.got[k][self.got_slot(u)])
-
-            return
-        slot = lax.rem(u, self.slots(k))
-        for way in (1, -1):
-            out_block, sends, in_block, takes = self.hop_ends(k, way)
-
-            @pl.when(due & sends)
-            def _():
-                self.hop_copy(k, u, way, out_block).wait_send()
-
-            @pl.when(due & takes)
-            def _():
-                self.hop_copy(k, u, way, in_block).wait_recv()
-                self.work[k][slot, in_block] += self.got[k][self.got_slot(u), (1 - way) // 2]
-
-        if self.path[k][1] == self.line - 1:
-            own = lax.axis_index("dp") - self.first_z
-
-            @pl.when(due if keeper is None else due & keeper)
-            def _():
-                pass_on(self.work[k][slot, own])
-
-
-def hops(line):
-    return [("z", t) for t in range(1, line)]
-
-
-def greet(bits, line):
-    barrier = pltpu.get_barrier_semaphore()
-    z, index = lax.axis_index("dp"), lax.axis_index("blk")
-    for bit in bits:
-        pl.semaphore_signal(barrier, inc=1, device_id=pair_of(bit)[1], device_id_type=pl.DeviceIdType.MESH)
-    for way in (1, -1):
-
-        @pl.when((z + way >= 0) & (z + way < line))
-        def _():
-            pl.semaphore_signal(
-                barrier, inc=1, device_id=(z + way, index), device_id_type=pl.DeviceIdType.MESH
-            )
-
-    beside = jnp.minimum(z, 1) + jnp.minimum(line - 1 - z, 1)
-    pl.semaphore_wait(barrier, len(bits) + beside)
-
-
-def step_streams(streams, step, steps, line, ready):
+                self.work[k + 1][slot] = self.work[k][own] + self.got[k][slot]
+
+
+def step_streams(streams, step):
     longest = max(len(stream.path) for stream in streams)
-    z, index = lax.axis_index("dp"), lax.axis_index("blk")
     for k in range(longest):
         for stream in streams:
             if k < len(stream.path):
                 stream.take(k, step)
-    for way in (1, -1):
-        there = (z + way >= 0) & (z + way < line)
-
-        @pl.when(there & (step >= 0) & (step < steps - 1))
-        def _():
-            pl.semaphore_signal(
-                ready.at[(1 - way) // 2],
-                inc=1,
-                device_id=(z + way, index),
-                device_id_type=pl.DeviceIdType.MESH,
-            )
-
-        @pl.when(there & (step > 0))
-        def _():
-            pl.semaphore_wait(ready.at[(1 + way) // 2], 1)
-
     for k in range(longest):
         for stream in streams:
             if k < len(stream.path):
                 stream.send(k, step)
 
 
+def line_bits(line):
+    return [("z", 1 << i) for i in range(line.bit_length() - 1)]
+
+
 def greet_all(blk_count, line):
     barrier = pltpu.get_barrier_semaphore()
     z, index = lax.axis_index("dp"), lax.axis_index("blk")
-    for step in range(1, blk_count):
-        pl.semaphore_signal(
-            barrier,
-            inc=1,
-            device_id=(z, lax.rem(index + step, blk_count)),
-            device_id_type=pl.DeviceIdType.MESH,
-        )
-    for way in (1, -1):
-
-        @pl.when((z + way >= 0) & (z + way < line))
-        def _():
-            pl.semaphore_signal(
-                barrier, inc=1, device_id=(z + way, index), device_id_type=pl.DeviceIdType.MESH
-            )
-
-    beside = jnp.minimum(z, 1) + jnp.minimum(line - 1 - z, 1)
-    pl.semaphore_wait(barrier, blk_count - 1 + beside)
+    peers = [(z, lax.rem(index + step, blk_count)) for step in range(1, blk_count)]
+    peers += [pair_of(name)[1] for name in line_bits(line)]
+    for peer in peers:
+        pl.semaphore_signal(barrier, inc=1, device_id=peer, device_id_type=pl.DeviceIdType.MESH)
+    pl.semaphore_wait(barrier, len(peers))
 
 
 def middle_kernel(
@@ -896,7 +750,6 @@
     part_got_sem,
     do_sent_sem,
     do_got_sem,
-    ready,
     *refs,
 ):
     n = pl.program_id(0)
@@ -984,7 +837,7 @@
         hidden_copy().wait()
         flip(own_rows)
 
-    step_streams(streams, n - 1, steps - 1, line, ready)
+    step_streams(streams, n - 1)
 
     @pl.when((n >= 1) & (n <= units))
     def _():
@@ -1006,18 +859,20 @@
             out_sum[part, :] += nn_dot(act, w_down_ref[...])
             back_sum[part, :] += nt_dot(gate_grad, w_gate_ref[...]) + nt_dot(up_grad, w_up_ref[...])
         u = n - 1
-        slot, long_slot = lax.rem(u, gate_stream.slots(0)), lax.rem(u, both_stream.slots(0))
+        slot = gate_stream.slot(u)
         each = width // line
-        shape = gate_stream.shape(gate_stream.dims[0])[1:-2] + (-1, FF_TILE)
+        zs = line.bit_length() - 1
+        shape = gate_stream.shape(gate_stream.names[0])[zs:-2] + (-1, FF_TILE)
         for m in range(line):
+            at = (slot,) + tuple(m >> i & 1 for i in reversed(range(zs)))
             part = slice(m * each, (m + 1) * each)
             gate_part = nn_dot(flipped[part, :], gate_grads[...]).astype(BF16)
             up_part = nn_dot(flipped[part, :], up_grads[...]).astype(BF16)
             gate_part, up_part = gate_part.reshape(shape), up_part.reshape(shape)
-            gate_stream.source[slot, m] = gate_part[..., :gate_rows, :]
-            up_stream.source[slot, m] = up_part[..., :gate_rows, :]
-            both_stream.source[long_slot, m, ..., :FF_TILE] = gate_part[..., gate_rows:, :]
-            both_stream.source[long_slot, m, ..., FF_TILE:] = up_part[..., gate_rows:, :]
+            gate_stream.source[at] = gate_part[..., :gate_rows, :]
+            up_stream.source[at] = up_part[..., :gate_rows, :]
+            both_stream.source[at + (..., slice(0, FF_TILE))] = gate_part[..., gate_rows:, :]
+            both_stream.source[at + (..., slice(FF_TILE, None))] = up_part[..., gate_rows:, :]
 
     @pl.when(n == units)
     def _():
@@ -1076,11 +931,12 @@
 
 def column_streams(line, bits, each, units):
     late = each // 4
-    dims = [("z", line)] + [(bit, 2) for bit in bits]
+    zs = line_bits(line)
+    names = zs[::-1] + bits
     return [
-        Stream(bits[::-1] + hops(line), dims, (each - late, FF_TILE), line, LAG, units),
-        Stream(bits + hops(line), dims, (each - late, FF_TILE), line, LAG, units),
-        Stream(hops(line) + bits, dims, (late, 2 * FF_TILE), line, LAG, units),
+        Stream(bits[::-1] + zs, names, (each - late, FF_TILE), LAG, units),
+        Stream(bits + zs, names, (each - late, FF_TILE), LAG, units),
+        Stream(zs + bits, names, (late, 2 * FF_TILE), LAG, units),
     ]
 
 
@@ -1120,7 +976,6 @@
         pltpu.SemaphoreType.DMA((2,)),
         pltpu.SemaphoreType.DMA((blk_count,)),
         pltpu.SemaphoreType.DMA((blk_count,)),
-        pltpu.SemaphoreType.REGULAR((2,)),
     ]
     for stream in streams:
         scratch += stream.scratch()
@@ -1187,7 +1042,6 @@
     moved,
     sent_sem,
     got_sem,
-    ready,
     *refs,
 ):
     size = qkv_ref.shape[0]
@@ -1197,48 +1051,34 @@
     index = lax.axis_index("blk")
     core = lax.rem(index, 2)
 
-    def move(target, source):
-        return pltpu.make_async_remote_copy(
-            src_ref=result.at[target],
-            dst_ref=moved.at[source],
-            send_sem=sent_sem.at[target],
-            recv_sem=got_sem.at[source],
-            device_id=(lax.axis_index("dp"), target),
-            device_id_type=pl.DeviceIdType.MESH,
-        )
-
-    low_half = streams[0].block[1]
-    mid_half = low_half + streams[1].block[1]
-
-    def finish_down(lanes):
-        def put(u, value):
-            rows = value.shape[0]
-            down_out_ref[pl.ds(pl.multiple_of(u * rows, rows), rows), lanes] = value
-
-        return put
+    def move(g, target, source):
+        return blk_copy(result.at[g], moved.at[g], sent_sem.at[g], got_sem.at[g], target, source)
+
+    half = streams[0].block[1]
+
+    def finish_low(u, value):
+        rows = value.shape[0]
+        down_out_ref[pl.ds(pl.multiple_of(u * rows, rows), rows), :half] = value
+
+    def finish_high(u, value):
+        rows = value.shape[0]
+        down_out_ref[pl.ds(pl.multiple_of(u * rows, rows), rows), half:] = value
 
     def finish_w_out(u, value):
         w_out_ref[:, pl.ds(pl.multiple_of(u * LANES, LANES), LANES)] = value
 
+    columns = w_out_ref.shape[1] // LANES
     at = 0
-    columns = w_out_ref.shape[1] // LANES
-    first_z = core * (line // 2)
-    for stream, finish, first, begin in (
-        (streams[0], finish_down(slice(0, low_half)), first_z, 0),
-        (streams[1], finish_down(slice(low_half, mid_half)), first_z, 0),
-        (streams[2], finish_down(slice(mid_half, None)), first_z, 0),
-        (streams[3], finish_w_out, None, 0),
-    ):
+    for stream, finish in zip(streams, (finish_low, finish_high, finish_w_out)):
         size_of = len(stream.scratch())
-        stream.bind(refs[at : at + size_of], finish, first, begin)
+        stream.bind(refs[at : at + size_of], finish)
         at += size_of
 
     @pl.when(n == 0)
     def _():
         greet_all(blocks, line)
-        down_out_ref[...] = jnp.zeros_like(down_out_ref)
-
-    step_streams(streams, n, pl.num_programs(0), line, ready)
+
+    step_streams(streams, n)
 
     @pl.when(n == 1)
     def _():
@@ -1271,28 +1111,30 @@
         rows = dy_own_ref.shape[0]
         made = nn_dot(acts[:, :rows], dy_own_ref[...]) + nn_dot(acts[:, rows:], dy_got_ref[...])
         made = made.astype(BF16)
-        parts = (made[:, :low_half], made[:, low_half:mid_half], made[:, mid_half:])
-        for stream, part in zip(streams[:3], parts):
-            shape = stream.shape(stream.dims[0])
-            stream.source[lax.rem(n, stream.slots(0))] = part.reshape(shape)
+        for i, stream in enumerate(streams[:2]):
+            shape = stream.shape(stream.names[0])[1:]
+            for side in range(2):
+                at = (2 * side + i) * half
+                stream.source[stream.slot(n), side] = made[:, at : at + half].reshape(shape)
 
     @pl.when(n < columns)
     def _():
-        stream = streams[3]
-        part = w_out_parts_ref[...].reshape(stream.shape(stream.dims[0]))
-        stream.source[lax.rem(n, stream.slots(0))] = part
+        stream = streams[2]
+        stream.source[stream.slot(n)] = w_out_parts_ref[...].reshape(stream.shape(stream.names[0]))
 
     row = lax.broadcasted_iota(jnp.int32, (block, 2 * block), 0)
     column = lax.broadcasted_iota(jnp.int32, (block, 2 * block), 1) % block
 
     pairs = (blocks + 1) * (blocks // 2)
     each = ATTEND_PAIRS
-    rounds = pairs // each
+    rounds = groups * pairs // each
 
     @pl.when((n >= 1) & (n <= rounds))
     def _():
         def pair(at, carry):
-            place = (n - 1) * each + at
+            number = (n - 1) * each + at
+            g = number // pairs
+            place = lax.rem(number, pairs)
             turn = place // (blocks // 2)
             m = lax.rem(place, blocks // 2)
             late = (turn + m) // blocks
@@ -1303,56 +1145,52 @@
             key_rows = pl.ds(key_at, block)
             stack = pl.ds(at, 2 * block)
             allowed = (row >= starts_ref[:, stack] - key_at) & (row - column <= (i - j) * block)
-            for g in range(groups):
-                query = queries[g, stack, :]
-                grad = grads[g, stack, :]
-                key = keys[g, key_rows, :]
-                scores = nt_dot(key, query)
-                probs = jnp.exp2(jnp.where(allowed, scores, MASKED))
-                pushed = (probs * nt_dot(values[g, key_rows, :], grad)).astype(BF16)
-                pair_grad[g, key_rows, LANES:] += nn_dot(probs.astype(BF16), grad[:, :LANES])
-                pair_grad[g, key_rows, :LANES] += nn_dot(pushed, query[:, :LANES])
-                query_grad[g, stack, :] += tn_dot(pushed, key[:, :LANES])
+            query = queries[g, stack, :]
+            grad = grads[g, stack, :]
+            key = keys[g, key_rows, :]
+            scores = nt_dot(key, query)
+            probs = jnp.exp2(jnp.where(allowed, scores, MASKED))
+            pushed = (probs * nt_dot(values[g, key_rows, :], grad)).astype(BF16)
+            pair_grad[g, key_rows, LANES:] += nn_dot(probs.astype(BF16), grad[:, :LANES])
+            pair_grad[g, key_rows, :LANES] += nn_dot(pushed, query[:, :LANES])
+            query_grad[g, stack, :] += tn_dot(pushed, key[:, :LANES])
             return carry
 
         lax.fori_loop(0, each, pair, 0, unroll=True)
 
-    @pl.when(n == rounds + 1)
-    def _():
-        low = low_lanes((block, LANES))
-
-        def finish(i, carry):
-            at = pl.multiple_of(i * block, block)
-            to = pl.multiple_of(i * 2 * block, 2 * block)
-            here = pl.ds(at, block)
-            for g in range(groups):
+    for g in range(groups):
+
+        @pl.when(n == (g + 1) * rounds // groups + 1)
+        def _():
+            low = low_lanes((block, LANES))
+
+            def finish(i, carry):
+                at = pl.multiple_of(i * block, block)
+                to = pl.multiple_of(i * 2 * block, 2 * block)
+                here = pl.ds(at, block)
                 first = query_grad[g, pl.ds(to, block), :]
                 second = query_grad[g, pl.ds(to + block, block), :]
                 joined = jnp.where(low, first, second) * HEAD_DIM ** (-0.5)
-                result[i, :, g * LANES : (g + 1) * LANES] = joined.astype(BF16)
-            for part in range(2):
-                sums = []
-                for g in range(groups):
-                    both = pair_grad[g, here, part * LANES : (part + 1) * LANES]
-                    sums.append(both + pltpu.roll(both, HEAD_DIM, 1))
-                joined = jnp.where(low, sums[0], sums[1])
-                if part == 0:
-                    joined = joined * (1.0 / LOG2_E)
-                lane = q_width + part * LANES
-                result[i, :, lane : lane + LANES] = joined.astype(BF16)
-            return carry
-
-        lax.fori_loop(0, blocks, finish, 0)
-        for step in range(blocks - 1, 0, -1):
-            move(lax.rem(index + step, blocks), index).start()
-        moved[index] = result[index]
+                result[g, i, :, :LANES] = joined.astype(BF16)
+                key = pair_grad[g, here, :LANES] * (1.0 / LOG2_E)
+                value = pair_grad[g, here, LANES:]
+                key = key + pltpu.roll(key, HEAD_DIM, 1)
+                value = value + pltpu.roll(value, HEAD_DIM, 1)
+                result[g, i, :, LANES:] = jnp.where(low, key, value).astype(BF16)
+                return carry
+
+            lax.fori_loop(0, blocks, finish, 0)
+            for step in range(blocks - 1, 0, -1):
+                move(g, lax.rem(index + step, blocks), index).start()
+            moved[g, index] = result[g, index]
 
     @pl.when(n == pl.num_programs(0) - 1)
     def _():
-        for step in range(1, blocks):
-            other = lax.rem(index + step, blocks)
-            move(other, other).wait()
-        moved_ref[...] = moved[...]
+        for g in range(groups):
+            for step in range(1, blocks):
+                other = lax.rem(index + step, blocks)
+                move(g, other, other).wait()
+            moved_ref[:, :, 2 * g * LANES : 2 * (g + 1) * LANES] = moved[g]
 
 
 def back(line, bits, qkv, logs, out, grad, starts, block, dy_own, dy_got, acts, w_out_parts):
@@ -1364,26 +1202,18 @@
     chips = line * 2 ** len(bits)
     down_rows = acts.shape[0] // (chips // 2)
     down_each = down_rows // units
-    dims = [("z", line // 2)] + [(bit, 2) for bit in bits]
-    quarter = model // 4
     w_rows = w_out_parts.shape[0] // chips // 2
     columns = w_out_parts.shape[1] // LANES
+    zs = line_bits(line)
+    names = [1] + zs[-2::-1] + bits
     streams = [
-        Stream(hops(line) + bits[::-1], dims, (down_each, quarter), line, LAG, units),
-        Stream(bits + hops(line), dims, (down_each, quarter * 3 // 2), line, LAG, units),
-        Stream(bits[::-1] + hops(line), dims, (down_each, quarter * 3 // 2), line, LAG, units),
-        Stream(
-            [1] + bits[::-1] + hops(line),
-            [("z", line)] + [(bit, 2) for bit in bits] + [(1, 2)],
-            (w_rows, LANES),
-            line,
-            LAG,
-            columns,
-        ),
+        Stream([1] + bits[::-1] + zs, names, (down_each, model // 4), LAG, units, swap=zs[-1]),
+        Stream([1] + bits + zs, names, (down_each, model // 4), LAG, units, swap=zs[-1]),
+        Stream([1] + zs + bits, zs[::-1] + bits + [1], (w_rows, LANES), LAG, columns),
     ]
     steps = max(
         [stream.steps() for stream in streams]
-        + [(size // block + 1) * (size // block // 2) // ATTEND_PAIRS + 3]
+        + [groups * (size // block + 1) * (size // block // 2) // ATTEND_PAIRS + 3]
     )
 
     def keep(shape):
@@ -1397,18 +1227,17 @@
         pltpu.VMEM((groups, 2 * size, 2 * LANES), BF16),
         pltpu.VMEM((groups, 2 * size, LANES), F32),
         pltpu.VMEM((groups, size, 2 * LANES), F32),
-        pltpu.VMEM((size // block, block, width), BF16),
-        pltpu.VMEM((size // block, block, width), BF16),
-        pltpu.SemaphoreType.DMA((size // block,)),
-        pltpu.SemaphoreType.DMA((size // block,)),
-        pltpu.SemaphoreType.REGULAR((2,)),
+        pltpu.VMEM((groups, size // block, block, 2 * LANES), BF16),
+        pltpu.VMEM((groups, size // block, block, 2 * LANES), BF16),
+        pltpu.SemaphoreType.DMA((groups, size // block)),
+        pltpu.SemaphoreType.DMA((groups, size // block)),
     ]
     for stream in streams:
         scratch += stream.scratch()
 
     outs = [
         (size // block, block, width),
-        (down_rows, model),
+        (down_rows, model // 2),
         (w_rows, w_out_parts.shape[1]),
     ]
     return pl.pallas_call(
@@ -1506,7 +1335,6 @@
     down_got,
     half_sent_sem,
     half_got_sem,
-    ready,
     *refs,
 ):
     n = pl.program_id(0)
@@ -1530,11 +1358,7 @@
         stream.bind(refs[at : at + count], finish)
         at += count
 
-    rounds = [pair_of(bit)[1] for bit in (1,) + tuple(bits)]
-    reach = 1
-    while reach < line:
-        rounds.append((z + reach * (1 - 2 * lax.rem(z // reach, 2)), index))
-        reach *= 2
+    rounds = [pair_of(name)[1] for name in [1] + list(bits) + line_bits(line)]
 
     rows = gate_ref.shape[0] // 2
     columns = gate_ref.shape[1]
@@ -1564,16 +1388,7 @@
         barrier = pltpu.get_barrier_semaphore()
         for peer in rounds:
             pl.semaphore_signal(barrier, inc=1, device_id=peer, device_id_type=pl.DeviceIdType.MESH)
-        for way in (1, -1):
-
-            @pl.when((z + way >= 0) & (z + way < line))
-            def _():
-                pl.semaphore_signal(
-                    barrier, inc=1, device_id=(z + way, index), device_id_type=pl.DeviceIdType.MESH
-                )
-
-        beside = jnp.minimum(z, 1) + jnp.minimum(line - 1 - z, 1)
-        pl.semaphore_wait(barrier, len(rounds) + beside)
+        pl.semaphore_wait(barrier, len(rounds))
         for copy in half_copies():
             copy.start()
         total[...] = jnp.zeros_like(total)
@@ -1589,17 +1404,11 @@
         gate_out_ref[:, other] = half_got[0]
         up_out_ref[:, own] = up_ref[keep, :]
         up_out_ref[:, other] = half_got[1]
-        holder = z // (line // 2)
-
-        @pl.when(holder == core)
-        def _():
-            down_out_ref[...] = down_ref[down_keep, :]
-
-        @pl.when(holder != core)
-        def _():
-            down_out_ref[...] = down_got[...]
-
-    step_streams(streams, n, steps, line, ready)
+        half = down_ref.shape[1]
+        down_out_ref[:, pl.ds(pl.multiple_of(core * half, LANES), half)] = down_ref[down_keep, :]
+        down_out_ref[:, pl.ds(pl.multiple_of((1 - core) * half, LANES), half)] = down_got[...]
+
+    step_streams(streams, n)
     sum_gains(rounds, n, units, gains, gains_got, gains_sent_sem, gains_got_sem)
 
     @pl.when(n == steps - 1)
@@ -1610,10 +1419,12 @@
     def _():
         hidden = hidden_ref[...]
 
-        def back(lane, head_gain, place):
-            got = jnp.concatenate(
+        def got_lanes(lane):
+            return jnp.concatenate(
                 [got_ref[0, :, lane : lane + LANES], got_ref[1, :, lane : lane + LANES]], axis=0
             ).astype(F32)
+
+        def back(got, lane, head_gain, place):
             turned = got * cos_ref[...] - half_partner(got) * sin_ref[...]
             block = proj_ref[0, :, lane : lane + LANES]
             scale = lax.rsqrt(head_means(block * block) + EPSILON)
@@ -1626,16 +1437,17 @@
         width = tokens_ref.shape[1]
         lines = width // LANES
         query = jnp.concatenate(
-            [back(at, q_gain_ref, 2 * lines) for at in range(0, q_width, LANES)], axis=1
+            [back(got_lanes(2 * at), at, q_gain_ref, 2 * lines) for at in range(0, q_width, LANES)],
+            axis=1,
         )
-        key = back(q_width, k_gain_ref, 2 * lines + 1)
-        lane = q_width + LANES
-        value = jnp.concatenate(
-            [got_ref[0, :, lane : lane + LANES], got_ref[1, :, lane : lane + LANES]], axis=0
-        )
+        first, second = got_lanes(LANES), got_lanes(3 * LANES)
+        low = low_lanes(first.shape)
+        key = jnp.where(low, first, pltpu.roll(second, HEAD_DIM, 1))
+        key = back(key, q_width, k_gain_ref, 2 * lines + 1)
+        value = jnp.where(low, pltpu.roll(first, HEAD_DIM, 1), second).astype(BF16)
         for stream, part in ((query_stream, query), (pair_stream, jnp.concatenate([key, value], axis=1))):
-            shape = stream.shape(stream.dims[0])
-            stream.source[lax.rem(n, stream.slots(0))] = tn_dot(hidden, part).astype(BF16).reshape(shape)
+            shape = stream.shape(stream.names[0])
+            stream.source[stream.slot(n)] = tn_dot(hidden, part).astype(BF16).reshape(shape)
 
         total[...] += (
             nt_dot(query, wq_ref[...]) + nt_dot(key, wk_ref[...]) + nt_dot(value, wv_ref[...])
@@ -1683,12 +1495,12 @@
     units = count // 2
     q_width = wq.shape[1] // units
     chips = line * 2 ** len(bits)
-    sides = [(bit, 2) for bit in bits]
-    dims = [("z", line)] + sides + [(1, 2)]
     mine = width // chips // 2
+    zs = line_bits(line)
+    names = zs[::-1] + bits + [1]
     streams = [
-        Stream([1] + bits[::-1] + hops(line), dims, (mine, q_width), line, LAST_LAG, units),
-        Stream([1] + bits + hops(line), dims, (mine, 2 * LANES), line, LAST_LAG, units),
+        Stream([1] + bits[::-1] + zs, names, (mine, q_width), LAST_LAG, units),
+        Stream([1] + bits + zs, names, (mine, 2 * LANES), LAST_LAG, units),
     ]
     rounds = 1 + len(bits) + (line - 1).bit_length()
     steps = max([stream.steps() for stream in streams] + [units + rounds + 2])
@@ -1713,7 +1525,6 @@
         pltpu.VMEM((down_rows, down_sum.shape[1]), BF16),
         pltpu.SemaphoreType.DMA((3,)),
         pltpu.SemaphoreType.DMA((3,)),
-        pltpu.SemaphoreType.REGULAR((2,)),
     ]
     for stream in streams:
         scratch += stream.scratch()
@@ -1725,7 +1536,7 @@
         ((mine, wv.shape[1]), BF16),
         ((half_rows, 2 * columns), BF16),
         ((half_rows, 2 * columns), BF16),
-        ((down_rows, down_sum.shape[1]), BF16),
+        ((down_rows, 2 * down_sum.shape[1]), BF16),
     ]
     return pl.pallas_call(
         functools.partial(finish_kernel, line, bits, streams, units),
@@ -1775,19 +1586,25 @@
     )
 
 
-def widen_kernel(*refs):
-    count = len(refs) // 2
-    for source, target in zip(refs[:count], refs[count:]):
+def widen_kernel(count, gains_ref, *refs):
+    for source, target in zip(refs[:count], refs[count : 2 * count]):
         target[...] = source[...].astype(F32)
-
-
-def widen(parts):
+    attn_ref, ffn_ref, heads_ref = refs[2 * count :]
+    lines = attn_ref.shape[0]
+    attn_ref[...] = gains_ref[:lines, :]
+    ffn_ref[...] = gains_ref[lines : 2 * lines, :]
+    both = gains_ref[2 * lines : 2 * lines + 2, :]
+    heads_ref[...] = both + pltpu.roll(both, HEAD_DIM, 1)
+
+
+def widen(gains, lines, parts):
+    shapes = [part.shape for part in parts] + [(lines, LANES), (lines, LANES), (2, LANES)]
     return pl.pallas_call(
-        widen_kernel,
+        functools.partial(widen_kernel, len(parts)),
         name="widen",
-        out_shape=[jax.ShapeDtypeStruct(part.shape, F32) for part in parts],
+        out_shape=[jax.ShapeDtypeStruct(shape, F32) for shape in shapes],
         compiler_params=kernel_params(),
-    )(*parts)
+    )(gains, *parts)
 
 
 def flip_pairs(count, bit):
@@ -1829,18 +1646,22 @@
         bit //= 2
     chip_dims = (dp_count,) + (2,) * len(bits)
     all_chips = dp_count * chips
-    places = index * tok_count + jnp.arange(tok_count, dtype=jnp.int32)
-    unused, positions = doc_layout(doc_lengths, places)
-    cosine, sine = rope_angles(positions)
-    cosine = jnp.tile(cosine.reshape(rows, -1), (1, 4))
-    sine = sine.reshape(rows, -1)
-    sine = jnp.concatenate([-sine, sine, -sine, sine], axis=1)
+    which = jnp.arange(doc_lengths.shape[1])
+    ends = jnp.sum(jnp.where(which[:, None] <= which[None, :], doc_lengths[:, :, None], 0), axis=1)
+    places = index * tok_count + jnp.arange(tok_count, dtype=jnp.int32)[None]
+    begins = jnp.max(jnp.where(places[:, :, None] >= ends[:, None, :], ends[:, None, :], 0), axis=2)
+    positions = (places - begins).reshape(rows, 1).astype(F32)
+    half_head = HEAD_DIM // 2
+    lane = jnp.arange(LANES)
+    freqs = ROPE_BASE ** (-(lane % half_head).astype(F32) / half_head)
+    angles = positions * freqs
+    cosine = jnp.cos(angles)
+    sine = jnp.sin(angles) * jnp.where(lane % HEAD_DIM < half_head, -1.0, 1.0)
     q_gain2 = jnp.tile(q_gain, 2)[None]
     k_gain2 = jnp.tile(k_gain, 2)[None]
     all_places = jnp.arange(size, dtype=jnp.int32)
-    row_lengths = lax.dynamic_slice_in_dim(doc_lengths, core, 1, axis=0)
-    unused, all_positions = doc_layout(row_lengths, all_places)
-    starts = all_places - all_positions[0]
+    own_ends = lax.dynamic_slice_in_dim(ends, core, 1, axis=0)
+    starts = jnp.max(jnp.where(all_places[:, None] >= own_ends, own_ends, 0), axis=1)
     starts_two = jnp.broadcast_to(
         starts.reshape(blk_count, 1, tok_count), (blk_count, 2, tok_count)
     ).reshape(1, 2 * size)
@@ -1901,13 +1722,10 @@
         up_sum,
         down_sum,
     )
-    sums = widen(sums + [w_out_sum])
+    *sums, gain_attn, gain_ffn, gain_heads = widen(gains, width // LANES, sums + [w_out_sum])
     grad_w_query, grad_w_key, grad_w_value, grad_w_gate, grad_w_up, grad_w_down, grad_w_out = sums
-    lines = width // LANES
-    gain_attn = gains[:lines].reshape(width)
-    gain_ffn = gains[lines : 2 * lines].reshape(width)
-    gain_query = gains[2 * lines, :HEAD_DIM] + gains[2 * lines, HEAD_DIM:]
-    gain_key = gains[2 * lines + 1, :HEAD_DIM] + gains[2 * lines + 1, HEAD_DIM:]
+    gain_attn, gain_ffn = gain_attn.reshape(width), gain_ffn.reshape(width)
+    gain_query, gain_key = gain_heads[0, :HEAD_DIM], gain_heads[1, :HEAD_DIM]
     return (
         output.reshape(tokens.shape),
         input_grad.reshape(tokens.shape),
@@ -1928,8 +1746,9 @@
 def fits(mesh):
     blk_count = mesh.shape["blk"]
     chips = blk_count // 2
-    power = blk_count & (blk_count - 1) == 0
-    return power and blk_count > 2 and (KV_HEADS * HEAD_DIM) == chips * LANES
+    line = mesh.shape["dp"]
+    power = blk_count & (blk_count - 1) == 0 and line & (line - 1) == 0
+    return power and blk_count > 2 and line > 1 and (KV_HEADS * HEAD_DIM) == chips * LANES
 
 
 def solution(mesh):

time: 342 us -> 324 us (0.947)
  Pallas kernels: 324 us -> 311 us
  other arithmetic: 6.38 us -> 2.8 us
    pallas_call x1, Pallas kernels: 115 us -> 108 us  [middle_layer(): pl.pallas_call(functools.partial(middle_kernel, line, bits, streams, unit...]
    pallas_call x1, Pallas kernels: 98.3 us -> 92.5 us  [back(): pl.pallas_call(functools.partial(back_kernel, groups, block, line, bits,...]
  transfers between devices with their start and end apart: 1 -> 1, of which waited for: 0 -> 0; matrix products, arithmetic and copies ran while one was open for 3% -> 2% of each run, Pallas kernels for 18% -> 19%
where the time goes in v6:
time: 324 us
  Pallas kernels  311 us (96%)
  local copies, waits for them, and re-layouts  8.68 us (3%)
    pallas_call x1, Pallas kernels, middle_layer(): pl.pallas_call(functools.partial(middle_kernel, line, bits, streams, unit...  108 us
    pallas_call x1, Pallas kernels, back(): pl.pallas_call(functools.partial(back_kernel, groups, block, line, bits,...  92.5 us
    pallas_call x1, Pallas kernels, finish(): pl.pallas_call(functools.partial(finish_kernel, line, bits, streams, unit...  46 us
    pallas_call x1, Pallas kernels, project(): pl.pallas_call(project_kernel, name='project', grid=(chips,), in_specs=[w...  32.3 us
    pallas_call x1, Pallas kernels, attend(): pl.pallas_call(functools.partial(attend_kernel, groups, block), name='att...  28.9 us
  transfers between devices with their start and end apart: 1, of which 0 were waited for; matrix products, arithmetic and copies ran while one was open for 2% of the time, Pallas kernels for 19%

profile of v6, /device:TPU:0, one launch (start us, length us, event | category | flops | bytes accessed | tf_op | source)
XLA Modules:
  0.0 323.6 jit_solution(1758026504020449314)
XLA Ops:
  0.6 0.5 collective-permute-start
  1.2 0.7 tile.4
  1.8 0.6 broadcast_in_dim_tile.6.q_gain_ref
  2.4 0.7 tile.5
  3.1 0.6 broadcast_in_dim_tile.7.k_gain_ref
  3.7 0.8 select_reduce_fusion.2
  4.4 0.1 select_reduce_fusion.1
  4.6 0.1 select_reduce_fusion
  4.7 0.6 reshape.121.starts_ref
  5.3 1.3 copy.28.starts_ref
  6.7 1.8 fusion
  8.5 32.3 %project.1 = (bf16[512,1024]{1,0:T(8,128)(2,1)}, f32[4,512,384]{2,1,0:T(8,128)}, bf16[8,256,512]{2,1,0:T(8,128)(2,1)}) custom-call(bf16[512,1024]{1,0:T(8,128)(2,1)} %bitcast.22, f32[1,1024]{1,0:T(1,128)} %bitcast.36, bf16[1024,1024]{1,0:T(8,128)(2,1)} %wq_ref.3, bf16[1024,512]{1,0:T(8,128)(2,1)} %wk_ref.3, bf16[1024,512]{1,0:T(8,128)(2,1)} %wv_ref.3, ...), custom_call_target="tpu_custom_call" | custom-call | tf_op jit(solution)/shard_map/project/pallas_call | solution.py:436
  40.8 28.9 %attend.1 = (bf16[8,256,256]{2,1,0:T(8,128)(2,1)}, bf16[2,4096,128]{2,1,0:T(8,128)(2,1)}, bf16[8,256,256]{2,1,0:T(8,128)(2,1)}) custom-call(bf16[2048,512]{1,0:T(8,128)(2,1)} %bitcast.25, s32[2048,1]{1,0:T(8,128)} %copy.28.starts_ref), custom_call_target="tpu_custom_call" | custom-call | tf_op jit(solution)/shard_map/attend/pallas_call | solution.py:591
  69.7 0.0 collective-permute-done.dy_got_ref
  69.8 0.0 copy-start
  69.8 1.0 copy-done
  70.7 108.4 %middle.1 = (bf16[512,1024]{1,0:T(8,128)(2,1)}, f32[512,1024]{1,0:T(8,128)}, f32[1,1024]{1,0:T(1,128)}, bf16[1024,1024]{1,0:T(8,128)(2,1)}, bf16[8,256,256]{2,1,...) custom-call(bf16[512,1024]{1,0:T(8,128)(2,1)} %bitcast.23, ...), custom_call_target="tpu_custom_call" | custom-call | tf_op jit(solution)/shard_map/middle/pallas_call | solution.py:994
  179.2 92.5 %back.1 = (bf16[8,256,512]{2,1,0:T(8,128)(2,1)}, bf16[288,512]{1,0:T(8,128)(2,1)}, bf16[32,1024]{1,0:T(8,128)(2,1)}) custom-call(bf16[2048,512]{1,0:T(8,128)(2,1)} %bitcast.26, bf16[2,4096,128]{2,1,0:T(8,128)(2,1)} %get-tuple-element.51.logs_ref, bf16[2048,256]{1,0:T(8,128)(2,1)} %bitcast.31, bf16[2048,256]{1,0:T(8,128)(2,1)} %bitcast.32, ...), custom_call_target="tpu_custom_call" | custom-call | tf_op jit(solution)/shard_map/back/pallas_call | solution.py:1243
  271.7 0.0 copy-start.1
  271.7 46.0 %finish.1 = (bf16[512,1024]{1,0:T(8,128)(2,1)}, f32[24,128]{1,0:T(8,128)}, bf16[32,1024]{1,0:T(8,128)(2,1)}, bf16[32,512]{1,0:T(8,128)(2,1)}, bf16[32,512]{1,0:T...) custom-call(bf16[8,256,512]{2,1,0:T(8,128)(2,1)} %get-tuple-element.56.got_ref, ...), custom_call_target="tpu_custom_call" | custom-call | tf_op jit(solution)/shard_map/finish/pallas_call | solution.py:1541
  317.7 2.7 widen.1
  320.4 1.3 slice_bitcast_fusion
  321.7 1.0 copy.32
  322.6 1.0 copy.33
  (11 shorter events, 0.1 us)
Async XLA Ops:
  0.6 69.1 %collective-permute-start = (bf16[512,1024]{1,0:T(8,128)(2,1)}, bf16[512,1024]{1,0:T(8,128)(2,1)S(1)}, u32[]{:S(2)}, u32[]{:S(2)}) collective-permute-start(bf16[512,1024]{1,0:T(8,128)(2,1)} %bitcast.28), channel_id=1, source_target_pairs={{0,1},{1,0},{2,3},{3,2},{4,5},{5,4},{6,7},{7,6},{8,9},{9,8},{10,11... | collective-permute-start | bytes 3145736 | tf_op jit(solution)/shard_map/ppermute | solution.py:1615
  69.8 1.0 copy-start
  271.7 49.9 %copy-start.1 = (bf16[512,1024]{1,0:T(8,128)(2,1)S(1)}, bf16[512,1024]{1,0:T(8,128)(2,1)}, u32[]{:S(2)}) copy-start(bf16[512,1024]{1,0:T(8,128)(2,1)} %get-tuple-element.50) | copy-start | bytes 3145732
  317.7 4.9 %copy-start.2 = (bf16[512,1024]{1,0:T(8,128)(2,1)S(1)}, bf16[512,1024]{1,0:T(8,128)(2,1)}, u32[]{:S(2)}) copy-start(bf16[512,1024]{1,0:T(8,128)(2,1)} %get-tuple-element.64) | copy-start | bytes 3145732

commit v7 on v6

--- a/solution.py
+++ b/solution.py
@@ -332,10 +332,6 @@
     )
 
 
-def blk_sems(count):
-    return [pltpu.SemaphoreType.DMA((count,)), pltpu.SemaphoreType.DMA((count,))]
-
-
 def head_means(values):
     rows = lax.broadcasted_iota(jnp.int32, (LANES, LANES), 0) // HEAD_DIM
     cols = lax.broadcasted_iota(jnp.int32, (LANES, LANES), 1) // HEAD_DIM
@@ -353,7 +349,41 @@
     return jnp.where(lane % HEAD_DIM < half, ahead, behind)
 
 
-def project_kernel(
+def low_lanes(shape):
+    return lax.broadcasted_iota(jnp.int32, shape, 1) < HEAD_DIM
+
+
+def parted(packed):
+    turned = pltpu.roll(packed.astype(F32), HEAD_DIM, 1).astype(BF16)
+    low = low_lanes(packed.shape)
+    return jnp.where(low, packed, turned), jnp.where(low, turned, packed)
+
+
+def stacked_heads(pair):
+    low = low_lanes(pair.shape)
+    none = jnp.zeros_like(pair)
+    return jnp.concatenate([jnp.where(low, pair, none), jnp.where(low, none, pair)], axis=0)
+
+
+def in_three(column):
+    lane = lax.broadcasted_iota(jnp.int32, (column.shape[0], LANES), 1)
+    wide = jnp.broadcast_to(column, (column.shape[0], LANES))
+    first = wide.astype(BF16).astype(F32)
+    second = (wide - first).astype(BF16).astype(F32)
+    third = wide - first - second
+    return jnp.where(
+        lane == 0, first, jnp.where(lane == 1, second, jnp.where(lane == 2, third, 0.0))
+    ).astype(BF16)
+
+
+def minus_three(rows):
+    lane = lax.broadcasted_iota(jnp.int32, (rows, LANES), 1)
+    return jnp.where(lane < 3, -1.0, 0.0).astype(BF16)
+
+
+def forward_kernel(
+    chips,
+    groups,
     tokens_ref,
     gain_ref,
     wq_ref,
@@ -363,247 +393,213 @@
     k_gain_ref,
     cos_ref,
     sin_ref,
+    starts_ref,
     hidden_ref,
     proj_ref,
-    got_ref,
+    qkv_ref,
+    out_ref,
+    logs_ref,
+    heads_ref,
     send,
     got,
+    keys,
+    values,
+    total,
+    out_send,
+    out_got,
     sent_sem,
     got_sem,
+    out_sent_sem,
+    out_got_sem,
 ):
-    rows = tokens_ref.shape[0]
-    n, chips = pl.program_id(0), pl.num_programs(0)
-    count = send.shape[0]
+    n = pl.program_id(0)
+    blocks, block = send.shape[1:3]
+    size = blocks * block
     index = lax.axis_index("blk")
     p = lax.rem(index // 2 + 1 + n, chips)
 
+    def give(g, p):
+        for part in range(2):
+            target = 2 * p + part
+
+            @pl.when(target != index)
+            def _():
+                blk_copy(send.at[g], got.at[g], sent_sem.at[g], got_sem.at[g], target, index).start()
+
+            @pl.when(target == index)
+            def _():
+                got[g, target] = send[g, target]
+
     @pl.when(n == 0)
     def _():
-        greet_blk(count)
+        greet_blk(blocks)
         inputs = tokens_ref[...].astype(F32)
         scale = lax.rsqrt(jnp.mean(inputs * inputs, axis=-1, keepdims=True) + EPSILON)
         hidden_ref[...] = (inputs * scale * gain_ref[...]).astype(BF16)
 
-    hidden = hidden_ref[...]
-    half = rows // 2
-
-    def put(block, lane):
-        send[2 * p, :, lane : lane + LANES] = block[:half]
-        send[2 * p + 1, :, lane : lane + LANES] = block[half:]
-
-    queries = nn_dot(hidden, wq_ref[...])
-    keys = nn_dot(hidden, wk_ref[...])
-    values = nn_dot(hidden, wv_ref[...])
-    q_width = queries.shape[1]
-    blocks = [(queries[:, at : at + LANES], at, q_gain_ref, QUERY_SCALE) for at in range(0, q_width, LANES)]
-    blocks.append((keys, q_width, k_gain_ref, 1.0))
-    for block, lane, head_gain, factor in blocks:
-        proj_ref[0, :, lane : lane + LANES] = block
-        scale = lax.rsqrt(head_means(block * block) + EPSILON)
-        normed = block * scale * head_gain[...]
-        turned = normed * cos_ref[...] + half_partner(normed) * sin_ref[...]
-        put((turned * factor).astype(BF16), lane)
-    put(values.astype(BF16), q_width + LANES)
-    for part in range(2):
-        target = 2 * p + part
-
-        @pl.when(target != index)
+    @pl.when(n < chips)
+    def _():
+        hidden = hidden_ref[...]
+        queries = nn_dot(hidden, wq_ref[...])
+        keys_of = nn_dot(hidden, wk_ref[...])
+        values_of = nn_dot(hidden, wv_ref[...])
+
+        def turn(part, lane, head_gain):
+            proj_ref[0, :, lane : lane + LANES] = part
+            scale = lax.rsqrt(head_means(part * part) + EPSILON)
+            normed = part * scale * head_gain[...]
+            return normed * cos_ref[...] + half_partner(normed) * sin_ref[...]
+
+        def put(g, lane, part):
+            for half in range(2):
+                send[g, 2 * p + half, :, lane : lane + LANES] = part[half * block : (half + 1) * block].astype(BF16)
+
+        key = turn(keys_of, groups * LANES, k_gain_ref)
+        low = low_lanes(key.shape)
+        for g in range(groups):
+            lanes = slice(g * LANES, (g + 1) * LANES)
+            put(g, 0, turn(queries[:, lanes], g * LANES, q_gain_ref) * QUERY_SCALE)
+            if g == 0:
+                put(g, LANES, jnp.where(low, key, pltpu.roll(values_of, HEAD_DIM, 1)))
+            else:
+                put(g, LANES, jnp.where(low, pltpu.roll(key, HEAD_DIM, 1), values_of))
+        give(0, p)
+
+    @pl.when(n == chips - 1)
+    def _():
+        for step in range(chips):
+            give(1, lax.rem(index // 2 + 1 + step, chips))
+
+    for g in range(groups):
+
+        @pl.when(n == chips + g * blocks)
         def _():
-            blk_copy(send, got, sent_sem, got_sem, target, index).start()
-
-        @pl.when(target == index)
+            for step in range(1, blocks):
+                other = lax.rem(index + step, blocks)
+                blk_copy(send.at[g], got.at[g], sent_sem.at[g], got_sem.at[g], other, other).wait()
+            for i in range(blocks):
+                here = slice(i * block, (i + 1) * block)
+                qkv_ref[g, here, :] = got[g, i]
+                keys[here, :], values[here, :LANES] = parted(got[g, i, :, LANES:])
+                values[here, LANES:] = jnp.ones((block, LANES), BF16)
+
+    @pl.when(n >= chips)
+    def _():
+        g = (n - chips) // blocks
+        here = lax.rem(index + 1 + lax.rem(n - chips, blocks), blocks)
+        at = pl.multiple_of(here * block, block)
+        starts = jnp.concatenate([starts_ref[pl.ds(at, block), :]] * 2, axis=0)
+        query = stacked_heads(got[g, here, :, :LANES])
+
+        def step(key_at, width, diagonal):
+            column = lax.broadcasted_iota(jnp.int32, (2 * block, width), 1)
+            allowed = column >= starts - key_at
+            if diagonal:
+                row = lax.broadcasted_iota(jnp.int32, (2 * block, width), 0) % block
+                allowed = allowed & (column <= row)
+            scores = nt_dot(query, keys[pl.ds(key_at, width), :])
+            weights = jnp.exp2(jnp.where(allowed, scores, MASKED)).astype(BF16)
+            part = nn_dot(weights, values[pl.ds(key_at, width), :])
+            if diagonal:
+                total[...] = part
+            else:
+                total[...] += part
+
+        step(at, block, True)
+
+        @pl.when(lax.rem(here, 2) == 1)
         def _():
-            got[target] = send[target]
-
-    @pl.when(n == chips - 1)
-    def _():
-        for step in range(1, count):
-            other = lax.rem(index + step, count)
-            blk_copy(send, got, sent_sem, got_sem, other, other).wait()
-        got_ref[...] = got[...]
-
-
-def project(tokens, gain, wq, wk, wv, q_gain, k_gain, cosine, sine):
+            step(pl.multiple_of((here - 1) * block, block), block, False)
+
+        def body(j, carry):
+            step(pl.multiple_of(j * 2 * block, 2 * block), 2 * block, False)
+            return carry
+
+        lax.fori_loop(0, here // 2, body, 0)
+        low = low_lanes((block, LANES))
+        to = pl.multiple_of(here * 2 * block, 2 * block)
+        sums = total[:, LANES:]
+        mean = total[:, :LANES] / sums
+        made = jnp.where(low, mean[:block], mean[block:]).astype(BF16)
+        out_send[g, here] = made
+        out_ref[here, :, pl.ds(pl.multiple_of(g * LANES, LANES), LANES)] = made
+        logs_ref[g, pl.ds(to, 2 * block), :] = in_three(jnp.log2(sums[:, :1]))
+
+        @pl.when(here != index)
+        def _():
+            blk_copy(
+                out_send.at[g], out_got.at[g], out_sent_sem.at[g], out_got_sem.at[g], here, index
+            ).start()
+
+        @pl.when(here == index)
+        def _():
+            out_got[g, here] = made
+
+    @pl.when(n == pl.num_programs(0) - 1)
+    def _():
+        for g in range(groups):
+            for step in range(1, blocks):
+                other = lax.rem(index + step, blocks)
+                blk_copy(
+                    out_send.at[g], out_got.at[g], out_sent_sem.at[g], out_got_sem.at[g], other, other
+                ).wait()
+            heads_ref[:, :, g * LANES : (g + 1) * LANES] = out_got[g]
+
+
+def forward(tokens, gain, wq, wk, wv, q_gain, k_gain, cosine, sine, starts):
     rows, width = tokens.shape
     chips = wk.shape[1] // LANES
     q_width = wq.shape[1] // chips
-    block_width = q_width + 2 * LANES
-    moved = (2 * chips, rows // 2, block_width)
+    groups, blocks, block = q_width // LANES, 2 * chips, rows // 2
+    size = blocks * block
+
+    def keep(shape):
+        return pl.BlockSpec(shape, lambda n: (0,) * len(shape), pipeline_mode=pl.Buffered(1))
 
     def at(n):
-        return lax.rem(lax.axis_index("blk") // 2 + 1 + n, chips)
-
+        return lax.rem(lax.axis_index("blk") // 2 + 1 + jnp.minimum(n, chips - 1), chips)
+
+    outs = [
+        ((rows, width), BF16),
+        ((chips, rows, q_width + LANES), F32),
+        ((groups, size, 2 * LANES), BF16),
+        ((blocks, block, q_width), BF16),
+        ((groups, 2 * size, LANES), BF16),
+        ((blocks, block, q_width), BF16),
+    ]
+    out_specs = [keep(shape) for shape, unused in outs]
+    out_specs[1] = pl.BlockSpec((1, rows, q_width + LANES), lambda n: (at(n), 0, 0))
+    moved, heads = (groups, blocks, block, 2 * LANES), (groups, blocks, block, LANES)
     return pl.pallas_call(
-        project_kernel,
-        name="project",
-        grid=(chips,),
+        functools.partial(forward_kernel, chips, groups),
+        name="forward",
+        grid=(chips + groups * blocks,),
         in_specs=[
-            whole_block((rows, width)),
-            whole_block((1, width)),
+            keep((rows, width)),
+            keep((1, width)),
             pl.BlockSpec((width, q_width), lambda n: (0, at(n))),
             pl.BlockSpec((width, LANES), lambda n: (0, at(n))),
             pl.BlockSpec((width, LANES), lambda n: (0, at(n))),
-            whole_block((1, LANES)),
-            whole_block((1, LANES)),
-            whole_block((rows, LANES)),
-            whole_block((rows, LANES)),
+            keep((1, LANES)),
+            keep((1, LANES)),
+            keep((rows, LANES)),
+            keep((rows, LANES)),
+            keep((size, 1)),
         ],
-        out_specs=[
-            whole_block((rows, width)),
-            pl.BlockSpec((1, rows, q_width + LANES), lambda n: (at(n), 0, 0)),
-            whole_block(moved),
-        ],
-        out_shape=[
-            jax.ShapeDtypeStruct((rows, width), BF16),
-            jax.ShapeDtypeStruct((chips, rows, q_width + LANES), F32),
-            jax.ShapeDtypeStruct(moved, BF16),
-        ],
-        scratch_shapes=[pltpu.VMEM(moved, BF16), pltpu.VMEM(moved, BF16)] + blk_sems(2 * chips),
-        compiler_params=kernel_params(collective_id=0, has_side_effects=True),
-    )(tokens, gain, wq, wk, wv, q_gain, k_gain, cosine, sine)
-
-
-def low_lanes(shape):
-    return lax.broadcasted_iota(jnp.int32, shape, 1) < HEAD_DIM
-
-
-def doubled(pair, group):
-    turned = pltpu.roll(pair.astype(F32), HEAD_DIM, 1).astype(BF16)
-    low = low_lanes(pair.shape)
-    return jnp.where(low, pair, turned) if group == 0 else jnp.where(low, turned, pair)
-
-
-def stacked_heads(pair):
-    low = low_lanes(pair.shape)
-    none = jnp.zeros_like(pair)
-    return jnp.concatenate([jnp.where(low, pair, none), jnp.where(low, none, pair)], axis=0)
-
-
-def in_three(column):
-    lane = lax.broadcasted_iota(jnp.int32, (column.shape[0], LANES), 1)
-    wide = jnp.broadcast_to(column, (column.shape[0], LANES))
-    first = wide.astype(BF16).astype(F32)
-    second = (wide - first).astype(BF16).astype(F32)
-    third = wide - first - second
-    return jnp.where(
-        lane == 0, first, jnp.where(lane == 1, second, jnp.where(lane == 2, third, 0.0))
-    ).astype(BF16)
-
-
-def minus_three(rows):
-    lane = lax.broadcasted_iota(jnp.int32, (rows, LANES), 1)
-    return jnp.where(lane < 3, -1.0, 0.0).astype(BF16)
-
-
-def attend_kernel(
-    groups,
-    block,
-    qkv_ref,
-    starts_ref,
-    out_ref,
-    logs_ref,
-    heads_ref,
-    keys,
-    values,
-    total,
-    got,
-    sent_sem,
-    got_sem,
-):
-    size = qkv_ref.shape[0]
-    blocks = size // block
-    q_width = groups * LANES
-    n = pl.program_id(0)
-    index = lax.axis_index("blk")
-    here = lax.rem(index + 1 + n, blocks)
-
-    @pl.when(n == 0)
-    def _():
-        greet_blk(blocks)
-        for g in range(groups):
-            keys[g] = doubled(qkv_ref[:, q_width : q_width + LANES], g)
-            values[g, :, :LANES] = doubled(qkv_ref[:, q_width + LANES : q_width + 2 * LANES], g)
-            values[g, :, LANES:] = jnp.ones((size, LANES), BF16)
-
-    at = pl.multiple_of(here * block, block)
-    starts = jnp.concatenate([starts_ref[pl.ds(at, block), :]] * 2, axis=0)
-    queries = [
-        stacked_heads(qkv_ref[pl.ds(at, block), g * LANES : (g + 1) * LANES]) for g in range(groups)
-    ]
-
-    def step(key_at, width, diagonal):
-        column = lax.broadcasted_iota(jnp.int32, (2 * block, width), 1)
-        allowed = column >= starts - key_at
-        if diagonal:
-            row = lax.broadcasted_iota(jnp.int32, (2 * block, width), 0) % block
-            allowed = allowed & (column <= row)
-        for g in range(groups):
-            scores = nt_dot(queries[g], keys[g, pl.ds(key_at, width), :])
-            weights = jnp.exp2(jnp.where(allowed, scores, MASKED)).astype(BF16)
-            part = nn_dot(weights, values[g, pl.ds(key_at, width), :])
-            if diagonal:
-                total[g] = part
-            else:
-                total[g] += part
-
-    step(at, block, True)
-
-    @pl.when(lax.rem(here, 2) == 1)
-    def _():
-        step(pl.multiple_of((here - 1) * block, block), block, False)
-
-    def body(j, carry):
-        step(pl.multiple_of(j * 2 * block, 2 * block), 2 * block, False)
-        return carry
-
-    lax.fori_loop(0, here // 2, body, 0)
-    low = low_lanes((block, LANES))
-    to = pl.multiple_of(here * 2 * block, 2 * block)
-    for g in range(groups):
-        sums = total[g, :, LANES:]
-        mean = total[g, :, :LANES] / sums
-        out_ref[here, :, g * LANES : (g + 1) * LANES] = jnp.where(low, mean[:block], mean[block:]).astype(BF16)
-        logs_ref[g, pl.ds(to, 2 * block), :] = in_three(jnp.log2(sums[:, :1]))
-
-    @pl.when(here != index)
-    def _():
-        blk_copy(out_ref, got, sent_sem, got_sem, here, index).start()
-
-    @pl.when(n == blocks - 1)
-    def _():
-        got[index] = out_ref[index]
-        for step in range(1, blocks):
-            other = lax.rem(index + step, blocks)
-            blk_copy(out_ref, got, sent_sem, got_sem, other, other).wait()
-        heads_ref[...] = got[...]
-
-
-def attend(qkv, starts, block):
-    size, width = qkv.shape
-    groups = (width - 2 * LANES) // LANES
-    blocks = size // block
-    heads = (blocks, block, groups * LANES)
-    logs = (groups, 2 * size, LANES)
-
-    def keep(shape):
-        return pl.BlockSpec(shape, lambda n: (0,) * len(shape), pipeline_mode=pl.Buffered(1))
-
-    return pl.pallas_call(
-        functools.partial(attend_kernel, groups, block),
-        name="attend",
-        grid=(blocks,),
-        in_specs=[keep((size, width)), keep((size, 1))],
-        out_specs=[keep(heads), keep(logs), keep(heads)],
-        out_shape=[jax.ShapeDtypeStruct(shape, BF16) for shape in (heads, logs, heads)],
+        out_specs=out_specs,
+        out_shape=[jax.ShapeDtypeStruct(shape, kind) for shape, kind in outs],
         scratch_shapes=[
-            pltpu.VMEM((groups, size, LANES), BF16),
-            pltpu.VMEM((groups, size, 2 * LANES), BF16),
-            pltpu.VMEM((groups, 2 * block, 2 * LANES), F32),
+            pltpu.VMEM(moved, BF16),
+            pltpu.VMEM(moved, BF16),
+            pltpu.VMEM((size, LANES), BF16),
+            pltpu.VMEM((size, 2 * LANES), BF16),
+            pltpu.VMEM((2 * block, 2 * LANES), F32),
+            pltpu.VMEM(heads, BF16),
             pltpu.VMEM(heads, BF16),
         ]
-        + blk_sems(blocks),
-        compiler_params=kernel_params(collective_id=1, has_side_effects=True),
-    )(qkv, starts)
+        + [pltpu.SemaphoreType.DMA((groups, blocks))] * 4,
+        compiler_params=kernel_params(collective_id=0, has_side_effects=True),
+    )(tokens, gain, wq, wk, wv, q_gain, k_gain, cosine, sine, starts)
 
 
 def pair_of(name):
@@ -1044,9 +1040,8 @@
     got_sem,
     *refs,
 ):
-    size = qkv_ref.shape[0]
+    size = qkv_ref.shape[1]
     blocks = size // block
-    q_width = groups * LANES
     n = pl.program_id(0)
     index = lax.axis_index("blk")
     core = lax.rem(index, 2)
@@ -1086,15 +1081,16 @@
         pair_grad[...] = jnp.zeros_like(pair_grad)
         for g in range(groups):
             lanes = slice(g * LANES, (g + 1) * LANES)
-            keys[g, :, :LANES] = doubled(qkv_ref[:, q_width : q_width + LANES], g)
+            key, value = parted(qkv_ref[g, :, LANES:])
+            keys[g, :, :LANES] = key
             keys[g, :, LANES:] = minus_three(size)
-            values[g, :, :LANES] = doubled(qkv_ref[:, q_width + LANES : q_width + 2 * LANES], g)
+            values[g, :, :LANES] = value
             values[g, :, LANES:] = minus_three(size)
 
             def fill(i, carry):
                 at = pl.multiple_of(i * block, block)
                 to = pl.multiple_of(i * 2 * block, 2 * block)
-                queries[g, pl.ds(to, 2 * block), :LANES] = stacked_heads(qkv_ref[pl.ds(at, block), lanes])
+                queries[g, pl.ds(to, 2 * block), :LANES] = stacked_heads(qkv_ref[g, pl.ds(at, block), :LANES])
                 queries[g, pl.ds(to, 2 * block), LANES:] = logs_ref[g, pl.ds(to, 2 * block), :]
                 grad = stacked_heads(grad_ref[pl.ds(at, block), lanes])
                 mean = stacked_heads(out_ref[pl.ds(at, block), lanes])
@@ -1194,8 +1190,7 @@
 
 
 def back(line, bits, qkv, logs, out, grad, starts, block, dy_own, dy_got, acts, w_out_parts):
-    size, width = qkv.shape
-    groups = (width - 2 * LANES) // LANES
+    groups, size, width = qkv.shape
     model = dy_own.shape[1]
     rows = acts.shape[1]
     units = acts.shape[0] // FF_TILE
@@ -1207,9 +1202,9 @@
     zs = line_bits(line)
     names = [1] + zs[-2::-1] + bits
     streams = [
+        Stream([1] + zs + bits, names, (down_each, model // 4), LAG, units, swap=zs[-1]),
         Stream([1] + bits[::-1] + zs, names, (down_each, model // 4), LAG, units, swap=zs[-1]),
-        Stream([1] + bits + zs, names, (down_each, model // 4), LAG, units, swap=zs[-1]),
-        Stream([1] + zs + bits, zs[::-1] + bits + [1], (w_rows, LANES), LAG, columns),
+        Stream([1] + bits + zs, zs[::-1] + bits + [1], (w_rows, LANES), LAG, columns),
     ]
     steps = max(
         [stream.steps() for stream in streams]
@@ -1236,7 +1231,7 @@
         scratch += stream.scratch()
 
     outs = [
-        (size // block, block, width),
+        (size // block, block, groups * width),
         (down_rows, model // 2),
         (w_rows, w_out_parts.shape[1]),
     ]
@@ -1669,11 +1664,18 @@
     grad_own = cotangent.reshape(rows, width)
     grad_got = swap_core(grad_own, blk_count)
 
-    hidden_in, proj, qkv = project(
-        flat, g_attn[None], w_query, w_key, w_value, q_gain2, k_gain2, cosine, sine
-    )
-    qkv = qkv.reshape(size, -1)
-    attended, logs, heads = attend(qkv, starts[:, None], tok_count)
+    hidden_in, proj, qkv, attended, logs, heads = forward(
+        flat,
+        g_attn[None],
+        w_query,
+        w_key,
+        w_value,
+        q_gain2,
+        k_gain2,
+        cosine,
+        sine,
+        starts[:, None],
+    )
     output, mid, ffn_gain_grad, w_out_parts, grad_heads, acts, gate_sum, up_sum = middle_layer(
         dp_count,
         bits,

time: 324 us -> 314 us (0.969)
  Pallas kernels: 311 us -> 301 us
    pallas_call x2 -> x1, Pallas kernels: 61.2 us -> 55.8 us  [forward(): pl.pallas_call(functools.partial(forward_kernel, chips, groups), name='fo...]
  transfers between devices with their start and end apart: 1 -> 1, of which waited for: 0 -> 0; matrix products, arithmetic and copies ran while one was open for 2% -> 2% of each run, Pallas kernels for 19% -> 18%
where the time goes in v7:
time: 314 us
  Pallas kernels  301 us (96%)
  local copies, waits for them, and re-layouts  8.68 us (3%)
    pallas_call x1, Pallas kernels, middle_layer(): pl.pallas_call(functools.partial(middle_kernel, line, bits, streams, unit...  107 us
    pallas_call x1, Pallas kernels, back(): pl.pallas_call(functools.partial(back_kernel, groups, block, line, bits,...  91 us
    pallas_call x1, Pallas kernels, forward(): pl.pallas_call(functools.partial(forward_kernel, chips, groups), name='fo...  55.8 us
    pallas_call x1, Pallas kernels, finish(): pl.pallas_call(functools.partial(finish_kernel, line, bits, streams, unit...  45.1 us
  transfers between devices with their start and end apart: 1, of which 0 were waited for; matrix products, arithmetic and copies ran while one was open for 2% of the time, Pallas kernels for 18%

profile of v7, /device:TPU:0, one launch (start us, length us, event | category | flops | bytes accessed | tf_op | source)
XLA Modules:
  0.0 313.9 jit_solution(1715440670760848316)
XLA Ops:
  0.6 0.5 collective-permute-start
  1.2 0.7 tile.4
  1.8 0.6 broadcast_in_dim_tile.6.q_gain_ref
  2.4 0.7 tile.5
  3.1 0.6 broadcast_in_dim_tile.7.k_gain_ref
  3.7 0.8 select_reduce_fusion.2
  4.4 0.1 select_reduce_fusion.1
  4.6 0.1 select_reduce_fusion
  4.7 0.6 reshape.117.starts_ref
  5.3 1.3 copy.28.starts_ref
  6.7 1.8 fusion
  8.5 55.8 %forward.1 = (bf16[512,1024]{1,0:T(8,128)(2,1)}, f32[4,512,384]{2,1,0:T(8,128)}, bf16[2,2048,256]{2,1,0:T(8,128)(2,1)}, bf16[8,256,256]{2,1,0:T(8,128)(2,1)}, bf...) custom-call(bf16[512,1024]{1,0:T(8,128)(2,1)} %bitcast.21, f32[1,1024]{1,0:T(1,128)} %bitcast.33, ...), custom_call_target="tpu_custom_call" | custom-call | tf_op jit(solution)/shard_map/forward/pallas_call | solution.py:573
  64.3 0.0 collective-permute-done.dy_got_ref
  64.3 0.0 copy-start
  64.3 1.0 copy-done
  65.3 106.7 %middle.1 = (bf16[512,1024]{1,0:T(8,128)(2,1)}, f32[512,1024]{1,0:T(8,128)}, f32[1,1024]{1,0:T(1,128)}, bf16[1024,1024]{1,0:T(8,128)(2,1)}, bf16[8,256,256]{2,1,...) custom-call(bf16[512,1024]{1,0:T(8,128)(2,1)} %bitcast.22, ...), custom_call_target="tpu_custom_call" | custom-call | tf_op jit(solution)/shard_map/middle/pallas_call | solution.py:990
  171.9 91.0 %back.1 = (bf16[8,256,512]{2,1,0:T(8,128)(2,1)}, bf16[288,512]{1,0:T(8,128)(2,1)}, bf16[32,1024]{1,0:T(8,128)(2,1)}) custom-call(bf16[2,2048,256]{2,1,0:T(8,128)(2,1)} %get-tuple-element.50.qkv_ref, bf16[2,4096,128]{2,1,0:T(8,128)(2,1)} %get-tuple-element.51.logs_ref, bf16[2048,256]{1,0:T(8,128)(2,1)} %bitcast.28, bf16[2048,256]{1,0:T(8,128)(2,1)} %bitcast.29, ...), custom_call_target="tpu_custom_call" | custom-call | tf_op jit(solution)/shard_map/back/pallas_call | solution.py:1238
  262.9 0.0 copy-start.1
  263.0 45.1 %finish.1 = (bf16[512,1024]{1,0:T(8,128)(2,1)}, f32[24,128]{1,0:T(8,128)}, bf16[32,1024]{1,0:T(8,128)(2,1)}, bf16[32,512]{1,0:T(8,128)(2,1)}, bf16[32,512]{1,0:T...) custom-call(bf16[8,256,512]{2,1,0:T(8,128)(2,1)} %get-tuple-element.56.got_ref, ...), custom_call_target="tpu_custom_call" | custom-call | tf_op jit(solution)/shard_map/finish/pallas_call | solution.py:1536
  308.1 2.7 widen.1
  310.7 1.3 slice_bitcast_fusion
  312.0 0.0 copy-done.1
  312.0 1.0 copy.32
  313.0 1.0 copy.33
  (10 shorter events, 0.1 us)
Async XLA Ops:
  0.6 63.7 %collective-permute-start = (bf16[512,1024]{1,0:T(8,128)(2,1)}, bf16[512,1024]{1,0:T(8,128)(2,1)S(1)}, u32[]{:S(2)}, u32[]{:S(2)}) collective-permute-start(bf16[512,1024]{1,0:T(8,128)(2,1)} %bitcast.25), channel_id=1, source_target_pairs={{0,1},{1,0},{2,3},{3,2},{4,5},{5,4},{6,7},{7,6},{8,9},{9,8},{10,11... | collective-permute-start | bytes 3145736 | tf_op jit(solution)/shard_map/ppermute | solution.py:1610
  64.3 1.0 copy-start
  262.9 49.1 %copy-start.1 = (bf16[512,1024]{1,0:T(8,128)(2,1)S(1)}, bf16[512,1024]{1,0:T(8,128)(2,1)}, u32[]{:S(2)}) copy-start(bf16[512,1024]{1,0:T(8,128)(2,1)} %get-tuple-element.49) | copy-start | bytes 3145732
  308.1 4.9 %copy-start.2 = (bf16[512,1024]{1,0:T(8,128)(2,1)S(1)}, bf16[512,1024]{1,0:T(8,128)(2,1)}, u32[]{:S(2)}) copy-start(bf16[512,1024]{1,0:T(8,128)(2,1)} %get-tuple-element.64) | copy-start | bytes 3145732

commit v8 on v7

--- a/solution.py
+++ b/solution.py
@@ -389,8 +389,7 @@
     wq_ref,
     wk_ref,
     wv_ref,
-    q_gain_ref,
-    k_gain_ref,
+    head_gains_ref,
     cos_ref,
     sin_ref,
     starts_ref,
@@ -447,18 +446,19 @@
         def turn(part, lane, head_gain):
             proj_ref[0, :, lane : lane + LANES] = part
             scale = lax.rsqrt(head_means(part * part) + EPSILON)
-            normed = part * scale * head_gain[...]
+            normed = part * scale * head_gain
             return normed * cos_ref[...] + half_partner(normed) * sin_ref[...]
 
         def put(g, lane, part):
             for half in range(2):
                 send[g, 2 * p + half, :, lane : lane + LANES] = part[half * block : (half + 1) * block].astype(BF16)
 
-        key = turn(keys_of, groups * LANES, k_gain_ref)
+        q_gain, k_gain = head_gains_ref[0:1, :], head_gains_ref[1:2, :]
+        key = turn(keys_of, groups * LANES, k_gain)
         low = low_lanes(key.shape)
         for g in range(groups):
             lanes = slice(g * LANES, (g + 1) * LANES)
-            put(g, 0, turn(queries[:, lanes], g * LANES, q_gain_ref) * QUERY_SCALE)
+            put(g, 0, turn(queries[:, lanes], g * LANES, q_gain) * QUERY_SCALE)
             if g == 0:
                 put(g, LANES, jnp.where(low, key, pltpu.roll(values_of, HEAD_DIM, 1)))
             else:
@@ -488,7 +488,9 @@
         g = (n - chips) // blocks
         here = lax.rem(index + 1 + lax.rem(n - chips, blocks), blocks)
         at = pl.multiple_of(here * block, block)
-        starts = jnp.concatenate([starts_ref[pl.ds(at, block), :]] * 2, axis=0)
+        row_at = pl.multiple_of(here * 2 * block, 2 * block)
+        lines = jnp.broadcast_to(starts_ref[:, pl.ds(row_at, 2 * block)], (LANES, 2 * block))
+        starts = lines.T[:, :1]
         query = stacked_heads(got[g, here, :, :LANES])
 
         def step(key_at, width, diagonal):
@@ -546,7 +548,7 @@
             heads_ref[:, :, g * LANES : (g + 1) * LANES] = out_got[g]
 
 
-def forward(tokens, gain, wq, wk, wv, q_gain, k_gain, cosine, sine, starts):
+def forward(tokens, gain, wq, wk, wv, head_gains, cosine, sine, starts):
     rows, width = tokens.shape
     chips = wk.shape[1] // LANES
     q_width = wq.shape[1] // chips
@@ -580,11 +582,10 @@
             pl.BlockSpec((width, q_width), lambda n: (0, at(n))),
             pl.BlockSpec((width, LANES), lambda n: (0, at(n))),
             pl.BlockSpec((width, LANES), lambda n: (0, at(n))),
-            keep((1, LANES)),
-            keep((1, LANES)),
+            keep((2, LANES)),
             keep((rows, LANES)),
             keep((rows, LANES)),
-            keep((size, 1)),
+            keep((1, 2 * size)),
         ],
         out_specs=out_specs,
         out_shape=[jax.ShapeDtypeStruct(shape, kind) for shape, kind in outs],
@@ -599,7 +600,7 @@
         ]
         + [pltpu.SemaphoreType.DMA((groups, blocks))] * 4,
         compiler_params=kernel_params(collective_id=0, has_side_effects=True),
-    )(tokens, gain, wq, wk, wv, q_gain, k_gain, cosine, sine, starts)
+    )(tokens, gain, wq, wk, wv, head_gains, cosine, sine, starts)
 
 
 def pair_of(name):
@@ -683,15 +684,10 @@
 
 
 def step_streams(streams, step):
-    longest = max(len(stream.path) for stream in streams)
-    for k in range(longest):
-        for stream in streams:
-            if k < len(stream.path):
-                stream.take(k, step)
-    for k in range(longest):
-        for stream in streams:
-            if k < len(stream.path):
-                stream.send(k, step)
+    for stream in streams:
+        for k in range(len(stream.path)):
+            stream.take(k, step)
+            stream.send(k, step)
 
 
 def line_bits(line):
@@ -1305,8 +1301,7 @@
     wq_ref,
     wk_ref,
     wv_ref,
-    q_gain_ref,
-    k_gain_ref,
+    head_gains_ref,
     cos_ref,
     sin_ref,
     ffn_gain_ref,
@@ -1414,6 +1409,8 @@
     def _():
         hidden = hidden_ref[...]
 
+        q_gain, k_gain = head_gains_ref[0:1, :], head_gains_ref[1:2, :]
+
         def got_lanes(lane):
             return jnp.concatenate(
                 [got_ref[0, :, lane : lane + LANES], got_ref[1, :, lane : lane + LANES]], axis=0
@@ -1425,20 +1422,20 @@
             scale = lax.rsqrt(head_means(block * block) + EPSILON)
             normal = block * scale
             gains[0, place : place + 1, :] += jnp.sum(turned * normal, axis=0, keepdims=True)
-            pushed = turned * head_gain[...]
+            pushed = turned * head_gain
             inner = head_means(pushed * normal)
             return (scale * (pushed - normal * inner)).astype(BF16)
 
         width = tokens_ref.shape[1]
         lines = width // LANES
         query = jnp.concatenate(
-            [back(got_lanes(2 * at), at, q_gain_ref, 2 * lines) for at in range(0, q_width, LANES)],
+            [back(got_lanes(2 * at), at, q_gain, 2 * lines) for at in range(0, q_width, LANES)],
             axis=1,
         )
         first, second = got_lanes(LANES), got_lanes(3 * LANES)
         low = low_lanes(first.shape)
         key = jnp.where(low, first, pltpu.roll(second, HEAD_DIM, 1))
-        key = back(key, q_width, k_gain_ref, 2 * lines + 1)
+        key = back(key, q_width, k_gain, 2 * lines + 1)
         value = jnp.where(low, pltpu.roll(first, HEAD_DIM, 1), second).astype(BF16)
         for stream, part in ((query_stream, query), (pair_stream, jnp.concatenate([key, value], axis=1))):
             shape = stream.shape(stream.names[0])
@@ -1476,8 +1473,7 @@
     wq,
     wk,
     wv,
-    q_gain,
-    k_gain,
+    head_gains,
     cosine,
     sine,
     ffn_gain,
@@ -1547,8 +1543,7 @@
             pl.BlockSpec((width, q_width), lambda n: (0, at(n))),
             pl.BlockSpec((width, LANES), lambda n: (0, at(n))),
             pl.BlockSpec((width, LANES), lambda n: (0, at(n))),
-            keep((1, LANES)),
-            keep((1, LANES)),
+            keep((2, LANES)),
             keep((rows, LANES)),
             keep((rows, LANES)),
             keep((1, width)),
@@ -1570,8 +1565,7 @@
         wq,
         wk,
         wv,
-        q_gain,
-        k_gain,
+        head_gains,
         cosine,
         sine,
         ffn_gain,
@@ -1584,16 +1578,18 @@
 def widen_kernel(count, gains_ref, *refs):
     for source, target in zip(refs[:count], refs[count : 2 * count]):
         target[...] = source[...].astype(F32)
-    attn_ref, ffn_ref, heads_ref = refs[2 * count :]
+    attn_ref, ffn_ref, query_ref, key_ref = refs[2 * count :]
     lines = attn_ref.shape[0]
     attn_ref[...] = gains_ref[:lines, :]
     ffn_ref[...] = gains_ref[lines : 2 * lines, :]
     both = gains_ref[2 * lines : 2 * lines + 2, :]
-    heads_ref[...] = both + pltpu.roll(both, HEAD_DIM, 1)
+    both = (both + pltpu.roll(both, HEAD_DIM, 1))[:, :HEAD_DIM]
+    query_ref[...] = both[0:1]
+    key_ref[...] = both[1:2]
 
 
 def widen(gains, lines, parts):
-    shapes = [part.shape for part in parts] + [(lines, LANES), (lines, LANES), (2, LANES)]
+    shapes = [part.shape for part in parts] + [(lines, LANES)] * 2 + [(1, HEAD_DIM)] * 2
     return pl.pallas_call(
         functools.partial(widen_kernel, len(parts)),
         name="widen",
@@ -1652,8 +1648,7 @@
     angles = positions * freqs
     cosine = jnp.cos(angles)
     sine = jnp.sin(angles) * jnp.where(lane % HEAD_DIM < half_head, -1.0, 1.0)
-    q_gain2 = jnp.tile(q_gain, 2)[None]
-    k_gain2 = jnp.tile(k_gain, 2)[None]
+    head_gains = jnp.concatenate([q_gain, q_gain, k_gain, k_gain]).reshape(2, LANES)
     all_places = jnp.arange(size, dtype=jnp.int32)
     own_ends = lax.dynamic_slice_in_dim(ends, core, 1, axis=0)
     starts = jnp.max(jnp.where(all_places[:, None] >= own_ends, own_ends, 0), axis=1)
@@ -1670,11 +1665,10 @@
         w_query,
         w_key,
         w_value,
-        q_gain2,
-        k_gain2,
+        head_gains,
         cosine,
         sine,
-        starts[:, None],
+        starts_two,
     )
     output, mid, ffn_gain_grad, w_out_parts, grad_heads, acts, gate_sum, up_sum = middle_layer(
         dp_count,
@@ -1715,8 +1709,7 @@
         w_query,
         w_key,
         w_value,
-        q_gain2,
-        k_gain2,
+        head_gains,
         cosine,
         sine,
         ffn_gain_grad,
@@ -1724,10 +1717,10 @@
         up_sum,
         down_sum,
     )
-    *sums, gain_attn, gain_ffn, gain_heads = widen(gains, width // LANES, sums + [w_out_sum])
+    *sums, gain_attn, gain_ffn, gain_query, gain_key = widen(gains, width // LANES, sums + [w_out_sum])
     grad_w_query, grad_w_key, grad_w_value, grad_w_gate, grad_w_up, grad_w_down, grad_w_out = sums
     gain_attn, gain_ffn = gain_attn.reshape(width), gain_ffn.reshape(width)
-    gain_query, gain_key = gain_heads[0, :HEAD_DIM], gain_heads[1, :HEAD_DIM]
+    gain_query, gain_key = gain_query[0], gain_key[0]
     return (
         output.reshape(tokens.shape),
         input_grad.reshape(tokens.shape),

time: 314 us -> 305 us (0.971)
  local copies, waits for them, and re-layouts: 8.68 us -> 3.57 us
  Pallas kernels: 301 us -> 296 us
  transfers between devices with their start and end apart: 1 -> 1, of which waited for: 0 -> 0; matrix products, arithmetic and copies ran while one was open for 2% -> 2% of each run, Pallas kernels for 18% -> 19%
where the time goes in v8:
time: 305 us
  Pallas kernels  296 us (97%)
  other arithmetic  4.15 us (1%)
  local copies, waits for them, and re-layouts  3.57 us (1%)
    pallas_call x1, Pallas kernels, middle_layer(): pl.pallas_call(functools.partial(middle_kernel, line, bits, streams, unit...  106 us
    pallas_call x1, Pallas kernels, back(): pl.pallas_call(functools.partial(back_kernel, groups, block, line, bits,...  88.4 us
    pallas_call x1, Pallas kernels, forward(): pl.pallas_call(functools.partial(forward_kernel, chips, groups), name='fo...  56.9 us
    pallas_call x1, Pallas kernels, finish(): pl.pallas_call(functools.partial(finish_kernel, line, bits, streams, unit...  42 us
  transfers between devices with their start and end apart: 1, of which 0 were waited for; matrix products, arithmetic and copies ran while one was open for 2% of the time, Pallas kernels for 19%

profile of v8, /device:TPU:0, one launch (start us, length us, event | category | flops | bytes accessed | tf_op | source)
XLA Modules:
  0.0 304.9 jit_solution(4311933759074857233)
XLA Ops:
  0.6 0.5 collective-permute-start
  1.2 0.8 select_reduce_fusion.2
  1.9 0.1 select_reduce_fusion.1
  2.1 0.1 select_reduce_fusion
  2.2 0.6 reshape.115.starts_ref
  2.8 1.4 maximum_bitcast_fusion.head_gains_ref
  4.2 1.8 fusion
  6.0 56.9 %forward.1 = (bf16[512,1024]{1,0:T(8,128)(2,1)}, f32[4,512,384]{2,1,0:T(8,128)}, bf16[2,2048,256]{2,1,0:T(8,128)(2,1)}, bf16[8,256,256]{2,1,0:T(8,128)(2,1)}, bf...) custom-call(bf16[512,1024]{1,0:T(8,128)(2,1)} %bitcast.20, f32[1,1024]{1,0:T(1,128)} %bitcast.31, ...), custom_call_target="tpu_custom_call" | custom-call | tf_op jit(solution)/shard_map/forward/pallas_call | solution.py:575
  62.9 0.0 collective-permute-done.dy_got_ref
  62.9 0.0 copy-start
  62.9 1.0 copy-done
  63.9 106.0 %middle.1 = (bf16[512,1024]{1,0:T(8,128)(2,1)}, f32[512,1024]{1,0:T(8,128)}, f32[1,1024]{1,0:T(1,128)}, bf16[1024,1024]{1,0:T(8,128)(2,1)}, bf16[8,256,256]{2,1,...) custom-call(bf16[512,1024]{1,0:T(8,128)(2,1)} %bitcast.21, ...), custom_call_target="tpu_custom_call" | custom-call | tf_op jit(solution)/shard_map/middle/pallas_call | solution.py:986
  169.9 88.4 %back.1 = (bf16[8,256,512]{2,1,0:T(8,128)(2,1)}, bf16[288,512]{1,0:T(8,128)(2,1)}, bf16[32,1024]{1,0:T(8,128)(2,1)}) custom-call(bf16[2,2048,256]{2,1,0:T(8,128)(2,1)} %get-tuple-element.51.qkv_ref, bf16[2,4096,128]{2,1,0:T(8,128)(2,1)} %get-tuple-element.52.logs_ref, bf16[2048,256]{1,0:T(8,128)(2,1)} %bitcast.27, bf16[2048,256]{1,0:T(8,128)(2,1)} %bitcast.28, ...), custom_call_target="tpu_custom_call" | custom-call | tf_op jit(solution)/shard_map/back/pallas_call | solution.py:1234
  258.3 0.0 copy-start.1
  258.3 42.0 %finish.1 = (bf16[512,1024]{1,0:T(8,128)(2,1)}, f32[24,128]{1,0:T(8,128)}, bf16[32,1024]{1,0:T(8,128)(2,1)}, bf16[32,512]{1,0:T(8,128)(2,1)}, bf16[32,512]{1,0:T...) custom-call(bf16[8,256,512]{2,1,0:T(8,128)(2,1)} %get-tuple-element.57.got_ref, ...), custom_call_target="tpu_custom_call" | custom-call | tf_op jit(solution)/shard_map/finish/pallas_call | solution.py:1532
  300.3 0.0 copy-start.2
  300.3 2.7 widen.1
  302.9 0.0 copy-done.1
  302.9 1.0 copy.30
  303.9 0.0 copy-done.2
  303.9 1.0 copy.31
  (8 shorter events, 0.0 us)
Async XLA Ops:
  0.6 62.2 %collective-permute-start = (bf16[512,1024]{1,0:T(8,128)(2,1)}, bf16[512,1024]{1,0:T(8,128)(2,1)S(1)}, u32[]{:S(2)}, u32[]{:S(2)}) collective-permute-start(bf16[512,1024]{1,0:T(8,128)(2,1)} %bitcast.24), channel_id=1, source_target_pairs={{0,1},{1,0},{2,3},{3,2},{4,5},{5,4},{6,7},{7,6},{8,9},{9,8},{10,11... | collective-permute-start | bytes 3145736 | tf_op jit(solution)/shard_map/ppermute | solution.py:1606
  62.9 1.0 copy-start
  258.3 44.7 %copy-start.1 = (bf16[512,1024]{1,0:T(8,128)(2,1)S(1)}, bf16[512,1024]{1,0:T(8,128)(2,1)}, u32[]{:S(2)}) copy-start(bf16[512,1024]{1,0:T(8,128)(2,1)} %get-tuple-element.50) | copy-start | bytes 3145732
  300.3 3.7 %copy-start.2 = (bf16[512,1024]{1,0:T(8,128)(2,1)S(1)}, bf16[512,1024]{1,0:T(8,128)(2,1)}, u32[]{:S(2)}) copy-start(bf16[512,1024]{1,0:T(8,128)(2,1)} %get-tuple-element.65) | copy-start | bytes 3145732

commit v9 on v8

--- a/solution.py
+++ b/solution.py
@@ -465,11 +465,6 @@
                 put(g, LANES, jnp.where(low, pltpu.roll(key, HEAD_DIM, 1), values_of))
         give(0, p)
 
-    @pl.when(n == chips - 1)
-    def _():
-        for step in range(chips):
-            give(1, lax.rem(index // 2 + 1 + step, chips))
-
     for g in range(groups):
 
         @pl.when(n == chips + g * blocks)
@@ -477,6 +472,9 @@
             for step in range(1, blocks):
                 other = lax.rem(index + step, blocks)
                 blk_copy(send.at[g], got.at[g], sent_sem.at[g], got_sem.at[g], other, other).wait()
+            if g + 1 < groups:
+                for step in range(chips):
+                    give(g + 1, lax.rem(index // 2 + 1 + step, chips))
             for i in range(blocks):
                 here = slice(i * block, (i + 1) * block)
                 qkv_ref[g, here, :] = got[g, i]

time: 305 us -> 304 us (level)
  transfers between devices with their start and end apart: 1 -> 1, of which waited for: 0 -> 0; matrix products, arithmetic and copies ran while one was open for 2% -> 2% of each run, Pallas kernels for 19% -> 18%
where the time goes in v9:
time: 304 us
  Pallas kernels  295 us (97%)
  other arithmetic  4.15 us (1%)
  local copies, waits for them, and re-layouts  3.57 us (1%)
    pallas_call x1, Pallas kernels, middle_layer(): pl.pallas_call(functools.partial(middle_kernel, line, bits, streams, unit...  106 us
    pallas_call x1, Pallas kernels, back(): pl.pallas_call(functools.partial(back_kernel, groups, block, line, bits,...  88.4 us
    pallas_call x1, Pallas kernels, forward(): pl.pallas_call(functools.partial(forward_kernel, chips, groups), name='fo...  56.1 us
    pallas_call x1, Pallas kernels, finish(): pl.pallas_call(functools.partial(finish_kernel, line, bits, streams, unit...  41.9 us
  transfers between devices with their start and end apart: 1, of which 0 were waited for; matrix products, arithmetic and copies ran while one was open for 2% of the time, Pallas kernels for 18%

profile of v9, /device:TPU:0, one launch (start us, length us, event | category | flops | bytes accessed | tf_op | source)
XLA Modules:
  0.0 304.3 jit_solution(3921499551788632990)
XLA Ops:
  0.6 0.5 collective-permute-start
  1.2 0.8 select_reduce_fusion.2
  1.9 0.1 select_reduce_fusion.1
  2.1 0.1 select_reduce_fusion
  2.2 0.6 reshape.115.starts_ref
  2.8 1.4 maximum_bitcast_fusion.head_gains_ref
  4.2 1.8 fusion
  6.0 56.1 %forward.1 = (bf16[512,1024]{1,0:T(8,128)(2,1)}, f32[4,512,384]{2,1,0:T(8,128)}, bf16[2,2048,256]{2,1,0:T(8,128)(2,1)}, bf16[8,256,256]{2,1,0:T(8,128)(2,1)}, bf...) custom-call(bf16[512,1024]{1,0:T(8,128)(2,1)} %bitcast.20, f32[1,1024]{1,0:T(1,128)} %bitcast.31, ...), custom_call_target="tpu_custom_call" | custom-call | tf_op jit(solution)/shard_map/forward/pallas_call | solution.py:573
  62.1 0.0 collective-permute-done.dy_got_ref
  62.1 0.0 copy-start
  62.2 1.0 copy-done
  63.1 106.3 %middle.1 = (bf16[512,1024]{1,0:T(8,128)(2,1)}, f32[512,1024]{1,0:T(8,128)}, f32[1,1024]{1,0:T(1,128)}, bf16[1024,1024]{1,0:T(8,128)(2,1)}, bf16[8,256,256]{2,1,...) custom-call(bf16[512,1024]{1,0:T(8,128)(2,1)} %bitcast.21, ...), custom_call_target="tpu_custom_call" | custom-call | tf_op jit(solution)/shard_map/middle/pallas_call | solution.py:984
  169.4 88.4 %back.1 = (bf16[8,256,512]{2,1,0:T(8,128)(2,1)}, bf16[288,512]{1,0:T(8,128)(2,1)}, bf16[32,1024]{1,0:T(8,128)(2,1)}) custom-call(bf16[2,2048,256]{2,1,0:T(8,128)(2,1)} %get-tuple-element.51.qkv_ref, bf16[2,4096,128]{2,1,0:T(8,128)(2,1)} %get-tuple-element.52.logs_ref, bf16[2048,256]{1,0:T(8,128)(2,1)} %bitcast.27, bf16[2048,256]{1,0:T(8,128)(2,1)} %bitcast.28, ...), custom_call_target="tpu_custom_call" | custom-call | tf_op jit(solution)/shard_map/back/pallas_call | solution.py:1232
  257.7 0.0 copy-start.1
  257.8 41.9 %finish.1 = (bf16[512,1024]{1,0:T(8,128)(2,1)}, f32[24,128]{1,0:T(8,128)}, bf16[32,1024]{1,0:T(8,128)(2,1)}, bf16[32,512]{1,0:T(8,128)(2,1)}, bf16[32,512]{1,0:T...) custom-call(bf16[8,256,512]{2,1,0:T(8,128)(2,1)} %get-tuple-element.57.got_ref, ...), custom_call_target="tpu_custom_call" | custom-call | tf_op jit(solution)/shard_map/finish/pallas_call | solution.py:1530
  299.7 0.0 copy-start.2
  299.7 2.7 widen.1
  302.4 0.0 copy-done.1
  302.4 1.0 copy.30
  303.3 0.0 copy-done.2
  303.3 1.0 copy.31
  (8 shorter events, 0.0 us)
Async XLA Ops:
  0.6 61.5 %collective-permute-start = (bf16[512,1024]{1,0:T(8,128)(2,1)}, bf16[512,1024]{1,0:T(8,128)(2,1)S(1)}, u32[]{:S(2)}, u32[]{:S(2)}) collective-permute-start(bf16[512,1024]{1,0:T(8,128)(2,1)} %bitcast.24), channel_id=1, source_target_pairs={{0,1},{1,0},{2,3},{3,2},{4,5},{5,4},{6,7},{7,6},{8,9},{9,8},{10,11... | collective-permute-start | bytes 3145736 | tf_op jit(solution)/shard_map/ppermute | solution.py:1604
  62.1 1.0 copy-start
  257.7 44.6 %copy-start.1 = (bf16[512,1024]{1,0:T(8,128)(2,1)S(1)}, bf16[512,1024]{1,0:T(8,128)(2,1)}, u32[]{:S(2)}) copy-start(bf16[512,1024]{1,0:T(8,128)(2,1)} %get-tuple-element.50) | copy-start | bytes 3145732
  299.7 3.7 %copy-start.2 = (bf16[512,1024]{1,0:T(8,128)(2,1)S(1)}, bf16[512,1024]{1,0:T(8,128)(2,1)}, u32[]{:S(2)}) copy-start(bf16[512,1024]{1,0:T(8,128)(2,1)} %get-tuple-element.65) | copy-start | bytes 3145732
